TPU v7x, 128 devices: a whole 4x4x4 slice. The times are simulated.
128 devices in a mesh: gy: 8 (over x, core), gx: 8 (over z, y_lo), ctx: 2 (over y_hi).
Axes of the slice: x: 4, y: 4 (y_hi: 2, y_lo: 2; y = y_hi * 2 + y_lo), z: 4, core: 2. Of those that a mesh axis runs over, the one named last changes fastest.
Arguments:
- fine: bfloat16 [256, 256, 128], P(('gy', 'ctx'), 'gx'), may hold values from -6 to 6
- context: bfloat16 [64, 64, 512], P('gy', 'gx', 'ctx'), may hold values from -6 to 6
- interp_rows: bfloat16 [34, 10], replicated, may hold values from -2 to 2
- interp_cols: bfloat16 [34, 10], replicated, may hold values from -2 to 2
- fine_weight: bfloat16 [3, 3, 128, 128], replicated, may hold values from -0.078125 to 0.078125
- ctx_weight: bfloat16 [3, 3, 512, 128], replicated, may hold values from -0.09375 to 0.09375
- conv_weight: bfloat16 [3, 3, 128, 128], replicated, may hold values from -0.1875 to 0.1875
- hidden_weight: bfloat16 [128, 1024], replicated, may hold values from -0.5 to 0.5
- bin_weight: bfloat16 [1024, 512], replicated, may hold values from -0.75 to 0.75
- cell_index: int32 [16, 8, 256], P(('gy', 'ctx'), 'gx'), may hold values from 0 to 511, as said below
- counts: int32 [16, 8], P(('gy', 'ctx'), 'gx'), may hold values from 0 to 256, as said below
- labels: int32 [16, 8, 256], P(('gy', 'ctx'), 'gx'), may hold values from 0 to 511
Outputs:
- loss: float32 [], replicated
- grad_fine_weight: float32 [3, 3, 128, 128], replicated
- grad_ctx_weight: float32 [3, 3, 512, 128], P(None, None, 'ctx')
- grad_conv_weight: float32 [3, 3, 128, 128], replicated
- grad_hidden_weight: float32 [128, 1024], replicated
- grad_bin_weight: float32 [1024, 512], replicated
Inputs may be any that keep to these rules, and one draw needn't show every extreme that they name: `cell_index`: within one device's slots the indices are distinct; slots at or past the count also hold valid indices. `counts`: some device has all 256 slots live in every draw.
All inputs are finite; a program needn't handle non-finite values.
Results may differ from a plain program's by a relative error of at most 0.01.
Values may be sent and summed in bfloat16 or wider, within the bound.
No kernel may reach another device: no remote copies, remote signals or barrier semaphores. Data moves between devices by JAX's collectives and lax.ppermute only.
A program may use at most 64 MiB of HBM per device.

v0:
```python
import jax
import jax.numpy as jnp
from jax import lax
from jax.sharding import PartitionSpec as P

HID = 1024
BINS = 512
CAP = 256


def extended(x, sides, width):
    for axis, dim in sides:
        count, length = (lax.axis_size(axis), x.shape[dim])
        up = [(i, (i + 1) % count) for i in range(count - 1)]
        down = [(j, i) for i, j in up]
        last = lax.slice_in_dim(x, length - width, length, axis=dim)
        first = lax.slice_in_dim(x, 0, width, axis=dim)
        before = lax.ppermute(last, axis, up)
        after = lax.ppermute(first, axis, down)
        x = jnp.concatenate([before, x, after], axis=dim)
    return x


def silu_grad(v):
    s = jax.nn.sigmoid(v)
    return s * (1.0 + v * (1.0 - s))


def conv_rows(padded, weight, rows, cols):
    total = None
    for dy in range(3):
        for dx in range(3):
            patch = padded[dy : dy + rows, dx : dx + cols, :].reshape(rows * cols, -1)
            term = jnp.dot(patch, weight[dy, dx], preferred_element_type=jnp.float32)
            total = term if total is None else total + term
    return total.reshape(rows, cols, -1)


def weight_grad(padded, grad, rows, cols):
    flat_grad = grad.reshape(rows * cols, -1)
    parts = []
    for dy in range(3):
        for dx in range(3):
            patch = padded[dy : dy + rows, dx : dx + cols, :].reshape(rows * cols, -1)
            parts.append(
                lax.dot_general(
                    patch, flat_grad, (((0,), (0,)), ((), ())), preferred_element_type=jnp.float32
                )
            )
    return jnp.stack(parts).reshape(3, 3, padded.shape[2], flat_grad.shape[1])


def conv_back(gpad, weight, rows, cols):
    total = None
    for dy in range(3):
        for dx in range(3):
            patch = gpad[2 - dy : 2 - dy + rows, 2 - dx : 2 - dx + cols, :].reshape(rows * cols, -1)
            term = lax.dot_general(
                patch, weight[dy, dx], (((1,), (1,)), ((), ())), preferred_element_type=jnp.float32
            )
            total = term if total is None else total + term
    return total.reshape(rows, cols, -1)


def context_field(block, row_mat, col_mat, row_start, grid_rows, col_start, grid_cols):
    mid = jnp.einsum("ia,abk->ibk", row_mat, block, preferred_element_type=jnp.float32).astype(
        jnp.bfloat16
    )
    wide = jnp.einsum("jb,ibk->ijk", col_mat, mid, preferred_element_type=jnp.float32)
    grow = row_start + jnp.arange(row_mat.shape[0], dtype=jnp.int32) - 1
    gcol = col_start + jnp.arange(col_mat.shape[0], dtype=jnp.int32) - 1
    keep = ((grow >= 0) & (grow < grid_rows))[:, None] & ((gcol >= 0) & (gcol < grid_cols))[None, :]
    return (wide * keep[:, :, None].astype(jnp.float32)).astype(jnp.bfloat16)


def head_rows(rows, lab, weight, hidden_weight, bin_weight):
    z = jnp.dot(rows, hidden_weight, preferred_element_type=jnp.float32)
    act = jax.nn.silu(z).astype(jnp.bfloat16)
    logits = jnp.dot(act, bin_weight, preferred_element_type=jnp.float32)
    top = jax.nn.logsumexp(logits, axis=1)
    onehot = (lab[:, None] == jnp.arange(logits.shape[1], dtype=jnp.int32)[None, :]).astype(
        jnp.float32
    )
    picked = jnp.sum(logits * onehot, axis=1)
    loss = jnp.sum(weight * (top - picked))
    probs = jnp.exp(logits - top[:, None])
    dlogits = ((probs - onehot) * weight[:, None]).astype(jnp.bfloat16)
    gbin = lax.dot_general(
        act, dlogits, (((0,), (0,)), ((), ())), preferred_element_type=jnp.float32
    )
    dact = lax.dot_general(
        dlogits, bin_weight, (((1,), (1,)), ((), ())), preferred_element_type=jnp.float32
    )
    dz = (dact * silu_grad(z)).astype(jnp.bfloat16)
    ghid = lax.dot_general(rows, dz, (((0,), (0,)), ((), ())), preferred_element_type=jnp.float32)
    drows = lax.dot_general(
        dz, hidden_weight, (((1,), (1,)), ((), ())), preferred_element_type=jnp.float32
    )
    return (loss, ghid, gbin, drows)


def local(
    fine,
    context,
    interp_rows,
    interp_cols,
    fine_weight,
    ctx_weight,
    conv_weight,
    hidden_weight,
    bin_weight,
    cell_index,
    counts,
    labels,
):
    rows, cols, width = fine.shape
    ctx_count = lax.axis_size("ctx")
    ctx_pos = lax.axis_index("ctx")
    tile_rows = rows * ctx_count
    grid_rows = lax.axis_size("gy") * tile_rows
    grid_cols = lax.axis_size("gx") * cols
    row_anchor = lax.axis_index("gy") * tile_rows
    col_anchor = lax.axis_index("gx") * cols
    fine_pad = extended(fine, ((("gy", "ctx"), 0), ("gx", 1)), 1)
    pre_one = conv_rows(fine_pad, fine_weight, rows, cols)
    coarse_pad = extended(context, (("gy", 0), ("gx", 1)), 1)
    coarse_all = lax.all_gather(coarse_pad, "ctx", axis=2, tiled=True)
    row_mat = lax.dynamic_slice_in_dim(interp_rows, ctx_pos * rows, rows + 2, 0)
    field = context_field(
        coarse_all,
        row_mat,
        interp_cols,
        row_anchor + ctx_pos * rows,
        grid_rows,
        col_anchor,
        grid_cols,
    )
    pre_one = pre_one + conv_rows(field, ctx_weight, rows, cols)
    h_one = jax.nn.silu(pre_one).astype(jnp.bfloat16)
    h_one_pad = extended(h_one, ((("gy", "ctx"), 0), ("gx", 1)), 1)
    pre_two = conv_rows(h_one_pad, conv_weight, rows, cols)
    h_two = jax.nn.silu(pre_two).astype(jnp.bfloat16)
    flat_cells = h_two.reshape(rows * cols, width)
    own_idx = cell_index[0, 0]
    own_lab = labels[0, 0]
    own_num = counts[0, 0]
    own_rows = flat_cells[own_idx]
    total = lax.psum(own_num.astype(jnp.float32), ("gy", "gx", "ctx"))
    block = min(512, CAP)
    init = (
        jnp.zeros((), jnp.float32),
        jnp.zeros((width, HID), jnp.float32),
        jnp.zeros((HID, BINS), jnp.float32),
    )
    weight_all = (jnp.arange(CAP, dtype=jnp.int32) < own_num).astype(jnp.float32) / total

    def visit(step, carry):
        loss, ghid, gbin, back = carry
        part_loss, part_hid, part_bin, drows = head_rows(
            own_rows, own_lab, weight_all, hidden_weight, bin_weight
        )
        return (loss + part_loss, ghid + part_hid, gbin + part_bin, drows)

    loss, ghid, gbin, grad_rows = lax.fori_loop(
        0, CAP // block, visit, init + (jnp.zeros((CAP, width), jnp.float32),)
    )
    grad_cells = (
        jnp.zeros((rows * cols, width), jnp.float32)
        .at[own_idx]
        .add(grad_rows)
        .reshape(rows, cols, width)
    )
    g_two = (grad_cells * silu_grad(pre_two)).astype(jnp.bfloat16)
    gconv = weight_grad(h_one_pad, g_two, rows, cols)
    g_two_pad = extended(g_two, ((("gy", "ctx"), 0), ("gx", 1)), 1)
    g_one = (conv_back(g_two_pad, conv_weight, rows, cols) * silu_grad(pre_one)).astype(
        jnp.bfloat16
    )
    gfine = weight_grad(fine_pad, g_one, rows, cols)
    gctx = lax.psum_scatter(
        weight_grad(field, g_one, rows, cols), "ctx", scatter_dimension=2, tiled=True
    )
    gctx = lax.psum(gctx, ("gy", "gx"))
    loss, ghid, gbin, gfine, gconv = lax.psum((loss, ghid, gbin, gfine, gconv), ("gy", "gx", "ctx"))
    return (loss, gfine, gctx, gconv, ghid, gbin)


def solution(mesh):
    in_specs = (
        P(("gy", "ctx"), "gx", None),
        P("gy", "gx", "ctx"),
        P(),
        P(),
        P(),
        P(),
        P(),
        P(),
        P(),
        P(("gy", "ctx"), "gx", None),
        P(("gy", "ctx"), "gx"),
        P(("gy", "ctx"), "gx", None),
    )
    out_specs = (P(), P(), P(None, None, "ctx", None), P(), P(), P())
    return jax.shard_map(local, mesh=mesh, in_specs=in_specs, out_specs=out_specs, check_vma=False)
```

profile of v0, /device:TPU:1, one launch (start us, length us, event | category | flops | bytes accessed | tf_op | source)
XLA Modules:
  0.0 902.4 jit_solution(3108579532577103106)
XLA Ops:
  8.9 3.3 collective-permute-start.5
  12.2 3.1 collective-permute-start.4
  16.0 4.1 collective-permute-start.1
  20.1 2.7 collective-permute-start
  24.3 67.8 %psum.49 = f32[]{:T(128)} all-reduce(f32[]{:T(128)S(6)} %convert_element_type.58), channel_id=1, replica_groups=mesh['gy'=8,'gx'=8,'ctx'=2] {'gy','gx','ctx'}, use_global_device_ids=true, to_apply=%region_0.1 | all-reduce | flops 1 | bytes 8 | tf_op jit(solution)/shard_map/psum | solution.py:148
  93.5 2.4 collective-permute-start.6
  95.9 1.3 collective-permute-start.7
  98.3 4.0 collective-permute-start.2
  102.3 1.3 collective-permute-start.3
  105.6 5.5 all_gather.3
  117.6 4.4 collective-permute-start.8
  122.0 4.8 collective-permute-start.9
  126.8 1.8 collective-permute-done.9
  128.6 4.7 collective-permute-start.10
  133.3 1.3 collective-permute-start.11
  134.8 4.1 collective-permute-done.11
  145.9 1.5 scatter_custom_fusion
  147.4 1.1 multiply_convert_fusion.5
  148.5 6.3 collective-permute-start.12
  154.9 1.9 collective-permute-start.13
  157.9 2.9 collective-permute-done.13
  160.8 1.3 collective-permute-start.14
  162.1 4.9 collective-permute-start.15
  173.1 1.4 copy-done.1
  178.0 2.0 fusion.149
  183.2 33.4 %reduce-scatter.2.cloned.1.call-done = f32[3,3,256,128]{3,2,1,0:T(8,128)} async-done(((f32[3,3,512,128]{3,2,1,0:T(8,128)}), f32[3,3,256,128]{3,2,1,0:T(8,128)}) %reduce-scatter.2.cloned.1.call-update) | async-done | bytes 1179664 | tf_op jit(solution)/shard_map/reduce_scatter | solution.py:180
  216.6 65.8 %psum.50 = f32[]{:T(128)} all-reduce(f32[]{:T(128)} %get-tuple-element.41), channel_id=1, replica_groups=mesh['gy'=8,'gx'=8,'ctx'=2] {'gy','gx','ctx'}, use_global_device_ids=true, to_apply=%region_5.6 | all-reduce | flops 1 | bytes 8 | tf_op jit(solution)/shard_map/psum | solution.py:184
  282.3 74.7 %all-reduce.6.cloned.1.call-done = (f32[3,3,128,128]{3,2,1,0:T(8,128)}, f32[3,3,128,128]{3,2,1,0:T(8,128)}, f32[128,1024]{1,0:T(8,128)}, f32[1024,512]{1,0:T(8,128)}) async-done(((f32[3,3,128,128]{3,2,1,0:T(8,128)}, f32[3,3,128,128]{3,2,1,0:T(8,128)}, f32[128,1024]{1,0:T(8,128)}, f32[1024,512]{1,0:T(8,128)}), (f32[3,3,128,128]{3,2,1,0:T(8,128)}, f32[3,3,128,128]{3,2,1,0:T(8,128)}, f32[128,1024]{1,0:T(8,128)}, ...) | async-done | bytes 3801104 | tf_op jit(solution)/shard_map/psum | solution.py:184
  357.0 530.5 %all-reduce.4.cloned.1.call-done = f32[3,3,256,128]{3,2,1,0:T(8,128)} async-done(((f32[3,3,256,128]{3,2,1,0:T(8,128)}), f32[3,3,256,128]{3,2,1,0:T(8,128)}) %all-reduce.4.cloned.1.call-update) | async-done | bytes 1179664 | tf_op jit(solution)/shard_map/psum | solution.py:183
  887.5 2.0 copy.64
  889.5 2.5 copy.65
  893.6 1.3 copy.68
  (217 shorter events, 34.3 us)
Async XLA Ops:
  8.0 134.4 %copy-start = (bf16[1024,512]{1,0:T(8,128)(2,1)S(1)}, bf16[1024,512]{1,0:T(8,128)(2,1)}, u32[]{:S(2)}) copy-start(bf16[1024,512]{1,0:T(8,128)(2,1)} %param.20) | copy-start | bytes 3145732
  8.0 103.0 %copy-start.37 = (bf16[34,10]{0,1:T(8,128)(2,1)S(1)}, bf16[34,10]{0,1:T(8,128)(2,1)}, u32[]{:S(2)}) copy-start(bf16[34,10]{0,1:T(8,128)(2,1)} %param.14) | copy-start | bytes 2044
  8.0 103.3 %copy-start.38 = (bf16[34,10]{0,1:T(8,128)(2,1)S(1)}, bf16[34,10]{0,1:T(8,128)(2,1)}, u32[]{:S(2)}) copy-start(bf16[34,10]{0,1:T(8,128)(2,1)} %param.15) | copy-start | bytes 2044
  8.0 208.5 %reduce-scatter.2.cloned.1.call-start = ((), (), s32[]{:S(2)}) async-start(), calls=%async_computation.1 | async-start | bytes 3538944 | tf_op jit(solution)/shard_map/reduce_scatter | solution.py:180
  8.9 84.6 %collective-permute-start.5 = (bf16[1,8,256]{2,1,0:T(8,128)(2,1)S(1)}, bf16[1,8,256]{2,1,0:T(8,128)(2,1)S(1)}, u32[]{:S(2)}, u32[]{:S(2)}) collective-permute-start(bf16[1,8,256]{2,1,0:T(8,128)(2,1)S(1)} %get-tuple-element.98), channel_id=1, source_target_pairs={{16,0},{32,16},{48,32},{64,48},{80,64},{96,80},{112,96},{17,1},{33... | collective-permute-start | bytes 12296 | tf_op jit(solution)/shard_map/ppermute | solution.py:19
  12.2 80.5 %collective-permute-start.4 = (bf16[1,8,256]{2,1,0:T(8,128)(2,1)S(1)}, bf16[1,8,256]{2,1,0:T(8,128)(2,1)S(1)}, u32[]{:S(2)}, u32[]{:S(2)}) collective-permute-start(bf16[1,8,256]{2,1,0:T(8,128)(2,1)S(1)} %get-tuple-element.99), channel_id=1, source_target_pairs={{0,16},{16,32},{32,48},{48,64},{64,80},{80,96},{96,112},{1,17},{17... | collective-permute-start | bytes 12296 | tf_op jit(solution)/shard_map/ppermute | solution.py:18
  16.0 82.2 %collective-permute-start.1 = (bf16[1,32,128]{2,1,0:T(8,128)(2,1)S(1)}, bf16[1,32,128]{2,1,0:T(8,128)(2,1)S(1)}, u32[]{:S(2)}, u32[]{:S(2)}) collective-permute-start(bf16[1,32,128]{2,1,0:T(8,128)(2,1)S(1)} %get-tuple-element.94), channel_id=1, source_target_pairs={{1,0},{16,1},{17,16},{32,17},{33,32},{48,33},{49,48},{64,49},{65,6... | collective-permute-start | bytes 24584 | tf_op jit(solution)/shard_map/ppermute | solution.py:19
  20.1 77.1 %collective-permute-start = (bf16[1,32,128]{2,1,0:T(8,128)(2,1)S(1)}, bf16[1,32,128]{2,1,0:T(8,128)(2,1)S(1)}, u32[]{:S(2)}, u32[]{:S(2)}) collective-permute-start(bf16[1,32,128]{2,1,0:T(8,128)(2,1)S(1)} %get-tuple-element.95), channel_id=1, source_target_pairs={{0,1},{1,16},{16,17},{17,32},{32,33},{33,48},{48,49},{49,64},{64,6... | collective-permute-start | bytes 24584 | tf_op jit(solution)/shard_map/ppermute | solution.py:18
  93.5 12.0 %collective-permute-start.6 = (bf16[10,1,256]{2,1,0:T(2,128)(2,1)S(1)}, bf16[10,1,256]{2,1,0:T(2,128)(2,1)S(1)}, u32[]{:S(2)}, u32[]{:S(2)}) collective-permute-start(bf16[10,1,256]{2,1,0:T(2,128)(2,1)S(1)} %get-tuple-element.96), channel_id=1, source_target_pairs={{0,2},{2,4},{4,6},{6,8},{8,10},{10,12},{12,14},{1,3},{3,5},{5,7},{... | collective-permute-start | bytes 15368 | tf_op jit(solution)/shard_map/ppermute | solution.py:18
  95.9 9.6 %collective-permute-start.7 = (bf16[10,1,256]{2,1,0:T(2,128)(2,1)S(1)}, bf16[10,1,256]{2,1,0:T(2,128)(2,1)S(1)}, u32[]{:S(2)}, u32[]{:S(2)}) collective-permute-start(bf16[10,1,256]{2,1,0:T(2,128)(2,1)S(1)} %get-tuple-element.97), channel_id=1, source_target_pairs={{2,0},{4,2},{6,4},{8,6},{10,8},{12,10},{14,12},{3,1},{5,3},{7,5},{... | collective-permute-start | bytes 15368 | tf_op jit(solution)/shard_map/ppermute | solution.py:19
  98.2 12.8 %copy-start.35 = (bf16[17,32,128]{2,1,0:T(8,128)(2,1)}, bf16[17,32,128]{2,1,0:T(8,128)(2,1)S(1)}, u32[]{:S(2)}) copy-start(bf16[17,32,128]{2,1,0:T(8,128)(2,1)S(1)} %get-tuple-element.91) | copy-start | bytes 417796
  98.2 5.4 copy-start.32
  98.3 17.5 %collective-permute-start.2 = (bf16[18,1,128]{2,1,0:T(2,128)(2,1)S(1)}, bf16[18,1,128]{2,1,0:T(2,128)(2,1)S(1)}, u32[]{:S(2)}, u32[]{:S(2)}) collective-permute-start(bf16[18,1,128]{2,1,0:T(2,128)(2,1)S(1)} %get-tuple-element.81), channel_id=1, source_target_pairs={{0,2},{2,4},{4,6},{6,8},{8,10},{10,12},{12,14},{1,3},{3,5},{5,7},{... | collective-permute-start | bytes 13832 | tf_op jit(solution)/shard_map/ppermute | solution.py:18
  102.3 13.5 %collective-permute-start.3 = (bf16[18,1,128]{2,1,0:T(2,128)(2,1)S(1)}, bf16[18,1,128]{2,1,0:T(2,128)(2,1)S(1)}, u32[]{:S(2)}, u32[]{:S(2)}) collective-permute-start(bf16[18,1,128]{2,1,0:T(2,128)(2,1)S(1)} %get-tuple-element.82), channel_id=1, source_target_pairs={{2,0},{4,2},{6,4},{8,6},{10,8},{12,10},{14,12},{3,1},{5,3},{7,5},{... | collective-permute-start | bytes 13832 | tf_op jit(solution)/shard_map/ppermute | solution.py:19
  116.9 17.7 %copy-start.10 = (bf16[3,3,128,128]{3,2,1,0:T(8,128)(2,1)S(1)}, bf16[3,3,128,128]{3,2,1,0:T(8,128)(2,1)}, u32[]{:S(2)}) copy-start(bf16[3,3,128,128]{3,2,1,0:T(8,128)(2,1)} %param.18) | copy-start | bytes 884740
  117.6 9.2 %collective-permute-start.8 = (bf16[1,32,128]{2,1,0:T(8,128)(2,1)S(1)}, bf16[1,32,128]{2,1,0:T(8,128)(2,1)S(1)}, u32[]{:S(2)}, u32[]{:S(2)}) collective-permute-start(bf16[1,32,128]{2,1,0:T(8,128)(2,1)S(1)} %get-tuple-element.89), channel_id=1, source_target_pairs={{0,1},{1,16},{16,17},{17,32},{32,33},{33,48},{48,49},{49,64},{64,6... | collective-permute-start | bytes 24584 | tf_op jit(solution)/shard_map/ppermute | solution.py:18
  122.0 6.6 collective-permute-start.9
  126.8 17.3 %copy-start.40 = (f32[256]{0:T(256)}, f32[256]{0:T(256)S(1)}, u32[]{:S(2)}) copy-start(f32[256]{0:T(256)S(1)} %compare_select_fusion.1) | copy-start | bytes 3076
  128.6 6.2 collective-permute-start.10
  133.3 5.6 collective-permute-start.11
  147.4 20.9 %copy-start.11 = (bf16[3,3,128,128]{3,2,1,0:T(8,128)(2,1)S(1)}, bf16[3,3,128,128]{3,2,1,0:T(8,128)(2,1)}, u32[]{:S(2)}) copy-start(bf16[3,3,128,128]{3,2,1,0:T(8,128)(2,1)} %param.18) | copy-start | bytes 884740
  148.5 9.4 %collective-permute-start.12 = (bf16[1,32,128]{2,1,0:T(8,128)(2,1)S(1)}, bf16[1,32,128]{2,1,0:T(8,128)(2,1)S(1)}, u32[]{:S(2)}, u32[]{:S(2)}) collective-permute-start(bf16[1,32,128]{2,1,0:T(8,128)(2,1)S(1)} %get-tuple-element.85), channel_id=1, source_target_pairs={{0,1},{1,16},{16,17},{17,32},{32,33},{33,48},{48,49},{49,64},{64,6... | collective-permute-start | bytes 24584 | tf_op jit(solution)/shard_map/ppermute | solution.py:18
  154.9 5.9 collective-permute-start.13
  157.9 11.2 %copy-start.18 = (bf16[512,128]{1,0:T(8,128)(2,1)}, bf16[512,128]{1,0:T(8,128)(2,1)S(1)}, u32[]{:S(2)}) copy-start(bf16[512,128]{1,0:T(8,128)(2,1)S(1)} %multiply_convert_fusion.4) | copy-start | bytes 393220
  160.8 7.2 collective-permute-start.14
  162.1 5.9 collective-permute-start.15
  174.6 182.5 %all-reduce.6.cloned.1.call-start = ((), (), s32[]{:S(2)}) async-start(), calls=%async_computation.3 | async-start | bytes 7602176 | tf_op jit(solution)/shard_map/psum | solution.py:184
  176.9 3.2 copy-start.14
  183.1 704.4 %all-reduce.4.cloned.1.call-start = ((), (), s32[]{:S(2)}) async-start(), calls=%async_computation.2 | async-start | bytes 2359296 | tf_op jit(solution)/shard_map/psum | solution.py:183
  357.0 535.0 %copy-start.12 = (f32[3,3,128,128]{3,2,1,0:T(8,128)S(1)}, f32[3,3,128,128]{3,2,1,0:T(8,128)}, u32[]{:S(2)}) copy-start(f32[3,3,128,128]{3,2,1,0:T(8,128)} %get-tuple-element.114) | copy-start | bytes 1769476
  887.5 5.3 copy-start.17
  889.5 4.1 copy-start.2
  (31 other events, 51.7 us)
Sparse Core Ops, SparseCore 0:
  174.7 41.8 reduce-scatter.1
Sparse Core Ops, SparseCore 1:
  183.2 173.8 all-reduce.5
  359.5 527.9 all-reduce.3
where the time goes:
time: 904 us; the launch traced here: 902 us
  waiting for transfers between devices  647 us (72%)
  blocking collectives  139 us (15%)
  starting transfers between devices  51.8 us (6%)
  matrix products  23.4 us (3%)
  between operations  18.2 us (2%)
  local copies, waits for them, and re-layouts  16.5 us (2%)
    psum x1, waiting for transfers between devices, local(): gctx = lax.psum(gctx, ('gy', 'gx'))  530 us
    psum x1, waiting for transfers between devices, local(): lax.psum((loss, ghid, gbin, gfine, gconv), ('gy', 'gx', 'ctx'))  74.7 us
    psum x1, blocking collectives, local(): total = lax.psum(own_num.astype(jnp.float32), ('gy', 'gx', 'ctx'))  67.8 us
    psum x1, blocking collectives, local(): lax.psum((loss, ghid, gbin, gfine, gconv), ('gy', 'gx', 'ctx'))  65.8 us
    reduce_scatter x1, waiting for transfers between devices, local(): lax.psum_scatter(weight_grad(field, g_one, rows, cols), 'ctx', scatter_di...  33.4 us
    ppermute x8, starting transfers between devices, extended(): before = lax.ppermute(last, axis, up)  32.4 us
    ppermute x8, starting transfers between devices, extended(): after = lax.ppermute(first, axis, down)  19.3 us
  transfers between devices with their start and end apart: 19, of which 6 were waited for; matrix products, arithmetic and copies ran while one was open for 2% of the time, Pallas kernels for 0%

commit v1 on v0

v1 whole, which is shorter than its diff:
```python
import jax
import jax.numpy as jnp
import numpy as np
from jax import lax
from jax.sharding import Mesh
from jax.sharding import PartitionSpec as P

HID = 1024
BINS = 512
CAP = 256
ROWS = 16
COLS = 32
C = 128
K = 512
HALF = 256
SHARD = 96
PEERS = 64
BODY = 12032

GY = ("x", "core")
GX = ("z", "yl")
TALL = ("x", "core", "yh")
PLANE = ("x", "z", "yl", "yh")

BF = jnp.bfloat16
F32 = jnp.float32


def silu_grad(v):
    s = jax.nn.sigmoid(v)
    return s * (1.0 + v * (1.0 - s))


def conv_rows(padded, weight, rows, cols):
    total = None
    for dy in range(3):
        for dx in range(3):
            patch = padded[dy : dy + rows, dx : dx + cols, :].reshape(rows * cols, -1)
            term = jnp.dot(patch, weight[dy, dx], preferred_element_type=F32)
            total = term if total is None else total + term
    return total.reshape(rows, cols, -1)


def weight_grad(padded, grad, rows, cols):
    flat_grad = grad.reshape(rows * cols, -1)
    parts = []
    for dy in range(3):
        for dx in range(3):
            patch = padded[dy : dy + rows, dx : dx + cols, :].reshape(rows * cols, -1)
            parts.append(
                lax.dot_general(
                    patch, flat_grad, (((0,), (0,)), ((), ())), preferred_element_type=F32
                )
            )
    return jnp.stack(parts)


def conv_back(gpad, weight, rows, cols):
    total = None
    for dy in range(3):
        for dx in range(3):
            patch = gpad[2 - dy : 2 - dy + rows, 2 - dx : 2 - dx + cols, :].reshape(rows * cols, -1)
            term = lax.dot_general(
                patch, weight[dy, dx], (((1,), (1,)), ((), ())), preferred_element_type=F32
            )
            total = term if total is None else total + term
    return total.reshape(rows, cols, -1)


def shift(x, axis, count, step):
    pairs = [(i, i + step) for i in range(count) if 0 <= i + step < count]
    return lax.ppermute(x, axis, pairs)


def side_swap(x):
    own = [(2 * t + c, 2 * t + 1 - c) for t in range(8) for c in range(2)]
    return lax.ppermute(x, TALL, own)


def outer_swap(x):
    pairs = []
    for t in range(7):
        pairs += [(2 * t + 1, 2 * t + 2), (2 * t + 2, 2 * t + 1)]
    return lax.ppermute(x, TALL, pairs)


def context_field(block, row_mat, col_mat, row_start, col_start):
    mid = jnp.einsum("ia,abk->ibk", row_mat, block, preferred_element_type=F32).astype(BF)
    wide = jnp.einsum("jb,ibk->ijk", col_mat, mid, preferred_element_type=F32)
    grow = row_start + jnp.arange(row_mat.shape[0], dtype=jnp.int32) - 1
    gcol = col_start + jnp.arange(col_mat.shape[0], dtype=jnp.int32) - 1
    keep = ((grow >= 0) & (grow < 256))[:, None] & ((gcol >= 0) & (gcol < 256))[None, :]
    return (wide * keep[:, :, None].astype(F32)).astype(BF)


def split3(v):
    hi = v.astype(BF)
    rest = v - hi.astype(F32)
    mid = rest.astype(BF)
    low = (rest - mid.astype(F32)).astype(BF)
    return [hi, mid, low]


def head(rows, lab, weight, hidden_weight, bin_weight):
    z = jnp.dot(rows, hidden_weight, preferred_element_type=F32)
    act = jax.nn.silu(z).astype(BF)
    logits = jnp.dot(act, bin_weight, preferred_element_type=F32)
    top = jax.nn.logsumexp(logits, axis=1)
    onehot = (lab[:, None] == jnp.arange(BINS, dtype=jnp.int32)[None, :]).astype(F32)
    picked = jnp.sum(logits * onehot, axis=1)
    loss = jnp.sum((weight * (top - picked))[:CAP])
    probs = jnp.exp(logits - top[:, None])
    dlogits = ((probs - onehot) * weight[:, None]).astype(BF)
    gbin = lax.dot_general(
        act[:CAP], dlogits[:CAP], (((0,), (0,)), ((), ())), preferred_element_type=F32
    )
    dact = lax.dot_general(
        dlogits, bin_weight, (((1,), (1,)), ((), ())), preferred_element_type=F32
    )
    dz = (dact * silu_grad(z)).astype(BF)
    ghid = lax.dot_general(
        rows[:CAP], dz[:CAP], (((0,), (0,)), ((), ())), preferred_element_type=F32
    )
    drows = lax.dot_general(
        dz, hidden_weight, (((1,), (1,)), ((), ())), preferred_element_type=F32
    )
    return loss, ghid, gbin, drows


def local(
    fine,
    context,
    interp_rows,
    interp_cols,
    fine_weight,
    ctx_weight,
    conv_weight,
    hidden_weight,
    bin_weight,
    cell_index,
    counts,
    labels,
):
    core = lax.axis_index("core")
    half = lax.axis_index("yh")
    gy = lax.axis_index(GY)
    gx = lax.axis_index(GX)
    lower = half == 1

    own_idx = cell_index[0, 0]
    own_lab = labels[0, 0]
    own_num = counts[0, 0]
    live = jnp.arange(CAP, dtype=jnp.int32) < own_num

    spot = own_idx[:, None] == jnp.arange(ROWS * COLS, dtype=jnp.int32)[None, :]
    code = jnp.sum(
        jnp.where(spot & live[:, None], own_lab[:, None] + 1, 0), axis=0, dtype=jnp.int32
    )
    digits = jnp.stack([code // 32, code % 32], axis=1).astype(BF).reshape(ROWS, COLS, 2)

    fine_dig = jnp.concatenate([fine, jnp.pad(digits, ((0, 0), (0, 0), (0, 126)))], axis=0)

    def pack_cols(col):
        return jnp.concatenate([fine_dig[:, col], context[:, min(col, 7)].reshape(16, C)], axis=0)

    west = shift(pack_cols(COLS - 1), GX, 8, 1)
    east = shift(pack_cols(0), GX, 8, -1)
    wide = jnp.concatenate([west[:32, None], fine_dig, east[:32, None]], axis=1)
    fine_w, dig_w = wide[:ROWS], wide[ROWS:]
    ctx_w = jnp.concatenate(
        [west[32:].reshape(8, 1, HALF), context, east[32:].reshape(8, 1, HALF)], axis=1
    )
    edge = lambda v, last: lax.dynamic_slice_in_dim(v, jnp.where(last, v.shape[0] - 1, 0), 1, 0)
    inner = jnp.concatenate([edge(fine_w, ~lower), edge(dig_w, ~lower)], axis=0).reshape(68, C)
    outer = jnp.concatenate([edge(fine_w, lower), edge(dig_w, lower)], axis=0).reshape(68, C)
    inner = side_swap(jnp.concatenate([inner, ctx_w.reshape(160, C)], axis=0))
    outer = outer_swap(outer)
    inner_edge = inner[:68].reshape(2, 34, C)
    outer_edge = outer.reshape(2, 34, C)
    before = jnp.where(lower, inner_edge, outer_edge)
    after = jnp.where(lower, outer_edge, inner_edge)
    fine_pad = jnp.concatenate([before[:1], fine_w, after[:1]], axis=0)
    dig_pad = jnp.concatenate([before[1:], dig_w, after[1:]], axis=0)[:, :, :2]
    ctx_o = inner[68:].reshape(8, 10, HALF)
    ctx_all = jnp.where(
        lower,
        jnp.concatenate([ctx_o, ctx_w], axis=2),
        jnp.concatenate([ctx_w, ctx_o], axis=2),
    )
    north = shift(ctx_all[7:8], GY, 8, 1)
    south = shift(ctx_all[0:1], GY, 8, -1)
    block = jnp.concatenate([north, ctx_all, south], axis=0)

    row_anchor = gy * 32 + half * ROWS
    col_anchor = gx * COLS
    row_mat = lax.dynamic_slice_in_dim(interp_rows, half * ROWS, ROWS + 2, 0)
    field = context_field(block, row_mat, interp_cols, row_anchor, col_anchor)
    pre_one = conv_rows(fine_pad, fine_weight, ROWS, COLS) + conv_rows(field, ctx_weight, ROWS, COLS)
    h_one = jax.nn.silu(pre_one).astype(BF)

    west = shift(h_one[:, COLS - 2 :].reshape(32, C), GX, 8, 1)
    east = shift(h_one[:, :2].reshape(32, C), GX, 8, -1)
    wide = jnp.concatenate([west.reshape(ROWS, 2, C), h_one, east.reshape(ROWS, 2, C)], axis=1)
    two = lambda v, last: lax.dynamic_slice_in_dim(v, jnp.where(last, ROWS - 2, 0), 2, 0)
    inner = side_swap(two(wide, ~lower).reshape(72, C)).reshape(2, 36, C)
    outer = outer_swap(two(wide, lower).reshape(72, C)).reshape(2, 36, C)
    h_pad = jnp.concatenate(
        [jnp.where(lower, inner, outer), wide, jnp.where(lower, outer, inner)], axis=0
    )
    pre_two = conv_rows(h_pad, conv_weight, ROWS + 2, COLS + 2)
    h_two = jax.nn.silu(pre_two).astype(BF)

    own_rows = h_two[1 : 1 + ROWS, 1 : 1 + COLS].reshape(ROWS * COLS, C)[own_idx]

    def ring(v):
        parts = [v[0], v[ROWS + 1], v[1 : 1 + ROWS, 0], v[1 : 1 + ROWS, COLS + 1]]
        return jnp.concatenate(parts, axis=0)

    ring_code = jnp.sum(ring(dig_pad).astype(jnp.int32) * jnp.array([32, 1], jnp.int32), axis=1)
    rows = jnp.concatenate([own_rows, ring(h_two)], axis=0)
    lab = jnp.concatenate([own_lab, ring_code - 1])
    weight = jnp.concatenate([live, ring_code > 0]).astype(F32)
    loss, ghid, gbin, drows = head(rows, lab, weight, hidden_weight, bin_weight)
    inside = (
        jnp.zeros((ROWS * COLS, C), F32).at[own_idx].add(drows[:CAP]).reshape(ROWS, COLS, C)
    )
    round_ = drows[CAP:]
    cells = jnp.concatenate(
        [
            round_[68:84].reshape(ROWS, 1, C),
            inside,
            round_[84:100].reshape(ROWS, 1, C),
        ],
        axis=1,
    )
    dh_two = jnp.concatenate(
        [round_[0:34].reshape(1, 34, C), cells, round_[34:68].reshape(1, 34, C)], axis=0
    )
    g_two = (dh_two * silu_grad(pre_two)).astype(BF)
    gconv = weight_grad(h_pad[1 : 3 + ROWS, 1 : 3 + COLS], g_two[1 : 1 + ROWS, 1 : 1 + COLS], ROWS, COLS)
    g_one = (conv_back(g_two, conv_weight, ROWS, COLS) * silu_grad(pre_one)).astype(BF)
    gfine = weight_grad(fine_pad, g_one, ROWS, COLS)
    gctx = weight_grad(field, g_one, ROWS, COLS)

    stats = jnp.stack([loss, own_num.astype(F32)])
    stat_rows = jnp.stack([jnp.pad(part, (0, C - 2)) for part in split3(stats)])
    rows_all = jnp.concatenate(
        [
            gctx.reshape(9, 2, HALF, C).transpose(1, 0, 2, 3).reshape(-1, C).astype(BF),
            gfine.reshape(-1, C).astype(BF),
            gconv.reshape(-1, C).astype(BF),
            ghid.reshape(C, 8, C).transpose(1, 0, 2).reshape(-1, C).astype(BF),
            gbin.reshape(HID, 4, C).transpose(1, 0, 2).reshape(-1, C).astype(BF),
            stat_rows,
            jnp.zeros((2 * PEERS * SHARD - BODY - 3, C), BF),
        ],
        axis=0,
    ).reshape(2, PEERS * SHARD, C)
    flip = [(0, 1), (1, 0)]
    keep = lax.dynamic_index_in_dim(rows_all, core, 0, False)
    give = lax.dynamic_index_in_dim(rows_all, 1 - core, 0, False)
    got = lax.ppermute(give, "core", flip)
    pair = keep.astype(F32) + got.astype(F32)
    place = BODY - PEERS * SHARD
    stat = split3(pair[place] + pair[place + 1] + pair[place + 2])
    plain = pair.astype(BF)
    fixed = lax.dynamic_update_slice_in_dim(plain, jnp.stack(stat), place, 0)
    pair = jnp.where(core == 1, fixed, plain)
    pieces = lax.all_to_all(pair.reshape(PEERS, SHARD, C), PLANE, 0, 0, tiled=True)
    mine = jnp.sum(pieces.astype(F32), axis=0)
    plain = mine.astype(BF)
    spot = place % SHARD
    stat = split3(mine[spot] + mine[spot + 1] + mine[spot + 2])
    fixed = lax.dynamic_update_slice_in_dim(plain, jnp.stack(stat), spot, 0)
    owner = (core == 1) & (lax.axis_index(PLANE) == place // SHARD)
    mine = jnp.where(owner, fixed, plain)
    half_sum = lax.all_to_all(
        jnp.broadcast_to(mine[None], (PEERS, SHARD, C)), PLANE, 0, 0, tiled=True
    ).reshape(PEERS * SHARD, C)
    other = lax.ppermute(half_sum, "core", flip)
    low = jnp.where(core == 0, half_sum, other)
    high = jnp.where(core == 0, other, half_sum)
    sums = jnp.concatenate([low, high], axis=0)
    stat = jnp.sum(sums[BODY : BODY + 3].astype(F32), axis=0)
    scale = 1.0 / stat[1]
    gctx = lax.dynamic_slice_in_dim(sums, half * 2304, 2304, 0).astype(F32) * scale
    rest = sums[4608:BODY].astype(F32) * scale
    return (
        stat[0] * scale,
        rest[:1152].reshape(3, 3, C, C),
        gctx.reshape(3, 3, HALF, C),
        rest[1152:2304].reshape(3, 3, C, C),
        rest[2304:3328].reshape(8, C, C).transpose(1, 0, 2).reshape(C, HID),
        rest[3328:].reshape(4, HID, C).transpose(1, 0, 2).reshape(HID, BINS),
    )


def solution(mesh):
    devices = np.asarray(mesh.devices).reshape(4, 2, 4, 2, 2)
    split = Mesh(devices, ("x", "core", "z", "yl", "yh"))
    in_specs = (
        P(TALL, GX, None),
        P(GY, GX, "yh"),
        P(),
        P(),
        P(),
        P(),
        P(),
        P(),
        P(),
        P(TALL, GX, None),
        P(TALL, GX),
        P(TALL, GX, None),
    )
    out_specs = (P(), P(), P(None, None, "yh", None), P(), P(), P())
    return jax.shard_map(local, mesh=split, in_specs=in_specs, out_specs=out_specs, check_vma=False)
```

time: 904 us -> 208 us (0.23)
  waiting for transfers between devices: 647 us -> 42.4 us
  blocking collectives: 139 us -> 26.7 us
  local copies, waits for them, and re-layouts: 16.5 us -> 43.5 us
  between operations: 18.2 us -> 5.71 us
  other arithmetic: 6.05 us -> 17.5 us
    psum x2 -> x0, waiting for transfers between devices: 605 us -> none  [the longest x1 530 us: local(): gctx = lax.psum(gctx, ('gy', 'gx'))]
    psum x2 -> x0, blocking collectives: 134 us -> none  [the longest x1 67.8 us: local(): total = lax.psum(own_num.astype(jnp.float32), ('gy', 'gx', 'ctx'))]
    reduce_scatter x1 -> x0, waiting for transfers between devices: 33.4 us -> none  [local(): lax.psum_scatter(weight_grad(field, g_one, rows, cols), 'ctx', scatter_di...]
    all_to_all x0 -> x1, blocking collectives: none -> 26.7 us  [local(): lax.all_to_all(jnp.broadcast_to(mine[None], (PEERS, SHARD, C)), PLANE, 0,...]
    all_to_all x0 -> x1, waiting for transfers between devices: none -> 23.3 us  [local(): lax.all_to_all(pair.reshape(PEERS, SHARD, C), PLANE, 0, 0, tiled=True)]
    ppermute x16 -> x12, starting transfers between devices: 51.7 us -> 31.4 us  [the longest x6 15.6 us: shift(): return lax.ppermute(x, axis, pairs)]
    all_to_all x0 -> x1, starting transfers between devices: none -> 12.2 us  [local(): lax.all_to_all(pair.reshape(PEERS, SHARD, C), PLANE, 0, 0, tiled=True)]
    concatenate x3 -> x4, local copies, waits for them, and re-layouts: 1 us -> 13.2 us  [the longest x1 12.8 us: local(): jnp.concatenate([gctx.reshape(9, 2, HALF, C).transpose(1, 0, 2, 3).reshap...]
  transfers between devices with their start and end apart: 19 -> 13, of which waited for: 6 -> 8; matrix products, arithmetic and copies ran while one was open for 2% -> 1% of each run, Pallas kernels for 0% -> 0%
where the time goes in v1:
time: 208 us; the launch traced here: 206 us
  starting transfers between devices  43.6 us (21%)
  local copies, waits for them, and re-layouts  43.5 us (21%)
  waiting for transfers between devices  42.4 us (20%)
  matrix products  26.8 us (13%)
  blocking collectives  26.7 us (13%)
  other arithmetic  17.5 us (8%)
  between operations  5.71 us (3%)
    all_to_all x1, blocking collectives, local(): lax.all_to_all(jnp.broadcast_to(mine[None], (PEERS, SHARD, C)), PLANE, 0,...  26.7 us
    all_to_all x1, waiting for transfers between devices, local(): lax.all_to_all(pair.reshape(PEERS, SHARD, C), PLANE, 0, 0, tiled=True)  23.3 us
    ppermute x6, starting transfers between devices, shift(): return lax.ppermute(x, axis, pairs)  15.6 us
    dot_general x27, matrix products, weight_grad(): lax.dot_general(patch, flat_grad, (((0,), (0,)), ((), ())), preferred_ele...  13.3 us
    concatenate x1, local copies, waits for them, and re-layouts, local(): jnp.concatenate([gctx.reshape(9, 2, HALF, C).transpose(1, 0, 2, 3).reshap...  12.8 us
    all_to_all x1, starting transfers between devices, local(): lax.all_to_all(pair.reshape(PEERS, SHARD, C), PLANE, 0, 0, tiled=True)  12.2 us
    ppermute x2, starting transfers between devices, outer_swap(): return lax.ppermute(x, TALL, pairs)  8.62 us
    dot_general x27, matrix products, conv_rows(): term = jnp.dot(patch, weight[dy, dx], preferred_element_type=F32)  8.06 us
  transfers between devices with their start and end apart: 13, of which 8 were waited for; matrix products, arithmetic and copies ran while one was open for 1% of the time, Pallas kernels for 0%

profile of v1, /device:TPU:1, one launch (start us, length us, event | category | flops | bytes accessed | tf_op | source)
XLA Modules:
  0.0 206.2 jit_solution(7783287566785161439)
XLA Ops:
  5.0 4.0 %collective-permute-start = (bf16[48,128]{1,0:T(8,128)(2,1)S(1)}, bf16[48,128]{1,0:T(8,128)(2,1)S(1)}, u32[]{:S(2)}, u32[]{:S(2)}) collective-permute-start(bf16[48,128]{1,0:T(8,128)(2,1)S(1)} %pad_maximum_fusion.19), channel_id=1, source_target_pairs={{0,2},{2,4},{4,6},{6,8},{8,10},{10,12},{12,14},{1,3},{3,5},{5,7},{... | collective-permute-start | bytes 36872 | tf_op jit(solution)/shard_map/ppermute | solution.py:72
  9.1 1.3 collective-permute-start.1
  11.3 2.3 %collective-permute-done.1 = bf16[48,128]{1,0:T(8,128)(2,1)S(1)} collective-permute-done((bf16[48,128]{1,0:T(8,128)(2,1)S(1)}, bf16[48,128]{1,0:T(8,128)(2,1)S(1)}, u32[]{:S(2)}, u32[]{:S(2)}) %collective-permute-start.1) | collective-permute-done | bytes 12320 | tf_op jit(solution)/shard_map/ppermute | solution.py:72
  14.8 6.5 %collective-permute-start.5 = (bf16[68,128]{1,0:T(8,128)(2,1)S(1)}, bf16[68,128]{1,0:T(8,128)(2,1)S(1)}, u32[]{:S(2)}, u32[]{:S(2)}) collective-permute-start(bf16[68,128]{1,0:T(8,128)(2,1)S(1)} %reshape.586), channel_id=1, source_target_pairs={{1,16},{16,1},{17,32},{32,17},{33,48},{48,33},{49,64},{64,49},{65,... | collective-permute-start | bytes 52232 | tf_op jit(solution)/shard_map/ppermute | solution.py:84
  21.4 1.3 collective-permute-start.2
  23.0 3.0 %collective-permute-done.2 = bf16[228,128]{1,0:T(8,128)(2,1)S(1)} collective-permute-done((bf16[228,128]{1,0:T(8,128)(2,1)S(1)}, bf16[228,128]{1,0:T(8,128)(2,1)S(1)}, u32[]{:S(2)}, u32[]{:S(2)}) %collective-permute-start.2) | collective-permute-done | bytes 58400 | tf_op jit(solution)/shard_map/ppermute | solution.py:77
  26.6 2.8 %collective-permute-start.3 = (bf16[1,10,512]{2,0,1:T(2,128)(2,1)S(1)}, bf16[1,10,512]{2,0,1:T(2,128)(2,1)S(1)}, u32[]{:S(2)}, u32[]{:S(2)}) collective-permute-start(bf16[1,10,512]{2,0,1:T(2,128)(2,1)S(1)} %get-tuple-element.108), channel_id=1, source_target_pairs={{0,16},{16,32},{32,48},{48,64},{64,80},{80,96},{96,112},{1,17},{17... | collective-permute-start | bytes 30728 | tf_op jit(solution)/shard_map/ppermute | solution.py:72
  29.4 1.9 collective-permute-start.4
  33.1 1.4 collective-permute-done.4
  39.6 1.3 collective-permute-start.7
  40.9 4.3 %collective-permute-start.6 = (bf16[32,128]{1,0:T(8,128)(2,1)S(1)}, bf16[32,128]{1,0:T(8,128)(2,1)S(1)}, u32[]{:S(2)}, u32[]{:S(2)}) collective-permute-start(bf16[32,128]{1,0:T(8,128)(2,1)S(1)} %bitcast.764), channel_id=1, source_target_pairs={{0,2},{2,4},{4,6},{6,8},{8,10},{10,12},{12,14},{1,3},{3,5},{5,7},{... | collective-permute-start | bytes 24584 | tf_op jit(solution)/shard_map/ppermute | solution.py:72
  46.1 2.4 %collective-permute-start.8 = (bf16[72,128]{1,0:T(8,128)(2,1)S(1)}, bf16[72,128]{1,0:T(8,128)(2,1)S(1)}, u32[]{:S(2)}, u32[]{:S(2)}) collective-permute-start(bf16[72,128]{1,0:T(8,128)(2,1)S(1)} %reshape.609), channel_id=1, source_target_pairs={{0,1},{1,0},{16,17},{17,16},{32,33},{33,32},{48,49},{49,48},{64,65... | collective-permute-start | bytes 55304 | tf_op jit(solution)/shard_map/ppermute | solution.py:77
  48.6 2.1 %collective-permute-start.9 = (bf16[72,128]{1,0:T(8,128)(2,1)S(1)}, bf16[72,128]{1,0:T(8,128)(2,1)S(1)}, u32[]{:S(2)}, u32[]{:S(2)}) collective-permute-start(bf16[72,128]{1,0:T(8,128)(2,1)S(1)} %reshape.610), channel_id=1, source_target_pairs={{1,16},{16,1},{17,32},{32,17},{33,48},{48,33},{49,64},{64,49},{65,... | collective-permute-start | bytes 55304 | tf_op jit(solution)/shard_map/ppermute | solution.py:84
  50.7 4.4 %collective-permute-done.9 = bf16[72,128]{1,0:T(8,128)(2,1)S(1)} collective-permute-done((bf16[72,128]{1,0:T(8,128)(2,1)S(1)}, bf16[72,128]{1,0:T(8,128)(2,1)S(1)}, u32[]{:S(2)}, u32[]{:S(2)}) %collective-permute-start.9) | collective-permute-done | bytes 18464 | tf_op jit(solution)/shard_map/ppermute | solution.py:84
  70.3 1.7 scatter_custom_fusion
  74.6 1.3 copy.198
  94.7 12.8 %concatenate.138 = bf16[12288,128]{1,0:T(8,128)(2,1)S(1)} concatenate(bf16[4608,128]{1,0:T(8,128)(2,1)} %bitcast.698, bf16[1152,128]{1,0:T(8,128)(2,1)} %bitcast.747, bf16[1152,128]{1,0:T(8,128)(2,1)} %bitcast.165, bf16[1024,128]{1,0:T(8,128)(2,1)S(1)} %bitcast.727, bf16[4096,128]{1,0:T(8,128)(2,1)} %bitcast.700, bf16[1,128]{1,0:T(2,128)(2,1)S(1)} %pad_bitcast_fusion.2, ...), dimensions={0} | concatenate | bytes 6291456 | tf_op jit(solution)/shard_map/concatenate | solution.py:247
  107.5 1.3 dynamic-slice_bitcast_fusion
  108.8 3.7 %collective-permute-done.10 = bf16[6144,128]{1,0:T(8,128)(2,1)} collective-permute-done((bf16[6144,128]{1,0:T(8,128)(2,1)}, bf16[6144,128]{1,0:T(8,128)(2,1)}, u32[]{:S(2)}, u32[]{:S(2)}) %collective-permute-start.10) | collective-permute-done | bytes 1572896 | tf_op jit(solution)/shard_map/ppermute | solution.py:262
  112.5 3.0 %fusion.232 = (bf16[6144,128]{1,0:T(8,128)(2,1)}, f32[6144,128]{1,0:T(8,128)S(1)}) fusion(bf16[6144,128]{1,0:T(8,128)(2,1)} %collective-permute-done.10, bf16[2,6144,128]{2,1,0:T(8,128)(2,1)S(1)} %bitcast.695, s32[]{:T(128)S(6)} %select_n.188), kind=kLoop, calls=%fused_computation.421 | loop fusion | flops 3145728 | bytes 7864324 | tf_op jit(solution)/shard_map/convert_element_type | solution.py:266
  116.2 1.3 select_n.193
  117.5 12.2 %all-to-all-start = ((bf16[64,96,128]{2,1,0:T(8,128)(2,1)}), bf16[64,96,128]{2,1,0:T(8,128)(2,1)S(1)}, u32[]{:S(2)}, u32[]{:S(2)}) async-start(bf16[64,96,128]{2,1,0:T(8,128)(2,1)} %bitcast.179), calls=%async_computation | async-start | bytes 3145728 | tf_op jit(solution)/shard_map/all_to_all | solution.py:269
  129.8 23.3 %all-to-all-done = bf16[64,96,128]{2,1,0:T(8,128)(2,1)S(1)} async-done(((bf16[64,96,128]{2,1,0:T(8,128)(2,1)}), bf16[64,96,128]{2,1,0:T(8,128)(2,1)S(1)}, u32[]{:S(2)}, u32[]{:S(2)}) %all-to-all-start) | async-done | bytes 1572896 | tf_op jit(solution)/shard_map/all_to_all | solution.py:269
  153.7 26.7 %all_to_all.10 = bf16[64,96,128]{2,1,0:T(8,128)(2,1)} all-to-all(bf16[64,96,128]{2,1,0:T(8,128)(2,1)S(1)} %broadcast_in_dim.53), channel_id=1, replica_groups=mesh['x'=4,'core'=2,'z'=4,'yl'=2,'yh'=2] {'x','z','yl','yh'}, dimensions={0} | all-to-all | bytes 3145728 | tf_op jit(solution)/shard_map/all_to_all | solution.py:277
  180.3 3.4 %collective-permute-start.11 = (bf16[6144,128]{1,0:T(8,128)(2,1)}, bf16[6144,128]{1,0:T(8,128)(2,1)}, u32[]{:S(2)}, u32[]{:S(2)}) collective-permute-start(bf16[6144,128]{1,0:T(8,128)(2,1)} %bitcast.180), channel_id=1, source_target_pairs={{0,16},{16,0},{1,17},{17,1},{2,18},{18,2},{3,19},{19,3},{4,20},{20... | collective-permute-start | bytes 4718600 | tf_op jit(solution)/shard_map/ppermute | solution.py:280
  183.7 3.4 %collective-permute-done.11 = bf16[6144,128]{1,0:T(8,128)(2,1)} collective-permute-done((bf16[6144,128]{1,0:T(8,128)(2,1)}, bf16[6144,128]{1,0:T(8,128)(2,1)}, u32[]{:S(2)}, u32[]{:S(2)}) %collective-permute-start.11) | collective-permute-done | bytes 1572896 | tf_op jit(solution)/shard_map/ppermute | solution.py:280
  187.1 2.1 %broadcast_select_fusion = (bf16[6144,128]{1,0:T(8,128)(2,1)S(1)}, bf16[6144,128]{1,0:T(8,128)(2,1)S(1)}) fusion(bf16[6144,128]{1,0:T(8,128)(2,1)} %collective-permute-done.11, pred[]{:T(512)S(6)} %eq.44, bf16[64,96,128]{2,1,0:T(8,128)(2,1)} %all_to_all.10), kind=kLoop, calls=%fused_computation.11 | loop fusion | flops 1572864 | bytes 6291457 | tf_op jit(solution)/shard_map/jit(_where)/select_n | solution.py:281
  192.7 1.5 slice.667
  194.8 3.1 %convert_multiply_fusion.1 = f32[2304,128]{1,0:T(8,128)} fusion(s32[]{:T(128)S(6)} %select_n.200, bf16[6144,128]{1,0:T(8,128)(2,1)S(1)} %get-tuple-element.46, bf16[6144,128]{1,0:T(8,128)(2,1)S(1)} %get-tuple-element.47, f32[]{:T(128)} %bitcast.182), kind=kLoop, calls=%fused_computation.29 | loop fusion | flops 1474560 | bytes 4325384 | tf_op jit(solution)/shard_map/mul | solution.py:286
  197.9 1.4 copy.199
  200.3 1.8 copy.200
  202.1 3.0 %copy.202 = f32[1024,512]{1,0:T(8,128)} copy(f32[1024,512]{0,1:T(8,128)} %bitcast.697) | data formatting | bytes 4194304
  (334 shorter events, 54.5 us)
Async XLA Ops:
  0.6 66.2 %copy-start = (bf16[1024,512]{1,0:T(8,128)(2,1)S(1)}, bf16[1024,512]{1,0:T(8,128)(2,1)}, u32[]{:S(2)}) copy-start(bf16[1024,512]{1,0:T(8,128)(2,1)} %param.21) | copy-start | bytes 3145732
  0.6 13.9 %copy-start.3 = (bf16[16,32,128]{2,1,0:T(8,128)(2,1)S(1)}, bf16[16,32,128]{2,1,0:T(8,128)(2,1)}, u32[]{:S(2)}) copy-start(bf16[16,32,128]{2,1,0:T(8,128)(2,1)} %param.13) | copy-start | bytes 393220
  5.0 6.2 %collective-permute-start = (bf16[48,128]{1,0:T(8,128)(2,1)S(1)}, bf16[48,128]{1,0:T(8,128)(2,1)S(1)}, u32[]{:S(2)}, u32[]{:S(2)}) collective-permute-start(bf16[48,128]{1,0:T(8,128)(2,1)S(1)} %pad_maximum_fusion.19), channel_id=1, source_target_pairs={{0,2},{2,4},{4,6},{6,8},{8,10},{10,12},{12,14},{1,3},{3,5},{5,7},{... | collective-permute-start | bytes 36872 | tf_op jit(solution)/shard_map/ppermute | solution.py:72
  9.1 4.5 %collective-permute-start.1 = (bf16[48,128]{1,0:T(8,128)(2,1)S(1)}, bf16[48,128]{1,0:T(8,128)(2,1)S(1)}, u32[]{:S(2)}, u32[]{:S(2)}) collective-permute-start(bf16[48,128]{1,0:T(8,128)(2,1)S(1)} %pad_maximum_fusion.20), channel_id=1, source_target_pairs={{2,0},{4,2},{6,4},{8,6},{10,8},{12,10},{14,12},{3,1},{5,3},{7,5},{... | collective-permute-start | bytes 36872 | tf_op jit(solution)/shard_map/ppermute | solution.py:72
  11.2 15.1 %copy-start.60 = (s32[2]{0:T(128)S(1)}, s32[2]{0:T(128)}, u32[]{:S(2)}) copy-start(s32[2]{0:T(128)} %constant.126.clone) | copy-start | bytes 28
  14.7 16.8 %copy-start.51 = (bf16[3,3,128,128]{3,2,1,0:T(8,128)(2,1)S(1)}, bf16[3,3,128,128]{3,2,1,0:T(8,128)(2,1)}, u32[]{:S(2)}) copy-start(bf16[3,3,128,128]{3,2,1,0:T(8,128)(2,1)} %param.17) | copy-start | bytes 884740
  14.8 8.2 %collective-permute-start.5 = (bf16[68,128]{1,0:T(8,128)(2,1)S(1)}, bf16[68,128]{1,0:T(8,128)(2,1)S(1)}, u32[]{:S(2)}, u32[]{:S(2)}) collective-permute-start(bf16[68,128]{1,0:T(8,128)(2,1)S(1)} %reshape.586), channel_id=1, source_target_pairs={{1,16},{16,1},{17,32},{32,17},{33,48},{48,33},{49,64},{64,49},{65,... | collective-permute-start | bytes 52232 | tf_op jit(solution)/shard_map/ppermute | solution.py:84
  21.4 4.6 %collective-permute-start.2 = (bf16[228,128]{1,0:T(8,128)(2,1)S(1)}, bf16[228,128]{1,0:T(8,128)(2,1)S(1)}, u32[]{:S(2)}, u32[]{:S(2)}) collective-permute-start(bf16[228,128]{1,0:T(8,128)(2,1)S(1)} %pad_maximum_fusion.14), channel_id=1, source_target_pairs={{0,1},{1,0},{16,17},{17,16},{32,33},{33,32},{48,49},{49,48},{64,65... | collective-permute-start | bytes 175112 | tf_op jit(solution)/shard_map/ppermute | solution.py:77
  22.8 9.3 %copy-start.33 = (bf16[16,32,128]{2,1,0:T(8,128)(2,1)}, bf16[16,32,128]{2,1,0:T(8,128)(2,1)S(1)}, u32[]{:S(2)}) copy-start(bf16[16,32,128]{2,1,0:T(8,128)(2,1)S(1)} %get-tuple-element.60) | copy-start | bytes 393220
  22.8 9.7 %copy-start.31 = (bf16[16,32,128]{2,1,0:T(8,128)(2,1)}, bf16[16,32,128]{2,1,0:T(8,128)(2,1)S(1)}, u32[]{:S(2)}) copy-start(bf16[16,32,128]{2,1,0:T(8,128)(2,1)S(1)} %get-tuple-element.59) | copy-start | bytes 393220
  26.4 24.2 %copy-start.58 = (pred[100]{0:T(512)(128)(4,1)}, pred[100]{0:T(512)(128)(4,1)S(1)}, u32[]{:S(2)}) copy-start(pred[100]{0:T(512)(128)(4,1)S(1)} %broadcast_compare_fusion) | copy-start | bytes 304
  26.6 6.5 %collective-permute-start.3 = (bf16[1,10,512]{2,0,1:T(2,128)(2,1)S(1)}, bf16[1,10,512]{2,0,1:T(2,128)(2,1)S(1)}, u32[]{:S(2)}, u32[]{:S(2)}) collective-permute-start(bf16[1,10,512]{2,0,1:T(2,128)(2,1)S(1)} %get-tuple-element.108), channel_id=1, source_target_pairs={{0,16},{16,32},{32,48},{48,64},{64,80},{80,96},{96,112},{1,17},{17... | collective-permute-start | bytes 30728 | tf_op jit(solution)/shard_map/ppermute | solution.py:72
  29.4 5.1 %collective-permute-start.4 = (bf16[1,10,512]{2,0,1:T(2,128)(2,1)S(1)}, bf16[1,10,512]{2,0,1:T(2,128)(2,1)S(1)}, u32[]{:S(2)}, u32[]{:S(2)}) collective-permute-start(bf16[1,10,512]{2,0,1:T(2,128)(2,1)S(1)} %get-tuple-element.109), channel_id=1, source_target_pairs={{16,0},{32,16},{48,32},{64,48},{80,64},{96,80},{112,96},{17,1},{33... | collective-permute-start | bytes 30728 | tf_op jit(solution)/shard_map/ppermute | solution.py:72
  31.5 7.8 %copy-start.48 = (bf16[16,32,128]{2,1,0:T(8,128)(2,1)}, bf16[16,32,128]{2,1,0:T(8,128)(2,1)S(1)}, u32[]{:S(2)}) copy-start(bf16[16,32,128]{2,1,0:T(8,128)(2,1)S(1)} %get-tuple-element.89) | copy-start | bytes 393220
  35.9 2.7 %copy-start.8 = (bf16[16,32,512]{2,1,0:T(8,128)(2,1)}, bf16[16,32,512]{2,1,0:T(8,128)(2,1)S(1)}, u32[]{:S(2)}) copy-start(bf16[16,32,512]{2,1,0:T(8,128)(2,1)S(1)} %get-tuple-element.49) | copy-start | bytes 1572868
  35.9 3.0 %copy-start.16 = (bf16[16,32,512]{2,1,0:T(8,128)(2,1)}, bf16[16,32,512]{2,1,0:T(8,128)(2,1)S(1)}, u32[]{:S(2)}) copy-start(bf16[16,32,512]{2,1,0:T(8,128)(2,1)S(1)} %get-tuple-element.53) | copy-start | bytes 1572868
  35.9 3.0 %copy-start.18 = (bf16[16,32,512]{2,1,0:T(8,128)(2,1)}, bf16[16,32,512]{2,1,0:T(8,128)(2,1)S(1)}, u32[]{:S(2)}) copy-start(bf16[16,32,512]{2,1,0:T(8,128)(2,1)S(1)} %get-tuple-element.54) | copy-start | bytes 1572868
  36.0 3.0 %copy-start.20 = (bf16[16,32,512]{2,1,0:T(8,128)(2,1)}, bf16[16,32,512]{2,1,0:T(8,128)(2,1)S(1)}, u32[]{:S(2)}) copy-start(bf16[16,32,512]{2,1,0:T(8,128)(2,1)S(1)} %get-tuple-element.55) | copy-start | bytes 1572868
  36.0 3.0 %copy-start.6 = (bf16[16,32,512]{2,1,0:T(8,128)(2,1)}, bf16[16,32,512]{2,1,0:T(8,128)(2,1)S(1)}, u32[]{:S(2)}) copy-start(bf16[16,32,512]{2,1,0:T(8,128)(2,1)S(1)} %get-tuple-element.48) | copy-start | bytes 1572868
  39.0 6.2 %copy-start.57 = (s32[1,1,256]{2,1,0:T(1,128)S(1)}, s32[1,1,256]{2,1,0:T(1,128)}, u32[]{:S(2)}) copy-start(s32[1,1,256]{2,1,0:T(1,128)} %param.24) | copy-start | bytes 3076
  39.6 5.6 %collective-permute-start.7 = (bf16[32,128]{1,0:T(8,128)(2,1)S(1)}, bf16[32,128]{1,0:T(8,128)(2,1)S(1)}, u32[]{:S(2)}, u32[]{:S(2)}) collective-permute-start(bf16[32,128]{1,0:T(8,128)(2,1)S(1)} %bitcast.765), channel_id=1, source_target_pairs={{2,0},{4,2},{6,4},{8,6},{10,8},{12,10},{14,12},{3,1},{5,3},{7,5},{... | collective-permute-start | bytes 24584 | tf_op jit(solution)/shard_map/ppermute | solution.py:72
  40.9 5.1 %collective-permute-start.6 = (bf16[32,128]{1,0:T(8,128)(2,1)S(1)}, bf16[32,128]{1,0:T(8,128)(2,1)S(1)}, u32[]{:S(2)}, u32[]{:S(2)}) collective-permute-start(bf16[32,128]{1,0:T(8,128)(2,1)S(1)} %bitcast.764), channel_id=1, source_target_pairs={{0,2},{2,4},{4,6},{6,8},{8,10},{10,12},{12,14},{1,3},{3,5},{5,7},{... | collective-permute-start | bytes 24584 | tf_op jit(solution)/shard_map/ppermute | solution.py:72
  46.1 4.5 %collective-permute-start.8 = (bf16[72,128]{1,0:T(8,128)(2,1)S(1)}, bf16[72,128]{1,0:T(8,128)(2,1)S(1)}, u32[]{:S(2)}, u32[]{:S(2)}) collective-permute-start(bf16[72,128]{1,0:T(8,128)(2,1)S(1)} %reshape.609), channel_id=1, source_target_pairs={{0,1},{1,0},{16,17},{17,16},{32,33},{33,32},{48,49},{49,48},{64,65... | collective-permute-start | bytes 55304 | tf_op jit(solution)/shard_map/ppermute | solution.py:77
  48.6 6.6 %collective-permute-start.9 = (bf16[72,128]{1,0:T(8,128)(2,1)S(1)}, bf16[72,128]{1,0:T(8,128)(2,1)S(1)}, u32[]{:S(2)}, u32[]{:S(2)}) collective-permute-start(bf16[72,128]{1,0:T(8,128)(2,1)S(1)} %reshape.610), channel_id=1, source_target_pairs={{1,16},{16,1},{17,32},{32,17},{33,48},{48,33},{49,64},{64,49},{65,... | collective-permute-start | bytes 55304 | tf_op jit(solution)/shard_map/ppermute | solution.py:84
  57.7 3.0 %copy-start.23 = (bf16[3,3,128,128]{3,2,1,0:T(8,128)(2,1)S(1)}, bf16[3,3,128,128]{3,2,1,0:T(8,128)(2,1)}, u32[]{:S(2)}) copy-start(bf16[3,3,128,128]{3,2,1,0:T(8,128)(2,1)} %param.19) | copy-start | bytes 884740
  60.7 2.8 %copy-start.27 = (bf16[612,128]{1,0:T(8,128)(2,1)S(1)}, bf16[612,128]{1,0:T(8,128)(2,1)}, u32[]{:S(2)}) copy-start(bf16[612,128]{1,0:T(8,128)(2,1)} %reshape.615) | copy-start | bytes 470020
  80.7 3.4 %copy-start.24 = (bf16[3,3,128,128]{3,2,1,0:T(8,128)(2,1)S(1)}, bf16[3,3,128,128]{3,2,1,0:T(8,128)(2,1)}, u32[]{:S(2)}) copy-start(bf16[3,3,128,128]{3,2,1,0:T(8,128)(2,1)} %param.19) | copy-start | bytes 884740
  80.7 3.6 %copy-start.37 = (bf16[16,32,128]{2,1,0:T(8,128)(2,1)S(1)}, bf16[16,32,128]{2,1,0:T(8,128)(2,1)}, u32[]{:S(2)}) copy-start(bf16[16,32,128]{2,1,0:T(8,128)(2,1)} %get-tuple-element.73) | copy-start | bytes 393220
  108.8 3.8 %collective-permute-start.10 = (bf16[6144,128]{1,0:T(8,128)(2,1)}, bf16[6144,128]{1,0:T(8,128)(2,1)}, u32[]{:S(2)}, u32[]{:S(2)}) collective-permute-start(bf16[6144,128]{1,0:T(8,128)(2,1)} %dynamic-slice_bitcast_fusion), channel_id=1, source_target_pairs={{0,16},{16,0},{1,17},{17,1},{2,18},{18,2},{3,19},{19,3},{4,20},{20... | collective-permute-start | bytes 4718600 | tf_op jit(solution)/shard_map/ppermute | solution.py:262
  117.5 35.6 %all-to-all-start = ((bf16[64,96,128]{2,1,0:T(8,128)(2,1)}), bf16[64,96,128]{2,1,0:T(8,128)(2,1)S(1)}, u32[]{:S(2)}, u32[]{:S(2)}) async-start(bf16[64,96,128]{2,1,0:T(8,128)(2,1)} %bitcast.179), calls=%async_computation | async-start | bytes 3145728 | tf_op jit(solution)/shard_map/all_to_all | solution.py:269
  180.3 6.8 %collective-permute-start.11 = (bf16[6144,128]{1,0:T(8,128)(2,1)}, bf16[6144,128]{1,0:T(8,128)(2,1)}, u32[]{:S(2)}, u32[]{:S(2)}) collective-permute-start(bf16[6144,128]{1,0:T(8,128)(2,1)} %bitcast.180), channel_id=1, source_target_pairs={{0,16},{16,0},{1,17},{17,1},{2,18},{18,2},{3,19},{19,3},{4,20},{20... | collective-permute-start | bytes 4718600 | tf_op jit(solution)/shard_map/ppermute | solution.py:280
  202.1 3.0 %copy-start.1 = (bf16[1024,512]{1,0:T(8,128)(2,1)S(1)}, bf16[1024,512]{1,0:T(8,128)(2,1)}, u32[]{:S(2)}) copy-start(bf16[1024,512]{1,0:T(8,128)(2,1)} %param.21) | copy-start | bytes 3145732
  (42 other events, 59.8 us)

commit v2 on v1

v2 whole, which is shorter than its diff:
```python
import functools

import jax
import jax.numpy as jnp
import numpy as np
from jax import lax
from jax.experimental import pallas as pl
from jax.experimental.pallas import tpu as pltpu
from jax.sharding import Mesh
from jax.sharding import PartitionSpec as P

HID = 1024
BINS = 512
CAP = 256
ROWS = 16
COLS = 32
C = 128
K = 512
HALF = 256
SHARD = 96
PEERS = 64
BODY = 12032

GY = ("x", "core")
GX = ("z", "yl")
TALL = ("x", "core", "yh")
PLANE = ("x", "z", "yl", "yh")

BF = jnp.bfloat16
F32 = jnp.float32


def shift(x, axis, count, step):
    pairs = [(i, i + step) for i in range(count) if 0 <= i + step < count]
    return lax.ppermute(x, axis, pairs)


def side_swap(x):
    own = [(2 * t + c, 2 * t + 1 - c) for t in range(8) for c in range(2)]
    return lax.ppermute(x, TALL, own)


def outer_swap(x):
    pairs = []
    for t in range(7):
        pairs += [(2 * t + 1, 2 * t + 2), (2 * t + 2, 2 * t + 1)]
    return lax.ppermute(x, TALL, pairs)


WIDE = 48
EXT = 896
SLOTS = 384
KEEP = PEERS * SHARD
STAT = BODY - KEEP
VMEM = pltpu.CompilerParams(vmem_limit_bytes=56 * 1024 * 1024)


def vmem(n):
    return [pl.BlockSpec(memory_space=pltpu.VMEM)] * n


SMEM = pl.BlockSpec(memory_space=pltpu.SMEM)
ANY = pl.BlockSpec(memory_space=pl.ANY)


def dot(a, b):
    return jnp.dot(a, b, preferred_element_type=F32)


def dot_t(a, b):
    return lax.dot_general(a, b, (((1,), (1,)), ((), ())), preferred_element_type=F32)


def t_dot(a, b):
    return lax.dot_general(a, b, (((0,), (0,)), ((), ())), preferred_element_type=F32)


def iota(shape, dim):
    return lax.broadcasted_iota(jnp.int32, shape, dim)


def split3(v):
    hi = v.astype(BF)
    rest = v - hi.astype(F32)
    mid = rest.astype(BF)
    low = (rest - mid.astype(F32)).astype(BF)
    return [hi.astype(F32), mid.astype(F32), low.astype(F32)]


def stat_rows(v, like):
    hi, mid, low = split3(v)
    row = iota(like, 0)
    out = jnp.where(row == 0, hi, jnp.where(row == 1, mid, jnp.where(row == 2, low, 0.0)))
    return out


def first_conv_kernel(sc, rmat, cmat, block, finep, w_fine, w_ctx, xc, h1, sg, fscr, mid):
    half, row0, col0 = sc[1], sc[2], sc[3]
    r = rmat[pl.ds(pl.multiple_of(half * ROWS, ROWS), 32), :]
    fi = iota((288, 32), 0) // 16
    grow = row0 + fi - 1
    pick = (fi == iota((288, 32), 1)) & (grow >= 0) & (grow < 256)
    left = dot(pick.astype(F32).astype(BF), r).astype(BF)
    spread = (iota((16, 160), 0) == iota((16, 160), 1) // 16).astype(F32).astype(BF)
    full = dot(left, spread)
    same = (iota((288, 160), 0) % 16) == (iota((288, 160), 1) % 16)
    kron = jnp.where(same, full, 0.0).astype(BF)
    mid[...] = dot(kron, block[...]).astype(BF)
    cols = []
    for dx in range(3):
        gcol = col0 + iota((32, 16), 0) + dx - 1
        ok = (gcol >= 0) & (gcol < 256)
        cols.append(jnp.where(ok, cmat[dx : dx + 32, :], 0.0))
    cols = jnp.concatenate(cols, axis=0).astype(BF)
    for i in range(ROWS + 2):
        wide = dot(cols, mid[16 * i : 16 * i + 16, :]).astype(BF)
        for dx in range(3):
            xc[32 * i : 32 * i + 32, 384 + 512 * dx : 896 + 512 * dx] = wide[32 * dx : 32 * dx + 32]
    fscr[...] = finep[...].astype(F32)
    for i in range(ROWS + 2):
        for dx in range(3):
            at = WIDE * i + dx
            xc[32 * i : 32 * i + 32, 128 * dx : 128 * dx + 128] = fscr[at : at + 32, :].astype(BF)
    for part in range(2):
        base = 256 * part
        acc = None
        for dy in range(3):
            rows = slice(base + 32 * dy, base + 32 * dy + 256)
            term = dot(xc[rows, :384], w_fine[384 * dy : 384 * dy + 384, :])
            term += dot(xc[rows, 384:], w_ctx[1536 * dy : 1536 * dy + 1536, :])
            acc = term if acc is None else acc + term
        s = jax.nn.sigmoid(acc)
        h1[base : base + 256, :] = (acc * s).astype(BF)
        sg[base : base + 256, :] = s * (1.0 + acc * (1.0 - s))


def rest_kernel(
    sc, hb, hw, ha, xc, sg1, idx_s, idx_l, lab, cw, hid, binw, keep, give,
    hp, hx, sg2, h2, rows_s, act, sgz, dl, dz, gscr, gx, g2w, g1w, buf, sem,
):
    core = sc[0]
    hp[0:96, :] = hb[...].astype(F32)
    hp[96:864, :] = hw[...].astype(F32)
    hp[864:960, :] = ha[...].astype(F32)
    hp[960:1000, :] = jnp.zeros((40, C), F32)
    for dx in range(3):
        hx[:, 128 * dx : 128 * dx + 128] = hp[dx : dx + 992, :].astype(BF)
    for part in range(7):
        at = 128 * part
        acc = None
        for dy in range(3):
            term = dot(hx[at + WIDE * dy : at + WIDE * dy + 128, :], cw[384 * dy : 384 * dy + 384, :])
            acc = term if acc is None else acc + term
        s = jax.nn.sigmoid(acc)
        h2[at : at + 128, :] = (acc * s).astype(BF)
        sg2[at : at + 128, :] = s * (1.0 + acc * (1.0 - s))
    loss = jnp.zeros((), F32)
    for part in range(3):
        sl = slice(128 * part, 128 * part + 128)
        pick = (idx_s[sl, :] == iota((128, EXT), 1)).astype(F32).astype(BF)
        rows = dot(pick, h2[...]).astype(BF)
        rows_s[sl, :] = rows
        z = dot(rows, hid[...])
        s = jax.nn.sigmoid(z)
        act[sl, :] = (z * s).astype(BF)
        sgz[sl, :] = s * (1.0 + z * (1.0 - s))
        logits = dot(act[sl, :], binw[...])
        peak = jnp.max(logits, axis=1, keepdims=True)
        top = peak + jnp.log(jnp.sum(jnp.exp(logits - peak), axis=1, keepdims=True))
        lb = lab[sl, :]
        onehot = (lb == iota((128, BINS), 1)).astype(F32)
        live = (lb >= 0).astype(F32)
        if part < 2:
            picked = jnp.sum(logits * onehot, axis=1, keepdims=True)
            loss += jnp.sum(live * (top - picked))
        dl[sl, :] = ((jnp.exp(logits - top) - onehot) * live).astype(BF)
        dact = dot_t(dl[sl, :], binw[...])
        dz[sl, :] = (dact * sgz[sl, :]).astype(BF)
        drows = dot_t(dz[sl, :], hid[...])
        hi = drows.astype(BF)
        gscr[sl, 0:128] = hi
        gscr[sl, 128:256] = (drows - hi.astype(F32)).astype(BF)

    def put(row, value):
        buf[(row // KEEP) ^ core, pl.ds(row % KEEP, value.shape[0]), :] = value.astype(BF)

    for n in range(4):
        put(7936 + 1024 * n, t_dot(act[0:CAP, :], dl[0:CAP, 128 * n : 128 * n + 128]))
    ghid = t_dot(rows_s[0:CAP, :], dz[0:CAP, :])
    for n in range(8):
        put(6912 + 128 * n, ghid[:, 128 * n : 128 * n + 128])
    for part in range(7):
        at = 128 * part
        spread = (idx_l[...] == iota((128, SLOTS), 0) + at).astype(F32).astype(BF)
        both = dot(spread, gscr[...])
        gx[at : at + 128, :] = (both[:, :128] + both[:, 128:]) * sg2[at : at + 128, :]
    gx[EXT : EXT + 8, :] = jnp.zeros((8, C), F32)

    g2w[...] = jnp.zeros_like(g2w)
    col = iota((768, C), 0) % WIDE
    own = jnp.where((col >= 1) & (col <= COLS), gx[WIDE : WIDE + 768, :], 0.0).astype(BF)
    for dy in range(3):
        g2w[WIDE * (1 + dy) : WIDE * (1 + dy) + 768, 128 * dy : 128 * dy + 128] = own
    for dx in range(3):
        part = t_dot(hx[0:960, 128 * dx : 128 * dx + 128], g2w[...])
        for dy in range(3):
            put(5760 + 128 * (3 * dy + dx), part[:, 128 * dy : 128 * dy + 128])

    for i in range(ROWS + 2):
        for dx in range(3):
            at = WIDE * i + 2 - dx
            hx[32 * i : 32 * i + 32, 128 * dx : 128 * dx + 128] = gx[at : at + 32, :].astype(BF)
    g1w[...] = jnp.zeros_like(g1w)
    for part in range(2):
        base = 256 * part
        acc = None
        for dy in range(3):
            at = base + 32 * (2 - dy)
            back = jnp.concatenate(
                [cw[384 * dy + 128 * dx : 384 * dy + 128 * dx + 128, :] for dx in range(3)], axis=1
            )
            term = dot_t(hx[at : at + 256, :], back)
            acc = term if acc is None else acc + term
        g1 = (acc * sg1[base : base + 256, :]).astype(BF)
        for dy in range(3):
            at = base + 32 * dy
            g1w[at : at + 256, 128 * dy : 128 * dy + 128] = g1
    for dx in range(3):
        part = t_dot(xc[:, 128 * dx : 128 * dx + 128], g1w[...])
        for dy in range(3):
            put(4608 + 128 * (3 * dy + dx), part[:, 128 * dy : 128 * dy + 128])
        for side in range(2):
            at = 384 + 512 * dx + 256 * side
            part = t_dot(xc[:, at : at + 256], g1w[...])
            for dy in range(3):
                put(2304 * side + 256 * (3 * dy + dx), part[:, 128 * dy : 128 * dy + 128])
    lane = iota((1, C), 1)
    stats = jnp.where(lane == 0, loss, jnp.where(lane == 1, sc[4].astype(F32), 0.0))
    put(BODY, stat_rows(stats, (16, C)))
    put(BODY + 16, jnp.zeros((2 * KEEP - BODY - 16, C), F32))
    one = pltpu.make_async_copy(buf.at[0], keep, sem.at[0])
    two = pltpu.make_async_copy(buf.at[1], give, sem.at[1])
    one.start()
    two.start()
    one.wait()
    two.wait()


def pair_kernel(sc, keep, got, out):
    out[...] = (keep[...].astype(F32) + got[...].astype(F32)).astype(BF)

    @pl.when((pl.program_id(0) == 3) & (sc[0] == 1))
    def _():
        at = STAT - 4608
        rows = keep[at : at + 16, :].astype(F32) + got[at : at + 16, :].astype(F32)
        out[at : at + 16, :] = stat_rows(jnp.sum(rows, axis=0, keepdims=True), (16, C)).astype(BF)


def spread_kernel(sc, pieces, out, mine):
    acc = pieces[0].astype(F32)
    for i in range(1, PEERS):
        acc += pieces[i].astype(F32)
    mine[...] = acc.astype(BF)
    at = STAT % SHARD

    @pl.when(sc[5] == 1)
    def _():
        rows = acc[at : at + 16]
        mine[at : at + 16, :] = stat_rows(jnp.sum(rows, axis=0, keepdims=True), (16, C)).astype(BF)

    for i in range(PEERS):
        out[i] = mine[...]


def finish_kernel(sc, own, other, loss, gfine, gctx, gconv, ghid, gbin, src, vf, vx, vc, vh, vb, sin, sout):
    core, half = sc[0], sc[1]
    a = pltpu.make_async_copy(own, src.at[core], sin.at[0])
    b = pltpu.make_async_copy(other, src.at[1 - core], sin.at[1])
    a.start()
    b.start()
    a.wait()
    b.wait()
    stats = jnp.sum(src[1, STAT : STAT + 16, :].astype(F32), axis=0, keepdims=True)
    lane = iota((1, C), 1)
    total = jnp.sum(jnp.where(lane == 1, stats, 0.0))
    scale = 1.0 / total
    loss[0, 0] = jnp.sum(jnp.where(lane == 0, stats, 0.0)) * scale

    def get(row, n):
        return src[row // KEEP, row % KEEP : row % KEEP + n, :].astype(F32) * scale

    outs = []

    def send(view, dst, n):
        c = pltpu.make_async_copy(view, dst, sout.at[n])
        c.start()
        outs.append(c)

    for n in range(4):
        vb[:, 128 * n : 128 * n + 128] = get(7936 + 1024 * n, 1024)
    send(vb, gbin, 0)
    at = pl.multiple_of(half * 2304, 128)
    for n in range(9):
        part = src[0, pl.ds(at + 256 * n, 256), :].astype(F32) * scale
        vx[256 * n : 256 * n + 256, :] = part
    send(vx, gctx, 1)
    vf[...] = get(4608, 1152)
    send(vf, gfine, 2)
    for n in range(9):
        vc[128 * n : 128 * n + 128, :] = get(5760 + 128 * n, 128)
    send(vc, gconv, 3)
    for n in range(8):
        vh[:, 128 * n : 128 * n + 128] = get(6912 + 128 * n, 128)
    send(vh, ghid, 4)
    for c in outs:
        c.wait()


def sds(shape, dtype):
    return jax.ShapeDtypeStruct(shape, dtype)


def first_conv(sc, rmat, cmat, block, finep, w_fine, w_ctx):
    return pl.pallas_call(
        first_conv_kernel,
        out_shape=(sds((576, 1920), BF), sds((512, C), BF), sds((512, C), F32)),
        in_specs=[SMEM] + vmem(6),
        out_specs=tuple(vmem(3)),
        scratch_shapes=[pltpu.VMEM((18 * WIDE, C), F32), pltpu.VMEM((288, K), BF)],
        compiler_params=VMEM,
        name="first_conv",
    )(sc, rmat, cmat, block, finep, w_fine, w_ctx)


def rest(*args):
    v = pltpu.VMEM
    return pl.pallas_call(
        rest_kernel,
        out_shape=(sds((KEEP, C), BF), sds((KEEP, C), BF)),
        in_specs=[SMEM] + vmem(len(args) - 1),
        out_specs=(ANY, ANY),
        scratch_shapes=[
            v((1000, C), F32),
            v((992, 384), BF),
            v((EXT, C), F32),
            v((EXT, C), BF),
            v((SLOTS, C), BF),
            v((SLOTS, HID), BF),
            v((SLOTS, HID), F32),
            v((SLOTS, BINS), BF),
            v((SLOTS, HID), BF),
            v((SLOTS, 256), BF),
            v((EXT + 8, C), F32),
            v((960, 384), BF),
            v((576, 384), BF),
            v((2, KEEP, C), BF),
            pltpu.SemaphoreType.DMA((2,)),
        ],
        compiler_params=VMEM,
        name="rest",
    )(*args)


def pair_sum(sc, keep, got):
    spec = pl.BlockSpec((KEEP // 4, C), lambda i: (i, 0))
    return pl.pallas_call(
        pair_kernel,
        grid=(4,),
        out_shape=sds((KEEP, C), BF),
        in_specs=[SMEM, spec, spec],
        out_specs=spec,
        name="pair_sum",
    )(sc, keep, got)


def spread(sc, pieces):
    return pl.pallas_call(
        spread_kernel,
        out_shape=sds((PEERS, SHARD, C), BF),
        in_specs=[SMEM] + vmem(1),
        out_specs=vmem(1)[0],
        scratch_shapes=[pltpu.VMEM((SHARD, C), BF)],
        compiler_params=VMEM,
        name="spread",
    )(sc, pieces)


def finish(sc, own, other):
    v = pltpu.VMEM
    shapes = [(1152, C), (2304, C), (1152, C), (C, HID), (HID, BINS)]
    return pl.pallas_call(
        finish_kernel,
        out_shape=(sds((1, 1), F32),) + tuple(sds(s, F32) for s in shapes),
        in_specs=[SMEM, ANY, ANY],
        out_specs=(SMEM,) + (ANY,) * 5,
        scratch_shapes=[v((2, KEEP, C), BF)]
        + [v(s, F32) for s in shapes]
        + [pltpu.SemaphoreType.DMA((2,)), pltpu.SemaphoreType.DMA((5,))],
        compiler_params=VMEM,
        name="finish",
    )(sc, own, other)


def ring_cells():
    cells = [(0, c) for c in range(34)] + [(17, c) for c in range(34)]
    cells += [(r, 0) for r in range(1, 17)] + [(r, 33) for r in range(1, 17)]
    return np.array([WIDE * r + c for r, c in cells] + [-1] * 28, np.int32)


def local(
    fine,
    context,
    interp_rows,
    interp_cols,
    fine_weight,
    ctx_weight,
    conv_weight,
    hidden_weight,
    bin_weight,
    cell_index,
    counts,
    labels,
):
    core = lax.axis_index("core")
    half = lax.axis_index("yh")
    gy = lax.axis_index(GY)
    gx = lax.axis_index(GX)
    lower = half == 1

    own_idx = cell_index[0, 0]
    own_lab = labels[0, 0]
    own_num = counts[0, 0]
    live = jnp.arange(CAP, dtype=jnp.int32) < own_num

    spot = own_idx[:, None] == jnp.arange(ROWS * COLS, dtype=jnp.int32)[None, :]
    code = jnp.sum(
        jnp.where(spot & live[:, None], own_lab[:, None] + 1, 0), axis=0, dtype=jnp.int32
    )
    digits = jnp.stack([code // 32, code % 32], axis=1).astype(BF).reshape(ROWS, COLS, 2)

    fine_dig = jnp.concatenate([fine, jnp.pad(digits, ((0, 0), (0, 0), (0, 126)))], axis=0)

    def pack_cols(col):
        return jnp.concatenate([fine_dig[:, col], context[:, min(col, 7)].reshape(16, C)], axis=0)

    west = shift(pack_cols(COLS - 1), GX, 8, 1)
    east = shift(pack_cols(0), GX, 8, -1)
    wide = jnp.concatenate([west[:32, None], fine_dig, east[:32, None]], axis=1)
    fine_w, dig_w = wide[:ROWS], wide[ROWS:]
    ctx_w = jnp.concatenate(
        [west[32:].reshape(8, 1, HALF), context, east[32:].reshape(8, 1, HALF)], axis=1
    )
    edge = lambda v, last: lax.dynamic_slice_in_dim(v, jnp.where(last, v.shape[0] - 1, 0), 1, 0)
    inner = jnp.concatenate([edge(fine_w, ~lower), edge(dig_w, ~lower)], axis=0).reshape(68, C)
    outer = jnp.concatenate([edge(fine_w, lower), edge(dig_w, lower)], axis=0).reshape(68, C)
    inner = side_swap(jnp.concatenate([inner, ctx_w.reshape(160, C)], axis=0))
    outer = outer_swap(outer)
    inner_edge = inner[:68].reshape(2, 34, C)
    outer_edge = outer.reshape(2, 34, C)
    before = jnp.where(lower, inner_edge, outer_edge)
    after = jnp.where(lower, outer_edge, inner_edge)
    fine_pad = jnp.concatenate([before[:1], fine_w, after[:1]], axis=0)
    dig_pad = jnp.concatenate([before[1:], dig_w, after[1:]], axis=0)[:, :, :2]
    ctx_o = inner[68:].reshape(8, 10, HALF)
    ctx_all = jnp.where(
        lower,
        jnp.concatenate([ctx_o, ctx_w], axis=2),
        jnp.concatenate([ctx_w, ctx_o], axis=2),
    )
    north = shift(ctx_all[7:8], GY, 8, 1)
    south = shift(ctx_all[0:1], GY, 8, -1)
    block = jnp.concatenate([north, ctx_all, south], axis=0)

    row_anchor = gy * 32 + half * ROWS
    col_anchor = gx * COLS
    owner = (core == 1) & (lax.axis_index(PLANE) == STAT // SHARD)
    sc = jnp.stack([core, half, row_anchor, col_anchor, own_num, owner.astype(jnp.int32)])
    sc = jnp.concatenate([sc, jnp.zeros((2,), jnp.int32)])
    rmat = jnp.pad(interp_rows, ((0, 14), (0, 6)))
    cmat = jnp.pad(interp_cols.astype(F32), ((0, 14), (0, 6)))
    block16 = jnp.pad(block, ((0, 0), (0, 6), (0, 0))).reshape(160, K)
    finep = jnp.pad(fine_pad, ((0, 0), (0, WIDE - 34), (0, 0))).reshape(18 * WIDE, C)
    xc, h_flat, sg1 = first_conv(
        sc, rmat, cmat, block16, finep, fine_weight.reshape(1152, C), ctx_weight.reshape(4608, C)
    )
    h_one = h_flat.reshape(ROWS, COLS, C)

    west = shift(h_one[:, COLS - 2 :].reshape(32, C), GX, 8, 1)
    east = shift(h_one[:, :2].reshape(32, C), GX, 8, -1)
    wide = jnp.concatenate(
        [west.reshape(ROWS, 2, C), h_one, east.reshape(ROWS, 2, C), jnp.zeros((ROWS, 12, C), BF)],
        axis=1,
    )
    two = lambda v, last: lax.dynamic_slice_in_dim(v, jnp.where(last, ROWS - 2, 0), 2, 0)
    inner = side_swap(two(wide, ~lower).reshape(96, C))
    outer = outer_swap(two(wide, lower).reshape(96, C))
    hb = jnp.where(lower, inner, outer)
    ha = jnp.where(lower, outer, inner)

    def ring(v):
        parts = [v[0], v[ROWS + 1], v[1 : 1 + ROWS, 0], v[1 : 1 + ROWS, COLS + 1]]
        return jnp.concatenate(parts, axis=0)

    ring_code = jnp.sum(ring(dig_pad).astype(jnp.int32) * jnp.array([32, 1], jnp.int32), axis=1)
    lab = jnp.concatenate(
        [jnp.where(live, own_lab, -1), ring_code - 1, jnp.full((28,), -1, jnp.int32)]
    )
    spots = jnp.concatenate(
        [(own_idx // COLS + 1) * WIDE + own_idx % COLS + 1, jnp.asarray(ring_cells())]
    )
    keep, give = rest(
        sc, hb, wide.reshape(ROWS * WIDE, C), ha, xc, sg1, spots[:, None], spots[None, :],
        lab[:, None], conv_weight.reshape(1152, C), hidden_weight, bin_weight,
    )
    flip = [(0, 1), (1, 0)]
    pair = pair_sum(sc, keep, lax.ppermute(give, "core", flip))
    pieces = lax.all_to_all(pair.reshape(PEERS, SHARD, C), PLANE, 0, 0, tiled=True)
    mine = spread(sc, pieces)
    half_sum = lax.all_to_all(mine, PLANE, 0, 0, tiled=True).reshape(KEEP, C)
    other = lax.ppermute(half_sum, "core", flip)
    loss, gfine, gctx, gconv, ghid, gbin = finish(sc, half_sum, other)
    return (
        loss.reshape(()),
        gfine.reshape(3, 3, C, C),
        gctx.reshape(3, 3, HALF, C),
        gconv.reshape(3, 3, C, C),
        ghid,
        gbin,
    )


def solution(mesh):
    devices = np.asarray(mesh.devices).reshape(4, 2, 4, 2, 2)
    split = Mesh(devices, ("x", "core", "z", "yl", "yh"))
    in_specs = (
        P(TALL, GX, None),
        P(GY, GX, "yh"),
        P(),
        P(),
        P(),
        P(),
        P(),
        P(),
        P(),
        P(TALL, GX, None),
        P(TALL, GX),
        P(TALL, GX, None),
    )
    out_specs = (P(), P(), P(None, None, "yh", None), P(), P(), P())
    return jax.shard_map(local, mesh=split, in_specs=in_specs, out_specs=out_specs, check_vma=False)
```

time: 208 us -> 162 us (0.78)
  blocking collectives: 26.7 us -> 63.8 us
  Pallas kernels: 0 us -> 30.4 us
  local copies, waits for them, and re-layouts: 43.5 us -> 13.5 us
  waiting for transfers between devices: 42.4 us -> 12.6 us
  matrix products: 26.8 us -> 0 us
  starting transfers between devices: 43.6 us -> 32 us
  other arithmetic: 17.5 us -> 6.54 us
  between operations: 5.71 us -> 1.96 us
    all_to_all x1 -> x2, blocking collectives: 26.7 us -> 63.8 us  [the longest x1 37.1 us: local(): lax.all_to_all(pair.reshape(PEERS, SHARD, C), PLANE, 0, 0, tiled=True)]
    pallas_call x0 -> x5, Pallas kernels: none -> 30.4 us  [the longest x1 12.1 us: rest(): pl.pallas_call(rest_kernel, out_shape=(sds((KEEP, C), BF), sds((KEEP, C),...]
    dot_general x71 -> x0, matrix products: 26.8 us -> none  [the longest x27 13.3 us: weight_grad(): lax.dot_general(patch, flat_grad, (((0,), (0,)), ((), ())), preferred_ele...]
    all_to_all x1 -> x0, waiting for transfers between devices: 23.3 us -> none  [local(): lax.all_to_all(pair.reshape(PEERS, SHARD, C), PLANE, 0, 0, tiled=True)]
    all_to_all x1 -> x0, starting transfers between devices: 12.2 us -> none  [local(): lax.all_to_all(pair.reshape(PEERS, SHARD, C), PLANE, 0, 0, tiled=True)]
    concatenate x4 -> x5, local copies, waits for them, and re-layouts: 13.2 us -> 2.06 us  [the longest x1 1.3 us: local(): jnp.concatenate([fine, jnp.pad(digits, ((0, 0), (0, 0), (0, 126)))], axis=0)]
    reshape x13 -> x0, local copies, waits for them, and re-layouts: 5.1 us -> none  [the longest x9 5.05 us: conv_rows(): patch = padded[dy:dy + rows, dx:dx + cols, :].reshape(rows * cols, -1)]
    convert_element_type x15 -> x0, other arithmetic: 4.54 us -> none  [the longest x1 2.96 us: local(): plain = pair.astype(BF)]
  transfers between devices with their start and end apart: 13 -> 12, of which waited for: 8 -> 6; matrix products, arithmetic and copies ran while one was open for 1% -> 5% of each run, Pallas kernels for 0% -> 0%
where the time goes in v2:
time: 162 us; the launch traced here: 161 us
  blocking collectives  63.8 us (39%)
  starting transfers between devices  32 us (20%)
  Pallas kernels  30.4 us (19%)
  local copies, waits for them, and re-layouts  13.5 us (8%)
  waiting for transfers between devices  12.6 us (8%)
  other arithmetic  6.54 us (4%)
  between operations  1.96 us (1%)
    all_to_all x1, blocking collectives, local(): lax.all_to_all(pair.reshape(PEERS, SHARD, C), PLANE, 0, 0, tiled=True)  37.1 us
    all_to_all x1, blocking collectives, local(): half_sum = lax.all_to_all(mine, PLANE, 0, 0, tiled=True).reshape(KEEP, C)  26.7 us
    ppermute x6, starting transfers between devices, shift(): return lax.ppermute(x, axis, pairs)  16.9 us
    pallas_call x1, Pallas kernels, rest(): pl.pallas_call(rest_kernel, out_shape=(sds((KEEP, C), BF), sds((KEEP, C),...  12.1 us
    ppermute x2, starting transfers between devices, outer_swap(): return lax.ppermute(x, TALL, pairs)  9.38 us
    pallas_call x1, Pallas kernels, finish(): pl.pallas_call(finish_kernel, out_shape=(sds((1, 1), F32),) + tuple((sds(...  5.89 us
    pallas_call x1, Pallas kernels, first_conv(): pl.pallas_call(first_conv_kernel, out_shape=(sds((576, 1920), BF), sds((5...  5.52 us
    pallas_call x1, Pallas kernels, pair_sum(): pl.pallas_call(pair_kernel, grid=(4,), out_shape=sds((KEEP, C), BF), in_s...  3.99 us
  transfers between devices with their start and end apart: 12, of which 6 were waited for; matrix products, arithmetic and copies ran while one was open for 5% of the time, Pallas kernels for 0%

profile of v2, /device:TPU:1, one launch (start us, length us, event | category | flops | bytes accessed | tf_op | source)
XLA Modules:
  0.0 160.8 jit_solution(14014676866537665474)
XLA Ops:
  2.0 0.9 select_reduce_fusion
  2.9 0.9 slice_reduce_fusion.1
  3.8 1.3 copy.118
  5.8 1.1 copy.120
  7.0 1.3 collective-permute-start.1
  8.3 1.1 copy.119
  9.4 4.7 %collective-permute-start = (bf16[48,128]{1,0:T(8,128)(2,1)S(1)}, bf16[48,128]{1,0:T(8,128)(2,1)S(1)}, u32[]{:S(2)}, u32[]{:S(2)}) collective-permute-start(bf16[48,128]{1,0:T(8,128)(2,1)S(1)} %pad_maximum_fusion.6), channel_id=1, source_target_pairs={{0,2},{2,4},{4,6},{6,8},{8,10},{10,12},{12,14},{1,3},{3,5},{5,7},{... | collective-permute-start | bytes 36872 | tf_op jit(solution)/shard_map/ppermute | solution.py:35
  15.1 1.3 copy.121
  16.8 6.1 %collective-permute-start.5 = (bf16[68,128]{1,0:T(8,128)(2,1)S(1)}, bf16[68,128]{1,0:T(8,128)(2,1)S(1)}, u32[]{:S(2)}, u32[]{:S(2)}) collective-permute-start(bf16[68,128]{1,0:T(8,128)(2,1)S(1)} %reshape.209), channel_id=1, source_target_pairs={{1,16},{16,1},{17,32},{32,17},{33,48},{48,33},{49,64},{64,49},{65,... | collective-permute-start | bytes 52232 | tf_op jit(solution)/shard_map/ppermute | solution.py:47
  23.0 1.1 collective-permute-start.2
  28.1 3.7 %collective-permute-start.3 = (bf16[1,10,512]{2,1,0:T(8,128)(2,1)S(1)}, bf16[1,10,512]{2,1,0:T(8,128)(2,1)S(1)}, u32[]{:S(2)}, u32[]{:S(2)}) collective-permute-start(bf16[1,10,512]{2,1,0:T(8,128)(2,1)S(1)} %get-tuple-element.42), channel_id=1, source_target_pairs={{0,16},{16,32},{32,48},{48,64},{64,80},{80,96},{96,112},{1,17},{17... | collective-permute-start | bytes 30728 | tf_op jit(solution)/shard_map/ppermute | solution.py:35
  31.9 1.9 %collective-permute-start.4 = (bf16[1,10,512]{2,1,0:T(8,128)(2,1)S(1)}, bf16[1,10,512]{2,1,0:T(8,128)(2,1)S(1)}, u32[]{:S(2)}, u32[]{:S(2)}) collective-permute-start(bf16[1,10,512]{2,1,0:T(8,128)(2,1)S(1)} %get-tuple-element.43), channel_id=1, source_target_pairs={{16,0},{32,16},{48,32},{64,48},{80,64},{96,80},{112,96},{17,1},{33... | collective-permute-start | bytes 30728 | tf_op jit(solution)/shard_map/ppermute | solution.py:35
  34.6 2.3 %collective-permute-done.4 = bf16[1,10,512]{2,1,0:T(8,128)(2,1)S(1)} collective-permute-done((bf16[1,10,512]{2,1,0:T(8,128)(2,1)S(1)}, bf16[1,10,512]{2,1,0:T(8,128)(2,1)S(1)}, u32[]{:S(2)}, u32[]{:S(2)}) %collective-permute-start.4) | collective-permute-done | bytes 10272 | tf_op jit(solution)/shard_map/ppermute | solution.py:35
  37.6 5.5 %first_conv.1 = (bf16[576,1920]{1,0:T(8,128)(2,1)}, bf16[512,128]{1,0:T(8,128)(2,1)}, f32[512,128]{1,0:T(8,128)}) custom-call(s32[8]{0:T(128)} %concatenate.54.sc, bf16[48,16]{1,0:T(8,128)(2,1)} %pad.22.rmat, f32[48,16]{1,0:T(8,128)} %pad_convert_fusion.cmat, bf16[160,512]{1,0:T(8,128)(2,1)} %bitcast.51, bf16[864,128]{1,0:T(8,128)(2,1)} %bitcast.50, ...), custom_call_target="tpu_custom_call" | custom-call | tf_op jit(solution)/shard_map/first_conv/pallas_call | solution.py:324
  43.9 1.3 collective-permute-start.7
  45.2 4.0 %collective-permute-start.6 = (bf16[32,128]{1,0:T(8,128)(2,1)S(1)}, bf16[32,128]{1,0:T(8,128)(2,1)S(1)}, u32[]{:S(2)}, u32[]{:S(2)}) collective-permute-start(bf16[32,128]{1,0:T(8,128)(2,1)S(1)} %bitcast.62), channel_id=1, source_target_pairs={{0,2},{2,4},{4,6},{6,8},{8,10},{10,12},{12,14},{1,3},{3,5},{5,7},{... | collective-permute-start | bytes 24584 | tf_op jit(solution)/shard_map/ppermute | solution.py:35
  50.0 1.0 maximum_maximum_fusion
  51.1 1.2 collective-permute-start.8
  52.2 3.3 %collective-permute-start.9 = (bf16[96,128]{1,0:T(8,128)(2,1)S(1)}, bf16[96,128]{1,0:T(8,128)(2,1)S(1)}, u32[]{:S(2)}, u32[]{:S(2)}) collective-permute-start(bf16[96,128]{1,0:T(8,128)(2,1)S(1)} %bitcast.58), channel_id=1, source_target_pairs={{1,16},{16,1},{17,32},{32,17},{33,48},{48,33},{49,64},{64,49},{65,... | collective-permute-start | bytes 73736 | tf_op jit(solution)/shard_map/ppermute | solution.py:47
  55.6 0.8 broadcast_in_dim.44.lab
  56.4 2.5 %collective-permute-done.9 = bf16[96,128]{1,0:T(8,128)(2,1)S(1)} collective-permute-done((bf16[96,128]{1,0:T(8,128)(2,1)S(1)}, bf16[96,128]{1,0:T(8,128)(2,1)S(1)}, u32[]{:S(2)}, u32[]{:S(2)}) %collective-permute-start.9) | collective-permute-done | bytes 24608 | tf_op jit(solution)/shard_map/ppermute | solution.py:47
  59.5 12.1 %rest.1 = (bf16[6144,128]{1,0:T(8,128)(2,1)}, bf16[6144,128]{1,0:T(8,128)(2,1)}) custom-call(s32[8]{0:T(128)} %concatenate.54.sc, bf16[96,128]{1,0:T(8,128)(2,1)} %get-tuple-element.47.hb, bf16[768,128]{1,0:T(8,128)(2,1)} %bitcast.49, bf16[96,128]{1,0:T(8,128)(2,1)} %get-tuple-element.46.ha, bf16[576,1920]{1,0:T(8,128)(2,1)} %get-tuple-element.18.xc, ...), custom_call_target="tpu_custom_call" | custom-call | tf_op jit(solution)/shard_map/rest/pallas_call | solution.py:337
  71.7 3.6 %collective-permute-done.10.got = bf16[6144,128]{1,0:T(8,128)(2,1)S(1)} collective-permute-done((bf16[6144,128]{1,0:T(8,128)(2,1)}, bf16[6144,128]{1,0:T(8,128)(2,1)S(1)}, u32[]{:S(2)}, u32[]{:S(2)}) %collective-permute-start.10) | collective-permute-done | bytes 1572896 | tf_op jit(solution)/shard_map/ppermute | solution.py:516
  75.3 1.1 copy-done.1
  76.4 4.0 %pair_sum.1 = bf16[6144,128]{1,0:T(8,128)(2,1)} custom-call(s32[8]{0:T(128)} %concatenate.54.sc, bf16[6144,128]{1,0:T(8,128)(2,1)} %get-tuple-element.20.keep, bf16[6144,128]{1,0:T(8,128)(2,1)} %copy-done.1), custom_call_target="tpu_custom_call" | custom-call | tf_op jit(solution)/shard_map/pair_sum/pallas_call | solution.py:366
  80.4 37.1 %all_to_all.10.pieces = bf16[64,96,128]{2,1,0:T(8,128)(2,1)} all-to-all(bf16[64,96,128]{2,1,0:T(8,128)(2,1)} %bitcast.45), channel_id=1, replica_groups=mesh['x'=4,'core'=2,'z'=4,'yl'=2,'yh'=2] {'x','z','yl','yh'}, dimensions={0} | all-to-all | bytes 3145728 | tf_op jit(solution)/shard_map/all_to_all | solution.py:517
  117.5 3.0 %spread.1 = bf16[64,96,128]{2,1,0:T(8,128)(2,1)} custom-call(s32[8]{0:T(128)} %concatenate.54.sc, bf16[64,96,128]{2,1,0:T(8,128)(2,1)} %all_to_all.10.pieces), custom_call_target="tpu_custom_call" | custom-call | tf_op jit(solution)/shard_map/spread/pallas_call | solution.py:377
  120.5 26.7 %all_to_all.11 = bf16[64,96,128]{2,1,0:T(8,128)(2,1)S(1)} all-to-all(bf16[64,96,128]{2,1,0:T(8,128)(2,1)} %spread.1), channel_id=1, replica_groups=mesh['x'=4,'core'=2,'z'=4,'yl'=2,'yh'=2] {'x','z','yl','yh'}, dimensions={0} | all-to-all | bytes 3145728 | tf_op jit(solution)/shard_map/all_to_all | solution.py:519
  147.2 3.4 %collective-permute-start.11 = (bf16[6144,128]{1,0:T(8,128)(2,1)S(1)}, bf16[6144,128]{1,0:T(8,128)(2,1)S(1)}, u32[]{:S(2)}, u32[]{:S(2)}) collective-permute-start(bf16[6144,128]{1,0:T(8,128)(2,1)S(1)} %bitcast.46), channel_id=1, source_target_pairs={{0,16},{16,0},{1,17},{17,1},{2,18},{18,2},{3,19},{19,3},{4,20},{20... | collective-permute-start | bytes 4718600 | tf_op jit(solution)/shard_map/ppermute | solution.py:520
  150.6 3.0 %collective-permute-done.11.other = bf16[6144,128]{1,0:T(8,128)(2,1)S(1)} collective-permute-done((bf16[6144,128]{1,0:T(8,128)(2,1)S(1)}, bf16[6144,128]{1,0:T(8,128)(2,1)S(1)}, u32[]{:S(2)}, u32[]{:S(2)}) %collective-permute-start.11) | collective-permute-done | bytes 1572896 | tf_op jit(solution)/shard_map/ppermute | solution.py:520
  153.6 1.1 copy-done.2
  154.8 5.9 %finish.1 = (f32[1,1]{1,0:T(1,128)}, f32[1152,128]{1,0:T(8,128)}, f32[2304,128]{1,0:T(8,128)}, f32[1152,128]{1,0:T(8,128)}, f32[128,1024]{1,0:T(8,128)}, /*index=5*/f32[1024,512]{1,0:T(8,128)}) custom-call(s32[8]{0:T(128)} %concatenate.54.sc, bf16[6144,128]{1,0:T(8,128)(2,1)} %bitcast.47, bf16[6144,128]{1,0:T(8,128)(2,1)} %copy-done.2), custom_call_target="tpu_custom_call" | custom-call | tf_op jit(solution)/shard_map/finish/pallas_call | solution.py:391
  (95 shorter events, 10.6 us)
Async XLA Ops:
  5.3 8.8 %copy-start.7 = (s32[1,1,256]{2,1,0:T(1,128)S(1)}, s32[1,1,256]{2,1,0:T(1,128)}, u32[]{:S(2)}) copy-start(s32[1,1,256]{2,1,0:T(1,128)} %param.23) | copy-start | bytes 3076
  5.8 8.5 %copy-start.5 = (bf16[34,10]{0,1:T(8,128)(2,1)S(1)}, bf16[34,10]{0,1:T(8,128)(2,1)}, u32[]{:S(2)}) copy-start(bf16[34,10]{0,1:T(8,128)(2,1)} %param.17) | copy-start | bytes 2044
  7.0 9.4 %collective-permute-start.1 = (bf16[48,128]{1,0:T(8,128)(2,1)S(1)}, bf16[48,128]{1,0:T(8,128)(2,1)S(1)}, u32[]{:S(2)}, u32[]{:S(2)}) collective-permute-start(bf16[48,128]{1,0:T(8,128)(2,1)S(1)} %pad_maximum_fusion.7), channel_id=1, source_target_pairs={{2,0},{4,2},{6,4},{8,6},{10,8},{12,10},{14,12},{3,1},{5,3},{7,5},{... | collective-permute-start | bytes 36872 | tf_op jit(solution)/shard_map/ppermute | solution.py:35
  9.4 7.0 %collective-permute-start = (bf16[48,128]{1,0:T(8,128)(2,1)S(1)}, bf16[48,128]{1,0:T(8,128)(2,1)S(1)}, u32[]{:S(2)}, u32[]{:S(2)}) collective-permute-start(bf16[48,128]{1,0:T(8,128)(2,1)S(1)} %pad_maximum_fusion.6), channel_id=1, source_target_pairs={{0,2},{2,4},{4,6},{6,8},{8,10},{10,12},{12,14},{1,3},{3,5},{5,7},{... | collective-permute-start | bytes 36872 | tf_op jit(solution)/shard_map/ppermute | solution.py:35
  14.1 8.8 %copy-start.4 = (bf16[8,8,256]{2,1,0:T(8,128)(2,1)S(1)}, bf16[8,8,256]{2,1,0:T(8,128)(2,1)}, u32[]{:S(2)}) copy-start(bf16[8,8,256]{2,1,0:T(8,128)(2,1)} %param.15) | copy-start | bytes 98308
  14.3 9.8 %copy-start.8 = (s32[128]{0:T(128)S(1)}, s32[128]{0:T(128)}, u32[]{:S(2)}) copy-start(s32[128]{0:T(128)} %constant.101.clone) | copy-start | bytes 1540
  14.3 11.2 %copy-start.6 = (bf16[34,10]{0,1:T(8,128)(2,1)S(1)}, bf16[34,10]{0,1:T(8,128)(2,1)}, u32[]{:S(2)}) copy-start(bf16[34,10]{0,1:T(8,128)(2,1)} %param.16) | copy-start | bytes 2044
  16.4 18.1 %copy-start.9 = (s32[2]{0:T(128)S(1)}, s32[2]{0:T(128)}, u32[]{:S(2)}) copy-start(s32[2]{0:T(128)} %constant.100.clone) | copy-start | bytes 28
  16.8 10.4 %collective-permute-start.5 = (bf16[68,128]{1,0:T(8,128)(2,1)S(1)}, bf16[68,128]{1,0:T(8,128)(2,1)S(1)}, u32[]{:S(2)}, u32[]{:S(2)}) collective-permute-start(bf16[68,128]{1,0:T(8,128)(2,1)S(1)} %reshape.209), channel_id=1, source_target_pairs={{1,16},{16,1},{17,32},{32,17},{33,48},{48,33},{49,64},{64,49},{65,... | collective-permute-start | bytes 52232 | tf_op jit(solution)/shard_map/ppermute | solution.py:47
  23.0 4.6 %collective-permute-start.2 = (bf16[228,128]{1,0:T(8,128)(2,1)S(1)}, bf16[228,128]{1,0:T(8,128)(2,1)S(1)}, u32[]{:S(2)}, u32[]{:S(2)}) collective-permute-start(bf16[228,128]{1,0:T(8,128)(2,1)S(1)} %pad_maximum_fusion.3), channel_id=1, source_target_pairs={{0,1},{1,0},{16,17},{17,16},{32,33},{33,32},{48,49},{49,48},{64,65... | collective-permute-start | bytes 175112 | tf_op jit(solution)/shard_map/ppermute | solution.py:40
  28.1 6.5 %collective-permute-start.3 = (bf16[1,10,512]{2,1,0:T(8,128)(2,1)S(1)}, bf16[1,10,512]{2,1,0:T(8,128)(2,1)S(1)}, u32[]{:S(2)}, u32[]{:S(2)}) collective-permute-start(bf16[1,10,512]{2,1,0:T(8,128)(2,1)S(1)} %get-tuple-element.42), channel_id=1, source_target_pairs={{0,16},{16,32},{32,48},{48,64},{64,80},{80,96},{96,112},{1,17},{17... | collective-permute-start | bytes 30728 | tf_op jit(solution)/shard_map/ppermute | solution.py:35
  31.9 5.1 %collective-permute-start.4 = (bf16[1,10,512]{2,1,0:T(8,128)(2,1)S(1)}, bf16[1,10,512]{2,1,0:T(8,128)(2,1)S(1)}, u32[]{:S(2)}, u32[]{:S(2)}) collective-permute-start(bf16[1,10,512]{2,1,0:T(8,128)(2,1)S(1)} %get-tuple-element.43), channel_id=1, source_target_pairs={{16,0},{32,16},{48,32},{64,48},{80,64},{96,80},{112,96},{17,1},{33... | collective-permute-start | bytes 30728 | tf_op jit(solution)/shard_map/ppermute | solution.py:35
  43.9 5.3 %collective-permute-start.7 = (bf16[32,128]{1,0:T(8,128)(2,1)S(1)}, bf16[32,128]{1,0:T(8,128)(2,1)S(1)}, u32[]{:S(2)}, u32[]{:S(2)}) collective-permute-start(bf16[32,128]{1,0:T(8,128)(2,1)S(1)} %bitcast.63), channel_id=1, source_target_pairs={{2,0},{4,2},{6,4},{8,6},{10,8},{12,10},{14,12},{3,1},{5,3},{7,5},{... | collective-permute-start | bytes 24584 | tf_op jit(solution)/shard_map/ppermute | solution.py:35
  45.2 4.8 %collective-permute-start.6 = (bf16[32,128]{1,0:T(8,128)(2,1)S(1)}, bf16[32,128]{1,0:T(8,128)(2,1)S(1)}, u32[]{:S(2)}, u32[]{:S(2)}) collective-permute-start(bf16[32,128]{1,0:T(8,128)(2,1)S(1)} %bitcast.62), channel_id=1, source_target_pairs={{0,2},{2,4},{4,6},{6,8},{8,10},{10,12},{12,14},{1,3},{3,5},{5,7},{... | collective-permute-start | bytes 24584 | tf_op jit(solution)/shard_map/ppermute | solution.py:35
  51.0 8.5 %copy-start.3 = (bf16[16,48,128]{2,1,0:T(8,128)(2,1)}, bf16[16,48,128]{2,1,0:T(8,128)(2,1)S(1)}, u32[]{:S(2)}) copy-start(bf16[16,48,128]{2,1,0:T(8,128)(2,1)S(1)} %maximum_maximum_fusion) | copy-start | bytes 589828
  51.1 5.4 %collective-permute-start.8 = (bf16[96,128]{1,0:T(8,128)(2,1)S(1)}, bf16[96,128]{1,0:T(8,128)(2,1)S(1)}, u32[]{:S(2)}, u32[]{:S(2)}) collective-permute-start(bf16[96,128]{1,0:T(8,128)(2,1)S(1)} %bitcast.59), channel_id=1, source_target_pairs={{0,1},{1,0},{16,17},{17,16},{32,33},{33,32},{48,49},{49,48},{64,65... | collective-permute-start | bytes 73736 | tf_op jit(solution)/shard_map/ppermute | solution.py:40
  52.2 6.6 %collective-permute-start.9 = (bf16[96,128]{1,0:T(8,128)(2,1)S(1)}, bf16[96,128]{1,0:T(8,128)(2,1)S(1)}, u32[]{:S(2)}, u32[]{:S(2)}) collective-permute-start(bf16[96,128]{1,0:T(8,128)(2,1)S(1)} %bitcast.58), channel_id=1, source_target_pairs={{1,16},{16,1},{17,32},{32,17},{33,48},{48,33},{49,64},{64,49},{65,... | collective-permute-start | bytes 73736 | tf_op jit(solution)/shard_map/ppermute | solution.py:47
  71.6 3.7 %collective-permute-start.10 = (bf16[6144,128]{1,0:T(8,128)(2,1)}, bf16[6144,128]{1,0:T(8,128)(2,1)S(1)}, u32[]{:S(2)}, u32[]{:S(2)}) collective-permute-start(bf16[6144,128]{1,0:T(8,128)(2,1)} %get-tuple-element.21), channel_id=1, source_target_pairs={{0,16},{16,0},{1,17},{17,1},{2,18},{18,2},{3,19},{19,3},{4,20},{20... | collective-permute-start | bytes 4718600 | tf_op jit(solution)/shard_map/ppermute | solution.py:516
  75.3 1.1 copy-start.1
  147.2 6.4 %copy-start = (bf16[64,96,128]{2,1,0:T(8,128)(2,1)}, bf16[64,96,128]{2,1,0:T(8,128)(2,1)S(1)}, u32[]{:S(2)}) copy-start(bf16[64,96,128]{2,1,0:T(8,128)(2,1)S(1)} %all_to_all.11) | copy-start | bytes 4718596
  147.2 6.4 %collective-permute-start.11 = (bf16[6144,128]{1,0:T(8,128)(2,1)S(1)}, bf16[6144,128]{1,0:T(8,128)(2,1)S(1)}, u32[]{:S(2)}, u32[]{:S(2)}) collective-permute-start(bf16[6144,128]{1,0:T(8,128)(2,1)S(1)} %bitcast.46), channel_id=1, source_target_pairs={{0,16},{16,0},{1,17},{17,1},{2,18},{18,2},{3,19},{19,3},{4,20},{20... | collective-permute-start | bytes 4718600 | tf_op jit(solution)/shard_map/ppermute | solution.py:520
  153.6 1.1 copy-start.2

commit v3 on v2

v3 whole, which is shorter than its diff:
```python
import functools

import jax
import jax.numpy as jnp
import numpy as np
from jax import lax
from jax.experimental import pallas as pl
from jax.experimental.pallas import tpu as pltpu
from jax.sharding import Mesh
from jax.sharding import PartitionSpec as P

HID = 1024
BINS = 512
CAP = 256
ROWS = 16
COLS = 32
C = 128
K = 512
HALF = 256
SHARD = 96
PEERS = 64
BODY = 12032

GY = ("x", "core")
GX = ("z", "yl")
TALL = ("x", "core", "yh")
PLANE = ("x", "z", "yl", "yh")

BF = jnp.bfloat16
F32 = jnp.float32


def shift(x, axis, count, step):
    pairs = [(i, i + step) for i in range(count) if 0 <= i + step < count]
    return lax.ppermute(x, axis, pairs)


def side_swap(x):
    own = [(2 * t + c, 2 * t + 1 - c) for t in range(8) for c in range(2)]
    return lax.ppermute(x, TALL, own)


def outer_swap(x):
    pairs = []
    for t in range(7):
        pairs += [(2 * t + 1, 2 * t + 2), (2 * t + 2, 2 * t + 1)]
    return lax.ppermute(x, TALL, pairs)


WIDE = 48
EXT = 896
SLOTS = 384
KEEP = PEERS * SHARD
STAT = BODY // 2
MIB = 1024 * 1024
BUSY = pl.CostEstimate(flops=5_000_000_000, bytes_accessed=1_000_000, transcendentals=0)


def limit(mib):
    return pltpu.CompilerParams(vmem_limit_bytes=mib * MIB)


def vmem(n):
    return [pl.BlockSpec(memory_space=pltpu.VMEM)] * n


SMEM = pl.BlockSpec(memory_space=pltpu.SMEM)
ANY = pl.BlockSpec(memory_space=pl.ANY)
HBM = pl.BlockSpec(memory_space=pltpu.HBM)


def dot(a, b):
    return jnp.dot(a, b, preferred_element_type=F32)


def dot_t(a, b):
    return lax.dot_general(a, b, (((1,), (1,)), ((), ())), preferred_element_type=F32)


def t_dot(a, b):
    return lax.dot_general(a, b, (((0,), (0,)), ((), ())), preferred_element_type=F32)


def iota(shape, dim):
    return lax.broadcasted_iota(jnp.int32, shape, dim)


def split3(v):
    hi = v.astype(BF)
    rest = v - hi.astype(F32)
    mid = rest.astype(BF)
    low = (rest - mid.astype(F32)).astype(BF)
    return [hi.astype(F32), mid.astype(F32), low.astype(F32)]


def stat_rows(v, like):
    hi, mid, low = split3(v)
    row = iota(like, 0)
    out = jnp.where(row == 0, hi, jnp.where(row == 1, mid, jnp.where(row == 2, low, 0.0)))
    return out


def fetch(pairs, sem):
    copies = [pltpu.make_async_copy(src, dst, sem.at[n]) for n, (src, dst) in enumerate(pairs)]
    for c in copies:
        c.start()
    return copies


def edge_cols_kernel(fine_in, ctx_in, last, first, fine, ctx, fs, xs):
    fine[...] = fine_in[...]
    ctx[...] = ctx_in[...]
    fs[...] = fine[...].astype(F32)
    for side in range(2):
        xs[side] = ctx[:, 128 * side : 128 * side + 128].astype(F32)
    for out, fc, xc in ((last, COLS - 1, 7), (first, 0, 0)):
        out[0:16, :] = fs[pl.ds(fc, 16, stride=COLS), :].astype(BF)
        sides = [xs.at[side][pl.ds(xc, 8, stride=8), :] for side in range(2)]
        out[16:32, :] = jnp.concatenate(sides, axis=0).astype(BF)


def edge_rows_kernel(sc, fine, ctx, west, east, inner, outer, rows, xs):
    lower = sc[1] == 1
    rows[...] = jnp.zeros_like(rows)
    w, e = west[...].astype(F32), east[...].astype(F32)
    for n, r in ((0, 0), (1, ROWS - 1)):
        at = WIDE * n
        rows[at + 1 : at + 33, :] = fine[COLS * r : COLS * r + COLS, :].astype(F32)
        rows[at : at + 1, :] = w[r : r + 1, :]
        rows[at + 33 : at + 34, :] = e[r : r + 1, :]
    top, bottom = rows[0:WIDE, :].astype(BF), rows[WIDE : 2 * WIDE, :].astype(BF)
    inner[0:WIDE, :] = jnp.where(lower, top, bottom)
    outer[...] = jnp.where(lower, bottom, top)
    xs[...] = jnp.zeros_like(xs)
    for side in range(2):
        base = 128 * side
        for a in range(8):
            at = base + 16 * a
            xs[at + 1 : at + 9, :] = ctx[8 * a : 8 * a + 8, base : base + 128].astype(F32)
        xs[pl.ds(base, 8, stride=16), :] = w[16 + 8 * side : 24 + 8 * side, :]
        xs[pl.ds(base + 9, 8, stride=16), :] = e[16 + 8 * side : 24 + 8 * side, :]
    inner[WIDE:, :] = xs[...].astype(BF)


def column(row):
    n = row.shape[1]
    eye = iota((n, n), 0) == iota((n, n), 1)
    return jnp.sum(jnp.where(eye, row.astype(F32), 0.0), axis=1, keepdims=True)


def first_conv_kernel(
    sc, rows_in, cols_in, fine, west, east, mine, inner, outer, north, south, w_fine, w_ctx, idx_l, lab_l,
    xc_out, h1, sg, last, first, digs,
    fscr, mid, block, hscr, dscr, rmat, cmat, xc, xsem,
):
    half, row0, col0 = sc[1], sc[2], sc[3]
    lower = half == 1
    rmat[...] = jnp.zeros_like(rmat)
    cmat[...] = jnp.zeros_like(cmat)
    rmat[0:10, 0:34] = rows_in[...].astype(F32)
    cmat[0:10, 0:34] = cols_in[...].astype(F32)
    for part, got in ((half, mine), (1 - half, inner)):
        for side in range(2):
            lanes = pl.ds(pl.multiple_of(256 * part + 128 * side, 128), 128)
            block[16:144, lanes] = got[WIDE + 128 * side : WIDE + 128 * side + 128, :]
            which = 0 if got is mine else 32
            block[0:16, lanes] = north[which + 16 * side : which + 16 * side + 16, :]
            block[144:160, lanes] = south[which + 16 * side : which + 16 * side + 16, :]
    fi = iota((288, C), 0) // 16
    grow = row0 + fi - 1
    pick = (fi + 16 * half == iota((288, C), 1)) & (grow >= 0) & (grow < 256)
    left = dot_t(pick.astype(F32).astype(BF), rmat[...].astype(BF)).astype(BF)
    spread = (iota((16, 160), 0) == iota((16, 160), 1) // 16).astype(F32).astype(BF)
    full = dot(left, spread)
    same = (iota((288, 160), 0) % 16) == (iota((288, 160), 1) % 16)
    kron = jnp.where(same, full, 0.0).astype(BF)
    mid[...] = dot(kron, block[...]).astype(BF)
    cell = iota((96, C), 0)
    gcol = col0 + cell % 32 + cell // 32 - 1
    pick = (cell % 32 + cell // 32 == iota((96, C), 1)) & (gcol >= 0) & (gcol < 256)
    cols = dot_t(pick.astype(F32).astype(BF), cmat[...].astype(BF)).astype(BF)
    for i in range(ROWS + 2):
        wide = dot(cols, mid[16 * i : 16 * i + 16, :]).astype(BF)
        for dx in range(3):
            xc[32 * i : 32 * i + 32, 384 + 512 * dx : 896 + 512 * dx] = wide[32 * dx : 32 * dx + 32]
    for i in range(ROWS):
        at = WIDE * (i + 1) + 1
        fscr[at : at + 32, :] = fine[32 * i : 32 * i + 32, :].astype(F32)
    fscr[pl.ds(WIDE, 16, stride=WIDE), :] = west[0:16, :].astype(F32)
    fscr[pl.ds(WIDE + 33, 16, stride=WIDE), :] = east[0:16, :].astype(F32)
    a, b = inner[0:WIDE, :].astype(F32), outer[...].astype(F32)
    fscr[0:WIDE, :] = jnp.where(lower, a, b)
    fscr[17 * WIDE : 18 * WIDE, :] = jnp.where(lower, b, a)
    for i in range(ROWS + 2):
        for dx in range(3):
            at = WIDE * i + dx
            xc[32 * i : 32 * i + 32, 128 * dx : 128 * dx + 128] = fscr[at : at + 32, :].astype(BF)
    save = pltpu.make_async_copy(xc, xc_out, xsem)
    save.start()
    for part in range(2):
        base = 256 * part
        acc = None
        for dy in range(3):
            rows = slice(base + 32 * dy, base + 32 * dy + 256)
            term = dot(xc[rows, :384], w_fine[384 * dy : 384 * dy + 384, :])
            term += dot(xc[rows, 384:], w_ctx[1536 * dy : 1536 * dy + 1536, :])
            acc = term if acc is None else acc + term
        s = jax.nn.sigmoid(acc)
        h = (acc * s).astype(BF)
        h1[base : base + 256, :] = h
        hscr[base : base + 256, :] = h.astype(F32)
        sg[base : base + 256, :] = s * (1.0 + acc * (1.0 - s))
    code = jnp.where(iota((1, CAP), 1) < sc[4], lab_l[...] + 1, 0)
    kind = iota((C, CAP), 0)
    digit = jnp.where(kind == 0, code // 32, jnp.where(kind == 1, code % 32, 0))
    digit = digit.astype(F32).astype(BF)
    for part in range(4):
        at = 128 * part
        named = (idx_l[...] == iota((128, CAP), 0) + at).astype(F32).astype(BF)
        dscr[at : at + 128, :] = dot_t(named, digit)
    digs[0:32, :] = dscr[0:32, :].astype(BF)
    digs[32:64, :] = dscr[480:512, :].astype(BF)
    for out, c0, c1, cd in ((last, COLS - 2, COLS - 1, COLS - 1), (first, 0, 1, 0)):
        out[0:16, :] = hscr[pl.ds(c0, 16, stride=COLS), :].astype(BF)
        out[16:32, :] = hscr[pl.ds(c1, 16, stride=COLS), :].astype(BF)
        out[32:48, :] = dscr[pl.ds(cd, 16, stride=COLS), :].astype(BF)
    save.wait()


def h_rows_kernel(sc, h1, digs, west, east, wide, inner, outer, ws, ds):
    lower = sc[1] == 1
    w, e = west[...].astype(F32), east[...].astype(F32)
    ws[...] = jnp.zeros_like(ws)
    ds[...] = jnp.zeros_like(ds)
    for i in range(ROWS):
        ws[WIDE * i + 2 : WIDE * i + 34, :] = h1[32 * i : 32 * i + 32, :].astype(F32)
    for col, value in ((0, w[0:16]), (1, w[16:32]), (34, e[0:16]), (35, e[16:32])):
        ws[pl.ds(col, 16, stride=WIDE), :] = value
    for n, r in ((0, 0), (1, ROWS - 1)):
        at = WIDE * n
        ds[at + 1 : at + 33, :] = digs[32 * n : 32 * n + 32, :].astype(F32)
        ds[at : at + 1, :] = w[32 + r : 33 + r, :]
        ds[at + 33 : at + 34, :] = e[32 + r : 33 + r, :]
    wide[...] = ws[...].astype(BF)
    top, bottom = ws[0:96, :].astype(BF), ws[14 * WIDE : 16 * WIDE, :].astype(BF)
    inner[0:96, :] = jnp.where(lower, top, bottom)
    outer[0:96, :] = jnp.where(lower, bottom, top)
    top, bottom = ds[0:WIDE, :].astype(BF), ds[WIDE : 2 * WIDE, :].astype(BF)
    inner[96:144, :] = jnp.where(lower, top, bottom)
    outer[96:144, :] = jnp.where(lower, bottom, top)


def rest_kernel(
    sc, hw, inner, outer, west, east, xc_in, sg1, idx_l, ring_l, lab_l, cw, hid, binw,
    keep, give,
    hp, hx, sg2, h2, rows_s, act, sgz, dl, dz, gscr, gx, g2w, g1w, buf, xc, sem,
):
    (load,) = fetch([(xc_in, xc)], sem)
    core, lower = sc[0], sc[1] == 1
    a, b = inner[...].astype(F32), outer[...].astype(F32)
    before, after = jnp.where(lower, a, b), jnp.where(lower, b, a)
    hp[0:96, :] = before[0:96]
    hp[96:864, :] = hw[...].astype(F32)
    hp[864:960, :] = after[0:96]
    hp[960:1000, :] = jnp.zeros((40, C), F32)
    gx[...] = jnp.zeros_like(gx)
    gx[0:WIDE, :] = before[96:144]
    gx[17 * WIDE : 18 * WIDE, :] = after[96:144]
    gx[pl.ds(WIDE, 16, stride=WIDE), :] = west[32:48, :].astype(F32)
    gx[pl.ds(WIDE + 33, 16, stride=WIDE), :] = east[32:48, :].astype(F32)
    slot_l = idx_l[...] + 16 * (idx_l[...] // 32) + WIDE + 1
    slot_s = column(slot_l).astype(jnp.int32)
    ring_s = column(ring_l[...]).astype(jnp.int32)
    ring_pick = (ring_s == iota((128, EXT), 1)).astype(F32).astype(BF)
    code = dot(ring_pick, gx[0:EXT, :].astype(BF))
    lane = iota((128, C), 1)
    code = jnp.sum(jnp.where(lane == 0, 32.0 * code, jnp.where(lane == 1, code, 0.0)), axis=1, keepdims=True)
    own_lab = column(jnp.where(iota((1, CAP), 1) < sc[4], lab_l[...], -1)).astype(jnp.int32)
    for dx in range(3):
        hx[:, 128 * dx : 128 * dx + 128] = hp[dx : dx + 992, :].astype(BF)
    for part in range(7):
        at = 128 * part
        acc = None
        for dy in range(3):
            term = dot(hx[at + WIDE * dy : at + WIDE * dy + 128, :], cw[384 * dy : 384 * dy + 384, :])
            acc = term if acc is None else acc + term
        s = jax.nn.sigmoid(acc)
        h2[at : at + 128, :] = (acc * s).astype(BF)
        sg2[at : at + 128, :] = s * (1.0 + acc * (1.0 - s))
    loss = jnp.zeros((), F32)
    for part in range(3):
        sl = slice(128 * part, 128 * part + 128)
        pick = ring_pick
        if part < 2:
            pick = (slot_s[sl] == iota((128, EXT), 1)).astype(F32).astype(BF)
        rows = dot(pick, h2[...]).astype(BF)
        rows_s[sl, :] = rows
        z = dot(rows, hid[...])
        s = jax.nn.sigmoid(z)
        act[sl, :] = (z * s).astype(BF)
        sgz[sl, :] = s * (1.0 + z * (1.0 - s))
        logits = dot(act[sl, :], binw[...])
        peak = jnp.max(logits, axis=1, keepdims=True)
        top = peak + jnp.log(jnp.sum(jnp.exp(logits - peak), axis=1, keepdims=True))
        lb = own_lab[sl] if part < 2 else code.astype(jnp.int32) - 1
        onehot = (lb == iota((128, BINS), 1)).astype(F32)
        live = (lb >= 0).astype(F32)
        if part < 2:
            picked = jnp.sum(logits * onehot, axis=1, keepdims=True)
            loss += jnp.sum(live * (top - picked))
        dl[sl, :] = ((jnp.exp(logits - top) - onehot) * live).astype(BF)
        dact = dot_t(dl[sl, :], binw[...])
        dz[sl, :] = (dact * sgz[sl, :]).astype(BF)
        drows = dot_t(dz[sl, :], hid[...])
        hi = drows.astype(BF)
        gscr[sl, 0:128] = hi
        gscr[sl, 128:256] = (drows - hi.astype(F32)).astype(BF)

    def put(row, value):
        buf[(row // STAT) ^ core, pl.ds(row % STAT, value.shape[0]), :] = value.astype(BF)

    for n in range(4):
        put(7936 + 1024 * n, t_dot(act[0:CAP, :], dl[0:CAP, 128 * n : 128 * n + 128]))
    ghid = t_dot(rows_s[0:CAP, :], dz[0:CAP, :])
    for n in range(8):
        put(6912 + 128 * n, ghid[:, 128 * n : 128 * n + 128])
    for part in range(7):
        at = 128 * part
        cell = iota((128, CAP), 0) + at
        spread = jnp.concatenate(
            [(slot_l == cell).astype(F32), (ring_l[...] == cell[:, :128]).astype(F32)], axis=1
        ).astype(BF)
        both = dot(spread, gscr[...])
        gx[at : at + 128, :] = (both[:, :128] + both[:, 128:]) * sg2[at : at + 128, :]

    g2w[...] = jnp.zeros_like(g2w)
    col = iota((768, C), 0) % WIDE
    own = jnp.where((col >= 1) & (col <= COLS), gx[WIDE : WIDE + 768, :], 0.0).astype(BF)
    for dy in range(3):
        g2w[WIDE * (1 + dy) : WIDE * (1 + dy) + 768, 128 * dy : 128 * dy + 128] = own
    for dx in range(3):
        part = t_dot(hx[0:960, 128 * dx : 128 * dx + 128], g2w[...])
        for dy in range(3):
            put(5760 + 128 * (3 * dy + dx), part[:, 128 * dy : 128 * dy + 128])

    for i in range(ROWS + 2):
        for dx in range(3):
            at = WIDE * i + 2 - dx
            hx[32 * i : 32 * i + 32, 128 * dx : 128 * dx + 128] = gx[at : at + 32, :].astype(BF)
    g1w[...] = jnp.zeros_like(g1w)
    for part in range(2):
        base = 256 * part
        acc = None
        for dy in range(3):
            at = base + 32 * (2 - dy)
            back = jnp.concatenate(
                [cw[384 * dy + 128 * dx : 384 * dy + 128 * dx + 128, :] for dx in range(3)], axis=1
            )
            term = dot_t(hx[at : at + 256, :], back)
            acc = term if acc is None else acc + term
        g1 = (acc * sg1[base : base + 256, :]).astype(BF)
        for dy in range(3):
            at = base + 32 * dy
            g1w[at : at + 256, 128 * dy : 128 * dy + 128] = g1
    load.wait()
    for dx in range(3):
        part = t_dot(xc[:, 128 * dx : 128 * dx + 128], g1w[...])
        for dy in range(3):
            put(4608 + 128 * (3 * dy + dx), part[:, 128 * dy : 128 * dy + 128])
        for side in range(2):
            at = 384 + 512 * dx + 256 * side
            part = t_dot(xc[:, at : at + 256], g1w[...])
            for dy in range(3):
                put(2304 * side + 256 * (3 * dy + dx), part[:, 128 * dy : 128 * dy + 128])
    lane = iota((1, C), 1)
    stats = jnp.where(lane == 0, loss, jnp.where(lane == 1, sc[4].astype(F32), 0.0))
    for n in range(2):
        buf[n, STAT : STAT + 16, :] = stat_rows(stats, (16, C)).astype(BF)
        buf[n, STAT + 16 : KEEP, :] = jnp.zeros((KEEP - STAT - 16, C), BF)
    one = pltpu.make_async_copy(buf.at[0], keep, sem.at[0])
    two = pltpu.make_async_copy(buf.at[1], give, sem.at[1])
    one.start()
    two.start()
    one.wait()
    two.wait()


def pair_kernel(keep, got, out):
    out[...] = (keep[...].astype(F32) + got[...].astype(F32)).astype(BF)
    sl = slice(STAT, STAT + 16)
    rows = keep[sl, :].astype(F32) + got[sl, :].astype(F32)
    out[sl, :] = stat_rows(jnp.sum(rows, axis=0, keepdims=True), (16, C)).astype(BF)


def spread_kernel(sc, pieces, out, mine):
    acc = pieces[0].astype(F32)
    for i in range(1, PEERS):
        acc += pieces[i].astype(F32)
    mine[...] = acc.astype(BF)
    at = STAT % SHARD

    @pl.when(sc[5] == 1)
    def _():
        rows = acc[at : at + 16]
        mine[at : at + 16, :] = stat_rows(jnp.sum(rows, axis=0, keepdims=True), (16, C)).astype(BF)

    for i in range(PEERS):
        out[i] = mine[...]


def finish_kernel(second, sc, part, *refs):
    refs = refs[5:] if second else refs
    loss, gfine, gctx, gconv, ghid, gbin, vf, vx, vc, vh, vb, sem = refs
    half = sc[1]
    which = 1 - sc[0] if second else sc[0]
    stats = jnp.sum(part[STAT : STAT + 16, :].astype(F32), axis=0, keepdims=True)
    lane = iota((1, C), 1)
    total = jnp.sum(jnp.where(lane == 1, stats, 0.0))
    scale = 1.0 / total
    loss[0, 0] = jnp.sum(jnp.where(lane == 0, stats, 0.0)) * scale

    def get(row, n):
        at = row % STAT
        return part[at : at + n, :].astype(F32) * scale

    def run(copies):
        for c in copies:
            c.start()
        return copies

    @pl.when(which == 0)
    def _():
        at = pl.multiple_of(half * 2304, 128)
        for n in range(9):
            vx[256 * n : 256 * n + 256, :] = part[pl.ds(at + 256 * n, 256), :].astype(F32) * scale
        done = run([pltpu.make_async_copy(vx, gctx, sem.at[0])])
        vf[...] = get(4608, 1152)
        vc[0:256, :] = get(5760, 256)
        done += run(
            [
                pltpu.make_async_copy(vf, gfine, sem.at[1]),
                pltpu.make_async_copy(vc.at[0:256, :], gconv.at[0:256, :], sem.at[2]),
            ]
        )
        for c in done:
            c.wait()

    @pl.when(which == 1)
    def _():
        done = []
        for m in range(4):
            sl = slice(256 * m, 256 * m + 256)
            for n in range(4):
                vb[sl, 128 * n : 128 * n + 128] = get(7936 + 1024 * n + 256 * m, 256)
            done += run([pltpu.make_async_copy(vb.at[sl, :], gbin.at[sl, :], sem.at[m])])
        vc[256:1152, :] = get(6016, 896)
        for n in range(8):
            vh[:, 128 * n : 128 * n + 128] = get(6912 + 128 * n, 128)
        done += run(
            [
                pltpu.make_async_copy(vc.at[256:1152, :], gconv.at[256:1152, :], sem.at[4]),
                pltpu.make_async_copy(vh, ghid, sem.at[5]),
            ]
        )
        for c in done:
            c.wait()


def sds(shape, dtype):
    return jax.ShapeDtypeStruct(shape, dtype)


def edge_cols(fine, ctx):
    return pl.pallas_call(
        edge_cols_kernel,
        out_shape=(sds((32, C), BF),) * 2 + (sds((512, C), BF), sds((64, HALF), BF)),
        in_specs=vmem(2),
        out_specs=tuple(vmem(4)),
        scratch_shapes=[pltpu.VMEM((512, C), F32), pltpu.VMEM((2, 64, C), F32)],
        compiler_params=limit(4),
        cost_estimate=BUSY,
        name="edge_cols",
    )(fine, ctx)


def edge_rows(*args):
    return pl.pallas_call(
        edge_rows_kernel,
        out_shape=(sds((WIDE + 256, C), BF), sds((WIDE, C), BF)),
        in_specs=[SMEM] + vmem(4),
        out_specs=tuple(vmem(2)),
        scratch_shapes=[pltpu.VMEM((2 * WIDE, C), F32), pltpu.VMEM((256, C), F32)],
        compiler_params=limit(4),
        cost_estimate=BUSY,
        name="edge_rows",
    )(*args)


def first_conv(*args):
    v = pltpu.VMEM
    edge = sds((48, C), BF)
    return pl.pallas_call(
        first_conv_kernel,
        out_shape=(sds((576, 1920), BF), sds((512, C), BF), sds((512, C), F32), edge, edge, sds((64, C), BF)),
        in_specs=[SMEM] + vmem(len(args) - 1),
        out_specs=(HBM,) + tuple(vmem(5)),
        scratch_shapes=[
            v((18 * WIDE, C), F32),
            v((288, K), BF),
            v((160, K), BF),
            v((512, C), F32),
            v((512, C), F32),
            v((16, C), F32),
            v((16, C), F32),
            v((576, 1920), BF),
            pltpu.SemaphoreType.DMA,
        ],
        compiler_params=limit(20),
        cost_estimate=pl.CostEstimate(flops=900_000_000, bytes_accessed=5_000_000, transcendentals=0),
        name="first_conv",
    )(*args)


def h_rows(*args):
    edge = sds((144, C), BF)
    return pl.pallas_call(
        h_rows_kernel,
        out_shape=(sds((ROWS * WIDE, C), BF), edge, edge),
        in_specs=[SMEM] + vmem(len(args) - 1),
        out_specs=tuple(vmem(3)),
        scratch_shapes=[pltpu.VMEM((ROWS * WIDE, C), F32), pltpu.VMEM((2 * WIDE, C), F32)],
        compiler_params=limit(6),
        cost_estimate=BUSY,
        name="h_rows",
    )(*args)


def rest(*args):
    v = pltpu.VMEM
    return pl.pallas_call(
        rest_kernel,
        out_shape=(sds((KEEP, C), BF), sds((KEEP, C), BF)),
        in_specs=[SMEM] + vmem(5) + [HBM] + vmem(len(args) - 7),
        out_specs=(ANY, ANY),
        scratch_shapes=[
            v((1000, C), F32),
            v((992, 384), BF),
            v((EXT, C), F32),
            v((EXT, C), BF),
            v((SLOTS, C), BF),
            v((SLOTS, HID), BF),
            v((SLOTS, HID), F32),
            v((SLOTS, BINS), BF),
            v((SLOTS, HID), BF),
            v((SLOTS, 256), BF),
            v((EXT + 8, C), F32),
            v((960, 384), BF),
            v((576, 384), BF),
            v((2, KEEP, C), BF),
            v((576, 1920), BF),
            pltpu.SemaphoreType.DMA((2,)),
        ],
        compiler_params=limit(28),
        cost_estimate=pl.CostEstimate(flops=3_000_000_000, bytes_accessed=8_000_000, transcendentals=0),
        name="rest",
    )(*args)


def pair_sum(keep, got):
    return pl.pallas_call(
        pair_kernel,
        out_shape=sds((KEEP, C), BF),
        in_specs=vmem(2),
        out_specs=vmem(1)[0],
        compiler_params=limit(8),
        name="pair_sum",
    )(keep, got)


def spread(sc, pieces):
    return pl.pallas_call(
        spread_kernel,
        out_shape=sds((PEERS, SHARD, C), BF),
        in_specs=[SMEM] + vmem(1),
        out_specs=vmem(1)[0],
        scratch_shapes=[pltpu.VMEM((SHARD, C), BF)],
        compiler_params=limit(8),
        name="spread",
    )(sc, pieces)


def finish(sc, part, before=None):
    v = pltpu.VMEM
    shapes = [(1152, C), (2304, C), (1152, C), (C, HID), (HID, BINS)]
    more = () if before is None else tuple(before)
    return pl.pallas_call(
        functools.partial(finish_kernel, before is not None),
        out_shape=(sds((1, 1), F32),) + tuple(sds(s, F32) for s in shapes),
        in_specs=[SMEM] + vmem(1) + [ANY] * len(more),
        out_specs=(SMEM,) + (ANY,) * 5,
        input_output_aliases={2 + n: 1 + n for n in range(len(more))},
        scratch_shapes=[v(s, F32) for s in shapes] + [pltpu.SemaphoreType.DMA((6,))],
        compiler_params=limit(16),
        cost_estimate=pl.CostEstimate(flops=800_000, bytes_accessed=5_000_000, transcendentals=0),
        name="finish_other" if more else "finish_own",
    )(sc, part, *more)


def ring_cells():
    cells = [(0, c) for c in range(34)] + [(17, c) for c in range(34)]
    cells += [(r, 0) for r in range(1, 17)] + [(r, 33) for r in range(1, 17)]
    return np.array([WIDE * r + c for r, c in cells] + [-1] * 28, np.int32)


def local(
    fine,
    context,
    interp_rows,
    interp_cols,
    fine_weight,
    ctx_weight,
    conv_weight,
    hidden_weight,
    bin_weight,
    cell_index,
    counts,
    labels,
):
    core = lax.axis_index("core")
    half = lax.axis_index("yh")
    gy = lax.axis_index(GY)
    gx = lax.axis_index(GX)
    owner = lax.axis_index(PLANE) == STAT // SHARD
    zero = jnp.zeros((), jnp.int32)
    sc = jnp.stack(
        [core, half, gy * 32 + half * ROWS, gx * COLS, counts[0, 0], owner.astype(jnp.int32), zero, zero]
    )
    idx = cell_index.reshape(1, CAP)
    lab = labels.reshape(1, CAP)
    ring = jnp.asarray(ring_cells())

    last, first, fine, context = edge_cols(fine.reshape(512, C), context.reshape(64, HALF))
    west = shift(last, GX, 8, 1)
    east = shift(first, GX, 8, -1)
    mine, edge = edge_rows(sc, fine, context, west, east)
    inner = side_swap(mine)
    outer = outer_swap(edge)

    def ctx_row(a):
        picks = [v[WIDE + 128 * s + 16 * a :][:16] for v in (mine, inner) for s in range(2)]
        return jnp.concatenate(picks, axis=0)

    north = shift(ctx_row(7), GY, 8, 1)
    south = shift(ctx_row(0), GY, 8, -1)
    xc, h_one, sg1, last, first, digs = first_conv(
        sc, interp_rows.T, interp_cols.T, fine, west, east, mine, inner, outer, north, south,
        fine_weight.reshape(1152, C), ctx_weight.reshape(4608, C), idx, lab,
    )

    west = shift(last, GX, 8, 1)
    east = shift(first, GX, 8, -1)
    wide, inner, outer = h_rows(sc, h_one, digs, west, east)
    inner = side_swap(inner)
    outer = outer_swap(outer)
    keep, give = rest(
        sc, wide, inner, outer, west, east, xc, sg1, idx, ring[None, :], lab,
        conv_weight.reshape(1152, C), hidden_weight, bin_weight,
    )

    flip = [(0, 1), (1, 0)]
    pair = pair_sum(keep, lax.ppermute(give, "core", flip))
    pieces = lax.all_to_all(pair.reshape(PEERS, SHARD, C), PLANE, 0, 0, tiled=True)
    half_sum = lax.all_to_all(spread(sc, pieces), PLANE, 0, 0, tiled=True).reshape(KEEP, C)
    other = lax.ppermute(half_sum, "core", flip)
    outs = finish(sc, half_sum)
    loss, gfine, gctx, gconv, ghid, gbin = finish(sc, other, outs[1:])
    return (
        loss.reshape(()),
        gfine.reshape(3, 3, C, C),
        gctx.reshape(3, 3, HALF, C),
        gconv.reshape(3, 3, C, C),
        ghid,
        gbin,
    )


def solution(mesh):
    devices = np.asarray(mesh.devices).reshape(4, 2, 4, 2, 2)
    split = Mesh(devices, ("x", "core", "z", "yl", "yh"))
    in_specs = (
        P(TALL, GX, None),
        P(GY, GX, "yh"),
        P(),
        P(),
        P(),
        P(),
        P(),
        P(),
        P(),
        P(TALL, GX, None),
        P(TALL, GX),
        P(TALL, GX, None),
    )
    out_specs = (P(), P(), P(None, None, "yh", None), P(), P(), P())
    return jax.shard_map(local, mesh=split, in_specs=in_specs, out_specs=out_specs, check_vma=False)
```

time: 162 us -> 139 us (0.86)
  local copies, waits for them, and re-layouts: 13.5 us -> 1.79 us
  Pallas kernels: 30.4 us -> 21.3 us
  waiting for transfers between devices: 12.6 us -> 20 us
  other arithmetic: 6.54 us -> 0.01 us
  blocking collectives: 63.8 us -> 60.3 us
    ppermute x2, waiting for transfers between devices: 2.46 us -> 9.19 us  [outer_swap(): return lax.ppermute(x, TALL, pairs)]
    ppermute x2, starting transfers between devices: 9.38 us -> 4.07 us  [outer_swap(): return lax.ppermute(x, TALL, pairs)]
    ppermute x2, starting transfers between devices: 2.24 us -> 6.89 us  [side_swap(): return lax.ppermute(x, TALL, own)]
    slice x20 -> x2, local copies, waits for them, and re-layouts: 4.4 us -> 0.01 us  [ctx_row(): v[WIDE + 128 * s + 16 * a:][:16]]
    all_to_all x1, blocking collectives: 37.1 us -> 33.7 us  [local(): lax.all_to_all(pair.reshape(PEERS, SHARD, C), PLANE, 0, 0, tiled=True)]
    concatenate x14 -> x2, other arithmetic: 3.46 us -> 0.01 us  [ctx_row(): return jnp.concatenate(picks, axis=0)]
    ppermute x1, waiting for transfers between devices: 3.04 us -> 0.06 us  [local(): other = lax.ppermute(half_sum, 'core', flip)]
    pallas_call x2 -> x6, Pallas kernels: 9.88 us -> 7.17 us  [the longest x2 5.56 us: finish(): pl.pallas_call(functools.partial(finish_kernel, before is not None), out_...]
  transfers between devices with their start and end apart: 12 -> 12, of which waited for: 6 -> 7; matrix products, arithmetic and copies ran while one was open for 5% -> 0% of each run, Pallas kernels for 0% -> 2%
where the time goes in v3:
time: 139 us
  blocking collectives  60.3 us (43%)
  starting transfers between devices  33.5 us (24%)
  Pallas kernels  21.3 us (15%)
  waiting for transfers between devices  20 us (14%)
  local copies, waits for them, and re-layouts  1.79 us (1%)
  between operations  1.71 us (1%)
    all_to_all x1, blocking collectives, local(): lax.all_to_all(pair.reshape(PEERS, SHARD, C), PLANE, 0, 0, tiled=True)  33.7 us
    all_to_all x1, blocking collectives, local(): lax.all_to_all(spread(sc, pieces), PLANE, 0, 0, tiled=True).reshape(KEEP, C)  26.7 us
    ppermute x6, starting transfers between devices, shift(): return lax.ppermute(x, axis, pairs)  19 us
    pallas_call x1, Pallas kernels, rest(): pl.pallas_call(rest_kernel, out_shape=(sds((KEEP, C), BF), sds((KEEP, C),...  9.46 us
    ppermute x2, waiting for transfers between devices, outer_swap(): return lax.ppermute(x, TALL, pairs)  9.19 us
    ppermute x2, starting transfers between devices, side_swap(): return lax.ppermute(x, TALL, own)  6.89 us
    pallas_call x2, Pallas kernels, finish(): pl.pallas_call(functools.partial(finish_kernel, before is not None), out_...  5.56 us
    ppermute x6, waiting for transfers between devices, shift(): return lax.ppermute(x, axis, pairs)  5.54 us
  transfers between devices with their start and end apart: 12, of which 7 were waited for; matrix products, arithmetic and copies ran while one was open for 0% of the time, Pallas kernels for 2%

profile of v3, /device:TPU:1, one launch (start us, length us, event | category | flops | bytes accessed | tf_op | source)
XLA Modules:
  0.0 138.7 jit_solution(9561865346374514942)
XLA Ops:
  0.6 0.9 copy-done.5
  1.5 0.8 copy-done.6
  2.3 4.0 %collective-permute-start = (bf16[32,128]{1,0:T(8,128)(2,1)S(1)}, bf16[32,128]{1,0:T(8,128)(2,1)S(1)}, u32[]{:S(2)}, u32[]{:S(2)}) collective-permute-start(bf16[32,128]{1,0:T(8,128)(2,1)S(1)} %get-tuple-element.35), channel_id=1, source_target_pairs={{0,2},{2,4},{4,6},{6,8},{8,10},{10,12},{12,14},{1,3},{3,5},{5,7},{... | collective-permute-start | bytes 24584 | tf_op jit(solution)/shard_map/ppermute | solution.py:35
  6.4 1.3 collective-permute-start.1
  8.4 0.1 stack.27.sc
  8.4 2.4 %collective-permute-done.1.east = bf16[32,128]{1,0:T(8,128)(2,1)S(1)} collective-permute-done((bf16[32,128]{1,0:T(8,128)(2,1)S(1)}, bf16[32,128]{1,0:T(8,128)(2,1)S(1)}, u32[]{:S(2)}, u32[]{:S(2)}) %collective-permute-start.1) | collective-permute-done | bytes 8224 | tf_op jit(solution)/shard_map/ppermute | solution.py:35
  10.9 0.6 edge_rows.1
  11.5 3.0 %collective-permute-start.2 = (bf16[304,128]{1,0:T(8,128)(2,1)S(1)}, bf16[304,128]{1,0:T(8,128)(2,1)S(1)}, u32[]{:S(2)}, u32[]{:S(2)}) collective-permute-start(bf16[304,128]{1,0:T(8,128)(2,1)S(1)} %get-tuple-element.38.mine), channel_id=1, source_target_pairs={{0,1},{1,0},{16,17},{17,16},{32,33},{33,32},{48,49},{49,48},{64,65... | collective-permute-start | bytes 233480 | tf_op jit(solution)/shard_map/ppermute | solution.py:40
  14.5 1.8 %collective-permute-done.2.inner = bf16[304,128]{1,0:T(8,128)(2,1)S(1)} collective-permute-done((bf16[304,128]{1,0:T(8,128)(2,1)S(1)}, bf16[304,128]{1,0:T(8,128)(2,1)S(1)}, u32[]{:S(2)}, u32[]{:S(2)}) %collective-permute-start.2) | collective-permute-done | bytes 77856 | tf_op jit(solution)/shard_map/ppermute | solution.py:40
  16.3 6.2 %collective-permute-start.4 = (bf16[64,128]{1,0:T(8,128)(2,1)S(1)}, bf16[64,128]{1,0:T(8,128)(2,1)S(1)}, u32[]{:S(2)}, u32[]{:S(2)}) collective-permute-start(bf16[64,128]{1,0:T(8,128)(2,1)S(1)} %pad_maximum_fusion), channel_id=1, source_target_pairs={{0,16},{16,32},{32,48},{48,64},{64,80},{80,96},{96,112},{1,17},{17... | collective-permute-start | bytes 49160 | tf_op jit(solution)/shard_map/ppermute | solution.py:35
  22.5 1.9 %collective-permute-start.5 = (bf16[64,128]{1,0:T(8,128)(2,1)S(1)}, bf16[64,128]{1,0:T(8,128)(2,1)S(1)}, u32[]{:S(2)}, u32[]{:S(2)}) collective-permute-start(bf16[64,128]{1,0:T(8,128)(2,1)S(1)} %pad_maximum_fusion.1), channel_id=1, source_target_pairs={{16,0},{32,16},{48,32},{64,48},{80,64},{96,80},{112,96},{17,1},{33... | collective-permute-start | bytes 49160 | tf_op jit(solution)/shard_map/ppermute | solution.py:35
  24.4 2.2 %collective-permute-start.3 = (bf16[48,128]{1,0:T(8,128)(2,1)S(1)}, bf16[48,128]{1,0:T(8,128)(2,1)S(1)}, u32[]{:S(2)}, u32[]{:S(2)}) collective-permute-start(bf16[48,128]{1,0:T(8,128)(2,1)S(1)} %get-tuple-element.39), channel_id=1, source_target_pairs={{1,16},{16,1},{17,32},{32,17},{33,48},{48,33},{49,64},{64,49},{65,... | collective-permute-start | bytes 36872 | tf_op jit(solution)/shard_map/ppermute | solution.py:47
  26.6 4.4 %collective-permute-done.3.outer = bf16[48,128]{1,0:T(8,128)(2,1)S(1)} collective-permute-done((bf16[48,128]{1,0:T(8,128)(2,1)S(1)}, bf16[48,128]{1,0:T(8,128)(2,1)S(1)}, u32[]{:S(2)}, u32[]{:S(2)}) %collective-permute-start.3) | collective-permute-done | bytes 12320 | tf_op jit(solution)/shard_map/ppermute | solution.py:47
  31.0 3.7 %first_conv.1 = (bf16[576,1920]{1,0:T(8,128)(2,1)S(1)}, bf16[512,128]{1,0:T(8,128)(2,1)S(1)}, f32[512,128]{1,0:T(8,128)S(1)}, bf16[48,128]{1,0:T(8,128)(2,1)S(1)...) custom-call(s32[8]{0:T(128)S(1)} %stack.27.sc, bf16[10,34]{1,0:T(8,128)(2,1)S(1)} %bitcast.30, ...), custom_call_target="tpu_custom_call" | custom-call | flops 900000000 | bytes 5000000 | tf_op jit(solution)/shard_map/first_conv/pallas_call | solution.py:502
  34.7 4.3 %collective-permute-start.6 = (bf16[48,128]{1,0:T(8,128)(2,1)S(1)}, bf16[48,128]{1,0:T(8,128)(2,1)S(1)}, u32[]{:S(2)}, u32[]{:S(2)}) collective-permute-start(bf16[48,128]{1,0:T(8,128)(2,1)S(1)} %get-tuple-element.42), channel_id=1, source_target_pairs={{0,2},{2,4},{4,6},{6,8},{8,10},{10,12},{12,14},{1,3},{3,5},{5,7},{... | collective-permute-start | bytes 36872 | tf_op jit(solution)/shard_map/ppermute | solution.py:35
  39.1 1.3 collective-permute-start.7
  40.4 3.1 %collective-permute-done.7.east = bf16[48,128]{1,0:T(8,128)(2,1)S(1)} collective-permute-done((bf16[48,128]{1,0:T(8,128)(2,1)S(1)}, bf16[48,128]{1,0:T(8,128)(2,1)S(1)}, u32[]{:S(2)}, u32[]{:S(2)}) %collective-permute-start.7) | collective-permute-done | bytes 12320 | tf_op jit(solution)/shard_map/ppermute | solution.py:35
  43.5 0.6 h_rows.1
  44.1 3.9 %collective-permute-start.8 = (bf16[144,128]{1,0:T(8,128)(2,1)S(1)}, bf16[144,128]{1,0:T(8,128)(2,1)S(1)}, u32[]{:S(2)}, u32[]{:S(2)}) collective-permute-start(bf16[144,128]{1,0:T(8,128)(2,1)S(1)} %get-tuple-element.45), channel_id=1, source_target_pairs={{0,1},{1,0},{16,17},{17,16},{32,33},{33,32},{48,49},{49,48},{64,65... | collective-permute-start | bytes 110600 | tf_op jit(solution)/shard_map/ppermute | solution.py:40
  48.0 1.9 %collective-permute-start.9 = (bf16[144,128]{1,0:T(8,128)(2,1)S(1)}, bf16[144,128]{1,0:T(8,128)(2,1)S(1)}, u32[]{:S(2)}, u32[]{:S(2)}) collective-permute-start(bf16[144,128]{1,0:T(8,128)(2,1)S(1)} %get-tuple-element.46), channel_id=1, source_target_pairs={{1,16},{16,1},{17,32},{32,17},{33,48},{48,33},{49,64},{64,49},{65,... | collective-permute-start | bytes 110600 | tf_op jit(solution)/shard_map/ppermute | solution.py:47
  50.0 4.8 %collective-permute-done.9.outer = bf16[144,128]{1,0:T(8,128)(2,1)S(1)} collective-permute-done((bf16[144,128]{1,0:T(8,128)(2,1)S(1)}, bf16[144,128]{1,0:T(8,128)(2,1)S(1)}, u32[]{:S(2)}, u32[]{:S(2)}) %collective-permute-start.9) | collective-permute-done | bytes 36896 | tf_op jit(solution)/shard_map/ppermute | solution.py:47
  54.8 9.5 %rest.1 = (bf16[6144,128]{1,0:T(8,128)(2,1)S(1)}, bf16[6144,128]{1,0:T(8,128)(2,1)S(1)}) custom-call(s32[8]{0:T(128)S(1)} %stack.27.sc, bf16[768,128]{1,0:T(8,128)(2,1)S(1)} %get-tuple-element.44.hw, bf16[144,128]{1,0:T(8,128)(2,1)S(1)} %collective-permute-done.8.inner, bf16[144,128]{1,0:T(8,128)(2,1)S(1)} %collective-permute-done.9.outer, ...), custom_call_target="tpu_custom_call" | custom-call | flops 3000000000 | bytes 8000000 | tf_op jit(solution)/shard_map/rest/pallas_call | solution.py:540
  64.3 0.1 collective-permute-start.10
  64.4 3.4 %collective-permute-done.10.got = bf16[6144,128]{1,0:T(8,128)(2,1)S(1)} collective-permute-done((bf16[6144,128]{1,0:T(8,128)(2,1)S(1)}, bf16[6144,128]{1,0:T(8,128)(2,1)S(1)}, u32[]{:S(2)}, u32[]{:S(2)}) %collective-permute-start.10) | collective-permute-done | bytes 1572896 | tf_op jit(solution)/shard_map/ppermute | solution.py:671
  67.8 0.4 pair_sum.1
  68.2 33.7 %all_to_all.10.pieces = bf16[64,96,128]{2,1,0:T(8,128)(2,1)S(1)} all-to-all(bf16[64,96,128]{2,1,0:T(8,128)(2,1)S(1)} %bitcast.24), channel_id=1, replica_groups=mesh['x'=4,'core'=2,'z'=4,'yl'=2,'yh'=2] {'x','z','yl','yh'}, dimensions={0} | all-to-all | bytes 3145728 | tf_op jit(solution)/shard_map/all_to_all | solution.py:672
  101.8 1.0 spread.1
  102.8 26.7 %all_to_all.11 = bf16[64,96,128]{2,1,0:T(8,128)(2,1)S(1)} all-to-all(bf16[64,96,128]{2,1,0:T(8,128)(2,1)S(1)} %spread.1), channel_id=1, replica_groups=mesh['x'=4,'core'=2,'z'=4,'yl'=2,'yh'=2] {'x','z','yl','yh'}, dimensions={0} | all-to-all | bytes 3145728 | tf_op jit(solution)/shard_map/all_to_all | solution.py:673
  129.5 3.4 %collective-permute-start.11 = (bf16[6144,128]{1,0:T(8,128)(2,1)S(1)}, bf16[6144,128]{1,0:T(8,128)(2,1)S(1)}, u32[]{:S(2)}, u32[]{:S(2)}) collective-permute-start(bf16[6144,128]{1,0:T(8,128)(2,1)S(1)} %bitcast.22), channel_id=1, source_target_pairs={{0,16},{16,0},{1,17},{17,1},{2,18},{18,2},{3,19},{19,3},{4,20},{20... | collective-permute-start | bytes 4718600 | tf_op jit(solution)/shard_map/ppermute | solution.py:674
  132.9 3.0 %finish_own.1 = (f32[1,1]{1,0:T(1,128)}, f32[1152,128]{1,0:T(8,128)}, f32[2304,128]{1,0:T(8,128)}, f32[1152,128]{1,0:T(8,128)}, f32[128,1024]{1,0:T(8,128)}, /*index=5*/f32[1024,512]{1,0:T(8,128)}) custom-call(s32[8]{0:T(128)S(1)} %stack.27.sc, bf16[6144,128]{1,0:T(8,128)(2,1)S(1)} %bitcast.23), custom_call_target="tpu_custom_call" | custom-call | flops 800000 | bytes 5000000 | tf_op jit(solution)/shard_map/finish_own/pallas_call | solution.py:596
  135.9 0.1 collective-permute-done.11.part
  135.9 2.6 %finish_other.1 = (f32[1,1]{1,0:T(1,128)}, f32[1152,128]{1,0:T(8,128)}, f32[2304,128]{1,0:T(8,128)}, f32[1152,128]{1,0:T(8,128)}, f32[128,1024]{1,0:T(8,128)}, /*index=5*/f32[1024,512]{1,0:T(8,128)}) custom-call(s32[8]{0:T(128)S(1)} %stack.27.sc, ...), custom_call_target="tpu_custom_call", output_to_operand_aliasing={{1}: (2, {}), {2}: (3, {}), {3}: (4, {}), {4}: (5, {}), {5}... | custom-call | flops 800000 | bytes 5000000 | tf_op jit(solution)/shard_map/finish_other/pallas_call | solution.py:596
  (33 shorter events, 0.1 us)
Async XLA Ops:
  0.6 0.9 copy-start.5
  1.5 0.8 copy-start.6
  2.3 6.1 %collective-permute-start = (bf16[32,128]{1,0:T(8,128)(2,1)S(1)}, bf16[32,128]{1,0:T(8,128)(2,1)S(1)}, u32[]{:S(2)}, u32[]{:S(2)}) collective-permute-start(bf16[32,128]{1,0:T(8,128)(2,1)S(1)} %get-tuple-element.35), channel_id=1, source_target_pairs={{0,2},{2,4},{4,6},{6,8},{8,10},{10,12},{12,14},{1,3},{3,5},{5,7},{... | collective-permute-start | bytes 24584 | tf_op jit(solution)/shard_map/ppermute | solution.py:35
  6.4 4.5 %collective-permute-start.1 = (bf16[32,128]{1,0:T(8,128)(2,1)S(1)}, bf16[32,128]{1,0:T(8,128)(2,1)S(1)}, u32[]{:S(2)}, u32[]{:S(2)}) collective-permute-start(bf16[32,128]{1,0:T(8,128)(2,1)S(1)} %get-tuple-element.36), channel_id=1, source_target_pairs={{2,0},{4,2},{6,4},{8,6},{10,8},{12,10},{14,12},{3,1},{5,3},{7,5},{... | collective-permute-start | bytes 24584 | tf_op jit(solution)/shard_map/ppermute | solution.py:35
  10.8 20.1 %copy-start = (bf16[3,3,512,128]{3,2,1,0:T(8,128)(2,1)S(1)}, bf16[3,3,512,128]{3,2,1,0:T(8,128)(2,1)}, u32[]{:S(2)}) copy-start(bf16[3,3,512,128]{3,2,1,0:T(8,128)(2,1)} %param.18) | copy-start | bytes 3538948
  10.8 20.1 %copy-start.2 = (bf16[3,3,128,128]{3,2,1,0:T(8,128)(2,1)S(1)}, bf16[3,3,128,128]{3,2,1,0:T(8,128)(2,1)}, u32[]{:S(2)}) copy-start(bf16[3,3,128,128]{3,2,1,0:T(8,128)(2,1)} %param.17) | copy-start | bytes 884740
  10.8 20.1 %copy-start.7 = (bf16[34,10]{0,1:T(8,128)(2,1)S(1)}, bf16[34,10]{0,1:T(8,128)(2,1)}, u32[]{:S(2)}) copy-start(bf16[34,10]{0,1:T(8,128)(2,1)} %param.15) | copy-start | bytes 2044
  10.9 20.1 %copy-start.8 = (bf16[34,10]{0,1:T(8,128)(2,1)S(1)}, bf16[34,10]{0,1:T(8,128)(2,1)}, u32[]{:S(2)}) copy-start(bf16[34,10]{0,1:T(8,128)(2,1)} %param.16) | copy-start | bytes 2044
  10.9 20.1 %copy-start.9 = (s32[1,1,256]{2,1,0:T(1,128)S(1)}, s32[1,1,256]{2,1,0:T(1,128)}, u32[]{:S(2)}) copy-start(s32[1,1,256]{2,1,0:T(1,128)} %param.22) | copy-start | bytes 3076
  10.9 20.1 %copy-start.10 = (s32[1,1,256]{2,1,0:T(1,128)S(1)}, s32[1,1,256]{2,1,0:T(1,128)}, u32[]{:S(2)}) copy-start(s32[1,1,256]{2,1,0:T(1,128)} %param.24) | copy-start | bytes 3076
  11.5 4.8 %collective-permute-start.2 = (bf16[304,128]{1,0:T(8,128)(2,1)S(1)}, bf16[304,128]{1,0:T(8,128)(2,1)S(1)}, u32[]{:S(2)}, u32[]{:S(2)}) collective-permute-start(bf16[304,128]{1,0:T(8,128)(2,1)S(1)} %get-tuple-element.38.mine), channel_id=1, source_target_pairs={{0,1},{1,0},{16,17},{17,16},{32,33},{33,32},{48,49},{49,48},{64,65... | collective-permute-start | bytes 233480 | tf_op jit(solution)/shard_map/ppermute | solution.py:40
  16.3 14.6 %collective-permute-start.4 = (bf16[64,128]{1,0:T(8,128)(2,1)S(1)}, bf16[64,128]{1,0:T(8,128)(2,1)S(1)}, u32[]{:S(2)}, u32[]{:S(2)}) collective-permute-start(bf16[64,128]{1,0:T(8,128)(2,1)S(1)} %pad_maximum_fusion), channel_id=1, source_target_pairs={{0,16},{16,32},{32,48},{48,64},{64,80},{80,96},{96,112},{1,17},{17... | collective-permute-start | bytes 49160 | tf_op jit(solution)/shard_map/ppermute | solution.py:35
  22.5 8.5 %collective-permute-start.5 = (bf16[64,128]{1,0:T(8,128)(2,1)S(1)}, bf16[64,128]{1,0:T(8,128)(2,1)S(1)}, u32[]{:S(2)}, u32[]{:S(2)}) collective-permute-start(bf16[64,128]{1,0:T(8,128)(2,1)S(1)} %pad_maximum_fusion.1), channel_id=1, source_target_pairs={{16,0},{32,16},{48,32},{64,48},{80,64},{96,80},{112,96},{17,1},{33... | collective-permute-start | bytes 49160 | tf_op jit(solution)/shard_map/ppermute | solution.py:35
  24.4 6.5 %collective-permute-start.3 = (bf16[48,128]{1,0:T(8,128)(2,1)S(1)}, bf16[48,128]{1,0:T(8,128)(2,1)S(1)}, u32[]{:S(2)}, u32[]{:S(2)}) collective-permute-start(bf16[48,128]{1,0:T(8,128)(2,1)S(1)} %get-tuple-element.39), channel_id=1, source_target_pairs={{1,16},{16,1},{17,32},{32,17},{33,48},{48,33},{49,64},{64,49},{65,... | collective-permute-start | bytes 36872 | tf_op jit(solution)/shard_map/ppermute | solution.py:47
  34.7 5.6 %collective-permute-start.6 = (bf16[48,128]{1,0:T(8,128)(2,1)S(1)}, bf16[48,128]{1,0:T(8,128)(2,1)S(1)}, u32[]{:S(2)}, u32[]{:S(2)}) collective-permute-start(bf16[48,128]{1,0:T(8,128)(2,1)S(1)} %get-tuple-element.42), channel_id=1, source_target_pairs={{0,2},{2,4},{4,6},{6,8},{8,10},{10,12},{12,14},{1,3},{3,5},{5,7},{... | collective-permute-start | bytes 36872 | tf_op jit(solution)/shard_map/ppermute | solution.py:35
  39.1 4.4 %collective-permute-start.7 = (bf16[48,128]{1,0:T(8,128)(2,1)S(1)}, bf16[48,128]{1,0:T(8,128)(2,1)S(1)}, u32[]{:S(2)}, u32[]{:S(2)}) collective-permute-start(bf16[48,128]{1,0:T(8,128)(2,1)S(1)} %get-tuple-element.43), channel_id=1, source_target_pairs={{2,0},{4,2},{6,4},{8,6},{10,8},{12,10},{14,12},{3,1},{5,3},{7,5},{... | collective-permute-start | bytes 36872 | tf_op jit(solution)/shard_map/ppermute | solution.py:35
  43.5 11.3 %copy-start.1 = (bf16[1024,512]{1,0:T(8,128)(2,1)S(1)}, bf16[1024,512]{1,0:T(8,128)(2,1)}, u32[]{:S(2)}) copy-start(bf16[1024,512]{1,0:T(8,128)(2,1)} %binw.1) | copy-start | bytes 3145732
  43.5 11.3 %copy-start.3 = (bf16[3,3,128,128]{3,2,1,0:T(8,128)(2,1)S(1)}, bf16[3,3,128,128]{3,2,1,0:T(8,128)(2,1)}, u32[]{:S(2)}) copy-start(bf16[3,3,128,128]{3,2,1,0:T(8,128)(2,1)} %param.19) | copy-start | bytes 884740
  43.5 11.3 %copy-start.4 = (bf16[128,1024]{1,0:T(8,128)(2,1)S(1)}, bf16[128,1024]{1,0:T(8,128)(2,1)}, u32[]{:S(2)}) copy-start(bf16[128,1024]{1,0:T(8,128)(2,1)} %hid.1) | copy-start | bytes 786436
  43.5 11.3 %copy-start.11 = (s32[1,128]{1,0:T(1,128)S(1)}, s32[1,128]{1,0:T(1,128)}, u32[]{:S(2)}) copy-start(s32[1,128]{1,0:T(1,128)} %constant.37.ring_l) | copy-start | bytes 1540
  44.1 5.8 %collective-permute-start.8 = (bf16[144,128]{1,0:T(8,128)(2,1)S(1)}, bf16[144,128]{1,0:T(8,128)(2,1)S(1)}, u32[]{:S(2)}, u32[]{:S(2)}) collective-permute-start(bf16[144,128]{1,0:T(8,128)(2,1)S(1)} %get-tuple-element.45), channel_id=1, source_target_pairs={{0,1},{1,0},{16,17},{17,16},{32,33},{33,32},{48,49},{49,48},{64,65... | collective-permute-start | bytes 110600 | tf_op jit(solution)/shard_map/ppermute | solution.py:40
  48.0 6.8 %collective-permute-start.9 = (bf16[144,128]{1,0:T(8,128)(2,1)S(1)}, bf16[144,128]{1,0:T(8,128)(2,1)S(1)}, u32[]{:S(2)}, u32[]{:S(2)}) collective-permute-start(bf16[144,128]{1,0:T(8,128)(2,1)S(1)} %get-tuple-element.46), channel_id=1, source_target_pairs={{1,16},{16,1},{17,32},{32,17},{33,48},{48,33},{49,64},{64,49},{65,... | collective-permute-start | bytes 110600 | tf_op jit(solution)/shard_map/ppermute | solution.py:47
  64.3 3.5 %collective-permute-start.10 = (bf16[6144,128]{1,0:T(8,128)(2,1)S(1)}, bf16[6144,128]{1,0:T(8,128)(2,1)S(1)}, u32[]{:S(2)}, u32[]{:S(2)}) collective-permute-start(bf16[6144,128]{1,0:T(8,128)(2,1)S(1)} %get-tuple-element.50), channel_id=1, source_target_pairs={{0,16},{16,0},{1,17},{17,1},{2,18},{18,2},{3,19},{19,3},{4,20},{20... | collective-permute-start | bytes 4718600 | tf_op jit(solution)/shard_map/ppermute | solution.py:671
  129.5 6.4 %collective-permute-start.11 = (bf16[6144,128]{1,0:T(8,128)(2,1)S(1)}, bf16[6144,128]{1,0:T(8,128)(2,1)S(1)}, u32[]{:S(2)}, u32[]{:S(2)}) collective-permute-start(bf16[6144,128]{1,0:T(8,128)(2,1)S(1)} %bitcast.22), channel_id=1, source_target_pairs={{0,16},{16,0},{1,17},{17,1},{2,18},{18,2},{3,19},{19,3},{4,20},{20... | collective-permute-start | bytes 4718600 | tf_op jit(solution)/shard_map/ppermute | solution.py:674

commit v4 on v3

v4 whole, which is shorter than its diff:
```python
import functools

import jax
import jax.numpy as jnp
import numpy as np
from jax import lax
from jax.experimental import pallas as pl
from jax.experimental.pallas import tpu as pltpu
from jax.sharding import Mesh
from jax.sharding import PartitionSpec as P

HID = 1024
BINS = 512
CAP = 256
ROWS = 16
COLS = 32
C = 128
K = 512
HALF = 256
SHARD = 96
PEERS = 64
BODY = 12032

GY = ("x", "core")
GX = ("z", "yl")
TALL = ("x", "core", "yh")
PLANE = ("x", "z", "yl", "yh")

BF = jnp.bfloat16
F32 = jnp.float32


def shift(x, axis, count, step):
    pairs = [(i, i + step) for i in range(count) if 0 <= i + step < count]
    return lax.ppermute(x, axis, pairs)


def side_swap(x):
    own = [(2 * t + c, 2 * t + 1 - c) for t in range(8) for c in range(2)]
    return lax.ppermute(x, TALL, own)


def outer_swap(x):
    pairs = []
    for t in range(7):
        pairs += [(2 * t + 1, 2 * t + 2), (2 * t + 2, 2 * t + 1)]
    return lax.ppermute(x, TALL, pairs)


WIDE = 48
EXT = 896
SLOTS = 384
KEEP = PEERS * SHARD
STAT = BODY // 2
MIB = 1024 * 1024
BUSY = pl.CostEstimate(flops=5_000_000_000, bytes_accessed=1_000_000, transcendentals=0)


def limit(mib):
    return pltpu.CompilerParams(vmem_limit_bytes=mib * MIB)


def vmem(n):
    return [pl.BlockSpec(memory_space=pltpu.VMEM)] * n


ANY = pl.BlockSpec(memory_space=pl.ANY)


def dot(a, b):
    return jnp.dot(a, b, preferred_element_type=F32)


def dot_t(a, b):
    return lax.dot_general(a, b, (((1,), (1,)), ((), ())), preferred_element_type=F32)


def t_dot(a, b):
    return lax.dot_general(a, b, (((0,), (0,)), ((), ())), preferred_element_type=F32)


def iota(shape, dim):
    return lax.broadcasted_iota(jnp.int32, shape, dim)


def split3(v):
    hi = v.astype(BF)
    rest = v - hi.astype(F32)
    mid = rest.astype(BF)
    low = (rest - mid.astype(F32)).astype(BF)
    return [hi.astype(F32), mid.astype(F32), low.astype(F32)]


def stat_rows(v, like):
    hi, mid, low = split3(v)
    row = iota(like, 0)
    out = jnp.where(row == 0, hi, jnp.where(row == 1, mid, jnp.where(row == 2, low, 0.0)))
    return out


def edge_cols_kernel(fine_in, ctx_in, last, first, fine, ctx, fs, xs):
    fine[...] = fine_in[...]
    ctx[...] = ctx_in[...]
    fs[...] = fine[...].astype(F32)
    for side in range(2):
        xs[side] = ctx[:, 128 * side : 128 * side + 128].astype(F32)
    for out, fc, xc in ((last, COLS - 1, 7), (first, 0, 0)):
        out[0:16, :] = fs[pl.ds(fc, 16, stride=COLS), :].astype(BF)
        sides = [xs.at[side][pl.ds(xc, 8, stride=8), :] for side in range(2)]
        out[16:32, :] = jnp.concatenate(sides, axis=0).astype(BF)


def edge_rows_kernel(fine, ctx, west, east, inner, outer, rows, xs):
    lower = lax.axis_index("yh") == 1
    rows[...] = jnp.zeros_like(rows)
    w, e = west[...].astype(F32), east[...].astype(F32)
    for n, r in ((0, 0), (1, ROWS - 1)):
        at = WIDE * n
        rows[at + 1 : at + 33, :] = fine[COLS * r : COLS * r + COLS, :].astype(F32)
        rows[at : at + 1, :] = w[r : r + 1, :]
        rows[at + 33 : at + 34, :] = e[r : r + 1, :]
    top, bottom = rows[0:WIDE, :].astype(BF), rows[WIDE : 2 * WIDE, :].astype(BF)
    inner[0:WIDE, :] = jnp.where(lower, top, bottom)
    outer[...] = jnp.where(lower, bottom, top)
    xs[...] = jnp.zeros_like(xs)
    for side in range(2):
        base = 128 * side
        for a in range(8):
            at = base + 16 * a
            xs[at + 1 : at + 9, :] = ctx[8 * a : 8 * a + 8, base : base + 128].astype(F32)
        xs[pl.ds(base, 8, stride=16), :] = w[16 + 8 * side : 24 + 8 * side, :]
        xs[pl.ds(base + 9, 8, stride=16), :] = e[16 + 8 * side : 24 + 8 * side, :]
    inner[WIDE:, :] = xs[...].astype(BF)


def ctx_rows_kernel(mine, inner, outer, down, up, rows):
    for n, got in enumerate((mine, inner)):
        for side in range(2):
            at, to = WIDE + 128 * side, 32 * n + 16 * side
            up[to : to + 16, :] = got[at : at + 16, :]
            down[to : to + 16, :] = got[at + 112 : at + 128, :]
    rows[0:WIDE, :] = inner[0:WIDE, :]
    rows[WIDE : 2 * WIDE, :] = outer[...]


def column(row):
    n = row.shape[1]
    eye = iota((n, n), 0) == iota((n, n), 1)
    return jnp.sum(jnp.where(eye, row.astype(F32), 0.0), axis=1, keepdims=True)


def first_conv_kernel(
    rows_in, cols_in, fine, west, east, mine, inner, rows, north, south, w_fine, w_ctx, idx_l, lab_l,
    xc, h1, sg, last, first, digs,
    fscr, mid, block, hscr, dscr, rmat, cmat, spot,
):
    spot[0] = lax.axis_index("yh")
    spot[1] = (2 * lax.axis_index("x") + lax.axis_index("core")) * 32
    spot[2] = (2 * lax.axis_index("z") + lax.axis_index("yl")) * COLS
    half, row0, col0 = spot[0], spot[1], spot[2]
    lower = half == 1
    for i in range(ROWS):
        at = WIDE * (i + 1) + 1
        fscr[at : at + 32, :] = fine[32 * i : 32 * i + 32, :].astype(F32)
    fscr[pl.ds(WIDE, 16, stride=WIDE), :] = west[0:16, :].astype(F32)
    fscr[pl.ds(WIDE + 33, 16, stride=WIDE), :] = east[0:16, :].astype(F32)
    a, b = rows[0:WIDE, :].astype(F32), rows[WIDE : 2 * WIDE, :].astype(F32)
    fscr[0:WIDE, :] = jnp.where(lower, a, b)
    fscr[17 * WIDE : 18 * WIDE, :] = jnp.where(lower, b, a)
    for i in range(ROWS + 2):
        for dx in range(3):
            at = WIDE * i + dx
            xc[32 * i : 32 * i + 32, 128 * dx : 128 * dx + 128] = fscr[at : at + 32, :].astype(BF)
    rmat[...] = jnp.zeros_like(rmat)
    cmat[...] = jnp.zeros_like(cmat)
    grow = row0 + iota((10, 34), 1) - 1
    gcol = col0 + iota((10, 34), 1) - 1
    rmat[0:10, 0:34] = jnp.where((grow >= 0) & (grow < 256), rows_in[...].astype(F32), 0.0)
    cmat[0:10, 0:34] = jnp.where((gcol >= 0) & (gcol < 256), cols_in[...].astype(F32), 0.0)
    for side in range(2):
        own = pl.ds(pl.multiple_of(256 * half + 128 * side, 128), 128)
        other = pl.ds(pl.multiple_of(256 * (1 - half) + 128 * side, 128), 128)
        for n, lanes, got in ((0, own, mine), (32, other, inner)):
            sl = slice(n + 16 * side, n + 16 * side + 16)
            block[0:16, lanes] = north[sl, :]
            block[16:144, lanes] = got[WIDE + 128 * side : WIDE + 128 * side + 128, :]
            block[144:160, lanes] = south[sl, :]
    pick = (iota((288, C), 0) >> 4) + 16 * half == iota((288, C), 1)
    left = dot_t(pick.astype(F32).astype(BF), rmat[...].astype(BF)).astype(BF)
    spread = (iota((16, 160), 0) == iota((16, 160), 1) >> 4).astype(F32).astype(BF)
    full = dot(left, spread)
    same = (iota((288, 160), 0) & 15) == (iota((288, 160), 1) & 15)
    kron = jnp.where(same, full, 0.0).astype(BF)
    mid[...] = dot(kron, block[...]).astype(BF)
    cell = iota((96, C), 0)
    pick = (cell & 31) + (cell >> 5) == iota((96, C), 1)
    left = dot_t(pick.astype(F32).astype(BF), cmat[...].astype(BF)).astype(BF)
    for i in range(ROWS + 2):
        wide = dot(left, mid[16 * i : 16 * i + 16, :]).astype(BF)
        for dx in range(3):
            xc[32 * i : 32 * i + 32, 384 + 512 * dx : 896 + 512 * dx] = wide[32 * dx : 32 * dx + 32]
    acc = None
    for dy in range(3):
        rows = slice(32 * dy, 32 * dy + 512)
        term = dot(xc[rows, :384], w_fine[384 * dy : 384 * dy + 384, :])
        term += dot(xc[rows, 384:], w_ctx[1536 * dy : 1536 * dy + 1536, :])
        acc = term if acc is None else acc + term
    s = jax.nn.sigmoid(acc)
    h = (acc * s).astype(BF)
    h1[...] = h
    hscr[...] = h.astype(F32)
    sg[...] = s * (1.0 + acc * (1.0 - s))
    code = lab_l[...] + 1
    kind = iota((C, CAP), 0)
    digit = jnp.where(kind == 0, code >> 5, jnp.where(kind == 1, code & 31, 0))
    digit = digit.astype(F32).astype(BF)
    named = (idx_l[...] == iota((512, CAP), 0)).astype(F32).astype(BF)
    dscr[...] = dot_t(named, digit)
    digs[0:32, :] = dscr[0:32, :].astype(BF)
    digs[32:64, :] = dscr[480:512, :].astype(BF)
    for out, c0, c1, cd in ((last, COLS - 2, COLS - 1, COLS - 1), (first, 0, 1, 0)):
        out[0:16, :] = hscr[pl.ds(c0, 16, stride=COLS), :].astype(BF)
        out[16:32, :] = hscr[pl.ds(c1, 16, stride=COLS), :].astype(BF)
        out[32:48, :] = dscr[pl.ds(cd, 16, stride=COLS), :].astype(BF)


def h_rows_kernel(h1, digs, west, east, wide, inner, outer, ws, ds):
    lower = lax.axis_index("yh") == 1
    w, e = west[...].astype(F32), east[...].astype(F32)
    ws[...] = jnp.zeros_like(ws)
    ds[...] = jnp.zeros_like(ds)
    for i in range(ROWS):
        ws[WIDE * i + 2 : WIDE * i + 34, :] = h1[32 * i : 32 * i + 32, :].astype(F32)
    for col, value in ((0, w[0:16]), (1, w[16:32]), (34, e[0:16]), (35, e[16:32])):
        ws[pl.ds(col, 16, stride=WIDE), :] = value
    for n, r in ((0, 0), (1, ROWS - 1)):
        at = WIDE * n
        ds[at + 1 : at + 33, :] = digs[32 * n : 32 * n + 32, :].astype(F32)
        ds[at : at + 1, :] = w[32 + r : 33 + r, :]
        ds[at + 33 : at + 34, :] = e[32 + r : 33 + r, :]
    wide[...] = ws[...].astype(BF)
    top, bottom = ws[0:96, :].astype(BF), ws[14 * WIDE : 16 * WIDE, :].astype(BF)
    inner[0:96, :] = jnp.where(lower, top, bottom)
    outer[0:96, :] = jnp.where(lower, bottom, top)
    top, bottom = ds[0:WIDE, :].astype(BF), ds[WIDE : 2 * WIDE, :].astype(BF)
    inner[96:144, :] = jnp.where(lower, top, bottom)
    outer[96:144, :] = jnp.where(lower, bottom, top)


def rest_kernel(
    hw, inner, outer, west, east, xc, sg1, idx_l, ring_l, lab_l, cw, hid, binw,
    keep, give,
    hp, hx, sg2, h2, rows_s, act, sgz, dl, dz, gscr, gx, g2w, g1w, buf, spot,
):
    spot[0] = lax.axis_index("core")
    spot[1] = lax.axis_index("yh")
    core, lower = spot[0], spot[1] == 1
    a, b = inner[...].astype(F32), outer[...].astype(F32)
    before, after = jnp.where(lower, a, b), jnp.where(lower, b, a)
    hp[0:96, :] = before[0:96]
    hp[96:864, :] = hw[...].astype(F32)
    hp[864:960, :] = after[0:96]
    hp[960:1000, :] = jnp.zeros((40, C), F32)
    gx[...] = jnp.zeros_like(gx)
    gx[0:WIDE, :] = before[96:144]
    gx[17 * WIDE : 18 * WIDE, :] = after[96:144]
    gx[pl.ds(WIDE, 16, stride=WIDE), :] = west[32:48, :].astype(F32)
    gx[pl.ds(WIDE + 33, 16, stride=WIDE), :] = east[32:48, :].astype(F32)
    slot_l = idx_l[...] + 16 * (idx_l[...] >> 5) + WIDE + 1
    slot_s = column(slot_l).astype(jnp.int32)
    ring_s = column(ring_l[...]).astype(jnp.int32)
    ring_pick = (ring_s == iota((128, EXT), 1)).astype(F32).astype(BF)
    code = dot(ring_pick, gx[0:EXT, :].astype(BF))
    lane = iota((128, C), 1)
    code = jnp.sum(jnp.where(lane == 0, 32.0 * code, jnp.where(lane == 1, code, 0.0)), axis=1, keepdims=True)
    own_lab = column(lab_l[...]).astype(jnp.int32)
    for dx in range(3):
        hx[:, 128 * dx : 128 * dx + 128] = hp[dx : dx + 992, :].astype(BF)
    for part in range(2):
        at = 448 * part
        acc = None
        for dy in range(3):
            term = dot(hx[at + WIDE * dy : at + WIDE * dy + 448, :], cw[384 * dy : 384 * dy + 384, :])
            acc = term if acc is None else acc + term
        s = jax.nn.sigmoid(acc)
        h2[at : at + 448, :] = (acc * s).astype(BF)
        sg2[at : at + 448, :] = s * (1.0 + acc * (1.0 - s))
    own_pick = (slot_s == iota((CAP, EXT), 1)).astype(F32).astype(BF)
    rows = dot(jnp.concatenate([own_pick, ring_pick], axis=0), h2[...]).astype(BF)
    rows_s[...] = rows
    z = dot(rows, hid[...])
    s = jax.nn.sigmoid(z)
    act[...] = (z * s).astype(BF)
    sgz[...] = s * (1.0 + z * (1.0 - s))
    logits = dot(act[...], binw[...])
    peak = jnp.max(logits, axis=1, keepdims=True)
    top = peak + jnp.log(jnp.sum(jnp.exp(logits - peak), axis=1, keepdims=True))
    labs = jnp.concatenate([own_lab, code.astype(jnp.int32) - 1], axis=0)
    hit = labs == iota((SLOTS, BINS), 1)
    live = (labs >= 0).astype(F32)
    picked = jnp.sum(jnp.where(hit, logits, 0.0), axis=1, keepdims=True)
    loss = jnp.sum((live * (top - picked))[:CAP])
    dl[...] = ((jnp.exp(logits - top) - hit.astype(F32)) * live).astype(BF)
    dz[...] = (dot_t(dl[...], binw[...]) * sgz[...]).astype(BF)
    drows = dot_t(dz[...], hid[...])
    hi = drows.astype(BF)
    gscr[:, 0:128] = hi
    gscr[:, 128:256] = (drows - hi.astype(F32)).astype(BF)

    def put(row, value):
        buf[row // STAT, pl.ds(row % STAT, value.shape[0]), :] = value.astype(BF)

    for n in range(4):
        put(7936 + 1024 * n, t_dot(act[0:CAP, :], dl[0:CAP, 128 * n : 128 * n + 128]))
    ghid = t_dot(rows_s[0:CAP, :], dz[0:CAP, :])
    for n in range(8):
        put(6912 + 128 * n, ghid[:, 128 * n : 128 * n + 128])
    lane = iota((1, C), 1)
    stats = jnp.where(lane == 0, loss, jnp.where(lane == 1, jnp.sum(live[:CAP]), 0.0))
    for n in range(2):
        buf[n, STAT : STAT + 16, :] = stat_rows(stats, (16, C)).astype(BF)
        buf[n, STAT + 16 : KEEP, :] = jnp.zeros((KEEP - STAT - 16, C), BF)
    cell = iota((EXT, CAP), 0)
    back = jnp.concatenate(
        [(slot_l == cell).astype(F32), (ring_l[...] == cell[:, :128]).astype(F32)], axis=1
    ).astype(BF)
    both = dot(back, gscr[...])
    gx[0:EXT, :] = (both[:, :128] + both[:, 128:]) * sg2[...]

    g2w[...] = jnp.zeros_like(g2w)
    col = iota((768, C), 0) % WIDE
    own = jnp.where((col >= 1) & (col <= COLS), gx[WIDE : WIDE + 768, :], 0.0).astype(BF)
    for dy in range(3):
        g2w[WIDE * (1 + dy) : WIDE * (1 + dy) + 768, 128 * dy : 128 * dy + 128] = own
    for dx in range(3):
        part = t_dot(hx[0:960, 128 * dx : 128 * dx + 128], g2w[...])
        for dy in range(3):
            put(5760 + 128 * (3 * dy + dx), part[:, 128 * dy : 128 * dy + 128])

    for i in range(ROWS + 2):
        for dx in range(3):
            at = WIDE * i + 2 - dx
            hx[32 * i : 32 * i + 32, 128 * dx : 128 * dx + 128] = gx[at : at + 32, :].astype(BF)
    g1w[...] = jnp.zeros_like(g1w)
    acc = None
    for dy in range(3):
        at = 32 * (2 - dy)
        back = jnp.concatenate(
            [cw[384 * dy + 128 * dx : 384 * dy + 128 * dx + 128, :] for dx in range(3)], axis=1
        )
        term = dot_t(hx[at : at + 512, :], back)
        acc = term if acc is None else acc + term
    g1 = (acc * sg1[...]).astype(BF)
    for dy in range(3):
        g1w[32 * dy : 32 * dy + 512, 128 * dy : 128 * dy + 128] = g1
    for dx in range(3):
        part = t_dot(xc[:, 128 * dx : 128 * dx + 128], g1w[...])
        for dy in range(3):
            put(4608 + 128 * (3 * dy + dx), part[:, 128 * dy : 128 * dy + 128])
    for dx in range(3):
        for side in range(2):
            at = 384 + 512 * dx + 256 * side
            part = t_dot(xc[:, at : at + 256], g1w[...])
            for dy in range(3):
                at = 2304 * side + 256 * (3 * dy + dx)
                put(at, part[:, 128 * dy : 128 * dy + 128])
    keep[...] = buf[core]
    give[...] = buf[1 - core]


def pair_kernel(keep, got, out):
    out[...] = (keep[...].astype(F32) + got[...].astype(F32)).astype(BF)
    sl = slice(STAT, STAT + 16)
    rows = keep[sl, :].astype(F32) + got[sl, :].astype(F32)
    out[sl, :] = stat_rows(jnp.sum(rows, axis=0, keepdims=True), (16, C)).astype(BF)


def spread_kernel(pieces, out, mine):
    acc = pieces[0].astype(F32)
    for i in range(1, PEERS):
        acc += pieces[i].astype(F32)
    mine[...] = acc.astype(BF)
    at = STAT % SHARD

    place = [lax.axis_index(a) for a in PLANE]
    owner = 16 * place[0] + 4 * place[1] + 2 * place[2] + place[3]

    @pl.when(owner == STAT // SHARD)
    def _():
        rows = acc[at : at + 16]
        mine[at : at + 16, :] = stat_rows(jnp.sum(rows, axis=0, keepdims=True), (16, C)).astype(BF)

    for i in range(PEERS):
        out[i] = mine[...]


def finish_kernel(second, part, *refs):
    refs = refs[5:] if second else refs
    if second:
        loss, refs = refs[5], refs[:5] + refs[6:]
    gfine, gctx, gconv, ghid, gbin, vf, vx, vc, vh, vb, sem = refs
    half = lax.axis_index("yh")
    which = lax.axis_index("core")
    which = 1 - which if second else which
    stats = jnp.sum(part[STAT : STAT + 16, :].astype(F32), axis=0, keepdims=True)
    lane = iota((1, C), 1)
    total = jnp.sum(jnp.where(lane == 1, stats, 0.0), axis=1, keepdims=True)
    scale = 1.0 / total
    if second:
        loss[...] = jnp.sum(jnp.where(lane == 0, stats, 0.0), axis=1, keepdims=True) * scale

    def get(row, n):
        at = row % STAT
        return part[at : at + n, :].astype(F32) * scale

    def send(done, view, out):
        c = pltpu.make_async_copy(view, out, sem.at[len(done)])
        c.start()
        done.append(c)

    @pl.when(which == 0)
    def _():
        done = []
        at = pl.multiple_of(half * 2304, 128)
        for n in range(9):
            sl = slice(256 * n, 256 * n + 256)
            vx[sl, :] = part[pl.ds(at + 256 * n, 256), :].astype(F32) * scale
            send(done, vx.at[sl, :], gctx.at[sl, :])
        for n in range(3):
            sl = slice(384 * n, 384 * n + 384)
            vf[sl, :] = get(4608 + 384 * n, 384)
            send(done, vf.at[sl, :], gfine.at[sl, :])
        vc[0:256, :] = get(5760, 256)
        send(done, vc.at[0:256, :], gconv.at[0:256, :])
        for c in done:
            c.wait()

    @pl.when(which == 1)
    def _():
        done = []
        for m in range(8):
            sl = slice(128 * m, 128 * m + 128)
            for n in range(4):
                vb[sl, 128 * n : 128 * n + 128] = get(7936 + 1024 * n + 128 * m, 128)
            send(done, vb.at[sl, :], gbin.at[sl, :])
        for n in range(2):
            sl = slice(256 + 448 * n, 704 + 448 * n)
            vc[sl, :] = get(6016 + 448 * n, 448)
            send(done, vc.at[sl, :], gconv.at[sl, :])
        for m in range(4):
            sl = slice(32 * m, 32 * m + 32)
            for n in range(8):
                vh[sl, 128 * n : 128 * n + 128] = get(6912 + 128 * n + 32 * m, 32)
            send(done, vh.at[sl, :], ghid.at[sl, :])
        for c in done:
            c.wait()


def sds(shape, dtype):
    return jax.ShapeDtypeStruct(shape, dtype)


def edge_cols(fine, ctx):
    return pl.pallas_call(
        edge_cols_kernel,
        out_shape=(sds((32, C), BF),) * 2 + (sds((512, C), BF), sds((64, HALF), BF)),
        in_specs=vmem(2),
        out_specs=tuple(vmem(4)),
        scratch_shapes=[pltpu.VMEM((512, C), F32), pltpu.VMEM((2, 64, C), F32)],
        compiler_params=limit(4),
        cost_estimate=BUSY,
        name="edge_cols",
    )(fine, ctx)


def edge_rows(*args):
    return pl.pallas_call(
        edge_rows_kernel,
        out_shape=(sds((WIDE + 256, C), BF), sds((WIDE, C), BF)),
        in_specs=vmem(4),
        out_specs=tuple(vmem(2)),
        scratch_shapes=[pltpu.VMEM((2 * WIDE, C), F32), pltpu.VMEM((256, C), F32)],
        compiler_params=limit(4),
        cost_estimate=BUSY,
        name="edge_rows",
    )(*args)


def ctx_rows(*args):
    return pl.pallas_call(
        ctx_rows_kernel,
        out_shape=(sds((64, C), BF), sds((64, C), BF), sds((2 * WIDE, C), BF)),
        in_specs=vmem(3),
        out_specs=tuple(vmem(3)),
        compiler_params=limit(4),
        cost_estimate=BUSY,
        name="ctx_rows",
    )(*args)


def first_conv(*args):
    v = pltpu.VMEM
    edge = sds((48, C), BF)
    return pl.pallas_call(
        first_conv_kernel,
        out_shape=(sds((576, 1920), BF), sds((512, C), BF), sds((512, C), F32), edge, edge, sds((64, C), BF)),
        in_specs=vmem(len(args)),
        out_specs=tuple(vmem(6)),
        scratch_shapes=[
            v((18 * WIDE, C), F32),
            v((288, K), BF),
            v((160, K), BF),
            v((512, C), F32),
            v((512, C), F32),
            v((16, C), F32),
            v((16, C), F32),
            pltpu.SMEM((4,), jnp.int32),
        ],
        compiler_params=limit(20),
        cost_estimate=pl.CostEstimate(flops=900_000_000, bytes_accessed=5_000_000, transcendentals=0),
        name="first_conv",
    )(*args)


def h_rows(*args):
    edge = sds((144, C), BF)
    return pl.pallas_call(
        h_rows_kernel,
        out_shape=(sds((ROWS * WIDE, C), BF), edge, edge),
        in_specs=vmem(len(args)),
        out_specs=tuple(vmem(3)),
        scratch_shapes=[pltpu.VMEM((ROWS * WIDE, C), F32), pltpu.VMEM((2 * WIDE, C), F32)],
        compiler_params=limit(6),
        cost_estimate=BUSY,
        name="h_rows",
    )(*args)


def rest(*args):
    v = pltpu.VMEM
    return pl.pallas_call(
        rest_kernel,
        out_shape=(sds((KEEP, C), BF), sds((KEEP, C), BF)),
        in_specs=vmem(len(args)),
        out_specs=tuple(vmem(2)),
        scratch_shapes=[
            v((1000, C), F32),
            v((992, 384), BF),
            v((EXT, C), F32),
            v((EXT, C), BF),
            v((SLOTS, C), BF),
            v((SLOTS, HID), BF),
            v((SLOTS, HID), F32),
            v((SLOTS, BINS), BF),
            v((SLOTS, HID), BF),
            v((SLOTS, 256), BF),
            v((EXT + 8, C), F32),
            v((960, 384), BF),
            v((576, 384), BF),
            v((2, KEEP, C), BF),
            pltpu.SMEM((4,), jnp.int32),
        ],
        compiler_params=limit(28),
        cost_estimate=pl.CostEstimate(flops=3_000_000_000, bytes_accessed=8_000_000, transcendentals=0),
        name="rest",
    )(*args)


def pair_sum(keep, got):
    return pl.pallas_call(
        pair_kernel,
        out_shape=sds((KEEP, C), BF),
        in_specs=vmem(2),
        out_specs=vmem(1)[0],
        compiler_params=limit(8),
        name="pair_sum",
    )(keep, got)


def spread(pieces):
    return pl.pallas_call(
        spread_kernel,
        out_shape=sds((PEERS, SHARD, C), BF),
        in_specs=vmem(1),
        out_specs=vmem(1)[0],
        scratch_shapes=[pltpu.VMEM((SHARD, C), BF)],
        compiler_params=limit(8),
        name="spread",
    )(pieces)


def finish(part, before=None):
    v = pltpu.VMEM
    shapes = [(1152, C), (2304, C), (1152, C), (C, HID), (HID, BINS)]
    second = before is not None
    more = tuple(before) if second else ()
    return pl.pallas_call(
        functools.partial(finish_kernel, second),
        out_shape=tuple(sds(s, F32) for s in shapes) + (sds((1, 1), F32),) * second,
        in_specs=vmem(1) + [ANY] * len(more),
        out_specs=(ANY,) * 5 + tuple(vmem(1)) * second,
        input_output_aliases={1 + n: n for n in range(len(more))},
        scratch_shapes=[v(s, F32) for s in shapes] + [pltpu.SemaphoreType.DMA((14,))],
        compiler_params=limit(16),
        cost_estimate=pl.CostEstimate(flops=800_000, bytes_accessed=5_000_000, transcendentals=0),
        name="finish_other" if second else "finish_own",
    )(part, *more)


def ring_cells():
    cells = [(0, c) for c in range(34)] + [(17, c) for c in range(34)]
    cells += [(r, 0) for r in range(1, 17)] + [(r, 33) for r in range(1, 17)]
    return np.array([WIDE * r + c for r, c in cells] + [-1] * 28, np.int32)


def local(
    fine,
    context,
    interp_rows,
    interp_cols,
    fine_weight,
    ctx_weight,
    conv_weight,
    hidden_weight,
    bin_weight,
    cell_index,
    counts,
    labels,
):
    idx = cell_index.reshape(1, CAP)
    live = jnp.arange(CAP, dtype=jnp.int32)[None, :] < counts
    lab = jnp.where(live, labels.reshape(1, CAP), -1)
    ring = jnp.asarray(ring_cells())

    last, first, fine, context = edge_cols(fine.reshape(512, C), context.reshape(64, HALF))
    west = shift(last, GX, 8, 1)
    east = shift(first, GX, 8, -1)
    mine, edge = edge_rows(fine, context, west, east)
    inner = side_swap(mine)
    outer = outer_swap(edge)
    down, up, rows = ctx_rows(mine, inner, outer)
    north = shift(down, GY, 8, 1)
    south = shift(up, GY, 8, -1)
    xc, h_one, sg1, last, first, digs = first_conv(
        interp_rows.T, interp_cols.T, fine, west, east, mine, inner, rows, north, south,
        fine_weight.reshape(1152, C), ctx_weight.reshape(4608, C), idx, lab,
    )

    west = shift(last, GX, 8, 1)
    east = shift(first, GX, 8, -1)
    wide, inner, outer = h_rows(h_one, digs, west, east)
    inner = side_swap(inner)
    outer = outer_swap(outer)
    keep, give = rest(
        wide, inner, outer, west, east, xc, sg1, idx, ring[None, :], lab,
        conv_weight.reshape(1152, C), hidden_weight, bin_weight,
    )

    flip = [(0, 1), (1, 0)]
    pair = pair_sum(keep, lax.ppermute(give, "core", flip))
    pieces = lax.all_to_all(pair.reshape(PEERS, SHARD, C), PLANE, 0, 0, tiled=True)
    half_sum = lax.all_to_all(spread(pieces), PLANE, 0, 0, tiled=True).reshape(KEEP, C)
    other = lax.ppermute(half_sum, "core", flip)
    outs = finish(half_sum)
    gfine, gctx, gconv, ghid, gbin, loss = finish(other, outs)
    return (
        loss.reshape(()),
        gfine.reshape(3, 3, C, C),
        gctx.reshape(3, 3, HALF, C),
        gconv.reshape(3, 3, C, C),
        ghid,
        gbin,
    )


def solution(mesh):
    devices = np.asarray(mesh.devices).reshape(4, 2, 4, 2, 2)
    split = Mesh(devices, ("x", "core", "z", "yl", "yh"))
    in_specs = (
        P(TALL, GX, None),
        P(GY, GX, "yh"),
        P(),
        P(),
        P(),
        P(),
        P(),
        P(),
        P(),
        P(TALL, GX, None),
        P(TALL, GX),
        P(TALL, GX, None),
    )
    out_specs = (P(), P(), P(None, None, "yh", None), P(), P(), P())
    return jax.shard_map(local, mesh=split, in_specs=in_specs, out_specs=out_specs, check_vma=False)
```

time: 139 us -> 133 us (0.957)
  Pallas kernels: 21.3 us -> 15.1 us
  waiting for transfers between devices: 20 us -> 18.2 us
  blocking collectives: 60.3 us -> 62 us
    ppermute x2, waiting for transfers between devices: 9.19 us -> 3.92 us  [outer_swap(): return lax.ppermute(x, TALL, pairs)]
    ppermute x2, starting transfers between devices: 4.07 us -> 8.27 us  [outer_swap(): return lax.ppermute(x, TALL, pairs)]
    ppermute x6, waiting for transfers between devices: 5.54 us -> 9.39 us  [shift(): return lax.ppermute(x, axis, pairs)]
    ppermute x2, starting transfers between devices: 6.89 us -> 3.45 us  [side_swap(): return lax.ppermute(x, TALL, own)]
    pallas_call x1, Pallas kernels: 9.46 us -> 7.52 us  [rest(): pl.pallas_call(rest_kernel, out_shape=(sds((KEEP, C), BF), sds((KEEP, C),...]
    all_to_all x1, blocking collectives: 33.7 us -> 35.6 us  [local(): lax.all_to_all(pair.reshape(PEERS, SHARD, C), PLANE, 0, 0, tiled=True)]
    pallas_call x2 -> x3, Pallas kernels: 5.56 us -> 3.83 us  [the longest x2 3.83 us: finish(): pl.pallas_call(functools.partial(finish_kernel, second), out_shape=tuple(...]
    ppermute x2, waiting for transfers between devices: 1.84 us -> 0.35 us  [side_swap(): return lax.ppermute(x, TALL, own)]
  transfers between devices with their start and end apart: 12 -> 12, of which waited for: 7 -> 8; matrix products, arithmetic and copies ran while one was open for 0% -> 0% of each run, Pallas kernels for 2% -> 1%
where the time goes in v4:
time: 133 us; the launch traced here: 132 us
  blocking collectives  62 us (47%)
  starting transfers between devices  33.7 us (25%)
  waiting for transfers between devices  18.2 us (14%)
  Pallas kernels  15.1 us (11%)
  local copies, waits for them, and re-layouts  1.71 us (1%)
  between operations  1.69 us (1%)
    all_to_all x1, blocking collectives, local(): lax.all_to_all(pair.reshape(PEERS, SHARD, C), PLANE, 0, 0, tiled=True)  35.6 us
    all_to_all x1, blocking collectives, local(): lax.all_to_all(spread(pieces), PLANE, 0, 0, tiled=True).reshape(KEEP, C)  26.4 us
    ppermute x6, starting transfers between devices, shift(): return lax.ppermute(x, axis, pairs)  18.5 us
    ppermute x6, waiting for transfers between devices, shift(): return lax.ppermute(x, axis, pairs)  9.39 us
    ppermute x2, starting transfers between devices, outer_swap(): return lax.ppermute(x, TALL, pairs)  8.27 us
    pallas_call x1, Pallas kernels, rest(): pl.pallas_call(rest_kernel, out_shape=(sds((KEEP, C), BF), sds((KEEP, C),...  7.52 us
    ppermute x2, waiting for transfers between devices, outer_swap(): return lax.ppermute(x, TALL, pairs)  3.92 us
    pallas_call x2, Pallas kernels, finish(): pl.pallas_call(functools.partial(finish_kernel, second), out_shape=tuple(...  3.83 us
  transfers between devices with their start and end apart: 12, of which 8 were waited for; matrix products, arithmetic and copies ran while one was open for 0% of the time, Pallas kernels for 1%

profile of v4, /device:TPU:1, one launch (start us, length us, event | category | flops | bytes accessed | tf_op | source)
XLA Modules:
  0.0 132.5 jit_solution(14348476854602106469)
XLA Ops:
  0.6 0.9 copy-done.5
  1.5 0.8 copy-done.6
  2.3 4.0 %collective-permute-start = (bf16[32,128]{1,0:T(8,128)(2,1)S(1)}, bf16[32,128]{1,0:T(8,128)(2,1)S(1)}, u32[]{:S(2)}, u32[]{:S(2)}) collective-permute-start(bf16[32,128]{1,0:T(8,128)(2,1)S(1)} %get-tuple-element.38), channel_id=1, source_target_pairs={{0,2},{2,4},{4,6},{6,8},{8,10},{10,12},{12,14},{1,3},{3,5},{5,7},{... | collective-permute-start | bytes 24584 | tf_op jit(solution)/shard_map/ppermute | solution.py:35
  6.4 1.3 collective-permute-start.1
  7.7 3.2 %collective-permute-done.1.east = bf16[32,128]{1,0:T(8,128)(2,1)S(1)} collective-permute-done((bf16[32,128]{1,0:T(8,128)(2,1)S(1)}, bf16[32,128]{1,0:T(8,128)(2,1)S(1)}, u32[]{:S(2)}, u32[]{:S(2)}) %collective-permute-start.1) | collective-permute-done | bytes 8224 | tf_op jit(solution)/shard_map/ppermute | solution.py:35
  10.9 3.0 %collective-permute-start.2 = (bf16[304,128]{1,0:T(8,128)(2,1)S(1)}, bf16[304,128]{1,0:T(8,128)(2,1)S(1)}, u32[]{:S(2)}, u32[]{:S(2)}) collective-permute-start(bf16[304,128]{1,0:T(8,128)(2,1)S(1)} %get-tuple-element.41.mine), channel_id=1, source_target_pairs={{0,1},{1,0},{16,17},{17,16},{32,33},{33,32},{48,49},{49,48},{64,65... | collective-permute-start | bytes 233480 | tf_op jit(solution)/shard_map/ppermute | solution.py:40
  13.9 4.1 %collective-permute-start.3 = (bf16[48,128]{1,0:T(8,128)(2,1)S(1)}, bf16[48,128]{1,0:T(8,128)(2,1)S(1)}, u32[]{:S(2)}, u32[]{:S(2)}) collective-permute-start(bf16[48,128]{1,0:T(8,128)(2,1)S(1)} %get-tuple-element.42), channel_id=1, source_target_pairs={{1,16},{16,1},{17,32},{32,17},{33,48},{48,33},{49,64},{64,49},{65,... | collective-permute-start | bytes 36872 | tf_op jit(solution)/shard_map/ppermute | solution.py:47
  18.7 0.0 copy-start.2
  18.8 1.6 %collective-permute-done.3.outer = bf16[48,128]{1,0:T(8,128)(2,1)S(1)} collective-permute-done((bf16[48,128]{1,0:T(8,128)(2,1)S(1)}, bf16[48,128]{1,0:T(8,128)(2,1)S(1)}, u32[]{:S(2)}, u32[]{:S(2)}) %collective-permute-start.3) | collective-permute-done | bytes 12320 | tf_op jit(solution)/shard_map/ppermute | solution.py:47
  20.4 6.0 %collective-permute-start.4 = (bf16[64,128]{1,0:T(8,128)(2,1)S(1)}, bf16[64,128]{1,0:T(8,128)(2,1)S(1)}, u32[]{:S(2)}, u32[]{:S(2)}) collective-permute-start(bf16[64,128]{1,0:T(8,128)(2,1)S(1)} %get-tuple-element.44), channel_id=1, source_target_pairs={{0,16},{16,32},{32,48},{48,64},{64,80},{80,96},{96,112},{1,17},{17... | collective-permute-start | bytes 49160 | tf_op jit(solution)/shard_map/ppermute | solution.py:35
  26.4 1.9 %collective-permute-start.5 = (bf16[64,128]{1,0:T(8,128)(2,1)S(1)}, bf16[64,128]{1,0:T(8,128)(2,1)S(1)}, u32[]{:S(2)}, u32[]{:S(2)}) collective-permute-start(bf16[64,128]{1,0:T(8,128)(2,1)S(1)} %get-tuple-element.45), channel_id=1, source_target_pairs={{16,0},{32,16},{48,32},{64,48},{80,64},{96,80},{112,96},{17,1},{33... | collective-permute-start | bytes 49160 | tf_op jit(solution)/shard_map/ppermute | solution.py:35
  28.4 3.1 %collective-permute-done.5.south = bf16[64,128]{1,0:T(8,128)(2,1)S(1)} collective-permute-done((bf16[64,128]{1,0:T(8,128)(2,1)S(1)}, bf16[64,128]{1,0:T(8,128)(2,1)S(1)}, u32[]{:S(2)}, u32[]{:S(2)}) %collective-permute-start.5) | collective-permute-done | bytes 16416 | tf_op jit(solution)/shard_map/ppermute | solution.py:35
  31.5 2.8 %first_conv.1 = (bf16[576,1920]{1,0:T(8,128)(2,1)S(1)}, bf16[512,128]{1,0:T(8,128)(2,1)S(1)}, f32[512,128]{1,0:T(8,128)S(1)}, bf16[48,128]{1,0:T(8,128)(2,1)S(1)...) custom-call(bf16[10,34]{1,0:T(8,128)(2,1)S(1)} %bitcast.26, bf16[10,34]{1,0:T(8,128)(2,1)S(1)} %bitcast.27, ...), custom_call_target="tpu_custom_call" | custom-call | flops 900000000 | bytes 5000000 | tf_op jit(solution)/shard_map/first_conv/pallas_call | solution.py:504
  34.3 3.9 %collective-permute-start.6 = (bf16[48,128]{1,0:T(8,128)(2,1)S(1)}, bf16[48,128]{1,0:T(8,128)(2,1)S(1)}, u32[]{:S(2)}, u32[]{:S(2)}) collective-permute-start(bf16[48,128]{1,0:T(8,128)(2,1)S(1)} %get-tuple-element.48), channel_id=1, source_target_pairs={{0,2},{2,4},{4,6},{6,8},{8,10},{10,12},{12,14},{1,3},{3,5},{5,7},{... | collective-permute-start | bytes 36872 | tf_op jit(solution)/shard_map/ppermute | solution.py:35
  38.2 1.3 collective-permute-start.7
  39.5 3.1 %collective-permute-done.7.east = bf16[48,128]{1,0:T(8,128)(2,1)S(1)} collective-permute-done((bf16[48,128]{1,0:T(8,128)(2,1)S(1)}, bf16[48,128]{1,0:T(8,128)(2,1)S(1)}, u32[]{:S(2)}, u32[]{:S(2)}) %collective-permute-start.7) | collective-permute-done | bytes 12320 | tf_op jit(solution)/shard_map/ppermute | solution.py:35
  42.7 0.1 h_rows.1
  42.8 0.5 collective-permute-start.8
  43.2 4.1 %collective-permute-start.9 = (bf16[144,128]{1,0:T(8,128)(2,1)S(1)}, bf16[144,128]{1,0:T(8,128)(2,1)S(1)}, u32[]{:S(2)}, u32[]{:S(2)}) collective-permute-start(bf16[144,128]{1,0:T(8,128)(2,1)S(1)} %get-tuple-element.52), channel_id=1, source_target_pairs={{1,16},{16,1},{17,32},{32,17},{33,48},{48,33},{49,64},{64,49},{65,... | collective-permute-start | bytes 110600 | tf_op jit(solution)/shard_map/ppermute | solution.py:47
  47.3 0.3 collective-permute-done.8.inner
  47.7 2.3 %collective-permute-done.9.outer = bf16[144,128]{1,0:T(8,128)(2,1)S(1)} collective-permute-done((bf16[144,128]{1,0:T(8,128)(2,1)S(1)}, bf16[144,128]{1,0:T(8,128)(2,1)S(1)}, u32[]{:S(2)}, u32[]{:S(2)}) %collective-permute-start.9) | collective-permute-done | bytes 36896 | tf_op jit(solution)/shard_map/ppermute | solution.py:47
  50.0 7.5 %rest.1 = (bf16[6144,128]{1,0:T(8,128)(2,1)S(1)}, bf16[6144,128]{1,0:T(8,128)(2,1)S(1)}) custom-call(bf16[768,128]{1,0:T(8,128)(2,1)S(1)} %get-tuple-element.50.hw, bf16[144,128]{1,0:T(8,128)(2,1)S(1)} %collective-permute-done.8.inner, bf16[144,128]{1,0:T(8,128)(2,1)S(1)} %collective-permute-done.9.outer, bf16[48,128]{1,0:T(8,128)(2,1)S(1)} %collective-permute-done.6.west, ...), custom_call_target="tpu_custom_call" | custom-call | flops 3000000000 | bytes 8000000 | tf_op jit(solution)/shard_map/rest/pallas_call | solution.py:541
  57.5 0.1 collective-permute-start.10
  57.6 3.4 %collective-permute-done.10.got = bf16[6144,128]{1,0:T(8,128)(2,1)S(1)} collective-permute-done((bf16[6144,128]{1,0:T(8,128)(2,1)S(1)}, bf16[6144,128]{1,0:T(8,128)(2,1)S(1)}, u32[]{:S(2)}, u32[]{:S(2)}) %collective-permute-start.10) | collective-permute-done | bytes 1572896 | tf_op jit(solution)/shard_map/ppermute | solution.py:660
  61.0 0.4 pair_sum.1
  61.4 35.6 %all_to_all.10.pieces = bf16[64,96,128]{2,1,0:T(8,128)(2,1)S(1)} all-to-all(bf16[64,96,128]{2,1,0:T(8,128)(2,1)S(1)} %bitcast.20), channel_id=1, replica_groups=mesh['x'=4,'core'=2,'z'=4,'yl'=2,'yh'=2] {'x','z','yl','yh'}, dimensions={0} | all-to-all | bytes 3145728 | tf_op jit(solution)/shard_map/all_to_all | solution.py:661
  97.0 0.4 spread.1
  97.5 26.4 %all_to_all.11 = bf16[64,96,128]{2,1,0:T(8,128)(2,1)S(1)} all-to-all(bf16[64,96,128]{2,1,0:T(8,128)(2,1)S(1)} %spread.1), channel_id=1, replica_groups=mesh['x'=4,'core'=2,'z'=4,'yl'=2,'yh'=2] {'x','z','yl','yh'}, dimensions={0} | all-to-all | bytes 3145728 | tf_op jit(solution)/shard_map/all_to_all | solution.py:662
  123.9 3.4 %collective-permute-start.11 = (bf16[6144,128]{1,0:T(8,128)(2,1)S(1)}, bf16[6144,128]{1,0:T(8,128)(2,1)S(1)}, u32[]{:S(2)}, u32[]{:S(2)}) collective-permute-start(bf16[6144,128]{1,0:T(8,128)(2,1)S(1)} %bitcast.18), channel_id=1, source_target_pairs={{0,16},{16,0},{1,17},{17,1},{2,18},{18,2},{3,19},{19,3},{4,20},{20... | collective-permute-start | bytes 4718600 | tf_op jit(solution)/shard_map/ppermute | solution.py:663
  127.3 1.9 %finish_own.1 = (f32[1152,128]{1,0:T(8,128)}, f32[2304,128]{1,0:T(8,128)}, f32[1152,128]{1,0:T(8,128)}, f32[128,1024]{1,0:T(8,128)}, f32[1024,512]{1,0:T(8,128)}) custom-call(bf16[6144,128]{1,0:T(8,128)(2,1)S(1)} %bitcast.19), custom_call_target="tpu_custom_call" | custom-call | flops 800000 | bytes 5000000 | tf_op jit(solution)/shard_map/finish_own/pallas_call | solution.py:597
  129.2 1.2 collective-permute-done.11.part
  130.3 2.0 %finish_other.1 = (f32[1152,128]{1,0:T(8,128)}, f32[2304,128]{1,0:T(8,128)}, f32[1152,128]{1,0:T(8,128)}, f32[128,1024]{1,0:T(8,128)}, f32[1024,512]{1,0:T(8,128)}, /*index=5*/f32[1,1]{1,0:T(1,128)}) custom-call(bf16[6144,128]{1,0:T(8,128)(2,1)S(1)} %collective-permute-done.11.part, ...), custom_call_target="tpu_custom_call", output_to_operand_aliasing={{0}: (1, {}), {1}: (2, {}), {2}: (3, {}), {3}: (4, {}), {4}... | custom-call | flops 800000 | bytes 5000000 | tf_op jit(solution)/shard_map/finish_other/pallas_call | solution.py:597
  (29 shorter events, 0.1 us)
Async XLA Ops:
  0.6 0.9 copy-start.5
  1.5 0.8 copy-start.6
  2.3 5.3 %collective-permute-start = (bf16[32,128]{1,0:T(8,128)(2,1)S(1)}, bf16[32,128]{1,0:T(8,128)(2,1)S(1)}, u32[]{:S(2)}, u32[]{:S(2)}) collective-permute-start(bf16[32,128]{1,0:T(8,128)(2,1)S(1)} %get-tuple-element.38), channel_id=1, source_target_pairs={{0,2},{2,4},{4,6},{6,8},{8,10},{10,12},{12,14},{1,3},{3,5},{5,7},{... | collective-permute-start | bytes 24584 | tf_op jit(solution)/shard_map/ppermute | solution.py:35
  6.4 4.5 %collective-permute-start.1 = (bf16[32,128]{1,0:T(8,128)(2,1)S(1)}, bf16[32,128]{1,0:T(8,128)(2,1)S(1)}, u32[]{:S(2)}, u32[]{:S(2)}) collective-permute-start(bf16[32,128]{1,0:T(8,128)(2,1)S(1)} %get-tuple-element.39), channel_id=1, source_target_pairs={{2,0},{4,2},{6,4},{8,6},{10,8},{12,10},{14,12},{3,1},{5,3},{7,5},{... | collective-permute-start | bytes 24584 | tf_op jit(solution)/shard_map/ppermute | solution.py:35
  10.9 9.5 %collective-permute-start.2 = (bf16[304,128]{1,0:T(8,128)(2,1)S(1)}, bf16[304,128]{1,0:T(8,128)(2,1)S(1)}, u32[]{:S(2)}, u32[]{:S(2)}) collective-permute-start(bf16[304,128]{1,0:T(8,128)(2,1)S(1)} %get-tuple-element.41.mine), channel_id=1, source_target_pairs={{0,1},{1,0},{16,17},{17,16},{32,33},{33,32},{48,49},{49,48},{64,65... | collective-permute-start | bytes 233480 | tf_op jit(solution)/shard_map/ppermute | solution.py:40
  13.9 6.5 %collective-permute-start.3 = (bf16[48,128]{1,0:T(8,128)(2,1)S(1)}, bf16[48,128]{1,0:T(8,128)(2,1)S(1)}, u32[]{:S(2)}, u32[]{:S(2)}) collective-permute-start(bf16[48,128]{1,0:T(8,128)(2,1)S(1)} %get-tuple-element.42), channel_id=1, source_target_pairs={{1,16},{16,1},{17,32},{32,17},{33,48},{48,33},{49,64},{64,49},{65,... | collective-permute-start | bytes 36872 | tf_op jit(solution)/shard_map/ppermute | solution.py:47
  18.7 9.7 %copy-start.11 = (s32[1,1,256]{2,1,0:T(1,128)S(1)}, s32[1,1,256]{2,1,0:T(1,128)}, u32[]{:S(2)}) copy-start(s32[1,1,256]{2,1,0:T(1,128)} %param.24) | copy-start | bytes 3076
  18.7 12.8 %copy-start = (bf16[3,3,512,128]{3,2,1,0:T(8,128)(2,1)S(1)}, bf16[3,3,512,128]{3,2,1,0:T(8,128)(2,1)}, u32[]{:S(2)}) copy-start(bf16[3,3,512,128]{3,2,1,0:T(8,128)(2,1)} %param.18) | copy-start | bytes 3538948
  18.7 12.8 %copy-start.2 = (bf16[3,3,128,128]{3,2,1,0:T(8,128)(2,1)S(1)}, bf16[3,3,128,128]{3,2,1,0:T(8,128)(2,1)}, u32[]{:S(2)}) copy-start(bf16[3,3,128,128]{3,2,1,0:T(8,128)(2,1)} %param.17) | copy-start | bytes 884740
  18.7 12.8 %copy-start.7 = (bf16[34,10]{0,1:T(8,128)(2,1)S(1)}, bf16[34,10]{0,1:T(8,128)(2,1)}, u32[]{:S(2)}) copy-start(bf16[34,10]{0,1:T(8,128)(2,1)} %param.15) | copy-start | bytes 2044
  18.7 12.8 %copy-start.8 = (bf16[34,10]{0,1:T(8,128)(2,1)S(1)}, bf16[34,10]{0,1:T(8,128)(2,1)}, u32[]{:S(2)}) copy-start(bf16[34,10]{0,1:T(8,128)(2,1)} %param.16) | copy-start | bytes 2044
  18.7 12.8 %copy-start.9 = (s32[1,1,256]{2,1,0:T(1,128)S(1)}, s32[1,1,256]{2,1,0:T(1,128)}, u32[]{:S(2)}) copy-start(s32[1,1,256]{2,1,0:T(1,128)} %param.22) | copy-start | bytes 3076
  20.4 8.0 %collective-permute-start.4 = (bf16[64,128]{1,0:T(8,128)(2,1)S(1)}, bf16[64,128]{1,0:T(8,128)(2,1)S(1)}, u32[]{:S(2)}, u32[]{:S(2)}) collective-permute-start(bf16[64,128]{1,0:T(8,128)(2,1)S(1)} %get-tuple-element.44), channel_id=1, source_target_pairs={{0,16},{16,32},{32,48},{48,64},{64,80},{80,96},{96,112},{1,17},{17... | collective-permute-start | bytes 49160 | tf_op jit(solution)/shard_map/ppermute | solution.py:35
  26.4 5.1 %collective-permute-start.5 = (bf16[64,128]{1,0:T(8,128)(2,1)S(1)}, bf16[64,128]{1,0:T(8,128)(2,1)S(1)}, u32[]{:S(2)}, u32[]{:S(2)}) collective-permute-start(bf16[64,128]{1,0:T(8,128)(2,1)S(1)} %get-tuple-element.45), channel_id=1, source_target_pairs={{16,0},{32,16},{48,32},{64,48},{80,64},{96,80},{112,96},{17,1},{33... | collective-permute-start | bytes 49160 | tf_op jit(solution)/shard_map/ppermute | solution.py:35
  34.3 5.2 %collective-permute-start.6 = (bf16[48,128]{1,0:T(8,128)(2,1)S(1)}, bf16[48,128]{1,0:T(8,128)(2,1)S(1)}, u32[]{:S(2)}, u32[]{:S(2)}) collective-permute-start(bf16[48,128]{1,0:T(8,128)(2,1)S(1)} %get-tuple-element.48), channel_id=1, source_target_pairs={{0,2},{2,4},{4,6},{6,8},{8,10},{10,12},{12,14},{1,3},{3,5},{5,7},{... | collective-permute-start | bytes 36872 | tf_op jit(solution)/shard_map/ppermute | solution.py:35
  38.2 4.4 %collective-permute-start.7 = (bf16[48,128]{1,0:T(8,128)(2,1)S(1)}, bf16[48,128]{1,0:T(8,128)(2,1)S(1)}, u32[]{:S(2)}, u32[]{:S(2)}) collective-permute-start(bf16[48,128]{1,0:T(8,128)(2,1)S(1)} %get-tuple-element.49), channel_id=1, source_target_pairs={{2,0},{4,2},{6,4},{8,6},{10,8},{12,10},{14,12},{3,1},{5,3},{7,5},{... | collective-permute-start | bytes 36872 | tf_op jit(solution)/shard_map/ppermute | solution.py:35
  42.7 7.3 %copy-start.1 = (bf16[1024,512]{1,0:T(8,128)(2,1)S(1)}, bf16[1024,512]{1,0:T(8,128)(2,1)}, u32[]{:S(2)}) copy-start(bf16[1024,512]{1,0:T(8,128)(2,1)} %binw.1) | copy-start | bytes 3145732
  42.7 7.3 %copy-start.3 = (bf16[3,3,128,128]{3,2,1,0:T(8,128)(2,1)S(1)}, bf16[3,3,128,128]{3,2,1,0:T(8,128)(2,1)}, u32[]{:S(2)}) copy-start(bf16[3,3,128,128]{3,2,1,0:T(8,128)(2,1)} %param.19) | copy-start | bytes 884740
  42.7 7.3 %copy-start.4 = (bf16[128,1024]{1,0:T(8,128)(2,1)S(1)}, bf16[128,1024]{1,0:T(8,128)(2,1)}, u32[]{:S(2)}) copy-start(bf16[128,1024]{1,0:T(8,128)(2,1)} %hid.1) | copy-start | bytes 786436
  42.7 7.3 %copy-start.10 = (s32[1,128]{1,0:T(1,128)S(1)}, s32[1,128]{1,0:T(1,128)}, u32[]{:S(2)}) copy-start(s32[1,128]{1,0:T(1,128)} %constant.8.ring_l) | copy-start | bytes 1540
  42.8 4.9 %collective-permute-start.8 = (bf16[144,128]{1,0:T(8,128)(2,1)S(1)}, bf16[144,128]{1,0:T(8,128)(2,1)S(1)}, u32[]{:S(2)}, u32[]{:S(2)}) collective-permute-start(bf16[144,128]{1,0:T(8,128)(2,1)S(1)} %get-tuple-element.51), channel_id=1, source_target_pairs={{0,1},{1,0},{16,17},{17,16},{32,33},{33,32},{48,49},{49,48},{64,65... | collective-permute-start | bytes 110600 | tf_op jit(solution)/shard_map/ppermute | solution.py:40
  43.2 6.8 %collective-permute-start.9 = (bf16[144,128]{1,0:T(8,128)(2,1)S(1)}, bf16[144,128]{1,0:T(8,128)(2,1)S(1)}, u32[]{:S(2)}, u32[]{:S(2)}) collective-permute-start(bf16[144,128]{1,0:T(8,128)(2,1)S(1)} %get-tuple-element.52), channel_id=1, source_target_pairs={{1,16},{16,1},{17,32},{32,17},{33,48},{48,33},{49,64},{64,49},{65,... | collective-permute-start | bytes 110600 | tf_op jit(solution)/shard_map/ppermute | solution.py:47
  57.5 3.5 %collective-permute-start.10 = (bf16[6144,128]{1,0:T(8,128)(2,1)S(1)}, bf16[6144,128]{1,0:T(8,128)(2,1)S(1)}, u32[]{:S(2)}, u32[]{:S(2)}) collective-permute-start(bf16[6144,128]{1,0:T(8,128)(2,1)S(1)} %get-tuple-element.56), channel_id=1, source_target_pairs={{0,16},{16,0},{1,17},{17,1},{2,18},{18,2},{3,19},{19,3},{4,20},{20... | collective-permute-start | bytes 4718600 | tf_op jit(solution)/shard_map/ppermute | solution.py:660
  123.9 6.4 %collective-permute-start.11 = (bf16[6144,128]{1,0:T(8,128)(2,1)S(1)}, bf16[6144,128]{1,0:T(8,128)(2,1)S(1)}, u32[]{:S(2)}, u32[]{:S(2)}) collective-permute-start(bf16[6144,128]{1,0:T(8,128)(2,1)S(1)} %bitcast.18), channel_id=1, source_target_pairs={{0,16},{16,0},{1,17},{17,1},{2,18},{18,2},{3,19},{19,3},{4,20},{20... | collective-permute-start | bytes 4718600 | tf_op jit(solution)/shard_map/ppermute | solution.py:663

commit v5 on v4

--- a/solution.py
+++ b/solution.py
@@ -48,6 +48,7 @@
 
 
 WIDE = 48
+CTX = 2 * WIDE
 EXT = 896
 SLOTS = 384
 KEEP = PEERS * SHARD
@@ -110,8 +111,7 @@
         out[16:32, :] = jnp.concatenate(sides, axis=0).astype(BF)
 
 
-def edge_rows_kernel(fine, ctx, west, east, inner, outer, rows, xs):
-    lower = lax.axis_index("yh") == 1
+def edge_rows_kernel(fine, ctx, west, east, inner, rows, xs):
     rows[...] = jnp.zeros_like(rows)
     w, e = west[...].astype(F32), east[...].astype(F32)
     for n, r in ((0, 0), (1, ROWS - 1)):
@@ -119,9 +119,7 @@
         rows[at + 1 : at + 33, :] = fine[COLS * r : COLS * r + COLS, :].astype(F32)
         rows[at : at + 1, :] = w[r : r + 1, :]
         rows[at + 33 : at + 34, :] = e[r : r + 1, :]
-    top, bottom = rows[0:WIDE, :].astype(BF), rows[WIDE : 2 * WIDE, :].astype(BF)
-    inner[0:WIDE, :] = jnp.where(lower, top, bottom)
-    outer[...] = jnp.where(lower, bottom, top)
+    inner[0:CTX, :] = rows[...].astype(BF)
     xs[...] = jnp.zeros_like(xs)
     for side in range(2):
         base = 128 * side
@@ -130,17 +128,18 @@
             xs[at + 1 : at + 9, :] = ctx[8 * a : 8 * a + 8, base : base + 128].astype(F32)
         xs[pl.ds(base, 8, stride=16), :] = w[16 + 8 * side : 24 + 8 * side, :]
         xs[pl.ds(base + 9, 8, stride=16), :] = e[16 + 8 * side : 24 + 8 * side, :]
-    inner[WIDE:, :] = xs[...].astype(BF)
-
-
-def ctx_rows_kernel(mine, inner, outer, down, up, rows):
+    inner[CTX:, :] = xs[...].astype(BF)
+
+
+def ctx_rows_kernel(mine, inner, down, up):
+    lower = lax.axis_index("yh") == 1
     for n, got in enumerate((mine, inner)):
         for side in range(2):
-            at, to = WIDE + 128 * side, 32 * n + 16 * side
+            at, to = CTX + 128 * side, 32 * n + 16 * side
             up[to : to + 16, :] = got[at : at + 16, :]
             down[to : to + 16, :] = got[at + 112 : at + 128, :]
-    rows[0:WIDE, :] = inner[0:WIDE, :]
-    rows[WIDE : 2 * WIDE, :] = outer[...]
+    up[64:112, :] = jnp.where(lower, inner[0:WIDE, :], mine[0:WIDE, :])
+    down[64:112, :] = jnp.where(lower, mine[WIDE:CTX, :], inner[WIDE:CTX, :])
 
 
 def column(row):
@@ -150,7 +149,7 @@
 
 
 def first_conv_kernel(
-    rows_in, cols_in, fine, west, east, mine, inner, rows, north, south, w_fine, w_ctx, idx_l, lab_l,
+    rows_in, cols_in, fine, west, east, mine, inner, north, south, w_fine, w_ctx, idx_l, lab_l,
     xc, h1, sg, last, first, digs,
     fscr, mid, block, hscr, dscr, rmat, cmat, spot,
 ):
@@ -164,9 +163,10 @@
         fscr[at : at + 32, :] = fine[32 * i : 32 * i + 32, :].astype(F32)
     fscr[pl.ds(WIDE, 16, stride=WIDE), :] = west[0:16, :].astype(F32)
     fscr[pl.ds(WIDE + 33, 16, stride=WIDE), :] = east[0:16, :].astype(F32)
-    a, b = rows[0:WIDE, :].astype(F32), rows[WIDE : 2 * WIDE, :].astype(F32)
-    fscr[0:WIDE, :] = jnp.where(lower, a, b)
-    fscr[17 * WIDE : 18 * WIDE, :] = jnp.where(lower, b, a)
+    above = jnp.where(lower, inner[WIDE:CTX, :], north[64:112, :])
+    below = jnp.where(lower, south[64:112, :], inner[0:WIDE, :])
+    fscr[0:WIDE, :] = above.astype(F32)
+    fscr[17 * WIDE : 18 * WIDE, :] = below.astype(F32)
     for i in range(ROWS + 2):
         for dx in range(3):
             at = WIDE * i + dx
@@ -183,7 +183,7 @@
         for n, lanes, got in ((0, own, mine), (32, other, inner)):
             sl = slice(n + 16 * side, n + 16 * side + 16)
             block[0:16, lanes] = north[sl, :]
-            block[16:144, lanes] = got[WIDE + 128 * side : WIDE + 128 * side + 128, :]
+            block[16:144, lanes] = got[CTX + 128 * side : CTX + 128 * side + 128, :]
             block[144:160, lanes] = south[sl, :]
     pick = (iota((288, C), 0) >> 4) + 16 * half == iota((288, C), 1)
     left = dot_t(pick.astype(F32).astype(BF), rmat[...].astype(BF)).astype(BF)
@@ -476,9 +476,9 @@
 def edge_rows(*args):
     return pl.pallas_call(
         edge_rows_kernel,
-        out_shape=(sds((WIDE + 256, C), BF), sds((WIDE, C), BF)),
+        out_shape=sds((CTX + 256, C), BF),
         in_specs=vmem(4),
-        out_specs=tuple(vmem(2)),
+        out_specs=vmem(1)[0],
         scratch_shapes=[pltpu.VMEM((2 * WIDE, C), F32), pltpu.VMEM((256, C), F32)],
         compiler_params=limit(4),
         cost_estimate=BUSY,
@@ -489,9 +489,9 @@
 def ctx_rows(*args):
     return pl.pallas_call(
         ctx_rows_kernel,
-        out_shape=(sds((64, C), BF), sds((64, C), BF), sds((2 * WIDE, C), BF)),
-        in_specs=vmem(3),
-        out_specs=tuple(vmem(3)),
+        out_shape=(sds((112, C), BF), sds((112, C), BF)),
+        in_specs=vmem(2),
+        out_specs=tuple(vmem(2)),
         compiler_params=limit(4),
         cost_estimate=BUSY,
         name="ctx_rows",
@@ -635,14 +635,13 @@
     last, first, fine, context = edge_cols(fine.reshape(512, C), context.reshape(64, HALF))
     west = shift(last, GX, 8, 1)
     east = shift(first, GX, 8, -1)
-    mine, edge = edge_rows(fine, context, west, east)
+    mine = edge_rows(fine, context, west, east)
     inner = side_swap(mine)
-    outer = outer_swap(edge)
-    down, up, rows = ctx_rows(mine, inner, outer)
+    down, up = ctx_rows(mine, inner)
     north = shift(down, GY, 8, 1)
     south = shift(up, GY, 8, -1)
     xc, h_one, sg1, last, first, digs = first_conv(
-        interp_rows.T, interp_cols.T, fine, west, east, mine, inner, rows, north, south,
+        interp_rows.T, interp_cols.T, fine, west, east, mine, inner, north, south,
         fine_weight.reshape(1152, C), ctx_weight.reshape(4608, C), idx, lab,
     )
 

time: 133 us -> 129 us (0.970)
  starting transfers between devices: 33.7 us -> 30.4 us
  blocking collectives: 62 us -> 59.1 us
  waiting for transfers between devices: 18.2 us -> 20.2 us
    ppermute x2 -> x1, starting transfers between devices: 8.27 us -> 1.91 us  [outer_swap(): return lax.ppermute(x, TALL, pairs)]
    all_to_all x1, blocking collectives: 35.6 us -> 32.5 us  [local(): lax.all_to_all(pair.reshape(PEERS, SHARD, C), PLANE, 0, 0, tiled=True)]
    ppermute x2, starting transfers between devices: 3.45 us -> 5.99 us  [side_swap(): return lax.ppermute(x, TALL, own)]
    ppermute x2 -> x1, waiting for transfers between devices: 3.92 us -> 4.84 us  [outer_swap(): return lax.ppermute(x, TALL, pairs)]
  transfers between devices with their start and end apart: 12 -> 11, of which waited for: 8 -> 7; matrix products, arithmetic and copies ran while one was open for 0% -> 0% of each run, Pallas kernels for 1% -> 1%
where the time goes in v5:
time: 129 us; the launch traced here: 128 us
  blocking collectives  59.1 us (46%)
  starting transfers between devices  30.4 us (24%)
  waiting for transfers between devices  20.2 us (16%)
  Pallas kernels  15.2 us (12%)
  local copies, waits for them, and re-layouts  1.71 us (1%)
  between operations  1.53 us (1%)
    all_to_all x1, blocking collectives, local(): lax.all_to_all(pair.reshape(PEERS, SHARD, C), PLANE, 0, 0, tiled=True)  32.5 us
    all_to_all x1, blocking collectives, local(): lax.all_to_all(spread(pieces), PLANE, 0, 0, tiled=True).reshape(KEEP, C)  26.6 us
    ppermute x6, starting transfers between devices, shift(): return lax.ppermute(x, axis, pairs)  19 us
    ppermute x6, waiting for transfers between devices, shift(): return lax.ppermute(x, axis, pairs)  9.52 us
    pallas_call x1, Pallas kernels, rest(): pl.pallas_call(rest_kernel, out_shape=(sds((KEEP, C), BF), sds((KEEP, C),...  7.52 us
    ppermute x2, starting transfers between devices, side_swap(): return lax.ppermute(x, TALL, own)  5.99 us
    ppermute x1, waiting for transfers between devices, outer_swap(): return lax.ppermute(x, TALL, pairs)  4.84 us
    pallas_call x2, Pallas kernels, finish(): pl.pallas_call(functools.partial(finish_kernel, second), out_shape=tuple(...  3.83 us
  transfers between devices with their start and end apart: 11, of which 7 were waited for; matrix products, arithmetic and copies ran while one was open for 0% of the time, Pallas kernels for 1%

profile of v5, /device:TPU:1, one launch (start us, length us, event | category | flops | bytes accessed | tf_op | source)
XLA Modules:
  0.0 128.1 jit_solution(8896196949311818645)
XLA Ops:
  0.6 0.9 copy-done.5
  1.5 0.8 copy-done.6
  2.3 4.0 %collective-permute-start = (bf16[32,128]{1,0:T(8,128)(2,1)S(1)}, bf16[32,128]{1,0:T(8,128)(2,1)S(1)}, u32[]{:S(2)}, u32[]{:S(2)}) collective-permute-start(bf16[32,128]{1,0:T(8,128)(2,1)S(1)} %get-tuple-element.35), channel_id=1, source_target_pairs={{0,2},{2,4},{4,6},{6,8},{8,10},{10,12},{12,14},{1,3},{3,5},{5,7},{... | collective-permute-start | bytes 24584 | tf_op jit(solution)/shard_map/ppermute | solution.py:35
  6.4 1.3 %collective-permute-start.1 = (bf16[32,128]{1,0:T(8,128)(2,1)S(1)}, bf16[32,128]{1,0:T(8,128)(2,1)S(1)}, u32[]{:S(2)}, u32[]{:S(2)}) collective-permute-start(bf16[32,128]{1,0:T(8,128)(2,1)S(1)} %get-tuple-element.36), channel_id=1, source_target_pairs={{2,0},{4,2},{6,4},{8,6},{10,8},{12,10},{14,12},{3,1},{5,3},{7,5},{... | collective-permute-start | bytes 24584 | tf_op jit(solution)/shard_map/ppermute | solution.py:35
  7.7 3.2 %collective-permute-done.1.east = bf16[32,128]{1,0:T(8,128)(2,1)S(1)} collective-permute-done((bf16[32,128]{1,0:T(8,128)(2,1)S(1)}, bf16[32,128]{1,0:T(8,128)(2,1)S(1)}, u32[]{:S(2)}, u32[]{:S(2)}) %collective-permute-start.1) | collective-permute-done | bytes 8224 | tf_op jit(solution)/shard_map/ppermute | solution.py:35
  10.9 3.0 %collective-permute-start.2 = (bf16[352,128]{1,0:T(8,128)(2,1)S(1)}, bf16[352,128]{1,0:T(8,128)(2,1)S(1)}, u32[]{:S(2)}, u32[]{:S(2)}) collective-permute-start(bf16[352,128]{1,0:T(8,128)(2,1)S(1)} %edge_rows.1.mine), channel_id=1, source_target_pairs={{0,1},{1,0},{16,17},{17,16},{32,33},{33,32},{48,49},{49,48},{64,65... | collective-permute-start | bytes 270344 | tf_op jit(solution)/shard_map/ppermute | solution.py:40
  14.5 0.0 copy-start.11
  14.6 0.0 copy-start.2
  14.6 0.0 copy-start.7
  14.6 1.2 collective-permute-done.2.inner
  15.9 6.2 %collective-permute-start.3 = (bf16[112,128]{1,0:T(8,128)(2,1)S(1)}, bf16[112,128]{1,0:T(8,128)(2,1)S(1)}, u32[]{:S(2)}, u32[]{:S(2)}) collective-permute-start(bf16[112,128]{1,0:T(8,128)(2,1)S(1)} %get-tuple-element.38), channel_id=1, source_target_pairs={{0,16},{16,32},{32,48},{48,64},{64,80},{80,96},{96,112},{1,17},{17... | collective-permute-start | bytes 86024 | tf_op jit(solution)/shard_map/ppermute | solution.py:35
  22.1 1.9 %collective-permute-start.4 = (bf16[112,128]{1,0:T(8,128)(2,1)S(1)}, bf16[112,128]{1,0:T(8,128)(2,1)S(1)}, u32[]{:S(2)}, u32[]{:S(2)}) collective-permute-start(bf16[112,128]{1,0:T(8,128)(2,1)S(1)} %get-tuple-element.39), channel_id=1, source_target_pairs={{16,0},{32,16},{48,32},{64,48},{80,64},{96,80},{112,96},{17,1},{33... | collective-permute-start | bytes 86024 | tf_op jit(solution)/shard_map/ppermute | solution.py:35
  24.0 3.2 %collective-permute-done.4.south = bf16[112,128]{1,0:T(8,128)(2,1)S(1)} collective-permute-done((bf16[112,128]{1,0:T(8,128)(2,1)S(1)}, bf16[112,128]{1,0:T(8,128)(2,1)S(1)}, u32[]{:S(2)}, u32[]{:S(2)}) %collective-permute-start.4) | collective-permute-done | bytes 28704 | tf_op jit(solution)/shard_map/ppermute | solution.py:35
  27.3 2.8 %first_conv.1 = (bf16[576,1920]{1,0:T(8,128)(2,1)S(1)}, bf16[512,128]{1,0:T(8,128)(2,1)S(1)}, f32[512,128]{1,0:T(8,128)S(1)}, bf16[48,128]{1,0:T(8,128)(2,1)S(1)...) custom-call(bf16[10,34]{1,0:T(8,128)(2,1)S(1)} %bitcast.26, bf16[10,34]{1,0:T(8,128)(2,1)S(1)} %bitcast.27, ...), custom_call_target="tpu_custom_call" | custom-call | flops 900000000 | bytes 5000000 | tf_op jit(solution)/shard_map/first_conv/pallas_call | solution.py:504
  30.1 4.3 %collective-permute-start.5 = (bf16[48,128]{1,0:T(8,128)(2,1)S(1)}, bf16[48,128]{1,0:T(8,128)(2,1)S(1)}, u32[]{:S(2)}, u32[]{:S(2)}) collective-permute-start(bf16[48,128]{1,0:T(8,128)(2,1)S(1)} %get-tuple-element.42), channel_id=1, source_target_pairs={{0,2},{2,4},{4,6},{6,8},{8,10},{10,12},{12,14},{1,3},{3,5},{5,7},{... | collective-permute-start | bytes 36872 | tf_op jit(solution)/shard_map/ppermute | solution.py:35
  34.4 1.3 %collective-permute-start.6 = (bf16[48,128]{1,0:T(8,128)(2,1)S(1)}, bf16[48,128]{1,0:T(8,128)(2,1)S(1)}, u32[]{:S(2)}, u32[]{:S(2)}) collective-permute-start(bf16[48,128]{1,0:T(8,128)(2,1)S(1)} %get-tuple-element.43), channel_id=1, source_target_pairs={{2,0},{4,2},{6,4},{8,6},{10,8},{12,10},{14,12},{3,1},{5,3},{7,5},{... | collective-permute-start | bytes 36872 | tf_op jit(solution)/shard_map/ppermute | solution.py:35
  35.7 3.1 %collective-permute-done.6.east = bf16[48,128]{1,0:T(8,128)(2,1)S(1)} collective-permute-done((bf16[48,128]{1,0:T(8,128)(2,1)S(1)}, bf16[48,128]{1,0:T(8,128)(2,1)S(1)}, u32[]{:S(2)}, u32[]{:S(2)}) %collective-permute-start.6) | collective-permute-done | bytes 12320 | tf_op jit(solution)/shard_map/ppermute | solution.py:35
  38.9 0.1 h_rows.1
  39.0 3.0 %collective-permute-start.7 = (bf16[144,128]{1,0:T(8,128)(2,1)S(1)}, bf16[144,128]{1,0:T(8,128)(2,1)S(1)}, u32[]{:S(2)}, u32[]{:S(2)}) collective-permute-start(bf16[144,128]{1,0:T(8,128)(2,1)S(1)} %get-tuple-element.45), channel_id=1, source_target_pairs={{0,1},{1,0},{16,17},{17,16},{32,33},{33,32},{48,49},{49,48},{64,65... | collective-permute-start | bytes 110600 | tf_op jit(solution)/shard_map/ppermute | solution.py:40
  42.0 1.9 %collective-permute-start.8 = (bf16[144,128]{1,0:T(8,128)(2,1)S(1)}, bf16[144,128]{1,0:T(8,128)(2,1)S(1)}, u32[]{:S(2)}, u32[]{:S(2)}) collective-permute-start(bf16[144,128]{1,0:T(8,128)(2,1)S(1)} %get-tuple-element.46), channel_id=1, source_target_pairs={{1,16},{16,1},{17,32},{32,17},{33,48},{48,33},{49,64},{64,49},{65,... | collective-permute-start | bytes 110600 | tf_op jit(solution)/shard_map/ppermute | solution.py:47
  43.9 4.8 %collective-permute-done.8.outer = bf16[144,128]{1,0:T(8,128)(2,1)S(1)} collective-permute-done((bf16[144,128]{1,0:T(8,128)(2,1)S(1)}, bf16[144,128]{1,0:T(8,128)(2,1)S(1)}, u32[]{:S(2)}, u32[]{:S(2)}) %collective-permute-start.8) | collective-permute-done | bytes 36896 | tf_op jit(solution)/shard_map/ppermute | solution.py:47
  48.8 7.5 %rest.1 = (bf16[6144,128]{1,0:T(8,128)(2,1)S(1)}, bf16[6144,128]{1,0:T(8,128)(2,1)S(1)}) custom-call(bf16[768,128]{1,0:T(8,128)(2,1)S(1)} %get-tuple-element.44.hw, bf16[144,128]{1,0:T(8,128)(2,1)S(1)} %collective-permute-done.7.inner, bf16[144,128]{1,0:T(8,128)(2,1)S(1)} %collective-permute-done.8.outer, bf16[48,128]{1,0:T(8,128)(2,1)S(1)} %collective-permute-done.5.west, ...), custom_call_target="tpu_custom_call" | custom-call | flops 3000000000 | bytes 8000000 | tf_op jit(solution)/shard_map/rest/pallas_call | solution.py:541
  56.3 0.1 collective-permute-start.9
  56.4 3.4 %collective-permute-done.9.got = bf16[6144,128]{1,0:T(8,128)(2,1)S(1)} collective-permute-done((bf16[6144,128]{1,0:T(8,128)(2,1)S(1)}, bf16[6144,128]{1,0:T(8,128)(2,1)S(1)}, u32[]{:S(2)}, u32[]{:S(2)}) %collective-permute-start.9) | collective-permute-done | bytes 1572896 | tf_op jit(solution)/shard_map/ppermute | solution.py:659
  59.8 0.4 pair_sum.1
  60.2 32.5 %all_to_all.10.pieces = bf16[64,96,128]{2,1,0:T(8,128)(2,1)S(1)} all-to-all(bf16[64,96,128]{2,1,0:T(8,128)(2,1)S(1)} %bitcast.20), channel_id=1, replica_groups=mesh['x'=4,'core'=2,'z'=4,'yl'=2,'yh'=2] {'x','z','yl','yh'}, dimensions={0} | all-to-all | bytes 3145728 | tf_op jit(solution)/shard_map/all_to_all | solution.py:660
  92.7 0.4 spread.1
  93.1 26.6 %all_to_all.11 = bf16[64,96,128]{2,1,0:T(8,128)(2,1)S(1)} all-to-all(bf16[64,96,128]{2,1,0:T(8,128)(2,1)S(1)} %spread.1), channel_id=1, replica_groups=mesh['x'=4,'core'=2,'z'=4,'yl'=2,'yh'=2] {'x','z','yl','yh'}, dimensions={0} | all-to-all | bytes 3145728 | tf_op jit(solution)/shard_map/all_to_all | solution.py:661
  119.7 3.4 %collective-permute-start.10 = (bf16[6144,128]{1,0:T(8,128)(2,1)S(1)}, bf16[6144,128]{1,0:T(8,128)(2,1)S(1)}, u32[]{:S(2)}, u32[]{:S(2)}) collective-permute-start(bf16[6144,128]{1,0:T(8,128)(2,1)S(1)} %bitcast.18), channel_id=1, source_target_pairs={{0,16},{16,0},{1,17},{17,1},{2,18},{18,2},{3,19},{19,3},{4,20},{20... | collective-permute-start | bytes 4718600 | tf_op jit(solution)/shard_map/ppermute | solution.py:662
  123.1 1.9 %finish_own.1 = (f32[1152,128]{1,0:T(8,128)}, f32[2304,128]{1,0:T(8,128)}, f32[1152,128]{1,0:T(8,128)}, f32[128,1024]{1,0:T(8,128)}, f32[1024,512]{1,0:T(8,128)}) custom-call(bf16[6144,128]{1,0:T(8,128)(2,1)S(1)} %bitcast.19), custom_call_target="tpu_custom_call" | custom-call | flops 800000 | bytes 5000000 | tf_op jit(solution)/shard_map/finish_own/pallas_call | solution.py:597
  125.0 1.2 collective-permute-done.10.part
  126.2 2.0 %finish_other.1 = (f32[1152,128]{1,0:T(8,128)}, f32[2304,128]{1,0:T(8,128)}, f32[1152,128]{1,0:T(8,128)}, f32[128,1024]{1,0:T(8,128)}, f32[1024,512]{1,0:T(8,128)}, /*index=5*/f32[1,1]{1,0:T(1,128)}) custom-call(bf16[6144,128]{1,0:T(8,128)(2,1)S(1)} %collective-permute-done.10.part, ...), custom_call_target="tpu_custom_call", output_to_operand_aliasing={{0}: (1, {}), {1}: (2, {}), {2}: (3, {}), {3}: (4, {}), {4}... | custom-call | flops 800000 | bytes 5000000 | tf_op jit(solution)/shard_map/finish_other/pallas_call | solution.py:597
  (27 shorter events, 0.1 us)
Async XLA Ops:
  0.6 0.9 copy-start.5
  1.5 0.8 copy-start.6
  2.3 5.3 %collective-permute-start = (bf16[32,128]{1,0:T(8,128)(2,1)S(1)}, bf16[32,128]{1,0:T(8,128)(2,1)S(1)}, u32[]{:S(2)}, u32[]{:S(2)}) collective-permute-start(bf16[32,128]{1,0:T(8,128)(2,1)S(1)} %get-tuple-element.35), channel_id=1, source_target_pairs={{0,2},{2,4},{4,6},{6,8},{8,10},{10,12},{12,14},{1,3},{3,5},{5,7},{... | collective-permute-start | bytes 24584 | tf_op jit(solution)/shard_map/ppermute | solution.py:35
  6.4 4.5 %collective-permute-start.1 = (bf16[32,128]{1,0:T(8,128)(2,1)S(1)}, bf16[32,128]{1,0:T(8,128)(2,1)S(1)}, u32[]{:S(2)}, u32[]{:S(2)}) collective-permute-start(bf16[32,128]{1,0:T(8,128)(2,1)S(1)} %get-tuple-element.36), channel_id=1, source_target_pairs={{2,0},{4,2},{6,4},{8,6},{10,8},{12,10},{14,12},{3,1},{5,3},{7,5},{... | collective-permute-start | bytes 24584 | tf_op jit(solution)/shard_map/ppermute | solution.py:35
  10.9 5.0 %collective-permute-start.2 = (bf16[352,128]{1,0:T(8,128)(2,1)S(1)}, bf16[352,128]{1,0:T(8,128)(2,1)S(1)}, u32[]{:S(2)}, u32[]{:S(2)}) collective-permute-start(bf16[352,128]{1,0:T(8,128)(2,1)S(1)} %edge_rows.1.mine), channel_id=1, source_target_pairs={{0,1},{1,0},{16,17},{17,16},{32,33},{33,32},{48,49},{49,48},{64,65... | collective-permute-start | bytes 270344 | tf_op jit(solution)/shard_map/ppermute | solution.py:40
  14.5 9.5 %copy-start.11 = (s32[1,1,256]{2,1,0:T(1,128)S(1)}, s32[1,1,256]{2,1,0:T(1,128)}, u32[]{:S(2)}) copy-start(s32[1,1,256]{2,1,0:T(1,128)} %param.24) | copy-start | bytes 3076
  14.5 12.7 %copy-start = (bf16[3,3,512,128]{3,2,1,0:T(8,128)(2,1)S(1)}, bf16[3,3,512,128]{3,2,1,0:T(8,128)(2,1)}, u32[]{:S(2)}) copy-start(bf16[3,3,512,128]{3,2,1,0:T(8,128)(2,1)} %param.18) | copy-start | bytes 3538948
  14.6 12.7 %copy-start.2 = (bf16[3,3,128,128]{3,2,1,0:T(8,128)(2,1)S(1)}, bf16[3,3,128,128]{3,2,1,0:T(8,128)(2,1)}, u32[]{:S(2)}) copy-start(bf16[3,3,128,128]{3,2,1,0:T(8,128)(2,1)} %param.17) | copy-start | bytes 884740
  14.6 12.7 %copy-start.7 = (bf16[34,10]{0,1:T(8,128)(2,1)S(1)}, bf16[34,10]{0,1:T(8,128)(2,1)}, u32[]{:S(2)}) copy-start(bf16[34,10]{0,1:T(8,128)(2,1)} %param.15) | copy-start | bytes 2044
  14.6 12.7 %copy-start.8 = (bf16[34,10]{0,1:T(8,128)(2,1)S(1)}, bf16[34,10]{0,1:T(8,128)(2,1)}, u32[]{:S(2)}) copy-start(bf16[34,10]{0,1:T(8,128)(2,1)} %param.16) | copy-start | bytes 2044
  14.6 12.7 %copy-start.9 = (s32[1,1,256]{2,1,0:T(1,128)S(1)}, s32[1,1,256]{2,1,0:T(1,128)}, u32[]{:S(2)}) copy-start(s32[1,1,256]{2,1,0:T(1,128)} %param.22) | copy-start | bytes 3076
  15.9 8.1 %collective-permute-start.3 = (bf16[112,128]{1,0:T(8,128)(2,1)S(1)}, bf16[112,128]{1,0:T(8,128)(2,1)S(1)}, u32[]{:S(2)}, u32[]{:S(2)}) collective-permute-start(bf16[112,128]{1,0:T(8,128)(2,1)S(1)} %get-tuple-element.38), channel_id=1, source_target_pairs={{0,16},{16,32},{32,48},{48,64},{64,80},{80,96},{96,112},{1,17},{17... | collective-permute-start | bytes 86024 | tf_op jit(solution)/shard_map/ppermute | solution.py:35
  22.1 5.2 %collective-permute-start.4 = (bf16[112,128]{1,0:T(8,128)(2,1)S(1)}, bf16[112,128]{1,0:T(8,128)(2,1)S(1)}, u32[]{:S(2)}, u32[]{:S(2)}) collective-permute-start(bf16[112,128]{1,0:T(8,128)(2,1)S(1)} %get-tuple-element.39), channel_id=1, source_target_pairs={{16,0},{32,16},{48,32},{64,48},{80,64},{96,80},{112,96},{17,1},{33... | collective-permute-start | bytes 86024 | tf_op jit(solution)/shard_map/ppermute | solution.py:35
  30.1 5.6 %collective-permute-start.5 = (bf16[48,128]{1,0:T(8,128)(2,1)S(1)}, bf16[48,128]{1,0:T(8,128)(2,1)S(1)}, u32[]{:S(2)}, u32[]{:S(2)}) collective-permute-start(bf16[48,128]{1,0:T(8,128)(2,1)S(1)} %get-tuple-element.42), channel_id=1, source_target_pairs={{0,2},{2,4},{4,6},{6,8},{8,10},{10,12},{12,14},{1,3},{3,5},{5,7},{... | collective-permute-start | bytes 36872 | tf_op jit(solution)/shard_map/ppermute | solution.py:35
  34.4 4.4 %collective-permute-start.6 = (bf16[48,128]{1,0:T(8,128)(2,1)S(1)}, bf16[48,128]{1,0:T(8,128)(2,1)S(1)}, u32[]{:S(2)}, u32[]{:S(2)}) collective-permute-start(bf16[48,128]{1,0:T(8,128)(2,1)S(1)} %get-tuple-element.43), channel_id=1, source_target_pairs={{2,0},{4,2},{6,4},{8,6},{10,8},{12,10},{14,12},{3,1},{5,3},{7,5},{... | collective-permute-start | bytes 36872 | tf_op jit(solution)/shard_map/ppermute | solution.py:35
  38.9 9.9 %copy-start.1 = (bf16[1024,512]{1,0:T(8,128)(2,1)S(1)}, bf16[1024,512]{1,0:T(8,128)(2,1)}, u32[]{:S(2)}) copy-start(bf16[1024,512]{1,0:T(8,128)(2,1)} %binw.1) | copy-start | bytes 3145732
  38.9 9.9 %copy-start.3 = (bf16[3,3,128,128]{3,2,1,0:T(8,128)(2,1)S(1)}, bf16[3,3,128,128]{3,2,1,0:T(8,128)(2,1)}, u32[]{:S(2)}) copy-start(bf16[3,3,128,128]{3,2,1,0:T(8,128)(2,1)} %param.19) | copy-start | bytes 884740
  38.9 9.9 %copy-start.4 = (bf16[128,1024]{1,0:T(8,128)(2,1)S(1)}, bf16[128,1024]{1,0:T(8,128)(2,1)}, u32[]{:S(2)}) copy-start(bf16[128,1024]{1,0:T(8,128)(2,1)} %hid.1) | copy-start | bytes 786436
  38.9 9.9 %copy-start.10 = (s32[1,128]{1,0:T(1,128)S(1)}, s32[1,128]{1,0:T(1,128)}, u32[]{:S(2)}) copy-start(s32[1,128]{1,0:T(1,128)} %constant.8.ring_l) | copy-start | bytes 1540
  39.0 4.9 %collective-permute-start.7 = (bf16[144,128]{1,0:T(8,128)(2,1)S(1)}, bf16[144,128]{1,0:T(8,128)(2,1)S(1)}, u32[]{:S(2)}, u32[]{:S(2)}) collective-permute-start(bf16[144,128]{1,0:T(8,128)(2,1)S(1)} %get-tuple-element.45), channel_id=1, source_target_pairs={{0,1},{1,0},{16,17},{17,16},{32,33},{33,32},{48,49},{49,48},{64,65... | collective-permute-start | bytes 110600 | tf_op jit(solution)/shard_map/ppermute | solution.py:40
  42.0 6.8 %collective-permute-start.8 = (bf16[144,128]{1,0:T(8,128)(2,1)S(1)}, bf16[144,128]{1,0:T(8,128)(2,1)S(1)}, u32[]{:S(2)}, u32[]{:S(2)}) collective-permute-start(bf16[144,128]{1,0:T(8,128)(2,1)S(1)} %get-tuple-element.46), channel_id=1, source_target_pairs={{1,16},{16,1},{17,32},{32,17},{33,48},{48,33},{49,64},{64,49},{65,... | collective-permute-start | bytes 110600 | tf_op jit(solution)/shard_map/ppermute | solution.py:47
  56.3 3.5 %collective-permute-start.9 = (bf16[6144,128]{1,0:T(8,128)(2,1)S(1)}, bf16[6144,128]{1,0:T(8,128)(2,1)S(1)}, u32[]{:S(2)}, u32[]{:S(2)}) collective-permute-start(bf16[6144,128]{1,0:T(8,128)(2,1)S(1)} %get-tuple-element.50), channel_id=1, source_target_pairs={{0,16},{16,0},{1,17},{17,1},{2,18},{18,2},{3,19},{19,3},{4,20},{20... | collective-permute-start | bytes 4718600 | tf_op jit(solution)/shard_map/ppermute | solution.py:659
  119.7 6.4 %collective-permute-start.10 = (bf16[6144,128]{1,0:T(8,128)(2,1)S(1)}, bf16[6144,128]{1,0:T(8,128)(2,1)S(1)}, u32[]{:S(2)}, u32[]{:S(2)}) collective-permute-start(bf16[6144,128]{1,0:T(8,128)(2,1)S(1)} %bitcast.18), channel_id=1, source_target_pairs={{0,16},{16,0},{1,17},{17,1},{2,18},{18,2},{3,19},{19,3},{4,20},{20... | collective-permute-start | bytes 4718600 | tf_op jit(solution)/shard_map/ppermute | solution.py:662

commit v6 on v5

--- a/solution.py
+++ b/solution.py
@@ -120,24 +120,26 @@
         rows[at : at + 1, :] = w[r : r + 1, :]
         rows[at + 33 : at + 34, :] = e[r : r + 1, :]
     inner[0:CTX, :] = rows[...].astype(BF)
-    xs[...] = jnp.zeros_like(xs)
     for side in range(2):
-        base = 128 * side
+        base = 80 * side
+        lanes = slice(128 * side, 128 * side + 128)
         for a in range(8):
-            at = base + 16 * a
-            xs[at + 1 : at + 9, :] = ctx[8 * a : 8 * a + 8, base : base + 128].astype(F32)
-        xs[pl.ds(base, 8, stride=16), :] = w[16 + 8 * side : 24 + 8 * side, :]
-        xs[pl.ds(base + 9, 8, stride=16), :] = e[16 + 8 * side : 24 + 8 * side, :]
+            at = base + 10 * a
+            xs[at + 1 : at + 9, :] = ctx[8 * a : 8 * a + 8, lanes].astype(F32)
+        xs[pl.ds(base, 8, stride=10), :] = w[16 + 8 * side : 24 + 8 * side, :]
+        xs[pl.ds(base + 9, 8, stride=10), :] = e[16 + 8 * side : 24 + 8 * side, :]
     inner[CTX:, :] = xs[...].astype(BF)
 
 
-def ctx_rows_kernel(mine, inner, down, up):
+def ctx_rows_kernel(mine, inner, down, up, xs):
     lower = lax.axis_index("yh") == 1
+    xs[160:, :] = jnp.zeros((16, C), F32)
     for n, got in enumerate((mine, inner)):
+        xs[0:160, :] = got[CTX:, :].astype(F32)
         for side in range(2):
-            at, to = CTX + 128 * side, 32 * n + 16 * side
-            up[to : to + 16, :] = got[at : at + 16, :]
-            down[to : to + 16, :] = got[at + 112 : at + 128, :]
+            at, to = 80 * side, 32 * n + 16 * side
+            up[to : to + 16, :] = xs[at : at + 16, :].astype(BF)
+            down[to : to + 16, :] = xs[at + 70 : at + 86, :].astype(BF)
     up[64:112, :] = jnp.where(lower, inner[0:WIDE, :], mine[0:WIDE, :])
     down[64:112, :] = jnp.where(lower, mine[WIDE:CTX, :], inner[WIDE:CTX, :])
 
@@ -151,7 +153,7 @@
 def first_conv_kernel(
     rows_in, cols_in, fine, west, east, mine, inner, north, south, w_fine, w_ctx, idx_l, lab_l,
     xc, h1, sg, last, first, digs,
-    fscr, mid, block, hscr, dscr, rmat, cmat, spot,
+    fscr, mid, block, hscr, dscr, rmat, cmat, xs, pre, spot,
 ):
     spot[0] = lax.axis_index("yh")
     spot[1] = (2 * lax.axis_index("x") + lax.axis_index("core")) * 32
@@ -177,13 +179,16 @@
     gcol = col0 + iota((10, 34), 1) - 1
     rmat[0:10, 0:34] = jnp.where((grow >= 0) & (grow < 256), rows_in[...].astype(F32), 0.0)
     cmat[0:10, 0:34] = jnp.where((gcol >= 0) & (gcol < 256), cols_in[...].astype(F32), 0.0)
-    for side in range(2):
-        own = pl.ds(pl.multiple_of(256 * half + 128 * side, 128), 128)
-        other = pl.ds(pl.multiple_of(256 * (1 - half) + 128 * side, 128), 128)
-        for n, lanes, got in ((0, own, mine), (32, other, inner)):
+    xs[160:, :] = jnp.zeros((16, C), F32)
+    for n, part, got in ((0, half, mine), (32, 1 - half, inner)):
+        xs[0:160, :] = got[CTX:, :].astype(F32)
+        for side in range(2):
+            lanes = pl.ds(pl.multiple_of(256 * part + 128 * side, 128), 128)
             sl = slice(n + 16 * side, n + 16 * side + 16)
             block[0:16, lanes] = north[sl, :]
-            block[16:144, lanes] = got[CTX + 128 * side : CTX + 128 * side + 128, :]
+            for a in range(8):
+                at = 80 * side + 10 * a
+                block[16 + 16 * a : 32 + 16 * a, lanes] = xs[at : at + 16, :].astype(BF)
             block[144:160, lanes] = south[sl, :]
     pick = (iota((288, C), 0) >> 4) + 16 * half == iota((288, C), 1)
     left = dot_t(pick.astype(F32).astype(BF), rmat[...].astype(BF)).astype(BF)
@@ -199,12 +204,10 @@
         wide = dot(left, mid[16 * i : 16 * i + 16, :]).astype(BF)
         for dx in range(3):
             xc[32 * i : 32 * i + 32, 384 + 512 * dx : 896 + 512 * dx] = wide[32 * dx : 32 * dx + 32]
-    acc = None
-    for dy in range(3):
-        rows = slice(32 * dy, 32 * dy + 512)
-        term = dot(xc[rows, :384], w_fine[384 * dy : 384 * dy + 384, :])
-        term += dot(xc[rows, 384:], w_ctx[1536 * dy : 1536 * dy + 1536, :])
-        acc = term if acc is None else acc + term
+    wf = jnp.concatenate([w_fine[384 * dy : 384 * dy + 384, :] for dy in range(3)], axis=1)
+    wc = jnp.concatenate([w_ctx[1536 * dy : 1536 * dy + 1536, :] for dy in range(3)], axis=1)
+    pre[...] = dot(xc[:, :384], wf) + dot(xc[:, 384:], wc)
+    acc = sum(pre[32 * dy : 32 * dy + 512, 128 * dy : 128 * dy + 128] for dy in range(3))
     s = jax.nn.sigmoid(acc)
     h = (acc * s).astype(BF)
     h1[...] = h
@@ -249,8 +252,8 @@
 
 def rest_kernel(
     hw, inner, outer, west, east, xc, sg1, idx_l, ring_l, lab_l, cw, hid, binw,
-    keep, give,
-    hp, hx, sg2, h2, rows_s, act, sgz, dl, dz, gscr, gx, g2w, g1w, buf, spot,
+    out,
+    hp, hx, sg2, h2, rows_s, act, sgz, dl, dz, gscr, gx, g2w, g1w, pre, spot,
 ):
     spot[0] = lax.axis_index("core")
     spot[1] = lax.axis_index("yh")
@@ -276,15 +279,12 @@
     own_lab = column(lab_l[...]).astype(jnp.int32)
     for dx in range(3):
         hx[:, 128 * dx : 128 * dx + 128] = hp[dx : dx + 992, :].astype(BF)
-    for part in range(2):
-        at = 448 * part
-        acc = None
-        for dy in range(3):
-            term = dot(hx[at + WIDE * dy : at + WIDE * dy + 448, :], cw[384 * dy : 384 * dy + 384, :])
-            acc = term if acc is None else acc + term
-        s = jax.nn.sigmoid(acc)
-        h2[at : at + 448, :] = (acc * s).astype(BF)
-        sg2[at : at + 448, :] = s * (1.0 + acc * (1.0 - s))
+    forth = jnp.concatenate([cw[384 * dy : 384 * dy + 384, :] for dy in range(3)], axis=1)
+    pre[...] = dot(hx[...], forth)
+    acc = sum(pre[WIDE * dy : WIDE * dy + EXT, 128 * dy : 128 * dy + 128] for dy in range(3))
+    s = jax.nn.sigmoid(acc)
+    h2[...] = (acc * s).astype(BF)
+    sg2[...] = s * (1.0 + acc * (1.0 - s))
     own_pick = (slot_s == iota((CAP, EXT), 1)).astype(F32).astype(BF)
     rows = dot(jnp.concatenate([own_pick, ring_pick], axis=0), h2[...]).astype(BF)
     rows_s[...] = rows
@@ -308,7 +308,7 @@
     gscr[:, 128:256] = (drows - hi.astype(F32)).astype(BF)
 
     def put(row, value):
-        buf[row // STAT, pl.ds(row % STAT, value.shape[0]), :] = value.astype(BF)
+        out[(row // STAT) ^ core, pl.ds(row % STAT, value.shape[0]), :] = value.astype(BF)
 
     for n in range(4):
         put(7936 + 1024 * n, t_dot(act[0:CAP, :], dl[0:CAP, 128 * n : 128 * n + 128]))
@@ -318,8 +318,8 @@
     lane = iota((1, C), 1)
     stats = jnp.where(lane == 0, loss, jnp.where(lane == 1, jnp.sum(live[:CAP]), 0.0))
     for n in range(2):
-        buf[n, STAT : STAT + 16, :] = stat_rows(stats, (16, C)).astype(BF)
-        buf[n, STAT + 16 : KEEP, :] = jnp.zeros((KEEP - STAT - 16, C), BF)
+        out[n, STAT : STAT + 16, :] = stat_rows(stats, (16, C)).astype(BF)
+        out[n, STAT + 16 : KEEP, :] = jnp.zeros((KEEP - STAT - 16, C), BF)
     cell = iota((EXT, CAP), 0)
     back = jnp.concatenate(
         [(slot_l == cell).astype(F32), (ring_l[...] == cell[:, :128]).astype(F32)], axis=1
@@ -328,8 +328,9 @@
     gx[0:EXT, :] = (both[:, :128] + both[:, 128:]) * sg2[...]
 
     g2w[...] = jnp.zeros_like(g2w)
-    col = iota((768, C), 0) % WIDE
-    own = jnp.where((col >= 1) & (col <= COLS), gx[WIDE : WIDE + 768, :], 0.0).astype(BF)
+    col = iota((WIDE, C), 0)
+    inside = jnp.where((col >= 1) & (col <= COLS), 1.0, 0.0)
+    own = (gx[WIDE : WIDE + 768, :] * jnp.concatenate([inside] * ROWS, axis=0)).astype(BF)
     for dy in range(3):
         g2w[WIDE * (1 + dy) : WIDE * (1 + dy) + 768, 128 * dy : 128 * dy + 128] = own
     for dx in range(3):
@@ -342,14 +343,12 @@
             at = WIDE * i + 2 - dx
             hx[32 * i : 32 * i + 32, 128 * dx : 128 * dx + 128] = gx[at : at + 32, :].astype(BF)
     g1w[...] = jnp.zeros_like(g1w)
-    acc = None
-    for dy in range(3):
-        at = 32 * (2 - dy)
-        back = jnp.concatenate(
-            [cw[384 * dy + 128 * dx : 384 * dy + 128 * dx + 128, :] for dx in range(3)], axis=1
-        )
-        term = dot_t(hx[at : at + 512, :], back)
-        acc = term if acc is None else acc + term
+    back = [
+        jnp.concatenate([cw[384 * dy + 128 * dx : 384 * dy + 128 * dx + 128, :] for dx in range(3)], axis=1)
+        for dy in range(3)
+    ]
+    pre[0:576, :] = dot_t(hx[0:576, :], jnp.concatenate(back, axis=0))
+    acc = sum(pre[64 - 32 * dy : 576 - 32 * dy, 128 * dy : 128 * dy + 128] for dy in range(3))
     g1 = (acc * sg1[...]).astype(BF)
     for dy in range(3):
         g1w[32 * dy : 32 * dy + 512, 128 * dy : 128 * dy + 128] = g1
@@ -360,15 +359,14 @@
     for dx in range(3):
         for side in range(2):
             at = 384 + 512 * dx + 256 * side
-            part = t_dot(xc[:, at : at + 256], g1w[...])
+            part = t_dot(g1w[...], xc[:, at : at + 256]).astype(BF)
             for dy in range(3):
                 at = 2304 * side + 256 * (3 * dy + dx)
-                put(at, part[:, 128 * dy : 128 * dy + 128])
-    keep[...] = buf[core]
-    give[...] = buf[1 - core]
-
-
-def pair_kernel(keep, got, out):
+                put(at, part[128 * dy : 128 * dy + 128, :].T)
+
+
+def pair_kernel(both, got, out):
+    keep = both.at[0]
     out[...] = (keep[...].astype(F32) + got[...].astype(F32)).astype(BF)
     sl = slice(STAT, STAT + 16)
     rows = keep[sl, :].astype(F32) + got[sl, :].astype(F32)
@@ -476,10 +474,10 @@
 def edge_rows(*args):
     return pl.pallas_call(
         edge_rows_kernel,
-        out_shape=sds((CTX + 256, C), BF),
+        out_shape=sds((CTX + 160, C), BF),
         in_specs=vmem(4),
         out_specs=vmem(1)[0],
-        scratch_shapes=[pltpu.VMEM((2 * WIDE, C), F32), pltpu.VMEM((256, C), F32)],
+        scratch_shapes=[pltpu.VMEM((2 * WIDE, C), F32), pltpu.VMEM((160, C), F32)],
         compiler_params=limit(4),
         cost_estimate=BUSY,
         name="edge_rows",
@@ -492,6 +490,7 @@
         out_shape=(sds((112, C), BF), sds((112, C), BF)),
         in_specs=vmem(2),
         out_specs=tuple(vmem(2)),
+        scratch_shapes=[pltpu.VMEM((176, C), F32)],
         compiler_params=limit(4),
         cost_estimate=BUSY,
         name="ctx_rows",
@@ -514,6 +513,8 @@
             v((512, C), F32),
             v((16, C), F32),
             v((16, C), F32),
+            v((176, C), F32),
+            v((576, 384), F32),
             pltpu.SMEM((4,), jnp.int32),
         ],
         compiler_params=limit(20),
@@ -540,9 +541,9 @@
     v = pltpu.VMEM
     return pl.pallas_call(
         rest_kernel,
-        out_shape=(sds((KEEP, C), BF), sds((KEEP, C), BF)),
+        out_shape=sds((2, KEEP, C), BF),
         in_specs=vmem(len(args)),
-        out_specs=tuple(vmem(2)),
+        out_specs=vmem(1)[0],
         scratch_shapes=[
             v((1000, C), F32),
             v((992, 384), BF),
@@ -557,7 +558,7 @@
             v((EXT + 8, C), F32),
             v((960, 384), BF),
             v((576, 384), BF),
-            v((2, KEEP, C), BF),
+            v((992, 384), F32),
             pltpu.SMEM((4,), jnp.int32),
         ],
         compiler_params=limit(28),
@@ -648,15 +649,15 @@
     west = shift(last, GX, 8, 1)
     east = shift(first, GX, 8, -1)
     wide, inner, outer = h_rows(h_one, digs, west, east)
+    outer = outer_swap(outer)
     inner = side_swap(inner)
-    outer = outer_swap(outer)
-    keep, give = rest(
+    both = rest(
         wide, inner, outer, west, east, xc, sg1, idx, ring[None, :], lab,
         conv_weight.reshape(1152, C), hidden_weight, bin_weight,
     )
 
     flip = [(0, 1), (1, 0)]
-    pair = pair_sum(keep, lax.ppermute(give, "core", flip))
+    pair = pair_sum(both, lax.ppermute(both[1], "core", flip))
     pieces = lax.all_to_all(pair.reshape(PEERS, SHARD, C), PLANE, 0, 0, tiled=True)
     half_sum = lax.all_to_all(spread(pieces), PLANE, 0, 0, tiled=True).reshape(KEEP, C)
     other = lax.ppermute(half_sum, "core", flip)

time: 129 us -> 128 us (level)
  no operation moved by 1% of the time
where the time goes in v6:
time: 128 us; the launch traced here: 127 us
  blocking collectives  59.1 us (46%)
  starting transfers between devices  30.4 us (24%)
  waiting for transfers between devices  19.9 us (16%)
  Pallas kernels  14.3 us (11%)
  local copies, waits for them, and re-layouts  1.81 us (1%)
  between operations  1.53 us (1%)
    all_to_all x1, blocking collectives, local(): lax.all_to_all(pair.reshape(PEERS, SHARD, C), PLANE, 0, 0, tiled=True)  32.5 us
    all_to_all x1, blocking collectives, local(): lax.all_to_all(spread(pieces), PLANE, 0, 0, tiled=True).reshape(KEEP, C)  26.6 us
    ppermute x6, starting transfers between devices, shift(): return lax.ppermute(x, axis, pairs)  19.1 us
    ppermute x6, waiting for transfers between devices, shift(): return lax.ppermute(x, axis, pairs)  9.52 us
    pallas_call x1, Pallas kernels, rest(): pl.pallas_call(rest_kernel, out_shape=sds((2, KEEP, C), BF), in_specs=vme...  6.97 us
    ppermute x2, starting transfers between devices, side_swap(): return lax.ppermute(x, TALL, own)  5.98 us
    ppermute x1, waiting for transfers between devices, outer_swap(): return lax.ppermute(x, TALL, pairs)  4.84 us
    pallas_call x2, Pallas kernels, finish(): pl.pallas_call(functools.partial(finish_kernel, second), out_shape=tuple(...  3.83 us
  transfers between devices with their start and end apart: 11, of which 7 were waited for; matrix products, arithmetic and copies ran while one was open for 0% of the time, Pallas kernels for 1%

profile of v6, /device:TPU:1, one launch (start us, length us, event | category | flops | bytes accessed | tf_op | source)
XLA Modules:
  0.0 127.1 jit_solution(8942499552162550228)
XLA Ops:
  0.6 0.9 copy-done.5
  1.5 0.8 copy-done.6
  2.3 4.0 %collective-permute-start = (bf16[32,128]{1,0:T(8,128)(2,1)S(1)}, bf16[32,128]{1,0:T(8,128)(2,1)S(1)}, u32[]{:S(2)}, u32[]{:S(2)}) collective-permute-start(bf16[32,128]{1,0:T(8,128)(2,1)S(1)} %get-tuple-element.33), channel_id=1, source_target_pairs={{0,2},{2,4},{4,6},{6,8},{8,10},{10,12},{12,14},{1,3},{3,5},{5,7},{... | collective-permute-start | bytes 24584 | tf_op jit(solution)/shard_map/ppermute | solution.py:35
  6.4 1.3 %collective-permute-start.1 = (bf16[32,128]{1,0:T(8,128)(2,1)S(1)}, bf16[32,128]{1,0:T(8,128)(2,1)S(1)}, u32[]{:S(2)}, u32[]{:S(2)}) collective-permute-start(bf16[32,128]{1,0:T(8,128)(2,1)S(1)} %get-tuple-element.34), channel_id=1, source_target_pairs={{2,0},{4,2},{6,4},{8,6},{10,8},{12,10},{14,12},{3,1},{5,3},{7,5},{... | collective-permute-start | bytes 24584 | tf_op jit(solution)/shard_map/ppermute | solution.py:35
  7.7 3.2 %collective-permute-done.1.east = bf16[32,128]{1,0:T(8,128)(2,1)S(1)} collective-permute-done((bf16[32,128]{1,0:T(8,128)(2,1)S(1)}, bf16[32,128]{1,0:T(8,128)(2,1)S(1)}, u32[]{:S(2)}, u32[]{:S(2)}) %collective-permute-start.1) | collective-permute-done | bytes 8224 | tf_op jit(solution)/shard_map/ppermute | solution.py:35
  10.9 3.0 %collective-permute-start.2 = (bf16[256,128]{1,0:T(8,128)(2,1)S(1)}, bf16[256,128]{1,0:T(8,128)(2,1)S(1)}, u32[]{:S(2)}, u32[]{:S(2)}) collective-permute-start(bf16[256,128]{1,0:T(8,128)(2,1)S(1)} %edge_rows.1.mine), channel_id=1, source_target_pairs={{0,1},{1,0},{16,17},{17,16},{32,33},{33,32},{48,49},{49,48},{64,65... | collective-permute-start | bytes 196616 | tf_op jit(solution)/shard_map/ppermute | solution.py:40
  14.5 0.0 copy-start.11
  14.5 0.0 copy-start
  14.6 1.0 collective-permute-done.2.inner
  15.6 6.2 %collective-permute-start.3 = (bf16[112,128]{1,0:T(8,128)(2,1)S(1)}, bf16[112,128]{1,0:T(8,128)(2,1)S(1)}, u32[]{:S(2)}, u32[]{:S(2)}) collective-permute-start(bf16[112,128]{1,0:T(8,128)(2,1)S(1)} %get-tuple-element.36), channel_id=1, source_target_pairs={{0,16},{16,32},{32,48},{48,64},{64,80},{80,96},{96,112},{1,17},{17... | collective-permute-start | bytes 86024 | tf_op jit(solution)/shard_map/ppermute | solution.py:35
  21.8 1.9 %collective-permute-start.4 = (bf16[112,128]{1,0:T(8,128)(2,1)S(1)}, bf16[112,128]{1,0:T(8,128)(2,1)S(1)}, u32[]{:S(2)}, u32[]{:S(2)}) collective-permute-start(bf16[112,128]{1,0:T(8,128)(2,1)S(1)} %get-tuple-element.37), channel_id=1, source_target_pairs={{16,0},{32,16},{48,32},{64,48},{80,64},{96,80},{112,96},{17,1},{33... | collective-permute-start | bytes 86024 | tf_op jit(solution)/shard_map/ppermute | solution.py:35
  23.7 3.2 %collective-permute-done.4.south = bf16[112,128]{1,0:T(8,128)(2,1)S(1)} collective-permute-done((bf16[112,128]{1,0:T(8,128)(2,1)S(1)}, bf16[112,128]{1,0:T(8,128)(2,1)S(1)}, u32[]{:S(2)}, u32[]{:S(2)}) %collective-permute-start.4) | collective-permute-done | bytes 28704 | tf_op jit(solution)/shard_map/ppermute | solution.py:35
  27.0 2.4 %first_conv.1 = (bf16[576,1920]{1,0:T(8,128)(2,1)S(1)}, bf16[512,128]{1,0:T(8,128)(2,1)S(1)}, f32[512,128]{1,0:T(8,128)S(1)}, bf16[48,128]{1,0:T(8,128)(2,1)S(1)...) custom-call(bf16[10,34]{1,0:T(8,128)(2,1)S(1)} %bitcast.28, bf16[10,34]{1,0:T(8,128)(2,1)S(1)} %bitcast.29, ...), custom_call_target="tpu_custom_call" | custom-call | flops 900000000 | bytes 5000000 | tf_op jit(solution)/shard_map/first_conv/pallas_call | solution.py:503
  29.4 4.3 %collective-permute-start.5 = (bf16[48,128]{1,0:T(8,128)(2,1)S(1)}, bf16[48,128]{1,0:T(8,128)(2,1)S(1)}, u32[]{:S(2)}, u32[]{:S(2)}) collective-permute-start(bf16[48,128]{1,0:T(8,128)(2,1)S(1)} %get-tuple-element.40), channel_id=1, source_target_pairs={{0,2},{2,4},{4,6},{6,8},{8,10},{10,12},{12,14},{1,3},{3,5},{5,7},{... | collective-permute-start | bytes 36872 | tf_op jit(solution)/shard_map/ppermute | solution.py:35
  33.8 1.3 %collective-permute-start.6 = (bf16[48,128]{1,0:T(8,128)(2,1)S(1)}, bf16[48,128]{1,0:T(8,128)(2,1)S(1)}, u32[]{:S(2)}, u32[]{:S(2)}) collective-permute-start(bf16[48,128]{1,0:T(8,128)(2,1)S(1)} %get-tuple-element.41), channel_id=1, source_target_pairs={{2,0},{4,2},{6,4},{8,6},{10,8},{12,10},{14,12},{3,1},{5,3},{7,5},{... | collective-permute-start | bytes 36872 | tf_op jit(solution)/shard_map/ppermute | solution.py:35
  35.1 3.1 %collective-permute-done.6.east = bf16[48,128]{1,0:T(8,128)(2,1)S(1)} collective-permute-done((bf16[48,128]{1,0:T(8,128)(2,1)S(1)}, bf16[48,128]{1,0:T(8,128)(2,1)S(1)}, u32[]{:S(2)}, u32[]{:S(2)}) %collective-permute-start.6) | collective-permute-done | bytes 12320 | tf_op jit(solution)/shard_map/ppermute | solution.py:35
  38.2 0.1 h_rows.1
  38.3 3.0 %collective-permute-start.7 = (bf16[144,128]{1,0:T(8,128)(2,1)S(1)}, bf16[144,128]{1,0:T(8,128)(2,1)S(1)}, u32[]{:S(2)}, u32[]{:S(2)}) collective-permute-start(bf16[144,128]{1,0:T(8,128)(2,1)S(1)} %get-tuple-element.43), channel_id=1, source_target_pairs={{0,1},{1,0},{16,17},{17,16},{32,33},{33,32},{48,49},{49,48},{64,65... | collective-permute-start | bytes 110600 | tf_op jit(solution)/shard_map/ppermute | solution.py:40
  41.3 1.9 %collective-permute-start.8 = (bf16[144,128]{1,0:T(8,128)(2,1)S(1)}, bf16[144,128]{1,0:T(8,128)(2,1)S(1)}, u32[]{:S(2)}, u32[]{:S(2)}) collective-permute-start(bf16[144,128]{1,0:T(8,128)(2,1)S(1)} %get-tuple-element.44), channel_id=1, source_target_pairs={{1,16},{16,1},{17,32},{32,17},{33,48},{48,33},{49,64},{64,49},{65,... | collective-permute-start | bytes 110600 | tf_op jit(solution)/shard_map/ppermute | solution.py:47
  43.2 4.8 %collective-permute-done.8.outer = bf16[144,128]{1,0:T(8,128)(2,1)S(1)} collective-permute-done((bf16[144,128]{1,0:T(8,128)(2,1)S(1)}, bf16[144,128]{1,0:T(8,128)(2,1)S(1)}, u32[]{:S(2)}, u32[]{:S(2)}) %collective-permute-start.8) | collective-permute-done | bytes 36896 | tf_op jit(solution)/shard_map/ppermute | solution.py:47
  48.1 7.0 %rest.1.both = bf16[2,6144,128]{2,1,0:T(8,128)(2,1)S(1)} custom-call(bf16[768,128]{1,0:T(8,128)(2,1)S(1)} %get-tuple-element.42.hw, bf16[144,128]{1,0:T(8,128)(2,1)S(1)} %collective-permute-done.7.inner, bf16[144,128]{1,0:T(8,128)(2,1)S(1)} %collective-permute-done.8.outer, bf16[48,128]{1,0:T(8,128)(2,1)S(1)} %collective-permute-done.5.west, ...), custom_call_target="tpu_custom_call" | custom-call | flops 3000000000 | bytes 8000000 | tf_op jit(solution)/shard_map/rest/pallas_call | solution.py:542
  55.1 0.1 slice_bitcast_fusion
  55.2 0.1 collective-permute-start.9
  55.3 3.4 %collective-permute-done.9.got = bf16[6144,128]{1,0:T(8,128)(2,1)S(1)} collective-permute-done((bf16[6144,128]{1,0:T(8,128)(2,1)S(1)}, bf16[6144,128]{1,0:T(8,128)(2,1)S(1)}, u32[]{:S(2)}, u32[]{:S(2)}) %collective-permute-start.9) | collective-permute-done | bytes 1572896 | tf_op jit(solution)/shard_map/ppermute | solution.py:660
  58.7 0.4 pair_sum.1
  59.1 32.5 %all_to_all.10.pieces = bf16[64,96,128]{2,1,0:T(8,128)(2,1)S(1)} all-to-all(bf16[64,96,128]{2,1,0:T(8,128)(2,1)S(1)} %bitcast.22), channel_id=1, replica_groups=mesh['x'=4,'core'=2,'z'=4,'yl'=2,'yh'=2] {'x','z','yl','yh'}, dimensions={0} | all-to-all | bytes 3145728 | tf_op jit(solution)/shard_map/all_to_all | solution.py:661
  91.6 0.4 spread.1
  92.1 26.6 %all_to_all.11 = bf16[64,96,128]{2,1,0:T(8,128)(2,1)S(1)} all-to-all(bf16[64,96,128]{2,1,0:T(8,128)(2,1)S(1)} %spread.1), channel_id=1, replica_groups=mesh['x'=4,'core'=2,'z'=4,'yl'=2,'yh'=2] {'x','z','yl','yh'}, dimensions={0} | all-to-all | bytes 3145728 | tf_op jit(solution)/shard_map/all_to_all | solution.py:662
  118.7 3.4 %collective-permute-start.10 = (bf16[6144,128]{1,0:T(8,128)(2,1)S(1)}, bf16[6144,128]{1,0:T(8,128)(2,1)S(1)}, u32[]{:S(2)}, u32[]{:S(2)}) collective-permute-start(bf16[6144,128]{1,0:T(8,128)(2,1)S(1)} %bitcast.20), channel_id=1, source_target_pairs={{0,16},{16,0},{1,17},{17,1},{2,18},{18,2},{3,19},{19,3},{4,20},{20... | collective-permute-start | bytes 4718600 | tf_op jit(solution)/shard_map/ppermute | solution.py:663
  122.1 1.9 %finish_own.1 = (f32[1152,128]{1,0:T(8,128)}, f32[2304,128]{1,0:T(8,128)}, f32[1152,128]{1,0:T(8,128)}, f32[128,1024]{1,0:T(8,128)}, f32[1024,512]{1,0:T(8,128)}) custom-call(bf16[6144,128]{1,0:T(8,128)(2,1)S(1)} %bitcast.21), custom_call_target="tpu_custom_call" | custom-call | flops 800000 | bytes 5000000 | tf_op jit(solution)/shard_map/finish_own/pallas_call | solution.py:598
  123.9 1.2 collective-permute-done.10.part
  125.1 2.0 %finish_other.1 = (f32[1152,128]{1,0:T(8,128)}, f32[2304,128]{1,0:T(8,128)}, f32[1152,128]{1,0:T(8,128)}, f32[128,1024]{1,0:T(8,128)}, f32[1024,512]{1,0:T(8,128)}, /*index=5*/f32[1,1]{1,0:T(1,128)}) custom-call(bf16[6144,128]{1,0:T(8,128)(2,1)S(1)} %collective-permute-done.10.part, ...), custom_call_target="tpu_custom_call", output_to_operand_aliasing={{0}: (1, {}), {1}: (2, {}), {2}: (3, {}), {3}: (4, {}), {4}... | custom-call | flops 800000 | bytes 5000000 | tf_op jit(solution)/shard_map/finish_other/pallas_call | solution.py:598
  (28 shorter events, 0.1 us)
Async XLA Ops:
  0.6 0.9 copy-start.5
  1.5 0.8 copy-start.6
  2.3 5.3 %collective-permute-start = (bf16[32,128]{1,0:T(8,128)(2,1)S(1)}, bf16[32,128]{1,0:T(8,128)(2,1)S(1)}, u32[]{:S(2)}, u32[]{:S(2)}) collective-permute-start(bf16[32,128]{1,0:T(8,128)(2,1)S(1)} %get-tuple-element.33), channel_id=1, source_target_pairs={{0,2},{2,4},{4,6},{6,8},{8,10},{10,12},{12,14},{1,3},{3,5},{5,7},{... | collective-permute-start | bytes 24584 | tf_op jit(solution)/shard_map/ppermute | solution.py:35
  6.4 4.5 %collective-permute-start.1 = (bf16[32,128]{1,0:T(8,128)(2,1)S(1)}, bf16[32,128]{1,0:T(8,128)(2,1)S(1)}, u32[]{:S(2)}, u32[]{:S(2)}) collective-permute-start(bf16[32,128]{1,0:T(8,128)(2,1)S(1)} %get-tuple-element.34), channel_id=1, source_target_pairs={{2,0},{4,2},{6,4},{8,6},{10,8},{12,10},{14,12},{3,1},{5,3},{7,5},{... | collective-permute-start | bytes 24584 | tf_op jit(solution)/shard_map/ppermute | solution.py:35
  10.9 4.7 %collective-permute-start.2 = (bf16[256,128]{1,0:T(8,128)(2,1)S(1)}, bf16[256,128]{1,0:T(8,128)(2,1)S(1)}, u32[]{:S(2)}, u32[]{:S(2)}) collective-permute-start(bf16[256,128]{1,0:T(8,128)(2,1)S(1)} %edge_rows.1.mine), channel_id=1, source_target_pairs={{0,1},{1,0},{16,17},{17,16},{32,33},{33,32},{48,49},{49,48},{64,65... | collective-permute-start | bytes 196616 | tf_op jit(solution)/shard_map/ppermute | solution.py:40
  14.5 9.2 %copy-start.11 = (s32[1,1,256]{2,1,0:T(1,128)S(1)}, s32[1,1,256]{2,1,0:T(1,128)}, u32[]{:S(2)}) copy-start(s32[1,1,256]{2,1,0:T(1,128)} %param.24) | copy-start | bytes 3076
  14.5 12.4 %copy-start = (bf16[3,3,512,128]{3,2,1,0:T(8,128)(2,1)S(1)}, bf16[3,3,512,128]{3,2,1,0:T(8,128)(2,1)}, u32[]{:S(2)}) copy-start(bf16[3,3,512,128]{3,2,1,0:T(8,128)(2,1)} %param.18) | copy-start | bytes 3538948
  14.5 12.4 %copy-start.2 = (bf16[3,3,128,128]{3,2,1,0:T(8,128)(2,1)S(1)}, bf16[3,3,128,128]{3,2,1,0:T(8,128)(2,1)}, u32[]{:S(2)}) copy-start(bf16[3,3,128,128]{3,2,1,0:T(8,128)(2,1)} %param.17) | copy-start | bytes 884740
  14.5 12.4 %copy-start.7 = (bf16[34,10]{0,1:T(8,128)(2,1)S(1)}, bf16[34,10]{0,1:T(8,128)(2,1)}, u32[]{:S(2)}) copy-start(bf16[34,10]{0,1:T(8,128)(2,1)} %param.15) | copy-start | bytes 2044
  14.6 12.4 %copy-start.8 = (bf16[34,10]{0,1:T(8,128)(2,1)S(1)}, bf16[34,10]{0,1:T(8,128)(2,1)}, u32[]{:S(2)}) copy-start(bf16[34,10]{0,1:T(8,128)(2,1)} %param.16) | copy-start | bytes 2044
  14.6 12.4 %copy-start.9 = (s32[1,1,256]{2,1,0:T(1,128)S(1)}, s32[1,1,256]{2,1,0:T(1,128)}, u32[]{:S(2)}) copy-start(s32[1,1,256]{2,1,0:T(1,128)} %param.22) | copy-start | bytes 3076
  15.6 8.1 %collective-permute-start.3 = (bf16[112,128]{1,0:T(8,128)(2,1)S(1)}, bf16[112,128]{1,0:T(8,128)(2,1)S(1)}, u32[]{:S(2)}, u32[]{:S(2)}) collective-permute-start(bf16[112,128]{1,0:T(8,128)(2,1)S(1)} %get-tuple-element.36), channel_id=1, source_target_pairs={{0,16},{16,32},{32,48},{48,64},{64,80},{80,96},{96,112},{1,17},{17... | collective-permute-start | bytes 86024 | tf_op jit(solution)/shard_map/ppermute | solution.py:35
  21.8 5.2 %collective-permute-start.4 = (bf16[112,128]{1,0:T(8,128)(2,1)S(1)}, bf16[112,128]{1,0:T(8,128)(2,1)S(1)}, u32[]{:S(2)}, u32[]{:S(2)}) collective-permute-start(bf16[112,128]{1,0:T(8,128)(2,1)S(1)} %get-tuple-element.37), channel_id=1, source_target_pairs={{16,0},{32,16},{48,32},{64,48},{80,64},{96,80},{112,96},{17,1},{33... | collective-permute-start | bytes 86024 | tf_op jit(solution)/shard_map/ppermute | solution.py:35
  29.4 5.6 %collective-permute-start.5 = (bf16[48,128]{1,0:T(8,128)(2,1)S(1)}, bf16[48,128]{1,0:T(8,128)(2,1)S(1)}, u32[]{:S(2)}, u32[]{:S(2)}) collective-permute-start(bf16[48,128]{1,0:T(8,128)(2,1)S(1)} %get-tuple-element.40), channel_id=1, source_target_pairs={{0,2},{2,4},{4,6},{6,8},{8,10},{10,12},{12,14},{1,3},{3,5},{5,7},{... | collective-permute-start | bytes 36872 | tf_op jit(solution)/shard_map/ppermute | solution.py:35
  33.8 4.4 %collective-permute-start.6 = (bf16[48,128]{1,0:T(8,128)(2,1)S(1)}, bf16[48,128]{1,0:T(8,128)(2,1)S(1)}, u32[]{:S(2)}, u32[]{:S(2)}) collective-permute-start(bf16[48,128]{1,0:T(8,128)(2,1)S(1)} %get-tuple-element.41), channel_id=1, source_target_pairs={{2,0},{4,2},{6,4},{8,6},{10,8},{12,10},{14,12},{3,1},{5,3},{7,5},{... | collective-permute-start | bytes 36872 | tf_op jit(solution)/shard_map/ppermute | solution.py:35
  38.2 9.9 %copy-start.1 = (bf16[1024,512]{1,0:T(8,128)(2,1)S(1)}, bf16[1024,512]{1,0:T(8,128)(2,1)}, u32[]{:S(2)}) copy-start(bf16[1024,512]{1,0:T(8,128)(2,1)} %binw.1) | copy-start | bytes 3145732
  38.2 9.9 %copy-start.3 = (bf16[3,3,128,128]{3,2,1,0:T(8,128)(2,1)S(1)}, bf16[3,3,128,128]{3,2,1,0:T(8,128)(2,1)}, u32[]{:S(2)}) copy-start(bf16[3,3,128,128]{3,2,1,0:T(8,128)(2,1)} %param.19) | copy-start | bytes 884740
  38.2 9.9 %copy-start.4 = (bf16[128,1024]{1,0:T(8,128)(2,1)S(1)}, bf16[128,1024]{1,0:T(8,128)(2,1)}, u32[]{:S(2)}) copy-start(bf16[128,1024]{1,0:T(8,128)(2,1)} %hid.1) | copy-start | bytes 786436
  38.2 9.9 %copy-start.10 = (s32[1,128]{1,0:T(1,128)S(1)}, s32[1,128]{1,0:T(1,128)}, u32[]{:S(2)}) copy-start(s32[1,128]{1,0:T(1,128)} %constant.8.ring_l) | copy-start | bytes 1540
  38.3 4.9 %collective-permute-start.7 = (bf16[144,128]{1,0:T(8,128)(2,1)S(1)}, bf16[144,128]{1,0:T(8,128)(2,1)S(1)}, u32[]{:S(2)}, u32[]{:S(2)}) collective-permute-start(bf16[144,128]{1,0:T(8,128)(2,1)S(1)} %get-tuple-element.43), channel_id=1, source_target_pairs={{0,1},{1,0},{16,17},{17,16},{32,33},{33,32},{48,49},{49,48},{64,65... | collective-permute-start | bytes 110600 | tf_op jit(solution)/shard_map/ppermute | solution.py:40
  41.3 6.8 %collective-permute-start.8 = (bf16[144,128]{1,0:T(8,128)(2,1)S(1)}, bf16[144,128]{1,0:T(8,128)(2,1)S(1)}, u32[]{:S(2)}, u32[]{:S(2)}) collective-permute-start(bf16[144,128]{1,0:T(8,128)(2,1)S(1)} %get-tuple-element.44), channel_id=1, source_target_pairs={{1,16},{16,1},{17,32},{32,17},{33,48},{48,33},{49,64},{64,49},{65,... | collective-permute-start | bytes 110600 | tf_op jit(solution)/shard_map/ppermute | solution.py:47
  55.2 3.5 %collective-permute-start.9 = (bf16[6144,128]{1,0:T(8,128)(2,1)S(1)}, bf16[6144,128]{1,0:T(8,128)(2,1)S(1)}, u32[]{:S(2)}, u32[]{:S(2)}) collective-permute-start(bf16[6144,128]{1,0:T(8,128)(2,1)S(1)} %slice_bitcast_fusion), channel_id=1, source_target_pairs={{0,16},{16,0},{1,17},{17,1},{2,18},{18,2},{3,19},{19,3},{4,20},{20... | collective-permute-start | bytes 4718600 | tf_op jit(solution)/shard_map/ppermute | solution.py:660
  118.7 6.4 %collective-permute-start.10 = (bf16[6144,128]{1,0:T(8,128)(2,1)S(1)}, bf16[6144,128]{1,0:T(8,128)(2,1)S(1)}, u32[]{:S(2)}, u32[]{:S(2)}) collective-permute-start(bf16[6144,128]{1,0:T(8,128)(2,1)S(1)} %bitcast.20), channel_id=1, source_target_pairs={{0,16},{16,0},{1,17},{17,1},{2,18},{18,2},{3,19},{19,3},{4,20},{20... | collective-permute-start | bytes 4718600 | tf_op jit(solution)/shard_map/ppermute | solution.py:663

commit v7 on v6

--- a/solution.py
+++ b/solution.py
@@ -150,15 +150,48 @@
     return jnp.sum(jnp.where(eye, row.astype(F32), 0.0), axis=1, keepdims=True)
 
 
+def plan_kernel(rows_in, cols_in, idx_l, ring_l, lab_l, after, kron, left, digs, pick, back, labs, rmat, cmat):
+    half = lax.axis_index("yh")
+    row0 = (2 * lax.axis_index("x") + lax.axis_index("core")) * 32
+    col0 = (2 * lax.axis_index("z") + lax.axis_index("yl")) * COLS
+    rmat[...] = jnp.zeros_like(rmat)
+    cmat[...] = jnp.zeros_like(cmat)
+    grow = row0 + iota((10, 34), 1) - 1
+    gcol = col0 + iota((10, 34), 1) - 1
+    rmat[0:10, 0:34] = jnp.where((grow >= 0) & (grow < 256), rows_in[...].astype(F32), 0.0)
+    cmat[0:10, 0:34] = jnp.where((gcol >= 0) & (gcol < 256), cols_in[...].astype(F32), 0.0)
+    chosen = (iota((288, C), 0) >> 4) + 16 * half == iota((288, C), 1)
+    side = dot_t(chosen.astype(F32).astype(BF), rmat[...].astype(BF)).astype(BF)
+    spread = (iota((16, 160), 0) == iota((16, 160), 1) >> 4).astype(F32).astype(BF)
+    full = dot(side, spread)
+    same = (iota((288, 160), 0) & 15) == (iota((288, 160), 1) & 15)
+    kron[...] = jnp.where(same, full, 0.0).astype(BF)
+    cell = iota((96, C), 0)
+    chosen = (cell & 31) + (cell >> 5) == iota((96, C), 1)
+    left[...] = dot_t(chosen.astype(F32).astype(BF), cmat[...].astype(BF)).astype(BF)
+    code = lab_l[...] + 1
+    kind = iota((C, CAP), 0)
+    digit = jnp.where(kind == 0, code >> 5, jnp.where(kind == 1, code & 31, 0))
+    named = (idx_l[...] == iota((512, CAP), 0)).astype(F32).astype(BF)
+    digs[...] = dot_t(named, digit.astype(F32).astype(BF)).astype(BF)
+    slot_l = idx_l[...] + 16 * (idx_l[...] >> 5) + WIDE + 1
+    slot_s = column(slot_l).astype(jnp.int32)
+    ring_s = column(ring_l[...]).astype(jnp.int32)
+    pick[0:CAP, :] = (slot_s == iota((CAP, EXT), 1)).astype(F32).astype(BF)
+    pick[CAP:, :] = (ring_s == iota((SLOTS - CAP, EXT), 1)).astype(F32).astype(BF)
+    cell = iota((EXT, CAP), 0)
+    back[:, 0:CAP] = (slot_l == cell).astype(F32).astype(BF)
+    back[:, CAP:] = (ring_l[...] == cell[:, :128]).astype(F32).astype(BF)
+    labs[...] = column(lab_l[...]).astype(jnp.int32)
+
+
 def first_conv_kernel(
-    rows_in, cols_in, fine, west, east, mine, inner, north, south, w_fine, w_ctx, idx_l, lab_l,
+    kron, left, dig, fine, west, east, mine, inner, north, south, w_fine, w_ctx,
     xc, h1, sg, last, first, digs,
-    fscr, mid, block, hscr, dscr, rmat, cmat, xs, pre, spot,
+    fscr, mid, block, hscr, dscr, xs, pre, spot,
 ):
     spot[0] = lax.axis_index("yh")
-    spot[1] = (2 * lax.axis_index("x") + lax.axis_index("core")) * 32
-    spot[2] = (2 * lax.axis_index("z") + lax.axis_index("yl")) * COLS
-    half, row0, col0 = spot[0], spot[1], spot[2]
+    half = spot[0]
     lower = half == 1
     for i in range(ROWS):
         at = WIDE * (i + 1) + 1
@@ -173,12 +206,6 @@
         for dx in range(3):
             at = WIDE * i + dx
             xc[32 * i : 32 * i + 32, 128 * dx : 128 * dx + 128] = fscr[at : at + 32, :].astype(BF)
-    rmat[...] = jnp.zeros_like(rmat)
-    cmat[...] = jnp.zeros_like(cmat)
-    grow = row0 + iota((10, 34), 1) - 1
-    gcol = col0 + iota((10, 34), 1) - 1
-    rmat[0:10, 0:34] = jnp.where((grow >= 0) & (grow < 256), rows_in[...].astype(F32), 0.0)
-    cmat[0:10, 0:34] = jnp.where((gcol >= 0) & (gcol < 256), cols_in[...].astype(F32), 0.0)
     xs[160:, :] = jnp.zeros((16, C), F32)
     for n, part, got in ((0, half, mine), (32, 1 - half, inner)):
         xs[0:160, :] = got[CTX:, :].astype(F32)
@@ -190,18 +217,9 @@
                 at = 80 * side + 10 * a
                 block[16 + 16 * a : 32 + 16 * a, lanes] = xs[at : at + 16, :].astype(BF)
             block[144:160, lanes] = south[sl, :]
-    pick = (iota((288, C), 0) >> 4) + 16 * half == iota((288, C), 1)
-    left = dot_t(pick.astype(F32).astype(BF), rmat[...].astype(BF)).astype(BF)
-    spread = (iota((16, 160), 0) == iota((16, 160), 1) >> 4).astype(F32).astype(BF)
-    full = dot(left, spread)
-    same = (iota((288, 160), 0) & 15) == (iota((288, 160), 1) & 15)
-    kron = jnp.where(same, full, 0.0).astype(BF)
-    mid[...] = dot(kron, block[...]).astype(BF)
-    cell = iota((96, C), 0)
-    pick = (cell & 31) + (cell >> 5) == iota((96, C), 1)
-    left = dot_t(pick.astype(F32).astype(BF), cmat[...].astype(BF)).astype(BF)
+    mid[...] = dot(kron[...], block[...]).astype(BF)
     for i in range(ROWS + 2):
-        wide = dot(left, mid[16 * i : 16 * i + 16, :]).astype(BF)
+        wide = dot(left[...], mid[16 * i : 16 * i + 16, :]).astype(BF)
         for dx in range(3):
             xc[32 * i : 32 * i + 32, 384 + 512 * dx : 896 + 512 * dx] = wide[32 * dx : 32 * dx + 32]
     wf = jnp.concatenate([w_fine[384 * dy : 384 * dy + 384, :] for dy in range(3)], axis=1)
@@ -213,12 +231,7 @@
     h1[...] = h
     hscr[...] = h.astype(F32)
     sg[...] = s * (1.0 + acc * (1.0 - s))
-    code = lab_l[...] + 1
-    kind = iota((C, CAP), 0)
-    digit = jnp.where(kind == 0, code >> 5, jnp.where(kind == 1, code & 31, 0))
-    digit = digit.astype(F32).astype(BF)
-    named = (idx_l[...] == iota((512, CAP), 0)).astype(F32).astype(BF)
-    dscr[...] = dot_t(named, digit)
+    dscr[...] = dig[...].astype(F32)
     digs[0:32, :] = dscr[0:32, :].astype(BF)
     digs[32:64, :] = dscr[480:512, :].astype(BF)
     for out, c0, c1, cd in ((last, COLS - 2, COLS - 1, COLS - 1), (first, 0, 1, 0)):
@@ -251,7 +264,7 @@
 
 
 def rest_kernel(
-    hw, inner, outer, west, east, xc, sg1, idx_l, ring_l, lab_l, cw, hid, binw,
+    hw, inner, outer, west, east, xc, sg1, pick, back, labs_s, cw, hid, binw,
     out,
     hp, hx, sg2, h2, rows_s, act, sgz, dl, dz, gscr, gx, g2w, g1w, pre, spot,
 ):
@@ -269,14 +282,9 @@
     gx[17 * WIDE : 18 * WIDE, :] = after[96:144]
     gx[pl.ds(WIDE, 16, stride=WIDE), :] = west[32:48, :].astype(F32)
     gx[pl.ds(WIDE + 33, 16, stride=WIDE), :] = east[32:48, :].astype(F32)
-    slot_l = idx_l[...] + 16 * (idx_l[...] >> 5) + WIDE + 1
-    slot_s = column(slot_l).astype(jnp.int32)
-    ring_s = column(ring_l[...]).astype(jnp.int32)
-    ring_pick = (ring_s == iota((128, EXT), 1)).astype(F32).astype(BF)
-    code = dot(ring_pick, gx[0:EXT, :].astype(BF))
+    code = dot(pick[CAP:, :], gx[0:EXT, :].astype(BF))
     lane = iota((128, C), 1)
     code = jnp.sum(jnp.where(lane == 0, 32.0 * code, jnp.where(lane == 1, code, 0.0)), axis=1, keepdims=True)
-    own_lab = column(lab_l[...]).astype(jnp.int32)
     for dx in range(3):
         hx[:, 128 * dx : 128 * dx + 128] = hp[dx : dx + 992, :].astype(BF)
     forth = jnp.concatenate([cw[384 * dy : 384 * dy + 384, :] for dy in range(3)], axis=1)
@@ -285,8 +293,7 @@
     s = jax.nn.sigmoid(acc)
     h2[...] = (acc * s).astype(BF)
     sg2[...] = s * (1.0 + acc * (1.0 - s))
-    own_pick = (slot_s == iota((CAP, EXT), 1)).astype(F32).astype(BF)
-    rows = dot(jnp.concatenate([own_pick, ring_pick], axis=0), h2[...]).astype(BF)
+    rows = dot(pick[...], h2[...]).astype(BF)
     rows_s[...] = rows
     z = dot(rows, hid[...])
     s = jax.nn.sigmoid(z)
@@ -295,7 +302,7 @@
     logits = dot(act[...], binw[...])
     peak = jnp.max(logits, axis=1, keepdims=True)
     top = peak + jnp.log(jnp.sum(jnp.exp(logits - peak), axis=1, keepdims=True))
-    labs = jnp.concatenate([own_lab, code.astype(jnp.int32) - 1], axis=0)
+    labs = jnp.concatenate([labs_s[...], code.astype(jnp.int32) - 1], axis=0)
     hit = labs == iota((SLOTS, BINS), 1)
     live = (labs >= 0).astype(F32)
     picked = jnp.sum(jnp.where(hit, logits, 0.0), axis=1, keepdims=True)
@@ -320,11 +327,7 @@
     for n in range(2):
         out[n, STAT : STAT + 16, :] = stat_rows(stats, (16, C)).astype(BF)
         out[n, STAT + 16 : KEEP, :] = jnp.zeros((KEEP - STAT - 16, C), BF)
-    cell = iota((EXT, CAP), 0)
-    back = jnp.concatenate(
-        [(slot_l == cell).astype(F32), (ring_l[...] == cell[:, :128]).astype(F32)], axis=1
-    ).astype(BF)
-    both = dot(back, gscr[...])
+    both = dot(back[...], gscr[...])
     gx[0:EXT, :] = (both[:, :128] + both[:, 128:]) * sg2[...]
 
     g2w[...] = jnp.zeros_like(g2w)
@@ -343,11 +346,11 @@
             at = WIDE * i + 2 - dx
             hx[32 * i : 32 * i + 32, 128 * dx : 128 * dx + 128] = gx[at : at + 32, :].astype(BF)
     g1w[...] = jnp.zeros_like(g1w)
-    back = [
+    flipped = [
         jnp.concatenate([cw[384 * dy + 128 * dx : 384 * dy + 128 * dx + 128, :] for dx in range(3)], axis=1)
         for dy in range(3)
     ]
-    pre[0:576, :] = dot_t(hx[0:576, :], jnp.concatenate(back, axis=0))
+    pre[0:576, :] = dot_t(hx[0:576, :], jnp.concatenate(flipped, axis=0))
     acc = sum(pre[64 - 32 * dy : 576 - 32 * dy, 128 * dy : 128 * dy + 128] for dy in range(3))
     g1 = (acc * sg1[...]).astype(BF)
     for dy in range(3):
@@ -497,6 +500,20 @@
     )(*args)
 
 
+def plan(*args):
+    shapes = [((288, 160), BF), ((96, 16), BF), ((512, C), BF), ((SLOTS, EXT), BF), ((EXT, SLOTS), BF)]
+    return pl.pallas_call(
+        plan_kernel,
+        out_shape=tuple(sds(*s) for s in shapes) + (sds((CAP, 1), jnp.int32),),
+        in_specs=vmem(len(args)),
+        out_specs=tuple(vmem(6)),
+        scratch_shapes=[pltpu.VMEM((16, C), F32), pltpu.VMEM((16, C), F32)],
+        compiler_params=limit(8),
+        cost_estimate=BUSY,
+        name="plan",
+    )(*args)
+
+
 def first_conv(*args):
     v = pltpu.VMEM
     edge = sds((48, C), BF)
@@ -511,8 +528,6 @@
             v((160, K), BF),
             v((512, C), F32),
             v((512, C), F32),
-            v((16, C), F32),
-            v((16, C), F32),
             v((176, C), F32),
             v((576, 384), F32),
             pltpu.SMEM((4,), jnp.int32),
@@ -636,14 +651,15 @@
     last, first, fine, context = edge_cols(fine.reshape(512, C), context.reshape(64, HALF))
     west = shift(last, GX, 8, 1)
     east = shift(first, GX, 8, -1)
+    kron, left, dig, pick, back, labs = plan(interp_rows.T, interp_cols.T, idx, ring[None, :], lab, last)
     mine = edge_rows(fine, context, west, east)
     inner = side_swap(mine)
     down, up = ctx_rows(mine, inner)
     north = shift(down, GY, 8, 1)
     south = shift(up, GY, 8, -1)
     xc, h_one, sg1, last, first, digs = first_conv(
-        interp_rows.T, interp_cols.T, fine, west, east, mine, inner, north, south,
-        fine_weight.reshape(1152, C), ctx_weight.reshape(4608, C), idx, lab,
+        kron, left, dig, fine, west, east, mine, inner, north, south,
+        fine_weight.reshape(1152, C), ctx_weight.reshape(4608, C),
     )
 
     west = shift(last, GX, 8, 1)
@@ -652,7 +668,7 @@
     outer = outer_swap(outer)
     inner = side_swap(inner)
     both = rest(
-        wide, inner, outer, west, east, xc, sg1, idx, ring[None, :], lab,
+        wide, inner, outer, west, east, xc, sg1, pick, back, labs,
         conv_weight.reshape(1152, C), hidden_weight, bin_weight,
     )
 

time: 128 us -> 128 us (level)
  blocking collectives: 59.1 us -> 60.8 us
  waiting for transfers between devices: 19.9 us -> 18.4 us
    ppermute x6, waiting for transfers between devices: 9.52 us -> 7.3 us  [shift(): return lax.ppermute(x, axis, pairs)]
    all_to_all x1, blocking collectives: 32.5 us -> 34.2 us  [local(): lax.all_to_all(pair.reshape(PEERS, SHARD, C), PLANE, 0, 0, tiled=True)]
  transfers between devices with their start and end apart: 11 -> 11, of which waited for: 7 -> 7; matrix products, arithmetic and copies ran while one was open for 0% -> 0% of each run, Pallas kernels for 1% -> 2%
where the time goes in v7:
time: 128 us; the launch traced here: 127 us
  blocking collectives  60.8 us (48%)
  starting transfers between devices  30.4 us (24%)
  waiting for transfers between devices  18.4 us (14%)
  Pallas kernels  14.3 us (11%)
  local copies, waits for them, and re-layouts  1.81 us (1%)
  between operations  1.53 us (1%)
    all_to_all x1, blocking collectives, local(): lax.all_to_all(pair.reshape(PEERS, SHARD, C), PLANE, 0, 0, tiled=True)  34.2 us
    all_to_all x1, blocking collectives, local(): lax.all_to_all(spread(pieces), PLANE, 0, 0, tiled=True).reshape(KEEP, C)  26.6 us
    ppermute x6, starting transfers between devices, shift(): return lax.ppermute(x, axis, pairs)  19.2 us
    ppermute x6, waiting for transfers between devices, shift(): return lax.ppermute(x, axis, pairs)  7.3 us
    pallas_call x1, Pallas kernels, rest(): pl.pallas_call(rest_kernel, out_shape=sds((2, KEEP, C), BF), in_specs=vme...  6.8 us
    ppermute x2, starting transfers between devices, side_swap(): return lax.ppermute(x, TALL, own)  5.85 us
    ppermute x1, waiting for transfers between devices, outer_swap(): return lax.ppermute(x, TALL, pairs)  4.84 us
    pallas_call x2, Pallas kernels, finish(): pl.pallas_call(functools.partial(finish_kernel, second), out_shape=tuple(...  3.83 us
  transfers between devices with their start and end apart: 11, of which 7 were waited for; matrix products, arithmetic and copies ran while one was open for 0% of the time, Pallas kernels for 2%

profile of v7, /device:TPU:1, one launch (start us, length us, event | category | flops | bytes accessed | tf_op | source)
XLA Modules:
  0.0 127.2 jit_solution(5631812431624313806)
XLA Ops:
  0.6 0.9 copy-done.5
  1.5 0.8 copy-done.6
  2.3 1.3 %collective-permute-start.1 = (bf16[32,128]{1,0:T(8,128)(2,1)S(1)}, bf16[32,128]{1,0:T(8,128)(2,1)S(1)}, u32[]{:S(2)}, u32[]{:S(2)}) collective-permute-start(bf16[32,128]{1,0:T(8,128)(2,1)S(1)} %get-tuple-element.43), channel_id=1, source_target_pairs={{2,0},{4,2},{6,4},{8,6},{10,8},{12,10},{14,12},{3,1},{5,3},{7,5},{... | collective-permute-start | bytes 24584 | tf_op jit(solution)/shard_map/ppermute | solution.py:35
  3.6 4.7 %collective-permute-start = (bf16[32,128]{1,0:T(8,128)(2,1)S(1)}, bf16[32,128]{1,0:T(8,128)(2,1)S(1)}, u32[]{:S(2)}, u32[]{:S(2)}) collective-permute-start(bf16[32,128]{1,0:T(8,128)(2,1)S(1)} %get-tuple-element.38.after), channel_id=1, source_target_pairs={{0,2},{2,4},{4,6},{6,8},{8,10},{10,12},{12,14},{1,3},{3,5},{5,7},{... | collective-permute-start | bytes 24584 | tf_op jit(solution)/shard_map/ppermute | solution.py:35
  9.0 0.1 collective-permute-done.west
  9.1 3.2 %collective-permute-start.2 = (bf16[256,128]{1,0:T(8,128)(2,1)S(1)}, bf16[256,128]{1,0:T(8,128)(2,1)S(1)}, u32[]{:S(2)}, u32[]{:S(2)}) collective-permute-start(bf16[256,128]{1,0:T(8,128)(2,1)S(1)} %edge_rows.1.mine), channel_id=1, source_target_pairs={{0,1},{1,0},{16,17},{17,16},{32,33},{33,32},{48,49},{49,48},{64,65... | collective-permute-start | bytes 196616 | tf_op jit(solution)/shard_map/ppermute | solution.py:40
  12.3 0.0 copy-start.10
  12.3 1.7 %collective-permute-done.2.inner = bf16[256,128]{1,0:T(8,128)(2,1)S(1)} collective-permute-done((bf16[256,128]{1,0:T(8,128)(2,1)S(1)}, bf16[256,128]{1,0:T(8,128)(2,1)S(1)}, u32[]{:S(2)}, u32[]{:S(2)}) %collective-permute-start.2) | collective-permute-done | bytes 65568 | tf_op jit(solution)/shard_map/ppermute | solution.py:40
  14.0 5.9 %collective-permute-start.3 = (bf16[112,128]{1,0:T(8,128)(2,1)S(1)}, bf16[112,128]{1,0:T(8,128)(2,1)S(1)}, u32[]{:S(2)}, u32[]{:S(2)}) collective-permute-start(bf16[112,128]{1,0:T(8,128)(2,1)S(1)} %get-tuple-element.45), channel_id=1, source_target_pairs={{0,16},{16,32},{32,48},{48,64},{64,80},{80,96},{96,112},{1,17},{17... | collective-permute-start | bytes 86024 | tf_op jit(solution)/shard_map/ppermute | solution.py:35
  19.9 1.9 %collective-permute-start.4 = (bf16[112,128]{1,0:T(8,128)(2,1)S(1)}, bf16[112,128]{1,0:T(8,128)(2,1)S(1)}, u32[]{:S(2)}, u32[]{:S(2)}) collective-permute-start(bf16[112,128]{1,0:T(8,128)(2,1)S(1)} %get-tuple-element.46), channel_id=1, source_target_pairs={{16,0},{32,16},{48,32},{64,48},{80,64},{96,80},{112,96},{17,1},{33... | collective-permute-start | bytes 86024 | tf_op jit(solution)/shard_map/ppermute | solution.py:35
  21.9 0.6 plan.1
  22.5 2.6 %collective-permute-done.4.south = bf16[112,128]{1,0:T(8,128)(2,1)S(1)} collective-permute-done((bf16[112,128]{1,0:T(8,128)(2,1)S(1)}, bf16[112,128]{1,0:T(8,128)(2,1)S(1)}, u32[]{:S(2)}, u32[]{:S(2)}) %collective-permute-start.4) | collective-permute-done | bytes 28704 | tf_op jit(solution)/shard_map/ppermute | solution.py:35
  25.1 2.1 %first_conv.1 = (bf16[576,1920]{1,0:T(8,128)(2,1)S(1)}, bf16[512,128]{1,0:T(8,128)(2,1)S(1)}, f32[512,128]{1,0:T(8,128)S(1)}, bf16[48,128]{1,0:T(8,128)(2,1)S(1)...) custom-call(bf16[288,160]{1,0:T(8,128)(2,1)S(1)} %get-tuple-element.39.kron, ...), custom_call_target="tpu_custom_call" | custom-call | flops 900000000 | bytes 5000000 | tf_op jit(solution)/shard_map/first_conv/pallas_call | solution.py:520
  27.2 4.1 %collective-permute-start.5 = (bf16[48,128]{1,0:T(8,128)(2,1)S(1)}, bf16[48,128]{1,0:T(8,128)(2,1)S(1)}, u32[]{:S(2)}, u32[]{:S(2)}) collective-permute-start(bf16[48,128]{1,0:T(8,128)(2,1)S(1)} %get-tuple-element.49), channel_id=1, source_target_pairs={{0,2},{2,4},{4,6},{6,8},{8,10},{10,12},{12,14},{1,3},{3,5},{5,7},{... | collective-permute-start | bytes 36872 | tf_op jit(solution)/shard_map/ppermute | solution.py:35
  31.3 1.3 %collective-permute-start.6 = (bf16[48,128]{1,0:T(8,128)(2,1)S(1)}, bf16[48,128]{1,0:T(8,128)(2,1)S(1)}, u32[]{:S(2)}, u32[]{:S(2)}) collective-permute-start(bf16[48,128]{1,0:T(8,128)(2,1)S(1)} %get-tuple-element.50), channel_id=1, source_target_pairs={{2,0},{4,2},{6,4},{8,6},{10,8},{12,10},{14,12},{3,1},{5,3},{7,5},{... | collective-permute-start | bytes 36872 | tf_op jit(solution)/shard_map/ppermute | solution.py:35
  32.7 4.6 %collective-permute-done.6.east = bf16[48,128]{1,0:T(8,128)(2,1)S(1)} collective-permute-done((bf16[48,128]{1,0:T(8,128)(2,1)S(1)}, bf16[48,128]{1,0:T(8,128)(2,1)S(1)}, u32[]{:S(2)}, u32[]{:S(2)}) %collective-permute-start.6) | collective-permute-done | bytes 12320 | tf_op jit(solution)/shard_map/ppermute | solution.py:35
  37.2 0.1 h_rows.1
  37.3 2.7 %collective-permute-start.7 = (bf16[144,128]{1,0:T(8,128)(2,1)S(1)}, bf16[144,128]{1,0:T(8,128)(2,1)S(1)}, u32[]{:S(2)}, u32[]{:S(2)}) collective-permute-start(bf16[144,128]{1,0:T(8,128)(2,1)S(1)} %get-tuple-element.52), channel_id=1, source_target_pairs={{0,1},{1,0},{16,17},{17,16},{32,33},{33,32},{48,49},{49,48},{64,65... | collective-permute-start | bytes 110600 | tf_op jit(solution)/shard_map/ppermute | solution.py:40
  40.0 1.9 %collective-permute-start.8 = (bf16[144,128]{1,0:T(8,128)(2,1)S(1)}, bf16[144,128]{1,0:T(8,128)(2,1)S(1)}, u32[]{:S(2)}, u32[]{:S(2)}) collective-permute-start(bf16[144,128]{1,0:T(8,128)(2,1)S(1)} %get-tuple-element.53), channel_id=1, source_target_pairs={{1,16},{16,1},{17,32},{32,17},{33,48},{48,33},{49,64},{64,49},{65,... | collective-permute-start | bytes 110600 | tf_op jit(solution)/shard_map/ppermute | solution.py:47
  42.0 4.8 %collective-permute-done.8.outer = bf16[144,128]{1,0:T(8,128)(2,1)S(1)} collective-permute-done((bf16[144,128]{1,0:T(8,128)(2,1)S(1)}, bf16[144,128]{1,0:T(8,128)(2,1)S(1)}, u32[]{:S(2)}, u32[]{:S(2)}) %collective-permute-start.8) | collective-permute-done | bytes 36896 | tf_op jit(solution)/shard_map/ppermute | solution.py:47
  46.8 6.8 %rest.1.both = bf16[2,6144,128]{2,1,0:T(8,128)(2,1)S(1)} custom-call(bf16[768,128]{1,0:T(8,128)(2,1)S(1)} %get-tuple-element.51.hw, bf16[144,128]{1,0:T(8,128)(2,1)S(1)} %collective-permute-done.7.inner, bf16[144,128]{1,0:T(8,128)(2,1)S(1)} %collective-permute-done.8.outer, bf16[48,128]{1,0:T(8,128)(2,1)S(1)} %collective-permute-done.5.west, ...), custom_call_target="tpu_custom_call" | custom-call | flops 3000000000 | bytes 8000000 | tf_op jit(solution)/shard_map/rest/pallas_call | solution.py:557
  53.6 0.1 slice_bitcast_fusion
  53.7 0.1 collective-permute-start.9
  53.8 3.4 %collective-permute-done.9.got = bf16[6144,128]{1,0:T(8,128)(2,1)S(1)} collective-permute-done((bf16[6144,128]{1,0:T(8,128)(2,1)S(1)}, bf16[6144,128]{1,0:T(8,128)(2,1)S(1)}, u32[]{:S(2)}, u32[]{:S(2)}) %collective-permute-start.9) | collective-permute-done | bytes 1572896 | tf_op jit(solution)/shard_map/ppermute | solution.py:676
  57.2 0.4 pair_sum.1
  57.6 34.2 %all_to_all.10.pieces = bf16[64,96,128]{2,1,0:T(8,128)(2,1)S(1)} all-to-all(bf16[64,96,128]{2,1,0:T(8,128)(2,1)S(1)} %bitcast.22), channel_id=1, replica_groups=mesh['x'=4,'core'=2,'z'=4,'yl'=2,'yh'=2] {'x','z','yl','yh'}, dimensions={0} | all-to-all | bytes 3145728 | tf_op jit(solution)/shard_map/all_to_all | solution.py:677
  91.8 0.4 spread.1
  92.2 26.6 %all_to_all.11 = bf16[64,96,128]{2,1,0:T(8,128)(2,1)S(1)} all-to-all(bf16[64,96,128]{2,1,0:T(8,128)(2,1)S(1)} %spread.1), channel_id=1, replica_groups=mesh['x'=4,'core'=2,'z'=4,'yl'=2,'yh'=2] {'x','z','yl','yh'}, dimensions={0} | all-to-all | bytes 3145728 | tf_op jit(solution)/shard_map/all_to_all | solution.py:678
  118.8 3.4 %collective-permute-start.10 = (bf16[6144,128]{1,0:T(8,128)(2,1)S(1)}, bf16[6144,128]{1,0:T(8,128)(2,1)S(1)}, u32[]{:S(2)}, u32[]{:S(2)}) collective-permute-start(bf16[6144,128]{1,0:T(8,128)(2,1)S(1)} %bitcast.20), channel_id=1, source_target_pairs={{0,16},{16,0},{1,17},{17,1},{2,18},{18,2},{3,19},{19,3},{4,20},{20... | collective-permute-start | bytes 4718600 | tf_op jit(solution)/shard_map/ppermute | solution.py:679
  122.2 1.9 %finish_own.1 = (f32[1152,128]{1,0:T(8,128)}, f32[2304,128]{1,0:T(8,128)}, f32[1152,128]{1,0:T(8,128)}, f32[128,1024]{1,0:T(8,128)}, f32[1024,512]{1,0:T(8,128)}) custom-call(bf16[6144,128]{1,0:T(8,128)(2,1)S(1)} %bitcast.21), custom_call_target="tpu_custom_call" | custom-call | flops 800000 | bytes 5000000 | tf_op jit(solution)/shard_map/finish_own/pallas_call | solution.py:613
  124.1 1.2 collective-permute-done.10.part
  125.2 2.0 %finish_other.1 = (f32[1152,128]{1,0:T(8,128)}, f32[2304,128]{1,0:T(8,128)}, f32[1152,128]{1,0:T(8,128)}, f32[128,1024]{1,0:T(8,128)}, f32[1024,512]{1,0:T(8,128)}, /*index=5*/f32[1,1]{1,0:T(1,128)}) custom-call(bf16[6144,128]{1,0:T(8,128)(2,1)S(1)} %collective-permute-done.10.part, ...), custom_call_target="tpu_custom_call", output_to_operand_aliasing={{0}: (1, {}), {1}: (2, {}), {2}: (3, {}), {3}: (4, {}), {4}... | custom-call | flops 800000 | bytes 5000000 | tf_op jit(solution)/shard_map/finish_other/pallas_call | solution.py:613
  (29 shorter events, 0.1 us)
Async XLA Ops:
  0.6 0.9 copy-start.5
  1.5 0.8 copy-start.6
  2.3 6.6 %collective-permute-start.1 = (bf16[32,128]{1,0:T(8,128)(2,1)S(1)}, bf16[32,128]{1,0:T(8,128)(2,1)S(1)}, u32[]{:S(2)}, u32[]{:S(2)}) collective-permute-start(bf16[32,128]{1,0:T(8,128)(2,1)S(1)} %get-tuple-element.43), channel_id=1, source_target_pairs={{2,0},{4,2},{6,4},{8,6},{10,8},{12,10},{14,12},{3,1},{5,3},{7,5},{... | collective-permute-start | bytes 24584 | tf_op jit(solution)/shard_map/ppermute | solution.py:35
  3.6 5.4 %collective-permute-start = (bf16[32,128]{1,0:T(8,128)(2,1)S(1)}, bf16[32,128]{1,0:T(8,128)(2,1)S(1)}, u32[]{:S(2)}, u32[]{:S(2)}) collective-permute-start(bf16[32,128]{1,0:T(8,128)(2,1)S(1)} %get-tuple-element.38.after), channel_id=1, source_target_pairs={{0,2},{2,4},{4,6},{6,8},{8,10},{10,12},{12,14},{1,3},{3,5},{5,7},{... | collective-permute-start | bytes 24584 | tf_op jit(solution)/shard_map/ppermute | solution.py:35
  9.1 3.2 %copy-start.11 = (s32[1,1,256]{2,1,0:T(1,128)S(1)}, s32[1,1,256]{2,1,0:T(1,128)}, u32[]{:S(2)}) copy-start(s32[1,1,256]{2,1,0:T(1,128)} %param.24) | copy-start | bytes 3076
  9.1 4.9 %collective-permute-start.2 = (bf16[256,128]{1,0:T(8,128)(2,1)S(1)}, bf16[256,128]{1,0:T(8,128)(2,1)S(1)}, u32[]{:S(2)}, u32[]{:S(2)}) collective-permute-start(bf16[256,128]{1,0:T(8,128)(2,1)S(1)} %edge_rows.1.mine), channel_id=1, source_target_pairs={{0,1},{1,0},{16,17},{17,16},{32,33},{33,32},{48,49},{49,48},{64,65... | collective-permute-start | bytes 196616 | tf_op jit(solution)/shard_map/ppermute | solution.py:40
  12.3 9.6 %copy-start.7 = (bf16[34,10]{0,1:T(8,128)(2,1)S(1)}, bf16[34,10]{0,1:T(8,128)(2,1)}, u32[]{:S(2)}) copy-start(bf16[34,10]{0,1:T(8,128)(2,1)} %param.15) | copy-start | bytes 2044
  12.3 9.6 %copy-start.8 = (bf16[34,10]{0,1:T(8,128)(2,1)S(1)}, bf16[34,10]{0,1:T(8,128)(2,1)}, u32[]{:S(2)}) copy-start(bf16[34,10]{0,1:T(8,128)(2,1)} %param.16) | copy-start | bytes 2044
  12.3 9.6 %copy-start.9 = (s32[1,1,256]{2,1,0:T(1,128)S(1)}, s32[1,1,256]{2,1,0:T(1,128)}, u32[]{:S(2)}) copy-start(s32[1,1,256]{2,1,0:T(1,128)} %param.22) | copy-start | bytes 3076
  12.3 9.6 %copy-start.10 = (s32[1,128]{1,0:T(1,128)S(1)}, s32[1,128]{1,0:T(1,128)}, u32[]{:S(2)}) copy-start(s32[1,128]{1,0:T(1,128)} %constant.8.ring_l) | copy-start | bytes 1540
  14.0 8.5 %collective-permute-start.3 = (bf16[112,128]{1,0:T(8,128)(2,1)S(1)}, bf16[112,128]{1,0:T(8,128)(2,1)S(1)}, u32[]{:S(2)}, u32[]{:S(2)}) collective-permute-start(bf16[112,128]{1,0:T(8,128)(2,1)S(1)} %get-tuple-element.45), channel_id=1, source_target_pairs={{0,16},{16,32},{32,48},{48,64},{64,80},{80,96},{96,112},{1,17},{17... | collective-permute-start | bytes 86024 | tf_op jit(solution)/shard_map/ppermute | solution.py:35
  19.9 5.2 %collective-permute-start.4 = (bf16[112,128]{1,0:T(8,128)(2,1)S(1)}, bf16[112,128]{1,0:T(8,128)(2,1)S(1)}, u32[]{:S(2)}, u32[]{:S(2)}) collective-permute-start(bf16[112,128]{1,0:T(8,128)(2,1)S(1)} %get-tuple-element.46), channel_id=1, source_target_pairs={{16,0},{32,16},{48,32},{64,48},{80,64},{96,80},{112,96},{17,1},{33... | collective-permute-start | bytes 86024 | tf_op jit(solution)/shard_map/ppermute | solution.py:35
  21.9 3.2 %copy-start = (bf16[3,3,512,128]{3,2,1,0:T(8,128)(2,1)S(1)}, bf16[3,3,512,128]{3,2,1,0:T(8,128)(2,1)}, u32[]{:S(2)}) copy-start(bf16[3,3,512,128]{3,2,1,0:T(8,128)(2,1)} %param.18) | copy-start | bytes 3538948
  21.9 3.2 %copy-start.2 = (bf16[3,3,128,128]{3,2,1,0:T(8,128)(2,1)S(1)}, bf16[3,3,128,128]{3,2,1,0:T(8,128)(2,1)}, u32[]{:S(2)}) copy-start(bf16[3,3,128,128]{3,2,1,0:T(8,128)(2,1)} %param.17) | copy-start | bytes 884740
  27.2 5.4 %collective-permute-start.5 = (bf16[48,128]{1,0:T(8,128)(2,1)S(1)}, bf16[48,128]{1,0:T(8,128)(2,1)S(1)}, u32[]{:S(2)}, u32[]{:S(2)}) collective-permute-start(bf16[48,128]{1,0:T(8,128)(2,1)S(1)} %get-tuple-element.49), channel_id=1, source_target_pairs={{0,2},{2,4},{4,6},{6,8},{8,10},{10,12},{12,14},{1,3},{3,5},{5,7},{... | collective-permute-start | bytes 36872 | tf_op jit(solution)/shard_map/ppermute | solution.py:35
  31.3 5.9 %collective-permute-start.6 = (bf16[48,128]{1,0:T(8,128)(2,1)S(1)}, bf16[48,128]{1,0:T(8,128)(2,1)S(1)}, u32[]{:S(2)}, u32[]{:S(2)}) collective-permute-start(bf16[48,128]{1,0:T(8,128)(2,1)S(1)} %get-tuple-element.50), channel_id=1, source_target_pairs={{2,0},{4,2},{6,4},{8,6},{10,8},{12,10},{14,12},{3,1},{5,3},{7,5},{... | collective-permute-start | bytes 36872 | tf_op jit(solution)/shard_map/ppermute | solution.py:35
  37.2 9.6 %copy-start.1 = (bf16[1024,512]{1,0:T(8,128)(2,1)S(1)}, bf16[1024,512]{1,0:T(8,128)(2,1)}, u32[]{:S(2)}) copy-start(bf16[1024,512]{1,0:T(8,128)(2,1)} %binw.1) | copy-start | bytes 3145732
  37.2 9.6 %copy-start.3 = (bf16[3,3,128,128]{3,2,1,0:T(8,128)(2,1)S(1)}, bf16[3,3,128,128]{3,2,1,0:T(8,128)(2,1)}, u32[]{:S(2)}) copy-start(bf16[3,3,128,128]{3,2,1,0:T(8,128)(2,1)} %param.19) | copy-start | bytes 884740
  37.2 9.6 %copy-start.4 = (bf16[128,1024]{1,0:T(8,128)(2,1)S(1)}, bf16[128,1024]{1,0:T(8,128)(2,1)}, u32[]{:S(2)}) copy-start(bf16[128,1024]{1,0:T(8,128)(2,1)} %hid.1) | copy-start | bytes 786436
  37.3 4.6 %collective-permute-start.7 = (bf16[144,128]{1,0:T(8,128)(2,1)S(1)}, bf16[144,128]{1,0:T(8,128)(2,1)S(1)}, u32[]{:S(2)}, u32[]{:S(2)}) collective-permute-start(bf16[144,128]{1,0:T(8,128)(2,1)S(1)} %get-tuple-element.52), channel_id=1, source_target_pairs={{0,1},{1,0},{16,17},{17,16},{32,33},{33,32},{48,49},{49,48},{64,65... | collective-permute-start | bytes 110600 | tf_op jit(solution)/shard_map/ppermute | solution.py:40
  40.0 6.8 %collective-permute-start.8 = (bf16[144,128]{1,0:T(8,128)(2,1)S(1)}, bf16[144,128]{1,0:T(8,128)(2,1)S(1)}, u32[]{:S(2)}, u32[]{:S(2)}) collective-permute-start(bf16[144,128]{1,0:T(8,128)(2,1)S(1)} %get-tuple-element.53), channel_id=1, source_target_pairs={{1,16},{16,1},{17,32},{32,17},{33,48},{48,33},{49,64},{64,49},{65,... | collective-permute-start | bytes 110600 | tf_op jit(solution)/shard_map/ppermute | solution.py:47
  53.7 3.5 %collective-permute-start.9 = (bf16[6144,128]{1,0:T(8,128)(2,1)S(1)}, bf16[6144,128]{1,0:T(8,128)(2,1)S(1)}, u32[]{:S(2)}, u32[]{:S(2)}) collective-permute-start(bf16[6144,128]{1,0:T(8,128)(2,1)S(1)} %slice_bitcast_fusion), channel_id=1, source_target_pairs={{0,16},{16,0},{1,17},{17,1},{2,18},{18,2},{3,19},{19,3},{4,20},{20... | collective-permute-start | bytes 4718600 | tf_op jit(solution)/shard_map/ppermute | solution.py:676
  118.8 6.4 %collective-permute-start.10 = (bf16[6144,128]{1,0:T(8,128)(2,1)S(1)}, bf16[6144,128]{1,0:T(8,128)(2,1)S(1)}, u32[]{:S(2)}, u32[]{:S(2)}) collective-permute-start(bf16[6144,128]{1,0:T(8,128)(2,1)S(1)} %bitcast.20), channel_id=1, source_target_pairs={{0,16},{16,0},{1,17},{17,1},{2,18},{18,2},{3,19},{19,3},{4,20},{20... | collective-permute-start | bytes 4718600 | tf_op jit(solution)/shard_map/ppermute | solution.py:679

commit v8 on v7

--- a/solution.py
+++ b/solution.py
@@ -102,9 +102,9 @@
 def edge_cols_kernel(fine_in, ctx_in, last, first, fine, ctx, fs, xs):
     fine[...] = fine_in[...]
     ctx[...] = ctx_in[...]
-    fs[...] = fine[...].astype(F32)
+    fs[0:512, :] = fine[...].astype(F32)
     for side in range(2):
-        xs[side] = ctx[:, 128 * side : 128 * side + 128].astype(F32)
+        xs[side, 0:64, :] = ctx[:, 128 * side : 128 * side + 128].astype(F32)
     for out, fc, xc in ((last, COLS - 1, 7), (first, 0, 0)):
         out[0:16, :] = fs[pl.ds(fc, 16, stride=COLS), :].astype(BF)
         sides = [xs.at[side][pl.ds(xc, 8, stride=8), :] for side in range(2)]
@@ -128,7 +128,7 @@
             xs[at + 1 : at + 9, :] = ctx[8 * a : 8 * a + 8, lanes].astype(F32)
         xs[pl.ds(base, 8, stride=10), :] = w[16 + 8 * side : 24 + 8 * side, :]
         xs[pl.ds(base + 9, 8, stride=10), :] = e[16 + 8 * side : 24 + 8 * side, :]
-    inner[CTX:, :] = xs[...].astype(BF)
+    inner[CTX:, :] = xs[0:160, :].astype(BF)
 
 
 def ctx_rows_kernel(mine, inner, down, up, xs):
@@ -229,9 +229,9 @@
     s = jax.nn.sigmoid(acc)
     h = (acc * s).astype(BF)
     h1[...] = h
-    hscr[...] = h.astype(F32)
+    hscr[0:512, :] = h.astype(F32)
     sg[...] = s * (1.0 + acc * (1.0 - s))
-    dscr[...] = dig[...].astype(F32)
+    dscr[0:512, :] = dig[...].astype(F32)
     digs[0:32, :] = dscr[0:32, :].astype(BF)
     digs[32:64, :] = dscr[480:512, :].astype(BF)
     for out, c0, c1, cd in ((last, COLS - 2, COLS - 1, COLS - 1), (first, 0, 1, 0)):
@@ -254,7 +254,7 @@
         ds[at + 1 : at + 33, :] = digs[32 * n : 32 * n + 32, :].astype(F32)
         ds[at : at + 1, :] = w[32 + r : 33 + r, :]
         ds[at + 33 : at + 34, :] = e[32 + r : 33 + r, :]
-    wide[...] = ws[...].astype(BF)
+    wide[...] = ws[0 : ROWS * WIDE, :].astype(BF)
     top, bottom = ws[0:96, :].astype(BF), ws[14 * WIDE : 16 * WIDE, :].astype(BF)
     inner[0:96, :] = jnp.where(lower, top, bottom)
     outer[0:96, :] = jnp.where(lower, bottom, top)
@@ -467,7 +467,7 @@
         out_shape=(sds((32, C), BF),) * 2 + (sds((512, C), BF), sds((64, HALF), BF)),
         in_specs=vmem(2),
         out_specs=tuple(vmem(4)),
-        scratch_shapes=[pltpu.VMEM((512, C), F32), pltpu.VMEM((2, 64, C), F32)],
+        scratch_shapes=[pltpu.VMEM((544, C), F32), pltpu.VMEM((2, 72, C), F32)],
         compiler_params=limit(4),
         cost_estimate=BUSY,
         name="edge_cols",
@@ -480,7 +480,7 @@
         out_shape=sds((CTX + 160, C), BF),
         in_specs=vmem(4),
         out_specs=vmem(1)[0],
-        scratch_shapes=[pltpu.VMEM((2 * WIDE, C), F32), pltpu.VMEM((160, C), F32)],
+        scratch_shapes=[pltpu.VMEM((2 * WIDE, C), F32), pltpu.VMEM((176, C), F32)],
         compiler_params=limit(4),
         cost_estimate=BUSY,
         name="edge_rows",
@@ -526,8 +526,8 @@
             v((18 * WIDE, C), F32),
             v((288, K), BF),
             v((160, K), BF),
-            v((512, C), F32),
-            v((512, C), F32),
+            v((544, C), F32),
+            v((544, C), F32),
             v((176, C), F32),
             v((576, 384), F32),
             pltpu.SMEM((4,), jnp.int32),
@@ -545,7 +545,7 @@
         out_shape=(sds((ROWS * WIDE, C), BF), edge, edge),
         in_specs=vmem(len(args)),
         out_specs=tuple(vmem(3)),
-        scratch_shapes=[pltpu.VMEM((ROWS * WIDE, C), F32), pltpu.VMEM((2 * WIDE, C), F32)],
+        scratch_shapes=[pltpu.VMEM((ROWS * WIDE + WIDE, C), F32), pltpu.VMEM((2 * WIDE, C), F32)],
         compiler_params=limit(6),
         cost_estimate=BUSY,
         name="h_rows",
@@ -649,8 +649,8 @@
     ring = jnp.asarray(ring_cells())
 
     last, first, fine, context = edge_cols(fine.reshape(512, C), context.reshape(64, HALF))
+    east = shift(first, GX, 8, -1)
     west = shift(last, GX, 8, 1)
-    east = shift(first, GX, 8, -1)
     kron, left, dig, pick, back, labs = plan(interp_rows.T, interp_cols.T, idx, ring[None, :], lab, last)
     mine = edge_rows(fine, context, west, east)
     inner = side_swap(mine)
@@ -662,8 +662,8 @@
         fine_weight.reshape(1152, C), ctx_weight.reshape(4608, C),
     )
 
+    east = shift(first, GX, 8, -1)
     west = shift(last, GX, 8, 1)
-    east = shift(first, GX, 8, -1)
     wide, inner, outer = h_rows(h_one, digs, west, east)
     outer = outer_swap(outer)
     inner = side_swap(inner)

time: 128 us -> 128 us (level)
  no operation moved by 1% of the time
where the time goes in v8:
time: 128 us; the launch traced here: 127 us
  blocking collectives  60.8 us (48%)
  starting transfers between devices  30.4 us (24%)
  waiting for transfers between devices  18.4 us (14%)
  Pallas kernels  14.3 us (11%)
  local copies, waits for them, and re-layouts  1.81 us (1%)
  between operations  1.53 us (1%)
    all_to_all x1, blocking collectives, local(): lax.all_to_all(pair.reshape(PEERS, SHARD, C), PLANE, 0, 0, tiled=True)  34.2 us
    all_to_all x1, blocking collectives, local(): lax.all_to_all(spread(pieces), PLANE, 0, 0, tiled=True).reshape(KEEP, C)  26.6 us
    ppermute x6, starting transfers between devices, shift(): return lax.ppermute(x, axis, pairs)  19.2 us
    ppermute x6, waiting for transfers between devices, shift(): return lax.ppermute(x, axis, pairs)  7.3 us
    pallas_call x1, Pallas kernels, rest(): pl.pallas_call(rest_kernel, out_shape=sds((2, KEEP, C), BF), in_specs=vme...  6.81 us
    ppermute x2, starting transfers between devices, side_swap(): return lax.ppermute(x, TALL, own)  5.85 us
    ppermute x1, waiting for transfers between devices, outer_swap(): return lax.ppermute(x, TALL, pairs)  4.84 us
    pallas_call x2, Pallas kernels, finish(): pl.pallas_call(functools.partial(finish_kernel, second), out_shape=tuple(...  3.83 us
  transfers between devices with their start and end apart: 11, of which 7 were waited for; matrix products, arithmetic and copies ran while one was open for 0% of the time, Pallas kernels for 2%

profile of v8, /device:TPU:1, one launch (start us, length us, event | category | flops | bytes accessed | tf_op | source)
XLA Modules:
  0.0 127.2 jit_solution(4928317053985658112)
XLA Ops:
  0.6 0.9 copy-done.5
  1.5 0.8 copy-done.6
  2.3 1.3 %collective-permute-start.1 = (bf16[32,128]{1,0:T(8,128)(2,1)S(1)}, bf16[32,128]{1,0:T(8,128)(2,1)S(1)}, u32[]{:S(2)}, u32[]{:S(2)}) collective-permute-start(bf16[32,128]{1,0:T(8,128)(2,1)S(1)} %get-tuple-element.43), channel_id=1, source_target_pairs={{2,0},{4,2},{6,4},{8,6},{10,8},{12,10},{14,12},{3,1},{5,3},{7,5},{... | collective-permute-start | bytes 24584 | tf_op jit(solution)/shard_map/ppermute | solution.py:35
  3.6 4.7 %collective-permute-start = (bf16[32,128]{1,0:T(8,128)(2,1)S(1)}, bf16[32,128]{1,0:T(8,128)(2,1)S(1)}, u32[]{:S(2)}, u32[]{:S(2)}) collective-permute-start(bf16[32,128]{1,0:T(8,128)(2,1)S(1)} %get-tuple-element.38.after), channel_id=1, source_target_pairs={{0,2},{2,4},{4,6},{6,8},{8,10},{10,12},{12,14},{1,3},{3,5},{5,7},{... | collective-permute-start | bytes 24584 | tf_op jit(solution)/shard_map/ppermute | solution.py:35
  9.0 0.1 collective-permute-done.west
  9.1 3.2 %collective-permute-start.2 = (bf16[256,128]{1,0:T(8,128)(2,1)S(1)}, bf16[256,128]{1,0:T(8,128)(2,1)S(1)}, u32[]{:S(2)}, u32[]{:S(2)}) collective-permute-start(bf16[256,128]{1,0:T(8,128)(2,1)S(1)} %edge_rows.1.mine), channel_id=1, source_target_pairs={{0,1},{1,0},{16,17},{17,16},{32,33},{33,32},{48,49},{49,48},{64,65... | collective-permute-start | bytes 196616 | tf_op jit(solution)/shard_map/ppermute | solution.py:40
  12.3 0.0 copy-start.10
  12.3 1.7 %collective-permute-done.2.inner = bf16[256,128]{1,0:T(8,128)(2,1)S(1)} collective-permute-done((bf16[256,128]{1,0:T(8,128)(2,1)S(1)}, bf16[256,128]{1,0:T(8,128)(2,1)S(1)}, u32[]{:S(2)}, u32[]{:S(2)}) %collective-permute-start.2) | collective-permute-done | bytes 65568 | tf_op jit(solution)/shard_map/ppermute | solution.py:40
  14.0 5.9 %collective-permute-start.3 = (bf16[112,128]{1,0:T(8,128)(2,1)S(1)}, bf16[112,128]{1,0:T(8,128)(2,1)S(1)}, u32[]{:S(2)}, u32[]{:S(2)}) collective-permute-start(bf16[112,128]{1,0:T(8,128)(2,1)S(1)} %get-tuple-element.45), channel_id=1, source_target_pairs={{0,16},{16,32},{32,48},{48,64},{64,80},{80,96},{96,112},{1,17},{17... | collective-permute-start | bytes 86024 | tf_op jit(solution)/shard_map/ppermute | solution.py:35
  19.9 1.9 %collective-permute-start.4 = (bf16[112,128]{1,0:T(8,128)(2,1)S(1)}, bf16[112,128]{1,0:T(8,128)(2,1)S(1)}, u32[]{:S(2)}, u32[]{:S(2)}) collective-permute-start(bf16[112,128]{1,0:T(8,128)(2,1)S(1)} %get-tuple-element.46), channel_id=1, source_target_pairs={{16,0},{32,16},{48,32},{64,48},{80,64},{96,80},{112,96},{17,1},{33... | collective-permute-start | bytes 86024 | tf_op jit(solution)/shard_map/ppermute | solution.py:35
  21.9 0.6 plan.1
  22.5 2.6 %collective-permute-done.4.south = bf16[112,128]{1,0:T(8,128)(2,1)S(1)} collective-permute-done((bf16[112,128]{1,0:T(8,128)(2,1)S(1)}, bf16[112,128]{1,0:T(8,128)(2,1)S(1)}, u32[]{:S(2)}, u32[]{:S(2)}) %collective-permute-start.4) | collective-permute-done | bytes 28704 | tf_op jit(solution)/shard_map/ppermute | solution.py:35
  25.1 2.1 %first_conv.1 = (bf16[576,1920]{1,0:T(8,128)(2,1)S(1)}, bf16[512,128]{1,0:T(8,128)(2,1)S(1)}, f32[512,128]{1,0:T(8,128)S(1)}, bf16[48,128]{1,0:T(8,128)(2,1)S(1)...) custom-call(bf16[288,160]{1,0:T(8,128)(2,1)S(1)} %get-tuple-element.39.kron, ...), custom_call_target="tpu_custom_call" | custom-call | flops 900000000 | bytes 5000000 | tf_op jit(solution)/shard_map/first_conv/pallas_call | solution.py:520
  27.2 4.1 %collective-permute-start.5 = (bf16[48,128]{1,0:T(8,128)(2,1)S(1)}, bf16[48,128]{1,0:T(8,128)(2,1)S(1)}, u32[]{:S(2)}, u32[]{:S(2)}) collective-permute-start(bf16[48,128]{1,0:T(8,128)(2,1)S(1)} %get-tuple-element.49), channel_id=1, source_target_pairs={{0,2},{2,4},{4,6},{6,8},{8,10},{10,12},{12,14},{1,3},{3,5},{5,7},{... | collective-permute-start | bytes 36872 | tf_op jit(solution)/shard_map/ppermute | solution.py:35
  31.3 1.3 %collective-permute-start.6 = (bf16[48,128]{1,0:T(8,128)(2,1)S(1)}, bf16[48,128]{1,0:T(8,128)(2,1)S(1)}, u32[]{:S(2)}, u32[]{:S(2)}) collective-permute-start(bf16[48,128]{1,0:T(8,128)(2,1)S(1)} %get-tuple-element.50), channel_id=1, source_target_pairs={{2,0},{4,2},{6,4},{8,6},{10,8},{12,10},{14,12},{3,1},{5,3},{7,5},{... | collective-permute-start | bytes 36872 | tf_op jit(solution)/shard_map/ppermute | solution.py:35
  32.7 4.6 %collective-permute-done.6.east = bf16[48,128]{1,0:T(8,128)(2,1)S(1)} collective-permute-done((bf16[48,128]{1,0:T(8,128)(2,1)S(1)}, bf16[48,128]{1,0:T(8,128)(2,1)S(1)}, u32[]{:S(2)}, u32[]{:S(2)}) %collective-permute-start.6) | collective-permute-done | bytes 12320 | tf_op jit(solution)/shard_map/ppermute | solution.py:35
  37.2 0.1 h_rows.1
  37.3 2.7 %collective-permute-start.7 = (bf16[144,128]{1,0:T(8,128)(2,1)S(1)}, bf16[144,128]{1,0:T(8,128)(2,1)S(1)}, u32[]{:S(2)}, u32[]{:S(2)}) collective-permute-start(bf16[144,128]{1,0:T(8,128)(2,1)S(1)} %get-tuple-element.52), channel_id=1, source_target_pairs={{0,1},{1,0},{16,17},{17,16},{32,33},{33,32},{48,49},{49,48},{64,65... | collective-permute-start | bytes 110600 | tf_op jit(solution)/shard_map/ppermute | solution.py:40
  40.0 1.9 %collective-permute-start.8 = (bf16[144,128]{1,0:T(8,128)(2,1)S(1)}, bf16[144,128]{1,0:T(8,128)(2,1)S(1)}, u32[]{:S(2)}, u32[]{:S(2)}) collective-permute-start(bf16[144,128]{1,0:T(8,128)(2,1)S(1)} %get-tuple-element.53), channel_id=1, source_target_pairs={{1,16},{16,1},{17,32},{32,17},{33,48},{48,33},{49,64},{64,49},{65,... | collective-permute-start | bytes 110600 | tf_op jit(solution)/shard_map/ppermute | solution.py:47
  42.0 4.8 %collective-permute-done.8.outer = bf16[144,128]{1,0:T(8,128)(2,1)S(1)} collective-permute-done((bf16[144,128]{1,0:T(8,128)(2,1)S(1)}, bf16[144,128]{1,0:T(8,128)(2,1)S(1)}, u32[]{:S(2)}, u32[]{:S(2)}) %collective-permute-start.8) | collective-permute-done | bytes 36896 | tf_op jit(solution)/shard_map/ppermute | solution.py:47
  46.8 6.8 %rest.1.both = bf16[2,6144,128]{2,1,0:T(8,128)(2,1)S(1)} custom-call(bf16[768,128]{1,0:T(8,128)(2,1)S(1)} %get-tuple-element.51.hw, bf16[144,128]{1,0:T(8,128)(2,1)S(1)} %collective-permute-done.7.inner, bf16[144,128]{1,0:T(8,128)(2,1)S(1)} %collective-permute-done.8.outer, bf16[48,128]{1,0:T(8,128)(2,1)S(1)} %collective-permute-done.5.west, ...), custom_call_target="tpu_custom_call" | custom-call | flops 3000000000 | bytes 8000000 | tf_op jit(solution)/shard_map/rest/pallas_call | solution.py:557
  53.6 0.1 slice_bitcast_fusion
  53.7 0.1 collective-permute-start.9
  53.8 3.4 %collective-permute-done.9.got = bf16[6144,128]{1,0:T(8,128)(2,1)S(1)} collective-permute-done((bf16[6144,128]{1,0:T(8,128)(2,1)S(1)}, bf16[6144,128]{1,0:T(8,128)(2,1)S(1)}, u32[]{:S(2)}, u32[]{:S(2)}) %collective-permute-start.9) | collective-permute-done | bytes 1572896 | tf_op jit(solution)/shard_map/ppermute | solution.py:676
  57.2 0.4 pair_sum.1
  57.6 34.2 %all_to_all.10.pieces = bf16[64,96,128]{2,1,0:T(8,128)(2,1)S(1)} all-to-all(bf16[64,96,128]{2,1,0:T(8,128)(2,1)S(1)} %bitcast.22), channel_id=1, replica_groups=mesh['x'=4,'core'=2,'z'=4,'yl'=2,'yh'=2] {'x','z','yl','yh'}, dimensions={0} | all-to-all | bytes 3145728 | tf_op jit(solution)/shard_map/all_to_all | solution.py:677
  91.8 0.4 spread.1
  92.2 26.6 %all_to_all.11 = bf16[64,96,128]{2,1,0:T(8,128)(2,1)S(1)} all-to-all(bf16[64,96,128]{2,1,0:T(8,128)(2,1)S(1)} %spread.1), channel_id=1, replica_groups=mesh['x'=4,'core'=2,'z'=4,'yl'=2,'yh'=2] {'x','z','yl','yh'}, dimensions={0} | all-to-all | bytes 3145728 | tf_op jit(solution)/shard_map/all_to_all | solution.py:678
  118.8 3.4 %collective-permute-start.10 = (bf16[6144,128]{1,0:T(8,128)(2,1)S(1)}, bf16[6144,128]{1,0:T(8,128)(2,1)S(1)}, u32[]{:S(2)}, u32[]{:S(2)}) collective-permute-start(bf16[6144,128]{1,0:T(8,128)(2,1)S(1)} %bitcast.20), channel_id=1, source_target_pairs={{0,16},{16,0},{1,17},{17,1},{2,18},{18,2},{3,19},{19,3},{4,20},{20... | collective-permute-start | bytes 4718600 | tf_op jit(solution)/shard_map/ppermute | solution.py:679
  122.2 1.9 %finish_own.1 = (f32[1152,128]{1,0:T(8,128)}, f32[2304,128]{1,0:T(8,128)}, f32[1152,128]{1,0:T(8,128)}, f32[128,1024]{1,0:T(8,128)}, f32[1024,512]{1,0:T(8,128)}) custom-call(bf16[6144,128]{1,0:T(8,128)(2,1)S(1)} %bitcast.21), custom_call_target="tpu_custom_call" | custom-call | flops 800000 | bytes 5000000 | tf_op jit(solution)/shard_map/finish_own/pallas_call | solution.py:613
  124.1 1.2 collective-permute-done.10.part
  125.2 2.0 %finish_other.1 = (f32[1152,128]{1,0:T(8,128)}, f32[2304,128]{1,0:T(8,128)}, f32[1152,128]{1,0:T(8,128)}, f32[128,1024]{1,0:T(8,128)}, f32[1024,512]{1,0:T(8,128)}, /*index=5*/f32[1,1]{1,0:T(1,128)}) custom-call(bf16[6144,128]{1,0:T(8,128)(2,1)S(1)} %collective-permute-done.10.part, ...), custom_call_target="tpu_custom_call", output_to_operand_aliasing={{0}: (1, {}), {1}: (2, {}), {2}: (3, {}), {3}: (4, {}), {4}... | custom-call | flops 800000 | bytes 5000000 | tf_op jit(solution)/shard_map/finish_other/pallas_call | solution.py:613
  (29 shorter events, 0.1 us)
Async XLA Ops:
  0.6 0.9 copy-start.5
  1.5 0.8 copy-start.6
  2.3 6.6 %collective-permute-start.1 = (bf16[32,128]{1,0:T(8,128)(2,1)S(1)}, bf16[32,128]{1,0:T(8,128)(2,1)S(1)}, u32[]{:S(2)}, u32[]{:S(2)}) collective-permute-start(bf16[32,128]{1,0:T(8,128)(2,1)S(1)} %get-tuple-element.43), channel_id=1, source_target_pairs={{2,0},{4,2},{6,4},{8,6},{10,8},{12,10},{14,12},{3,1},{5,3},{7,5},{... | collective-permute-start | bytes 24584 | tf_op jit(solution)/shard_map/ppermute | solution.py:35
  3.6 5.4 %collective-permute-start = (bf16[32,128]{1,0:T(8,128)(2,1)S(1)}, bf16[32,128]{1,0:T(8,128)(2,1)S(1)}, u32[]{:S(2)}, u32[]{:S(2)}) collective-permute-start(bf16[32,128]{1,0:T(8,128)(2,1)S(1)} %get-tuple-element.38.after), channel_id=1, source_target_pairs={{0,2},{2,4},{4,6},{6,8},{8,10},{10,12},{12,14},{1,3},{3,5},{5,7},{... | collective-permute-start | bytes 24584 | tf_op jit(solution)/shard_map/ppermute | solution.py:35
  9.1 3.2 %copy-start.11 = (s32[1,1,256]{2,1,0:T(1,128)S(1)}, s32[1,1,256]{2,1,0:T(1,128)}, u32[]{:S(2)}) copy-start(s32[1,1,256]{2,1,0:T(1,128)} %param.24) | copy-start | bytes 3076
  9.1 4.9 %collective-permute-start.2 = (bf16[256,128]{1,0:T(8,128)(2,1)S(1)}, bf16[256,128]{1,0:T(8,128)(2,1)S(1)}, u32[]{:S(2)}, u32[]{:S(2)}) collective-permute-start(bf16[256,128]{1,0:T(8,128)(2,1)S(1)} %edge_rows.1.mine), channel_id=1, source_target_pairs={{0,1},{1,0},{16,17},{17,16},{32,33},{33,32},{48,49},{49,48},{64,65... | collective-permute-start | bytes 196616 | tf_op jit(solution)/shard_map/ppermute | solution.py:40
  12.3 9.6 %copy-start.7 = (bf16[34,10]{0,1:T(8,128)(2,1)S(1)}, bf16[34,10]{0,1:T(8,128)(2,1)}, u32[]{:S(2)}) copy-start(bf16[34,10]{0,1:T(8,128)(2,1)} %param.15) | copy-start | bytes 2044
  12.3 9.6 %copy-start.8 = (bf16[34,10]{0,1:T(8,128)(2,1)S(1)}, bf16[34,10]{0,1:T(8,128)(2,1)}, u32[]{:S(2)}) copy-start(bf16[34,10]{0,1:T(8,128)(2,1)} %param.16) | copy-start | bytes 2044
  12.3 9.6 %copy-start.9 = (s32[1,1,256]{2,1,0:T(1,128)S(1)}, s32[1,1,256]{2,1,0:T(1,128)}, u32[]{:S(2)}) copy-start(s32[1,1,256]{2,1,0:T(1,128)} %param.22) | copy-start | bytes 3076
  12.3 9.6 %copy-start.10 = (s32[1,128]{1,0:T(1,128)S(1)}, s32[1,128]{1,0:T(1,128)}, u32[]{:S(2)}) copy-start(s32[1,128]{1,0:T(1,128)} %constant.8.ring_l) | copy-start | bytes 1540
  14.0 8.5 %collective-permute-start.3 = (bf16[112,128]{1,0:T(8,128)(2,1)S(1)}, bf16[112,128]{1,0:T(8,128)(2,1)S(1)}, u32[]{:S(2)}, u32[]{:S(2)}) collective-permute-start(bf16[112,128]{1,0:T(8,128)(2,1)S(1)} %get-tuple-element.45), channel_id=1, source_target_pairs={{0,16},{16,32},{32,48},{48,64},{64,80},{80,96},{96,112},{1,17},{17... | collective-permute-start | bytes 86024 | tf_op jit(solution)/shard_map/ppermute | solution.py:35
  19.9 5.2 %collective-permute-start.4 = (bf16[112,128]{1,0:T(8,128)(2,1)S(1)}, bf16[112,128]{1,0:T(8,128)(2,1)S(1)}, u32[]{:S(2)}, u32[]{:S(2)}) collective-permute-start(bf16[112,128]{1,0:T(8,128)(2,1)S(1)} %get-tuple-element.46), channel_id=1, source_target_pairs={{16,0},{32,16},{48,32},{64,48},{80,64},{96,80},{112,96},{17,1},{33... | collective-permute-start | bytes 86024 | tf_op jit(solution)/shard_map/ppermute | solution.py:35
  21.9 3.2 %copy-start = (bf16[3,3,512,128]{3,2,1,0:T(8,128)(2,1)S(1)}, bf16[3,3,512,128]{3,2,1,0:T(8,128)(2,1)}, u32[]{:S(2)}) copy-start(bf16[3,3,512,128]{3,2,1,0:T(8,128)(2,1)} %param.18) | copy-start | bytes 3538948
  21.9 3.2 %copy-start.2 = (bf16[3,3,128,128]{3,2,1,0:T(8,128)(2,1)S(1)}, bf16[3,3,128,128]{3,2,1,0:T(8,128)(2,1)}, u32[]{:S(2)}) copy-start(bf16[3,3,128,128]{3,2,1,0:T(8,128)(2,1)} %param.17) | copy-start | bytes 884740
  27.2 5.4 %collective-permute-start.5 = (bf16[48,128]{1,0:T(8,128)(2,1)S(1)}, bf16[48,128]{1,0:T(8,128)(2,1)S(1)}, u32[]{:S(2)}, u32[]{:S(2)}) collective-permute-start(bf16[48,128]{1,0:T(8,128)(2,1)S(1)} %get-tuple-element.49), channel_id=1, source_target_pairs={{0,2},{2,4},{4,6},{6,8},{8,10},{10,12},{12,14},{1,3},{3,5},{5,7},{... | collective-permute-start | bytes 36872 | tf_op jit(solution)/shard_map/ppermute | solution.py:35
  31.3 5.9 %collective-permute-start.6 = (bf16[48,128]{1,0:T(8,128)(2,1)S(1)}, bf16[48,128]{1,0:T(8,128)(2,1)S(1)}, u32[]{:S(2)}, u32[]{:S(2)}) collective-permute-start(bf16[48,128]{1,0:T(8,128)(2,1)S(1)} %get-tuple-element.50), channel_id=1, source_target_pairs={{2,0},{4,2},{6,4},{8,6},{10,8},{12,10},{14,12},{3,1},{5,3},{7,5},{... | collective-permute-start | bytes 36872 | tf_op jit(solution)/shard_map/ppermute | solution.py:35
  37.2 9.6 %copy-start.1 = (bf16[1024,512]{1,0:T(8,128)(2,1)S(1)}, bf16[1024,512]{1,0:T(8,128)(2,1)}, u32[]{:S(2)}) copy-start(bf16[1024,512]{1,0:T(8,128)(2,1)} %binw.1) | copy-start | bytes 3145732
  37.2 9.6 %copy-start.3 = (bf16[3,3,128,128]{3,2,1,0:T(8,128)(2,1)S(1)}, bf16[3,3,128,128]{3,2,1,0:T(8,128)(2,1)}, u32[]{:S(2)}) copy-start(bf16[3,3,128,128]{3,2,1,0:T(8,128)(2,1)} %param.19) | copy-start | bytes 884740
  37.2 9.6 %copy-start.4 = (bf16[128,1024]{1,0:T(8,128)(2,1)S(1)}, bf16[128,1024]{1,0:T(8,128)(2,1)}, u32[]{:S(2)}) copy-start(bf16[128,1024]{1,0:T(8,128)(2,1)} %hid.1) | copy-start | bytes 786436
  37.3 4.6 %collective-permute-start.7 = (bf16[144,128]{1,0:T(8,128)(2,1)S(1)}, bf16[144,128]{1,0:T(8,128)(2,1)S(1)}, u32[]{:S(2)}, u32[]{:S(2)}) collective-permute-start(bf16[144,128]{1,0:T(8,128)(2,1)S(1)} %get-tuple-element.52), channel_id=1, source_target_pairs={{0,1},{1,0},{16,17},{17,16},{32,33},{33,32},{48,49},{49,48},{64,65... | collective-permute-start | bytes 110600 | tf_op jit(solution)/shard_map/ppermute | solution.py:40
  40.0 6.8 %collective-permute-start.8 = (bf16[144,128]{1,0:T(8,128)(2,1)S(1)}, bf16[144,128]{1,0:T(8,128)(2,1)S(1)}, u32[]{:S(2)}, u32[]{:S(2)}) collective-permute-start(bf16[144,128]{1,0:T(8,128)(2,1)S(1)} %get-tuple-element.53), channel_id=1, source_target_pairs={{1,16},{16,1},{17,32},{32,17},{33,48},{48,33},{49,64},{64,49},{65,... | collective-permute-start | bytes 110600 | tf_op jit(solution)/shard_map/ppermute | solution.py:47
  53.7 3.5 %collective-permute-start.9 = (bf16[6144,128]{1,0:T(8,128)(2,1)S(1)}, bf16[6144,128]{1,0:T(8,128)(2,1)S(1)}, u32[]{:S(2)}, u32[]{:S(2)}) collective-permute-start(bf16[6144,128]{1,0:T(8,128)(2,1)S(1)} %slice_bitcast_fusion), channel_id=1, source_target_pairs={{0,16},{16,0},{1,17},{17,1},{2,18},{18,2},{3,19},{19,3},{4,20},{20... | collective-permute-start | bytes 4718600 | tf_op jit(solution)/shard_map/ppermute | solution.py:676
  118.8 6.4 %collective-permute-start.10 = (bf16[6144,128]{1,0:T(8,128)(2,1)S(1)}, bf16[6144,128]{1,0:T(8,128)(2,1)S(1)}, u32[]{:S(2)}, u32[]{:S(2)}) collective-permute-start(bf16[6144,128]{1,0:T(8,128)(2,1)S(1)} %bitcast.20), channel_id=1, source_target_pairs={{0,16},{16,0},{1,17},{17,1},{2,18},{18,2},{3,19},{19,3},{4,20},{20... | collective-permute-start | bytes 4718600 | tf_op jit(solution)/shard_map/ppermute | solution.py:679

commit v9 on v8

--- a/solution.py
+++ b/solution.py
@@ -150,7 +150,9 @@
     return jnp.sum(jnp.where(eye, row.astype(F32), 0.0), axis=1, keepdims=True)
 
 
-def plan_kernel(rows_in, cols_in, idx_l, ring_l, lab_l, after, kron, left, digs, pick, back, labs, rmat, cmat):
+def plan_kernel(
+    rows_in, cols_in, idx_l, ring_l, lab_l, w_fine, w_ctx, after, kron, left, digs, pick, back, labs, wide, rmat, cmat
+):
     half = lax.axis_index("yh")
     row0 = (2 * lax.axis_index("x") + lax.axis_index("core")) * 32
     col0 = (2 * lax.axis_index("z") + lax.axis_index("yl")) * COLS
@@ -183,10 +185,14 @@
     back[:, 0:CAP] = (slot_l == cell).astype(F32).astype(BF)
     back[:, CAP:] = (ring_l[...] == cell[:, :128]).astype(F32).astype(BF)
     labs[...] = column(lab_l[...]).astype(jnp.int32)
+    for dy in range(3):
+        lanes = slice(128 * dy, 128 * dy + 128)
+        wide[0:384, lanes] = w_fine[384 * dy : 384 * dy + 384, :]
+        wide[384:, lanes] = w_ctx[1536 * dy : 1536 * dy + 1536, :]
 
 
 def first_conv_kernel(
-    kron, left, dig, fine, west, east, mine, inner, north, south, w_fine, w_ctx,
+    kron, left, dig, fine, west, east, mine, inner, north, south, weights,
     xc, h1, sg, last, first, digs,
     fscr, mid, block, hscr, dscr, xs, pre, spot,
 ):
@@ -222,9 +228,7 @@
         wide = dot(left[...], mid[16 * i : 16 * i + 16, :]).astype(BF)
         for dx in range(3):
             xc[32 * i : 32 * i + 32, 384 + 512 * dx : 896 + 512 * dx] = wide[32 * dx : 32 * dx + 32]
-    wf = jnp.concatenate([w_fine[384 * dy : 384 * dy + 384, :] for dy in range(3)], axis=1)
-    wc = jnp.concatenate([w_ctx[1536 * dy : 1536 * dy + 1536, :] for dy in range(3)], axis=1)
-    pre[...] = dot(xc[:, :384], wf) + dot(xc[:, 384:], wc)
+    pre[...] = dot(xc[...], weights[...])
     acc = sum(pre[32 * dy : 32 * dy + 512, 128 * dy : 128 * dy + 128] for dy in range(3))
     s = jax.nn.sigmoid(acc)
     h = (acc * s).astype(BF)
@@ -504,11 +508,11 @@
     shapes = [((288, 160), BF), ((96, 16), BF), ((512, C), BF), ((SLOTS, EXT), BF), ((EXT, SLOTS), BF)]
     return pl.pallas_call(
         plan_kernel,
-        out_shape=tuple(sds(*s) for s in shapes) + (sds((CAP, 1), jnp.int32),),
+        out_shape=tuple(sds(*s) for s in shapes) + (sds((CAP, 1), jnp.int32), sds((1920, 384), BF)),
         in_specs=vmem(len(args)),
-        out_specs=tuple(vmem(6)),
+        out_specs=tuple(vmem(7)),
         scratch_shapes=[pltpu.VMEM((16, C), F32), pltpu.VMEM((16, C), F32)],
-        compiler_params=limit(8),
+        compiler_params=limit(12),
         cost_estimate=BUSY,
         name="plan",
     )(*args)
@@ -651,15 +655,17 @@
     last, first, fine, context = edge_cols(fine.reshape(512, C), context.reshape(64, HALF))
     east = shift(first, GX, 8, -1)
     west = shift(last, GX, 8, 1)
-    kron, left, dig, pick, back, labs = plan(interp_rows.T, interp_cols.T, idx, ring[None, :], lab, last)
+    kron, left, dig, pick, back, labs, weights = plan(
+        interp_rows.T, interp_cols.T, idx, ring[None, :], lab,
+        fine_weight.reshape(1152, C), ctx_weight.reshape(4608, C), last,
+    )
     mine = edge_rows(fine, context, west, east)
     inner = side_swap(mine)
     down, up = ctx_rows(mine, inner)
     north = shift(down, GY, 8, 1)
     south = shift(up, GY, 8, -1)
     xc, h_one, sg1, last, first, digs = first_conv(
-        kron, left, dig, fine, west, east, mine, inner, north, south,
-        fine_weight.reshape(1152, C), ctx_weight.reshape(4608, C),
+        kron, left, dig, fine, west, east, mine, inner, north, south, weights,
     )
 
     east = shift(first, GX, 8, -1)

time: 128 us -> 128 us (level)
  no operation moved by 1% of the time
where the time goes in v9:
time: 128 us; the launch traced here: 127 us
  blocking collectives  60.8 us (48%)
  starting transfers between devices  30.4 us (24%)
  waiting for transfers between devices  18.2 us (14%)
  Pallas kernels  14.6 us (11%)
  local copies, waits for them, and re-layouts  1.81 us (1%)
  between operations  1.54 us (1%)
    all_to_all x1, blocking collectives, local(): lax.all_to_all(pair.reshape(PEERS, SHARD, C), PLANE, 0, 0, tiled=True)  34.2 us
    all_to_all x1, blocking collectives, local(): lax.all_to_all(spread(pieces), PLANE, 0, 0, tiled=True).reshape(KEEP, C)  26.5 us
    ppermute x6, starting transfers between devices, shift(): return lax.ppermute(x, axis, pairs)  19.2 us
    ppermute x6, waiting for transfers between devices, shift(): return lax.ppermute(x, axis, pairs)  7.11 us
    pallas_call x1, Pallas kernels, rest(): pl.pallas_call(rest_kernel, out_shape=sds((2, KEEP, C), BF), in_specs=vme...  6.81 us
    ppermute x2, starting transfers between devices, side_swap(): return lax.ppermute(x, TALL, own)  5.85 us
    ppermute x1, waiting for transfers between devices, outer_swap(): return lax.ppermute(x, TALL, pairs)  4.84 us
    pallas_call x2, Pallas kernels, finish(): pl.pallas_call(functools.partial(finish_kernel, second), out_shape=tuple(...  3.83 us
  transfers between devices with their start and end apart: 11, of which 7 were waited for; matrix products, arithmetic and copies ran while one was open for 0% of the time, Pallas kernels for 2%

profile of v9, /device:TPU:1, one launch (start us, length us, event | category | flops | bytes accessed | tf_op | source)
XLA Modules:
  0.0 127.3 jit_solution(15963864897642556442)
XLA Ops:
  0.6 0.9 copy-done.5
  1.5 0.8 copy-done.6
  2.3 1.3 %collective-permute-start.1 = (bf16[32,128]{1,0:T(8,128)(2,1)S(1)}, bf16[32,128]{1,0:T(8,128)(2,1)S(1)}, u32[]{:S(2)}, u32[]{:S(2)}) collective-permute-start(bf16[32,128]{1,0:T(8,128)(2,1)S(1)} %get-tuple-element.44), channel_id=1, source_target_pairs={{2,0},{4,2},{6,4},{8,6},{10,8},{12,10},{14,12},{3,1},{5,3},{7,5},{... | collective-permute-start | bytes 24584 | tf_op jit(solution)/shard_map/ppermute | solution.py:35
  3.6 4.7 %collective-permute-start = (bf16[32,128]{1,0:T(8,128)(2,1)S(1)}, bf16[32,128]{1,0:T(8,128)(2,1)S(1)}, u32[]{:S(2)}, u32[]{:S(2)}) collective-permute-start(bf16[32,128]{1,0:T(8,128)(2,1)S(1)} %get-tuple-element.39.after), channel_id=1, source_target_pairs={{0,2},{2,4},{4,6},{6,8},{8,10},{10,12},{12,14},{1,3},{3,5},{5,7},{... | collective-permute-start | bytes 24584 | tf_op jit(solution)/shard_map/ppermute | solution.py:35
  9.0 0.1 collective-permute-done.west
  9.1 3.2 %collective-permute-start.2 = (bf16[256,128]{1,0:T(8,128)(2,1)S(1)}, bf16[256,128]{1,0:T(8,128)(2,1)S(1)}, u32[]{:S(2)}, u32[]{:S(2)}) collective-permute-start(bf16[256,128]{1,0:T(8,128)(2,1)S(1)} %edge_rows.1.mine), channel_id=1, source_target_pairs={{0,1},{1,0},{16,17},{17,16},{32,33},{33,32},{48,49},{49,48},{64,65... | collective-permute-start | bytes 196616 | tf_op jit(solution)/shard_map/ppermute | solution.py:40
  12.3 0.0 copy-start.10
  12.3 1.7 %collective-permute-done.2.inner = bf16[256,128]{1,0:T(8,128)(2,1)S(1)} collective-permute-done((bf16[256,128]{1,0:T(8,128)(2,1)S(1)}, bf16[256,128]{1,0:T(8,128)(2,1)S(1)}, u32[]{:S(2)}, u32[]{:S(2)}) %collective-permute-start.2) | collective-permute-done | bytes 65568 | tf_op jit(solution)/shard_map/ppermute | solution.py:40
  14.0 5.9 %collective-permute-start.3 = (bf16[112,128]{1,0:T(8,128)(2,1)S(1)}, bf16[112,128]{1,0:T(8,128)(2,1)S(1)}, u32[]{:S(2)}, u32[]{:S(2)}) collective-permute-start(bf16[112,128]{1,0:T(8,128)(2,1)S(1)} %get-tuple-element.46), channel_id=1, source_target_pairs={{0,16},{16,32},{32,48},{48,64},{64,80},{80,96},{96,112},{1,17},{17... | collective-permute-start | bytes 86024 | tf_op jit(solution)/shard_map/ppermute | solution.py:35
  19.9 1.9 %collective-permute-start.4 = (bf16[112,128]{1,0:T(8,128)(2,1)S(1)}, bf16[112,128]{1,0:T(8,128)(2,1)S(1)}, u32[]{:S(2)}, u32[]{:S(2)}) collective-permute-start(bf16[112,128]{1,0:T(8,128)(2,1)S(1)} %get-tuple-element.47), channel_id=1, source_target_pairs={{16,0},{32,16},{48,32},{64,48},{80,64},{96,80},{112,96},{17,1},{33... | collective-permute-start | bytes 86024 | tf_op jit(solution)/shard_map/ppermute | solution.py:35
  21.9 0.8 plan.1
  22.7 2.4 %collective-permute-done.4.south = bf16[112,128]{1,0:T(8,128)(2,1)S(1)} collective-permute-done((bf16[112,128]{1,0:T(8,128)(2,1)S(1)}, bf16[112,128]{1,0:T(8,128)(2,1)S(1)}, u32[]{:S(2)}, u32[]{:S(2)}) %collective-permute-start.4) | collective-permute-done | bytes 28704 | tf_op jit(solution)/shard_map/ppermute | solution.py:35
  25.1 2.2 %first_conv.1 = (bf16[576,1920]{1,0:T(8,128)(2,1)S(1)}, bf16[512,128]{1,0:T(8,128)(2,1)S(1)}, f32[512,128]{1,0:T(8,128)S(1)}, bf16[48,128]{1,0:T(8,128)(2,1)S(1)...) custom-call(bf16[288,160]{1,0:T(8,128)(2,1)S(1)} %get-tuple-element.40.kron, ...), custom_call_target="tpu_custom_call" | custom-call | flops 900000000 | bytes 5000000 | tf_op jit(solution)/shard_map/first_conv/pallas_call | solution.py:524
  27.3 4.1 %collective-permute-start.5 = (bf16[48,128]{1,0:T(8,128)(2,1)S(1)}, bf16[48,128]{1,0:T(8,128)(2,1)S(1)}, u32[]{:S(2)}, u32[]{:S(2)}) collective-permute-start(bf16[48,128]{1,0:T(8,128)(2,1)S(1)} %get-tuple-element.51), channel_id=1, source_target_pairs={{0,2},{2,4},{4,6},{6,8},{8,10},{10,12},{12,14},{1,3},{3,5},{5,7},{... | collective-permute-start | bytes 36872 | tf_op jit(solution)/shard_map/ppermute | solution.py:35
  31.4 1.3 %collective-permute-start.6 = (bf16[48,128]{1,0:T(8,128)(2,1)S(1)}, bf16[48,128]{1,0:T(8,128)(2,1)S(1)}, u32[]{:S(2)}, u32[]{:S(2)}) collective-permute-start(bf16[48,128]{1,0:T(8,128)(2,1)S(1)} %get-tuple-element.52), channel_id=1, source_target_pairs={{2,0},{4,2},{6,4},{8,6},{10,8},{12,10},{14,12},{3,1},{5,3},{7,5},{... | collective-permute-start | bytes 36872 | tf_op jit(solution)/shard_map/ppermute | solution.py:35
  32.7 4.6 %collective-permute-done.6.east = bf16[48,128]{1,0:T(8,128)(2,1)S(1)} collective-permute-done((bf16[48,128]{1,0:T(8,128)(2,1)S(1)}, bf16[48,128]{1,0:T(8,128)(2,1)S(1)}, u32[]{:S(2)}, u32[]{:S(2)}) %collective-permute-start.6) | collective-permute-done | bytes 12320 | tf_op jit(solution)/shard_map/ppermute | solution.py:35
  37.3 0.1 h_rows.1
  37.4 2.7 %collective-permute-start.7 = (bf16[144,128]{1,0:T(8,128)(2,1)S(1)}, bf16[144,128]{1,0:T(8,128)(2,1)S(1)}, u32[]{:S(2)}, u32[]{:S(2)}) collective-permute-start(bf16[144,128]{1,0:T(8,128)(2,1)S(1)} %get-tuple-element.54), channel_id=1, source_target_pairs={{0,1},{1,0},{16,17},{17,16},{32,33},{33,32},{48,49},{49,48},{64,65... | collective-permute-start | bytes 110600 | tf_op jit(solution)/shard_map/ppermute | solution.py:40
  40.1 1.9 %collective-permute-start.8 = (bf16[144,128]{1,0:T(8,128)(2,1)S(1)}, bf16[144,128]{1,0:T(8,128)(2,1)S(1)}, u32[]{:S(2)}, u32[]{:S(2)}) collective-permute-start(bf16[144,128]{1,0:T(8,128)(2,1)S(1)} %get-tuple-element.55), channel_id=1, source_target_pairs={{1,16},{16,1},{17,32},{32,17},{33,48},{48,33},{49,64},{64,49},{65,... | collective-permute-start | bytes 110600 | tf_op jit(solution)/shard_map/ppermute | solution.py:47
  42.1 4.8 %collective-permute-done.8.outer = bf16[144,128]{1,0:T(8,128)(2,1)S(1)} collective-permute-done((bf16[144,128]{1,0:T(8,128)(2,1)S(1)}, bf16[144,128]{1,0:T(8,128)(2,1)S(1)}, u32[]{:S(2)}, u32[]{:S(2)}) %collective-permute-start.8) | collective-permute-done | bytes 36896 | tf_op jit(solution)/shard_map/ppermute | solution.py:47
  46.9 6.8 %rest.1.both = bf16[2,6144,128]{2,1,0:T(8,128)(2,1)S(1)} custom-call(bf16[768,128]{1,0:T(8,128)(2,1)S(1)} %get-tuple-element.53.hw, bf16[144,128]{1,0:T(8,128)(2,1)S(1)} %collective-permute-done.7.inner, bf16[144,128]{1,0:T(8,128)(2,1)S(1)} %collective-permute-done.8.outer, bf16[48,128]{1,0:T(8,128)(2,1)S(1)} %collective-permute-done.5.west, ...), custom_call_target="tpu_custom_call" | custom-call | flops 3000000000 | bytes 8000000 | tf_op jit(solution)/shard_map/rest/pallas_call | solution.py:561
  53.7 0.1 slice_bitcast_fusion
  53.8 0.1 collective-permute-start.9
  53.9 3.4 %collective-permute-done.9.got = bf16[6144,128]{1,0:T(8,128)(2,1)S(1)} collective-permute-done((bf16[6144,128]{1,0:T(8,128)(2,1)S(1)}, bf16[6144,128]{1,0:T(8,128)(2,1)S(1)}, u32[]{:S(2)}, u32[]{:S(2)}) %collective-permute-start.9) | collective-permute-done | bytes 1572896 | tf_op jit(solution)/shard_map/ppermute | solution.py:682
  57.3 0.4 pair_sum.1
  57.7 34.2 %all_to_all.10.pieces = bf16[64,96,128]{2,1,0:T(8,128)(2,1)S(1)} all-to-all(bf16[64,96,128]{2,1,0:T(8,128)(2,1)S(1)} %bitcast.22), channel_id=1, replica_groups=mesh['x'=4,'core'=2,'z'=4,'yl'=2,'yh'=2] {'x','z','yl','yh'}, dimensions={0} | all-to-all | bytes 3145728 | tf_op jit(solution)/shard_map/all_to_all | solution.py:683
  91.9 0.4 spread.1
  92.4 26.5 %all_to_all.11 = bf16[64,96,128]{2,1,0:T(8,128)(2,1)S(1)} all-to-all(bf16[64,96,128]{2,1,0:T(8,128)(2,1)S(1)} %spread.1), channel_id=1, replica_groups=mesh['x'=4,'core'=2,'z'=4,'yl'=2,'yh'=2] {'x','z','yl','yh'}, dimensions={0} | all-to-all | bytes 3145728 | tf_op jit(solution)/shard_map/all_to_all | solution.py:684
  118.9 3.4 %collective-permute-start.10 = (bf16[6144,128]{1,0:T(8,128)(2,1)S(1)}, bf16[6144,128]{1,0:T(8,128)(2,1)S(1)}, u32[]{:S(2)}, u32[]{:S(2)}) collective-permute-start(bf16[6144,128]{1,0:T(8,128)(2,1)S(1)} %bitcast.20), channel_id=1, source_target_pairs={{0,16},{16,0},{1,17},{17,1},{2,18},{18,2},{3,19},{19,3},{4,20},{20... | collective-permute-start | bytes 4718600 | tf_op jit(solution)/shard_map/ppermute | solution.py:685
  122.3 1.9 %finish_own.1 = (f32[1152,128]{1,0:T(8,128)}, f32[2304,128]{1,0:T(8,128)}, f32[1152,128]{1,0:T(8,128)}, f32[128,1024]{1,0:T(8,128)}, f32[1024,512]{1,0:T(8,128)}) custom-call(bf16[6144,128]{1,0:T(8,128)(2,1)S(1)} %bitcast.21), custom_call_target="tpu_custom_call" | custom-call | flops 800000 | bytes 5000000 | tf_op jit(solution)/shard_map/finish_own/pallas_call | solution.py:617
  124.2 1.2 collective-permute-done.10.part
  125.4 2.0 %finish_other.1 = (f32[1152,128]{1,0:T(8,128)}, f32[2304,128]{1,0:T(8,128)}, f32[1152,128]{1,0:T(8,128)}, f32[128,1024]{1,0:T(8,128)}, f32[1024,512]{1,0:T(8,128)}, /*index=5*/f32[1,1]{1,0:T(1,128)}) custom-call(bf16[6144,128]{1,0:T(8,128)(2,1)S(1)} %collective-permute-done.10.part, ...), custom_call_target="tpu_custom_call", output_to_operand_aliasing={{0}: (1, {}), {1}: (2, {}), {2}: (3, {}), {3}: (4, {}), {4}... | custom-call | flops 800000 | bytes 5000000 | tf_op jit(solution)/shard_map/finish_other/pallas_call | solution.py:617
  (29 shorter events, 0.1 us)
Async XLA Ops:
  0.6 0.9 copy-start.5
  1.5 0.8 copy-start.6
  2.3 6.6 %collective-permute-start.1 = (bf16[32,128]{1,0:T(8,128)(2,1)S(1)}, bf16[32,128]{1,0:T(8,128)(2,1)S(1)}, u32[]{:S(2)}, u32[]{:S(2)}) collective-permute-start(bf16[32,128]{1,0:T(8,128)(2,1)S(1)} %get-tuple-element.44), channel_id=1, source_target_pairs={{2,0},{4,2},{6,4},{8,6},{10,8},{12,10},{14,12},{3,1},{5,3},{7,5},{... | collective-permute-start | bytes 24584 | tf_op jit(solution)/shard_map/ppermute | solution.py:35
  3.6 5.4 %collective-permute-start = (bf16[32,128]{1,0:T(8,128)(2,1)S(1)}, bf16[32,128]{1,0:T(8,128)(2,1)S(1)}, u32[]{:S(2)}, u32[]{:S(2)}) collective-permute-start(bf16[32,128]{1,0:T(8,128)(2,1)S(1)} %get-tuple-element.39.after), channel_id=1, source_target_pairs={{0,2},{2,4},{4,6},{6,8},{8,10},{10,12},{12,14},{1,3},{3,5},{5,7},{... | collective-permute-start | bytes 24584 | tf_op jit(solution)/shard_map/ppermute | solution.py:35
  9.1 3.2 %copy-start.11 = (s32[1,1,256]{2,1,0:T(1,128)S(1)}, s32[1,1,256]{2,1,0:T(1,128)}, u32[]{:S(2)}) copy-start(s32[1,1,256]{2,1,0:T(1,128)} %param.24) | copy-start | bytes 3076
  9.1 4.9 %collective-permute-start.2 = (bf16[256,128]{1,0:T(8,128)(2,1)S(1)}, bf16[256,128]{1,0:T(8,128)(2,1)S(1)}, u32[]{:S(2)}, u32[]{:S(2)}) collective-permute-start(bf16[256,128]{1,0:T(8,128)(2,1)S(1)} %edge_rows.1.mine), channel_id=1, source_target_pairs={{0,1},{1,0},{16,17},{17,16},{32,33},{33,32},{48,49},{49,48},{64,65... | collective-permute-start | bytes 196616 | tf_op jit(solution)/shard_map/ppermute | solution.py:40
  12.3 9.6 %copy-start = (bf16[3,3,512,128]{3,2,1,0:T(8,128)(2,1)S(1)}, bf16[3,3,512,128]{3,2,1,0:T(8,128)(2,1)}, u32[]{:S(2)}) copy-start(bf16[3,3,512,128]{3,2,1,0:T(8,128)(2,1)} %param.18) | copy-start | bytes 3538948
  12.3 9.6 %copy-start.2 = (bf16[3,3,128,128]{3,2,1,0:T(8,128)(2,1)S(1)}, bf16[3,3,128,128]{3,2,1,0:T(8,128)(2,1)}, u32[]{:S(2)}) copy-start(bf16[3,3,128,128]{3,2,1,0:T(8,128)(2,1)} %param.17) | copy-start | bytes 884740
  12.3 9.6 %copy-start.7 = (bf16[34,10]{0,1:T(8,128)(2,1)S(1)}, bf16[34,10]{0,1:T(8,128)(2,1)}, u32[]{:S(2)}) copy-start(bf16[34,10]{0,1:T(8,128)(2,1)} %param.15) | copy-start | bytes 2044
  12.3 9.6 %copy-start.8 = (bf16[34,10]{0,1:T(8,128)(2,1)S(1)}, bf16[34,10]{0,1:T(8,128)(2,1)}, u32[]{:S(2)}) copy-start(bf16[34,10]{0,1:T(8,128)(2,1)} %param.16) | copy-start | bytes 2044
  12.3 9.6 %copy-start.9 = (s32[1,1,256]{2,1,0:T(1,128)S(1)}, s32[1,1,256]{2,1,0:T(1,128)}, u32[]{:S(2)}) copy-start(s32[1,1,256]{2,1,0:T(1,128)} %param.22) | copy-start | bytes 3076
  12.3 9.6 %copy-start.10 = (s32[1,128]{1,0:T(1,128)S(1)}, s32[1,128]{1,0:T(1,128)}, u32[]{:S(2)}) copy-start(s32[1,128]{1,0:T(1,128)} %constant.8.ring_l) | copy-start | bytes 1540
  14.0 8.7 %collective-permute-start.3 = (bf16[112,128]{1,0:T(8,128)(2,1)S(1)}, bf16[112,128]{1,0:T(8,128)(2,1)S(1)}, u32[]{:S(2)}, u32[]{:S(2)}) collective-permute-start(bf16[112,128]{1,0:T(8,128)(2,1)S(1)} %get-tuple-element.46), channel_id=1, source_target_pairs={{0,16},{16,32},{32,48},{48,64},{64,80},{80,96},{96,112},{1,17},{17... | collective-permute-start | bytes 86024 | tf_op jit(solution)/shard_map/ppermute | solution.py:35
  19.9 5.2 %collective-permute-start.4 = (bf16[112,128]{1,0:T(8,128)(2,1)S(1)}, bf16[112,128]{1,0:T(8,128)(2,1)S(1)}, u32[]{:S(2)}, u32[]{:S(2)}) collective-permute-start(bf16[112,128]{1,0:T(8,128)(2,1)S(1)} %get-tuple-element.47), channel_id=1, source_target_pairs={{16,0},{32,16},{48,32},{64,48},{80,64},{96,80},{112,96},{17,1},{33... | collective-permute-start | bytes 86024 | tf_op jit(solution)/shard_map/ppermute | solution.py:35
  27.3 5.4 %collective-permute-start.5 = (bf16[48,128]{1,0:T(8,128)(2,1)S(1)}, bf16[48,128]{1,0:T(8,128)(2,1)S(1)}, u32[]{:S(2)}, u32[]{:S(2)}) collective-permute-start(bf16[48,128]{1,0:T(8,128)(2,1)S(1)} %get-tuple-element.51), channel_id=1, source_target_pairs={{0,2},{2,4},{4,6},{6,8},{8,10},{10,12},{12,14},{1,3},{3,5},{5,7},{... | collective-permute-start | bytes 36872 | tf_op jit(solution)/shard_map/ppermute | solution.py:35
  31.4 5.9 %collective-permute-start.6 = (bf16[48,128]{1,0:T(8,128)(2,1)S(1)}, bf16[48,128]{1,0:T(8,128)(2,1)S(1)}, u32[]{:S(2)}, u32[]{:S(2)}) collective-permute-start(bf16[48,128]{1,0:T(8,128)(2,1)S(1)} %get-tuple-element.52), channel_id=1, source_target_pairs={{2,0},{4,2},{6,4},{8,6},{10,8},{12,10},{14,12},{3,1},{5,3},{7,5},{... | collective-permute-start | bytes 36872 | tf_op jit(solution)/shard_map/ppermute | solution.py:35
  37.3 9.6 %copy-start.1 = (bf16[1024,512]{1,0:T(8,128)(2,1)S(1)}, bf16[1024,512]{1,0:T(8,128)(2,1)}, u32[]{:S(2)}) copy-start(bf16[1024,512]{1,0:T(8,128)(2,1)} %binw.1) | copy-start | bytes 3145732
  37.3 9.6 %copy-start.3 = (bf16[3,3,128,128]{3,2,1,0:T(8,128)(2,1)S(1)}, bf16[3,3,128,128]{3,2,1,0:T(8,128)(2,1)}, u32[]{:S(2)}) copy-start(bf16[3,3,128,128]{3,2,1,0:T(8,128)(2,1)} %param.19) | copy-start | bytes 884740
  37.3 9.6 %copy-start.4 = (bf16[128,1024]{1,0:T(8,128)(2,1)S(1)}, bf16[128,1024]{1,0:T(8,128)(2,1)}, u32[]{:S(2)}) copy-start(bf16[128,1024]{1,0:T(8,128)(2,1)} %hid.1) | copy-start | bytes 786436
  37.4 4.6 %collective-permute-start.7 = (bf16[144,128]{1,0:T(8,128)(2,1)S(1)}, bf16[144,128]{1,0:T(8,128)(2,1)S(1)}, u32[]{:S(2)}, u32[]{:S(2)}) collective-permute-start(bf16[144,128]{1,0:T(8,128)(2,1)S(1)} %get-tuple-element.54), channel_id=1, source_target_pairs={{0,1},{1,0},{16,17},{17,16},{32,33},{33,32},{48,49},{49,48},{64,65... | collective-permute-start | bytes 110600 | tf_op jit(solution)/shard_map/ppermute | solution.py:40
  40.1 6.8 %collective-permute-start.8 = (bf16[144,128]{1,0:T(8,128)(2,1)S(1)}, bf16[144,128]{1,0:T(8,128)(2,1)S(1)}, u32[]{:S(2)}, u32[]{:S(2)}) collective-permute-start(bf16[144,128]{1,0:T(8,128)(2,1)S(1)} %get-tuple-element.55), channel_id=1, source_target_pairs={{1,16},{16,1},{17,32},{32,17},{33,48},{48,33},{49,64},{64,49},{65,... | collective-permute-start | bytes 110600 | tf_op jit(solution)/shard_map/ppermute | solution.py:47
  53.8 3.5 %collective-permute-start.9 = (bf16[6144,128]{1,0:T(8,128)(2,1)S(1)}, bf16[6144,128]{1,0:T(8,128)(2,1)S(1)}, u32[]{:S(2)}, u32[]{:S(2)}) collective-permute-start(bf16[6144,128]{1,0:T(8,128)(2,1)S(1)} %slice_bitcast_fusion), channel_id=1, source_target_pairs={{0,16},{16,0},{1,17},{17,1},{2,18},{18,2},{3,19},{19,3},{4,20},{20... | collective-permute-start | bytes 4718600 | tf_op jit(solution)/shard_map/ppermute | solution.py:682
  118.9 6.4 %collective-permute-start.10 = (bf16[6144,128]{1,0:T(8,128)(2,1)S(1)}, bf16[6144,128]{1,0:T(8,128)(2,1)S(1)}, u32[]{:S(2)}, u32[]{:S(2)}) collective-permute-start(bf16[6144,128]{1,0:T(8,128)(2,1)S(1)} %bitcast.20), channel_id=1, source_target_pairs={{0,16},{16,0},{1,17},{17,1},{2,18},{18,2},{3,19},{19,3},{4,20},{20... | collective-permute-start | bytes 4718600 | tf_op jit(solution)/shard_map/ppermute | solution.py:685

commit v10 on v9

--- a/solution.py
+++ b/solution.py
@@ -151,7 +151,8 @@
 
 
 def plan_kernel(
-    rows_in, cols_in, idx_l, ring_l, lab_l, w_fine, w_ctx, after, kron, left, digs, pick, back, labs, wide, rmat, cmat
+    rows_in, cols_in, idx_l, ring_l, lab_l, w_fine, w_ctx, cw, after,
+    kron, left, digs, pick, back, labs, wide, forth, flipped, rmat, cmat,
 ):
     half = lax.axis_index("yh")
     row0 = (2 * lax.axis_index("x") + lax.axis_index("core")) * 32
@@ -189,6 +190,10 @@
         lanes = slice(128 * dy, 128 * dy + 128)
         wide[0:384, lanes] = w_fine[384 * dy : 384 * dy + 384, :]
         wide[384:, lanes] = w_ctx[1536 * dy : 1536 * dy + 1536, :]
+        forth[:, lanes] = cw[384 * dy : 384 * dy + 384, :]
+        for dx in range(3):
+            tap = cw[384 * dy + 128 * dx : 384 * dy + 128 * dx + 128, :]
+            flipped[lanes, 128 * dx : 128 * dx + 128] = tap
 
 
 def first_conv_kernel(
@@ -268,7 +273,7 @@
 
 
 def rest_kernel(
-    hw, inner, outer, west, east, xc, sg1, pick, back, labs_s, cw, hid, binw,
+    hw, inner, outer, west, east, xc, sg1, pick, back, labs_s, forth, flipped, hid, binw,
     out,
     hp, hx, sg2, h2, rows_s, act, sgz, dl, dz, gscr, gx, g2w, g1w, pre, spot,
 ):
@@ -291,8 +296,7 @@
     code = jnp.sum(jnp.where(lane == 0, 32.0 * code, jnp.where(lane == 1, code, 0.0)), axis=1, keepdims=True)
     for dx in range(3):
         hx[:, 128 * dx : 128 * dx + 128] = hp[dx : dx + 992, :].astype(BF)
-    forth = jnp.concatenate([cw[384 * dy : 384 * dy + 384, :] for dy in range(3)], axis=1)
-    pre[...] = dot(hx[...], forth)
+    pre[...] = dot(hx[...], forth[...])
     acc = sum(pre[WIDE * dy : WIDE * dy + EXT, 128 * dy : 128 * dy + 128] for dy in range(3))
     s = jax.nn.sigmoid(acc)
     h2[...] = (acc * s).astype(BF)
@@ -350,11 +354,7 @@
             at = WIDE * i + 2 - dx
             hx[32 * i : 32 * i + 32, 128 * dx : 128 * dx + 128] = gx[at : at + 32, :].astype(BF)
     g1w[...] = jnp.zeros_like(g1w)
-    flipped = [
-        jnp.concatenate([cw[384 * dy + 128 * dx : 384 * dy + 128 * dx + 128, :] for dx in range(3)], axis=1)
-        for dy in range(3)
-    ]
-    pre[0:576, :] = dot_t(hx[0:576, :], jnp.concatenate(flipped, axis=0))
+    pre[0:576, :] = dot_t(hx[0:576, :], flipped[...])
     acc = sum(pre[64 - 32 * dy : 576 - 32 * dy, 128 * dy : 128 * dy + 128] for dy in range(3))
     g1 = (acc * sg1[...]).astype(BF)
     for dy in range(3):
@@ -508,9 +508,9 @@
     shapes = [((288, 160), BF), ((96, 16), BF), ((512, C), BF), ((SLOTS, EXT), BF), ((EXT, SLOTS), BF)]
     return pl.pallas_call(
         plan_kernel,
-        out_shape=tuple(sds(*s) for s in shapes) + (sds((CAP, 1), jnp.int32), sds((1920, 384), BF)),
+        out_shape=tuple(sds(*s) for s in shapes) + (sds((CAP, 1), jnp.int32), sds((1920, 384), BF)) + (sds((384, 384), BF),) * 2,
         in_specs=vmem(len(args)),
-        out_specs=tuple(vmem(7)),
+        out_specs=tuple(vmem(9)),
         scratch_shapes=[pltpu.VMEM((16, C), F32), pltpu.VMEM((16, C), F32)],
         compiler_params=limit(12),
         cost_estimate=BUSY,
@@ -655,9 +655,9 @@
     last, first, fine, context = edge_cols(fine.reshape(512, C), context.reshape(64, HALF))
     east = shift(first, GX, 8, -1)
     west = shift(last, GX, 8, 1)
-    kron, left, dig, pick, back, labs, weights = plan(
+    kron, left, dig, pick, back, labs, weights, forth, flipped = plan(
         interp_rows.T, interp_cols.T, idx, ring[None, :], lab,
-        fine_weight.reshape(1152, C), ctx_weight.reshape(4608, C), last,
+        fine_weight.reshape(1152, C), ctx_weight.reshape(4608, C), conv_weight.reshape(1152, C), last,
     )
     mine = edge_rows(fine, context, west, east)
     inner = side_swap(mine)
@@ -675,7 +675,7 @@
     inner = side_swap(inner)
     both = rest(
         wide, inner, outer, west, east, xc, sg1, pick, back, labs,
-        conv_weight.reshape(1152, C), hidden_weight, bin_weight,
+        forth, flipped, hidden_weight, bin_weight,
     )
 
     flip = [(0, 1), (1, 0)]

time: 128 us -> 128 us (level)
  no operation moved by 1% of the time
where the time goes in v10:
time: 128 us; the launch traced here: 127 us
  blocking collectives  60.8 us (48%)
  starting transfers between devices  30.4 us (24%)
  waiting for transfers between devices  18.1 us (14%)
  Pallas kernels  14.6 us (11%)
  local copies, waits for them, and re-layouts  1.81 us (1%)
  between operations  1.71 us (1%)
    all_to_all x1, blocking collectives, local(): lax.all_to_all(pair.reshape(PEERS, SHARD, C), PLANE, 0, 0, tiled=True)  34.2 us
    all_to_all x1, blocking collectives, local(): lax.all_to_all(spread(pieces), PLANE, 0, 0, tiled=True).reshape(KEEP, C)  26.6 us
    ppermute x6, starting transfers between devices, shift(): return lax.ppermute(x, axis, pairs)  19.2 us
    ppermute x6, waiting for transfers between devices, shift(): return lax.ppermute(x, axis, pairs)  7.02 us
    pallas_call x1, Pallas kernels, rest(): pl.pallas_call(rest_kernel, out_shape=sds((2, KEEP, C), BF), in_specs=vme...  6.77 us
    ppermute x2, starting transfers between devices, side_swap(): return lax.ppermute(x, TALL, own)  5.85 us
    ppermute x1, waiting for transfers between devices, outer_swap(): return lax.ppermute(x, TALL, pairs)  4.84 us
    pallas_call x2, Pallas kernels, finish(): pl.pallas_call(functools.partial(finish_kernel, second), out_shape=tuple(...  3.83 us
  transfers between devices with their start and end apart: 11, of which 7 were waited for; matrix products, arithmetic and copies ran while one was open for 0% of the time, Pallas kernels for 2%

profile of v10, /device:TPU:1, one launch (start us, length us, event | category | flops | bytes accessed | tf_op | source)
XLA Modules:
  0.0 127.5 jit_solution(8049126637165244758)
XLA Ops:
  0.6 0.9 copy-done.5
  1.5 0.8 copy-done.6
  2.3 1.3 %collective-permute-start.1 = (bf16[32,128]{1,0:T(8,128)(2,1)S(1)}, bf16[32,128]{1,0:T(8,128)(2,1)S(1)}, u32[]{:S(2)}, u32[]{:S(2)}) collective-permute-start(bf16[32,128]{1,0:T(8,128)(2,1)S(1)} %get-tuple-element.46), channel_id=1, source_target_pairs={{2,0},{4,2},{6,4},{8,6},{10,8},{12,10},{14,12},{3,1},{5,3},{7,5},{... | collective-permute-start | bytes 24584 | tf_op jit(solution)/shard_map/ppermute | solution.py:35
  3.6 4.7 %collective-permute-start = (bf16[32,128]{1,0:T(8,128)(2,1)S(1)}, bf16[32,128]{1,0:T(8,128)(2,1)S(1)}, u32[]{:S(2)}, u32[]{:S(2)}) collective-permute-start(bf16[32,128]{1,0:T(8,128)(2,1)S(1)} %get-tuple-element.41.after), channel_id=1, source_target_pairs={{0,2},{2,4},{4,6},{6,8},{8,10},{10,12},{12,14},{1,3},{3,5},{5,7},{... | collective-permute-start | bytes 24584 | tf_op jit(solution)/shard_map/ppermute | solution.py:35
  9.0 0.1 collective-permute-done.west
  9.1 3.2 %collective-permute-start.2 = (bf16[256,128]{1,0:T(8,128)(2,1)S(1)}, bf16[256,128]{1,0:T(8,128)(2,1)S(1)}, u32[]{:S(2)}, u32[]{:S(2)}) collective-permute-start(bf16[256,128]{1,0:T(8,128)(2,1)S(1)} %edge_rows.1.mine), channel_id=1, source_target_pairs={{0,1},{1,0},{16,17},{17,16},{32,33},{33,32},{48,49},{49,48},{64,65... | collective-permute-start | bytes 196616 | tf_op jit(solution)/shard_map/ppermute | solution.py:40
  12.3 0.0 copy-start.10
  12.3 1.7 %collective-permute-done.2.inner = bf16[256,128]{1,0:T(8,128)(2,1)S(1)} collective-permute-done((bf16[256,128]{1,0:T(8,128)(2,1)S(1)}, bf16[256,128]{1,0:T(8,128)(2,1)S(1)}, u32[]{:S(2)}, u32[]{:S(2)}) %collective-permute-start.2) | collective-permute-done | bytes 65568 | tf_op jit(solution)/shard_map/ppermute | solution.py:40
  14.0 5.9 %collective-permute-start.3 = (bf16[112,128]{1,0:T(8,128)(2,1)S(1)}, bf16[112,128]{1,0:T(8,128)(2,1)S(1)}, u32[]{:S(2)}, u32[]{:S(2)}) collective-permute-start(bf16[112,128]{1,0:T(8,128)(2,1)S(1)} %get-tuple-element.48), channel_id=1, source_target_pairs={{0,16},{16,32},{32,48},{48,64},{64,80},{80,96},{96,112},{1,17},{17... | collective-permute-start | bytes 86024 | tf_op jit(solution)/shard_map/ppermute | solution.py:35
  19.9 1.9 %collective-permute-start.4 = (bf16[112,128]{1,0:T(8,128)(2,1)S(1)}, bf16[112,128]{1,0:T(8,128)(2,1)S(1)}, u32[]{:S(2)}, u32[]{:S(2)}) collective-permute-start(bf16[112,128]{1,0:T(8,128)(2,1)S(1)} %get-tuple-element.49), channel_id=1, source_target_pairs={{16,0},{32,16},{48,32},{64,48},{80,64},{96,80},{112,96},{17,1},{33... | collective-permute-start | bytes 86024 | tf_op jit(solution)/shard_map/ppermute | solution.py:35
  21.9 0.9 plan.1
  22.8 2.3 %collective-permute-done.4.south = bf16[112,128]{1,0:T(8,128)(2,1)S(1)} collective-permute-done((bf16[112,128]{1,0:T(8,128)(2,1)S(1)}, bf16[112,128]{1,0:T(8,128)(2,1)S(1)}, u32[]{:S(2)}, u32[]{:S(2)}) %collective-permute-start.4) | collective-permute-done | bytes 28704 | tf_op jit(solution)/shard_map/ppermute | solution.py:35
  25.1 2.2 %first_conv.1 = (bf16[576,1920]{1,0:T(8,128)(2,1)S(1)}, bf16[512,128]{1,0:T(8,128)(2,1)S(1)}, f32[512,128]{1,0:T(8,128)S(1)}, bf16[48,128]{1,0:T(8,128)(2,1)S(1)...) custom-call(bf16[288,160]{1,0:T(8,128)(2,1)S(1)} %get-tuple-element.42.kron, ...), custom_call_target="tpu_custom_call" | custom-call | flops 900000000 | bytes 5000000 | tf_op jit(solution)/shard_map/first_conv/pallas_call | solution.py:524
  27.3 4.1 %collective-permute-start.5 = (bf16[48,128]{1,0:T(8,128)(2,1)S(1)}, bf16[48,128]{1,0:T(8,128)(2,1)S(1)}, u32[]{:S(2)}, u32[]{:S(2)}) collective-permute-start(bf16[48,128]{1,0:T(8,128)(2,1)S(1)} %get-tuple-element.53), channel_id=1, source_target_pairs={{0,2},{2,4},{4,6},{6,8},{8,10},{10,12},{12,14},{1,3},{3,5},{5,7},{... | collective-permute-start | bytes 36872 | tf_op jit(solution)/shard_map/ppermute | solution.py:35
  31.4 1.3 %collective-permute-start.6 = (bf16[48,128]{1,0:T(8,128)(2,1)S(1)}, bf16[48,128]{1,0:T(8,128)(2,1)S(1)}, u32[]{:S(2)}, u32[]{:S(2)}) collective-permute-start(bf16[48,128]{1,0:T(8,128)(2,1)S(1)} %get-tuple-element.54), channel_id=1, source_target_pairs={{2,0},{4,2},{6,4},{8,6},{10,8},{12,10},{14,12},{3,1},{5,3},{7,5},{... | collective-permute-start | bytes 36872 | tf_op jit(solution)/shard_map/ppermute | solution.py:35
  32.8 4.6 %collective-permute-done.6.east = bf16[48,128]{1,0:T(8,128)(2,1)S(1)} collective-permute-done((bf16[48,128]{1,0:T(8,128)(2,1)S(1)}, bf16[48,128]{1,0:T(8,128)(2,1)S(1)}, u32[]{:S(2)}, u32[]{:S(2)}) %collective-permute-start.6) | collective-permute-done | bytes 12320 | tf_op jit(solution)/shard_map/ppermute | solution.py:35
  37.3 0.1 h_rows.1
  37.4 2.7 %collective-permute-start.7 = (bf16[144,128]{1,0:T(8,128)(2,1)S(1)}, bf16[144,128]{1,0:T(8,128)(2,1)S(1)}, u32[]{:S(2)}, u32[]{:S(2)}) collective-permute-start(bf16[144,128]{1,0:T(8,128)(2,1)S(1)} %get-tuple-element.56), channel_id=1, source_target_pairs={{0,1},{1,0},{16,17},{17,16},{32,33},{33,32},{48,49},{49,48},{64,65... | collective-permute-start | bytes 110600 | tf_op jit(solution)/shard_map/ppermute | solution.py:40
  40.1 1.9 %collective-permute-start.8 = (bf16[144,128]{1,0:T(8,128)(2,1)S(1)}, bf16[144,128]{1,0:T(8,128)(2,1)S(1)}, u32[]{:S(2)}, u32[]{:S(2)}) collective-permute-start(bf16[144,128]{1,0:T(8,128)(2,1)S(1)} %get-tuple-element.57), channel_id=1, source_target_pairs={{1,16},{16,1},{17,32},{32,17},{33,48},{48,33},{49,64},{64,49},{65,... | collective-permute-start | bytes 110600 | tf_op jit(solution)/shard_map/ppermute | solution.py:47
  42.1 4.8 %collective-permute-done.8.outer = bf16[144,128]{1,0:T(8,128)(2,1)S(1)} collective-permute-done((bf16[144,128]{1,0:T(8,128)(2,1)S(1)}, bf16[144,128]{1,0:T(8,128)(2,1)S(1)}, u32[]{:S(2)}, u32[]{:S(2)}) %collective-permute-start.8) | collective-permute-done | bytes 36896 | tf_op jit(solution)/shard_map/ppermute | solution.py:47
  46.9 6.8 %rest.1.both = bf16[2,6144,128]{2,1,0:T(8,128)(2,1)S(1)} custom-call(bf16[768,128]{1,0:T(8,128)(2,1)S(1)} %get-tuple-element.55.hw, bf16[144,128]{1,0:T(8,128)(2,1)S(1)} %collective-permute-done.7.inner, bf16[144,128]{1,0:T(8,128)(2,1)S(1)} %collective-permute-done.8.outer, bf16[48,128]{1,0:T(8,128)(2,1)S(1)} %collective-permute-done.5.west, ...), custom_call_target="tpu_custom_call" | custom-call | flops 3000000000 | bytes 8000000 | tf_op jit(solution)/shard_map/rest/pallas_call | solution.py:561
  53.7 0.1 slice_bitcast_fusion
  53.8 0.1 collective-permute-start.9
  53.9 3.4 %collective-permute-done.9.got = bf16[6144,128]{1,0:T(8,128)(2,1)S(1)} collective-permute-done((bf16[6144,128]{1,0:T(8,128)(2,1)S(1)}, bf16[6144,128]{1,0:T(8,128)(2,1)S(1)}, u32[]{:S(2)}, u32[]{:S(2)}) %collective-permute-start.9) | collective-permute-done | bytes 1572896 | tf_op jit(solution)/shard_map/ppermute | solution.py:682
  57.3 0.4 pair_sum.1
  57.7 34.2 %all_to_all.10.pieces = bf16[64,96,128]{2,1,0:T(8,128)(2,1)S(1)} all-to-all(bf16[64,96,128]{2,1,0:T(8,128)(2,1)S(1)} %bitcast.22), channel_id=1, replica_groups=mesh['x'=4,'core'=2,'z'=4,'yl'=2,'yh'=2] {'x','z','yl','yh'}, dimensions={0} | all-to-all | bytes 3145728 | tf_op jit(solution)/shard_map/all_to_all | solution.py:683
  91.9 0.4 spread.1
  92.3 26.6 %all_to_all.11 = bf16[64,96,128]{2,1,0:T(8,128)(2,1)S(1)} all-to-all(bf16[64,96,128]{2,1,0:T(8,128)(2,1)S(1)} %spread.1), channel_id=1, replica_groups=mesh['x'=4,'core'=2,'z'=4,'yl'=2,'yh'=2] {'x','z','yl','yh'}, dimensions={0} | all-to-all | bytes 3145728 | tf_op jit(solution)/shard_map/all_to_all | solution.py:684
  118.9 3.4 %collective-permute-start.10 = (bf16[6144,128]{1,0:T(8,128)(2,1)S(1)}, bf16[6144,128]{1,0:T(8,128)(2,1)S(1)}, u32[]{:S(2)}, u32[]{:S(2)}) collective-permute-start(bf16[6144,128]{1,0:T(8,128)(2,1)S(1)} %bitcast.20), channel_id=1, source_target_pairs={{0,16},{16,0},{1,17},{17,1},{2,18},{18,2},{3,19},{19,3},{4,20},{20... | collective-permute-start | bytes 4718600 | tf_op jit(solution)/shard_map/ppermute | solution.py:685
  122.3 1.9 %finish_own.1 = (f32[1152,128]{1,0:T(8,128)}, f32[2304,128]{1,0:T(8,128)}, f32[1152,128]{1,0:T(8,128)}, f32[128,1024]{1,0:T(8,128)}, f32[1024,512]{1,0:T(8,128)}) custom-call(bf16[6144,128]{1,0:T(8,128)(2,1)S(1)} %bitcast.21), custom_call_target="tpu_custom_call" | custom-call | flops 800000 | bytes 5000000 | tf_op jit(solution)/shard_map/finish_own/pallas_call | solution.py:617
  124.2 1.2 collective-permute-done.10.part
  125.3 2.0 %finish_other.1 = (f32[1152,128]{1,0:T(8,128)}, f32[2304,128]{1,0:T(8,128)}, f32[1152,128]{1,0:T(8,128)}, f32[128,1024]{1,0:T(8,128)}, f32[1024,512]{1,0:T(8,128)}, /*index=5*/f32[1,1]{1,0:T(1,128)}) custom-call(bf16[6144,128]{1,0:T(8,128)(2,1)S(1)} %collective-permute-done.10.part, ...), custom_call_target="tpu_custom_call", output_to_operand_aliasing={{0}: (1, {}), {1}: (2, {}), {2}: (3, {}), {3}: (4, {}), {4}... | custom-call | flops 800000 | bytes 5000000 | tf_op jit(solution)/shard_map/finish_other/pallas_call | solution.py:617
  (29 shorter events, 0.1 us)
Async XLA Ops:
  0.6 0.9 copy-start.5
  1.5 0.8 copy-start.6
  2.3 6.6 %collective-permute-start.1 = (bf16[32,128]{1,0:T(8,128)(2,1)S(1)}, bf16[32,128]{1,0:T(8,128)(2,1)S(1)}, u32[]{:S(2)}, u32[]{:S(2)}) collective-permute-start(bf16[32,128]{1,0:T(8,128)(2,1)S(1)} %get-tuple-element.46), channel_id=1, source_target_pairs={{2,0},{4,2},{6,4},{8,6},{10,8},{12,10},{14,12},{3,1},{5,3},{7,5},{... | collective-permute-start | bytes 24584 | tf_op jit(solution)/shard_map/ppermute | solution.py:35
  3.6 5.4 %collective-permute-start = (bf16[32,128]{1,0:T(8,128)(2,1)S(1)}, bf16[32,128]{1,0:T(8,128)(2,1)S(1)}, u32[]{:S(2)}, u32[]{:S(2)}) collective-permute-start(bf16[32,128]{1,0:T(8,128)(2,1)S(1)} %get-tuple-element.41.after), channel_id=1, source_target_pairs={{0,2},{2,4},{4,6},{6,8},{8,10},{10,12},{12,14},{1,3},{3,5},{5,7},{... | collective-permute-start | bytes 24584 | tf_op jit(solution)/shard_map/ppermute | solution.py:35
  9.1 3.2 %copy-start.11 = (s32[1,1,256]{2,1,0:T(1,128)S(1)}, s32[1,1,256]{2,1,0:T(1,128)}, u32[]{:S(2)}) copy-start(s32[1,1,256]{2,1,0:T(1,128)} %param.24) | copy-start | bytes 3076
  9.1 4.9 %collective-permute-start.2 = (bf16[256,128]{1,0:T(8,128)(2,1)S(1)}, bf16[256,128]{1,0:T(8,128)(2,1)S(1)}, u32[]{:S(2)}, u32[]{:S(2)}) collective-permute-start(bf16[256,128]{1,0:T(8,128)(2,1)S(1)} %edge_rows.1.mine), channel_id=1, source_target_pairs={{0,1},{1,0},{16,17},{17,16},{32,33},{33,32},{48,49},{49,48},{64,65... | collective-permute-start | bytes 196616 | tf_op jit(solution)/shard_map/ppermute | solution.py:40
  12.3 9.6 %copy-start = (bf16[3,3,512,128]{3,2,1,0:T(8,128)(2,1)S(1)}, bf16[3,3,512,128]{3,2,1,0:T(8,128)(2,1)}, u32[]{:S(2)}) copy-start(bf16[3,3,512,128]{3,2,1,0:T(8,128)(2,1)} %param.18) | copy-start | bytes 3538948
  12.3 9.6 %copy-start.2 = (bf16[3,3,128,128]{3,2,1,0:T(8,128)(2,1)S(1)}, bf16[3,3,128,128]{3,2,1,0:T(8,128)(2,1)}, u32[]{:S(2)}) copy-start(bf16[3,3,128,128]{3,2,1,0:T(8,128)(2,1)} %param.17) | copy-start | bytes 884740
  12.3 9.6 %copy-start.3 = (bf16[3,3,128,128]{3,2,1,0:T(8,128)(2,1)S(1)}, bf16[3,3,128,128]{3,2,1,0:T(8,128)(2,1)}, u32[]{:S(2)}) copy-start(bf16[3,3,128,128]{3,2,1,0:T(8,128)(2,1)} %param.19) | copy-start | bytes 884740
  12.3 9.6 %copy-start.7 = (bf16[34,10]{0,1:T(8,128)(2,1)S(1)}, bf16[34,10]{0,1:T(8,128)(2,1)}, u32[]{:S(2)}) copy-start(bf16[34,10]{0,1:T(8,128)(2,1)} %param.15) | copy-start | bytes 2044
  12.3 9.6 %copy-start.8 = (bf16[34,10]{0,1:T(8,128)(2,1)S(1)}, bf16[34,10]{0,1:T(8,128)(2,1)}, u32[]{:S(2)}) copy-start(bf16[34,10]{0,1:T(8,128)(2,1)} %param.16) | copy-start | bytes 2044
  12.3 9.6 %copy-start.9 = (s32[1,1,256]{2,1,0:T(1,128)S(1)}, s32[1,1,256]{2,1,0:T(1,128)}, u32[]{:S(2)}) copy-start(s32[1,1,256]{2,1,0:T(1,128)} %param.22) | copy-start | bytes 3076
  12.3 9.6 %copy-start.10 = (s32[1,128]{1,0:T(1,128)S(1)}, s32[1,128]{1,0:T(1,128)}, u32[]{:S(2)}) copy-start(s32[1,128]{1,0:T(1,128)} %constant.8.ring_l) | copy-start | bytes 1540
  14.0 8.8 %collective-permute-start.3 = (bf16[112,128]{1,0:T(8,128)(2,1)S(1)}, bf16[112,128]{1,0:T(8,128)(2,1)S(1)}, u32[]{:S(2)}, u32[]{:S(2)}) collective-permute-start(bf16[112,128]{1,0:T(8,128)(2,1)S(1)} %get-tuple-element.48), channel_id=1, source_target_pairs={{0,16},{16,32},{32,48},{48,64},{64,80},{80,96},{96,112},{1,17},{17... | collective-permute-start | bytes 86024 | tf_op jit(solution)/shard_map/ppermute | solution.py:35
  19.9 5.2 %collective-permute-start.4 = (bf16[112,128]{1,0:T(8,128)(2,1)S(1)}, bf16[112,128]{1,0:T(8,128)(2,1)S(1)}, u32[]{:S(2)}, u32[]{:S(2)}) collective-permute-start(bf16[112,128]{1,0:T(8,128)(2,1)S(1)} %get-tuple-element.49), channel_id=1, source_target_pairs={{16,0},{32,16},{48,32},{64,48},{80,64},{96,80},{112,96},{17,1},{33... | collective-permute-start | bytes 86024 | tf_op jit(solution)/shard_map/ppermute | solution.py:35
  27.3 5.4 %collective-permute-start.5 = (bf16[48,128]{1,0:T(8,128)(2,1)S(1)}, bf16[48,128]{1,0:T(8,128)(2,1)S(1)}, u32[]{:S(2)}, u32[]{:S(2)}) collective-permute-start(bf16[48,128]{1,0:T(8,128)(2,1)S(1)} %get-tuple-element.53), channel_id=1, source_target_pairs={{0,2},{2,4},{4,6},{6,8},{8,10},{10,12},{12,14},{1,3},{3,5},{5,7},{... | collective-permute-start | bytes 36872 | tf_op jit(solution)/shard_map/ppermute | solution.py:35
  31.4 5.9 %collective-permute-start.6 = (bf16[48,128]{1,0:T(8,128)(2,1)S(1)}, bf16[48,128]{1,0:T(8,128)(2,1)S(1)}, u32[]{:S(2)}, u32[]{:S(2)}) collective-permute-start(bf16[48,128]{1,0:T(8,128)(2,1)S(1)} %get-tuple-element.54), channel_id=1, source_target_pairs={{2,0},{4,2},{6,4},{8,6},{10,8},{12,10},{14,12},{3,1},{5,3},{7,5},{... | collective-permute-start | bytes 36872 | tf_op jit(solution)/shard_map/ppermute | solution.py:35
  37.3 9.6 %copy-start.1 = (bf16[1024,512]{1,0:T(8,128)(2,1)S(1)}, bf16[1024,512]{1,0:T(8,128)(2,1)}, u32[]{:S(2)}) copy-start(bf16[1024,512]{1,0:T(8,128)(2,1)} %binw.1) | copy-start | bytes 3145732
  37.3 9.6 %copy-start.4 = (bf16[128,1024]{1,0:T(8,128)(2,1)S(1)}, bf16[128,1024]{1,0:T(8,128)(2,1)}, u32[]{:S(2)}) copy-start(bf16[128,1024]{1,0:T(8,128)(2,1)} %hid.1) | copy-start | bytes 786436
  37.4 4.6 %collective-permute-start.7 = (bf16[144,128]{1,0:T(8,128)(2,1)S(1)}, bf16[144,128]{1,0:T(8,128)(2,1)S(1)}, u32[]{:S(2)}, u32[]{:S(2)}) collective-permute-start(bf16[144,128]{1,0:T(8,128)(2,1)S(1)} %get-tuple-element.56), channel_id=1, source_target_pairs={{0,1},{1,0},{16,17},{17,16},{32,33},{33,32},{48,49},{49,48},{64,65... | collective-permute-start | bytes 110600 | tf_op jit(solution)/shard_map/ppermute | solution.py:40
  40.1 6.8 %collective-permute-start.8 = (bf16[144,128]{1,0:T(8,128)(2,1)S(1)}, bf16[144,128]{1,0:T(8,128)(2,1)S(1)}, u32[]{:S(2)}, u32[]{:S(2)}) collective-permute-start(bf16[144,128]{1,0:T(8,128)(2,1)S(1)} %get-tuple-element.57), channel_id=1, source_target_pairs={{1,16},{16,1},{17,32},{32,17},{33,48},{48,33},{49,64},{64,49},{65,... | collective-permute-start | bytes 110600 | tf_op jit(solution)/shard_map/ppermute | solution.py:47
  53.8 3.5 %collective-permute-start.9 = (bf16[6144,128]{1,0:T(8,128)(2,1)S(1)}, bf16[6144,128]{1,0:T(8,128)(2,1)S(1)}, u32[]{:S(2)}, u32[]{:S(2)}) collective-permute-start(bf16[6144,128]{1,0:T(8,128)(2,1)S(1)} %slice_bitcast_fusion), channel_id=1, source_target_pairs={{0,16},{16,0},{1,17},{17,1},{2,18},{18,2},{3,19},{19,3},{4,20},{20... | collective-permute-start | bytes 4718600 | tf_op jit(solution)/shard_map/ppermute | solution.py:682
  118.9 6.4 %collective-permute-start.10 = (bf16[6144,128]{1,0:T(8,128)(2,1)S(1)}, bf16[6144,128]{1,0:T(8,128)(2,1)S(1)}, u32[]{:S(2)}, u32[]{:S(2)}) collective-permute-start(bf16[6144,128]{1,0:T(8,128)(2,1)S(1)} %bitcast.20), channel_id=1, source_target_pairs={{0,16},{16,0},{1,17},{17,1},{2,18},{18,2},{3,19},{19,3},{4,20},{20... | collective-permute-start | bytes 4718600 | tf_op jit(solution)/shard_map/ppermute | solution.py:685
